TPU v7x, 32 devices: a whole 2x2x4 slice. The times are simulated.
32 devices in a mesh: cfg: 1, gz: 32 (over z, y, x, core).
Axes of the slice: x: 2, y: 2, z: 4, core: 2. Of those that a mesh axis runs over, the one named last changes fastest.
Arguments:
- adjoint: float32 [128, 2, 3, 8, 128], P(('cfg', 'gz')), may hold values from -6 to 6
- flowed: float32 [128, 3, 4, 2, 3, 3, 128], P(('cfg', 'gz')), may hold values from -2.5 to 2.5
- source_slice: int32 [1], P('cfg'), may hold values from 12 to 19
- band_width: int32 [1], P('cfg'), may hold values from 8 to 15
- flow_steps: int32 [1], P('cfg'), may hold values from 1 to 4
Outputs:
- pulled_back: float32 [128, 2, 3, 8, 128], P(('cfg', 'gz'))
All inputs are finite; a program needn't handle non-finite values.
Results may differ from a plain program's by a relative error of at most 0.00002.
Values sent between devices are 32-bit elements; how exact they have to be, the bound alone decides.
No kernel may reach another device: no remote copies, remote signals or barrier semaphores. Data moves between devices by JAX's collectives and lax.ppermute only.
A program may use at most 64 MiB of HBM per device.

v0:
```python
import jax
import jax.numpy as jnp
from jax import lax
from jax.sharding import PartitionSpec as P

BAND = 32
LX = 8


def passed_along(array, axis, by):
    count = lax.axis_size(axis)
    return lax.ppermute(array, axis, [(i, (i + by) % count) for i in range(count)])


def shifted(array, axis, by):
    count = lax.axis_size(axis)
    pairs = [(i, i + by) for i in range(count) if 0 <= i + by < count]
    return lax.ppermute(array, axis, pairs)


def multiply(matrix, spinor, dagger):
    real_u = matrix[:, 0]
    imag_u = matrix[:, 1]
    real_v = spinor[:, 0]
    imag_v = spinor[:, 1]
    real_rows = []
    imag_rows = []
    for row_a in range(3):
        real_sum = None
        imag_sum = None
        for col_b in range(3):
            if dagger:
                entry_re = real_u[:, col_b, row_a][:, None, :]
                entry_im = -imag_u[:, col_b, row_a][:, None, :]
            else:
                entry_re = real_u[:, row_a, col_b][:, None, :]
                entry_im = imag_u[:, row_a, col_b][:, None, :]
            term_re = entry_re * real_v[:, col_b] - entry_im * imag_v[:, col_b]
            term_im = entry_re * imag_v[:, col_b] + entry_im * real_v[:, col_b]
            real_sum = term_re if real_sum is None else real_sum + term_re
            imag_sum = term_im if imag_sum is None else imag_sum + term_im
        real_rows.append(real_sum)
        imag_rows.append(imag_sum)
    return jnp.stack([jnp.stack(real_rows, axis=1), jnp.stack(imag_rows, axis=1)], axis=1)


def planar_terms(spinor, set_links):
    column_pos = jnp.arange(spinor.shape[-1], dtype=jnp.int32) % LX
    at_last = column_pos == LX - 1
    at_first = column_pos == 0
    ahead_x = multiply(
        set_links[:, 0],
        jnp.where(at_last, jnp.roll(spinor, LX - 1, -1), jnp.roll(spinor, -1, -1)),
        False,
    )
    hop_x = multiply(set_links[:, 0], spinor, True)
    behind_x = jnp.where(at_first, jnp.roll(hop_x, -(LX - 1), -1), jnp.roll(hop_x, 1, -1))
    ahead_y = multiply(set_links[:, 1], jnp.roll(spinor, -LX, -1), False)
    behind_y = jnp.roll(multiply(set_links[:, 1], spinor, True), LX, -1)
    return ahead_x + behind_x + ahead_y + behind_y


def body(adjoint, flowed, source_slice, band_width, flow_steps):
    row_count = adjoint.shape[0]
    per_plane = BAND // row_count
    first_row = lax.axis_index("gz") * row_count
    slice_pos = (first_row + jnp.arange(row_count, dtype=jnp.int32)) % BAND
    shape_rows = (row_count, 1, 1, 1, 1)
    distance = (slice_pos - source_slice[0]).astype(jnp.float32) / band_width[0].astype(jnp.float32)
    inside = (1.0 / (1.0 + distance * distance)).reshape(shape_rows)
    not_last = (slice_pos != BAND - 1).astype(jnp.float32).reshape(shape_rows)
    not_first = (slice_pos != 0).astype(jnp.float32).reshape(shape_rows)
    step_size = 0.25 / flow_steps[0].astype(jnp.float32)
    z_behind_links = passed_along(flowed[:, :, 2], "gz", per_plane)
    t_behind_links = shifted(flowed[-1:, :, 3], "gz", 1)

    def laplace(spinor, link_set):
        set_links = flowed[:, link_set]
        summed = planar_terms(spinor, set_links)
        z_above = passed_along(spinor, "gz", -per_plane)
        ahead_z = multiply(set_links[:, 2], z_above, False)
        z_below = passed_along(spinor, "gz", per_plane)
        behind_z = multiply(z_behind_links[:, link_set], z_below, True)
        t_above = shifted(spinor[:1], "gz", -1)
        ahead_t = (
            multiply(set_links[:, 3], jnp.concatenate([spinor[1:], t_above], axis=0), False)
            * not_last
        )
        t_going = spinor[-1:]
        t_below = shifted(t_going, "gz", 1)
        prior_links = jnp.concatenate([t_behind_links[:, link_set], set_links[:-1, 3]], axis=0)
        prior_field = jnp.concatenate([t_below, spinor[:-1]], axis=0)
        behind_t = multiply(prior_links, prior_field, True) * not_first
        summed = summed + ahead_z + behind_z + ahead_t + behind_t - 8.0 * spinor
        return inside * (step_size * summed)

    start = inside * adjoint
    third = 0.75 * laplace(start, 2)
    second = start + 8.0 / 9.0 * laplace(third, 1)
    return second + third + laplace(0.25 * second - 2.0 / 9.0 * third, 0)


def solution(mesh):
    in_specs = (
        P(("cfg", "gz"), None, None, None, None),
        P(("cfg", "gz"), None, None, None, None, None, None),
        P("cfg"),
        P("cfg"),
        P("cfg"),
    )
    out_specs = P(("cfg", "gz"), None, None, None, None)
    return jax.shard_map(body, mesh=mesh, in_specs=in_specs, out_specs=out_specs, check_vma=False)
```

profile of v0, /device:TPU:3, one launch (start us, length us, event | category | flops | bytes accessed | tf_op | source)
XLA Modules:
  0.0 55.8 jit_solution(17901837068730920170)
XLA Ops:
  1.3 1.0 %copy_multiply_fusion.1 = f32[4,2,3,8,128]{4,3,2,0,1:T(8,128)S(1)} fusion(f32[4,2,3,8,128]{4,3,2,1,0:T(8,128)} %param.5, f32[4]{0:T(128)S(1)} %fusion.133), kind=kLoop, calls=%fused_computation.111 | loop fusion | flops 24576 | bytes 196624 | tf_op jit(solution)/shard_map/mul | solution.py:97
  2.3 1.3 %collective-permute-start.2 = (f32[4,2,3,8,128]{4,3,2,0,1:T(8,128)S(1)}, f32[4,2,3,8,128]{4,3,2,0,1:T(8,128)S(1)}, u32[]{:S(2)}, u32[]{:S(2)}) collective-permute-start(f32[4,2,3,8,128]{4,3,2,0,1:T(8,128)S(1)} %copy_multiply_fusion.1), channel_id=1, source_target_pairs={{0,8},{1,9},{2,10},{3,11},{4,12},{5,13},{6,14},{7,15},{8,16},{9,17... | collective-permute-start | bytes 294920 | tf_op jit(solution)/shard_map/ppermute | solution.py:12
  3.6 2.1 %collective-permute-start = (f32[4,2,3,8,128]{4,3,2,0,1:T(8,128)S(1)}, f32[4,2,3,8,128]{4,3,2,0,1:T(8,128)S(1)}, u32[]{:S(2)}, u32[]{:S(2)}) collective-permute-start(f32[4,2,3,8,128]{4,3,2,0,1:T(8,128)S(1)} %copy_multiply_fusion.1), channel_id=1, source_target_pairs={{0,24},{1,25},{2,26},{3,27},{4,28},{5,29},{6,30},{7,31},{8,0},{9,1... | collective-permute-start | bytes 294920 | tf_op jit(solution)/shard_map/ppermute | solution.py:12
  5.7 0.8 %slice_bitcast_fusion.46 = f32[1,3,2,3,3,128]{5,2,4,3,1,0:T(2,128)S(1)} fusion(f32[4,3,4,2,3,3,128]{6,3,5,4,2,1,0:T(2,128)} %param.6), kind=kLoop, calls=%fused_computation.246 | loop fusion | bytes 55296 | tf_op jit(solution)/shard_map/squeeze | solution.py:75
  6.5 4.2 %collective-permute-start.4 = (f32[1,3,2,3,3,128]{5,2,4,3,1,0:T(2,128)S(1)}, f32[1,3,2,3,3,128]{5,2,4,3,1,0:T(2,128)S(1)}, u32[]{:S(2)}, u32[]{:S(2)}) collective-permute-start(f32[1,3,2,3,3,128]{5,2,4,3,1,0:T(2,128)S(1)} %slice_bitcast_fusion.46), channel_id=1, source_target_pairs={{0,1},{1,2},{2,3},{3,4},{4,5},{5,6},{6,7},{7,8},{8,9},{9,10},{10,1... | collective-permute-start | bytes 82952 | tf_op jit(solution)/shard_map/ppermute | solution.py:18
  10.7 1.9 %collective-permute-start.5 = (f32[1,2,3,8,128]{4,3,2,0,1:T(8,128)S(1)}, f32[1,2,3,8,128]{4,3,2,0,1:T(8,128)S(1)}, u32[]{:S(2)}, u32[]{:S(2)}) collective-permute-start(f32[1,2,3,8,128]{4,3,2,0,1:T(8,128)S(1)} %get-tuple-element.205), channel_id=1, source_target_pairs={{0,1},{1,2},{2,3},{3,4},{4,5},{5,6},{6,7},{7,8},{8,9},{9,10},{10,1... | collective-permute-start | bytes 73736 | tf_op jit(solution)/shard_map/ppermute | solution.py:18
  12.7 2.4 %collective-permute-start.3 = (f32[1,2,3,8,128]{4,3,2,0,1:T(8,128)S(1)}, f32[1,2,3,8,128]{4,3,2,0,1:T(8,128)S(1)}, u32[]{:S(2)}, u32[]{:S(2)}) collective-permute-start(f32[1,2,3,8,128]{4,3,2,0,1:T(8,128)S(1)} %get-tuple-element.206), channel_id=1, source_target_pairs={{1,0},{2,1},{3,2},{4,3},{5,4},{6,5},{7,6},{8,7},{9,8},{10,9},{11,1... | collective-permute-start | bytes 73736 | tf_op jit(solution)/shard_map/ppermute | solution.py:18
  15.5 0.2 slice_bitcast_fusion
  16.6 0.1 maximum_select_fusion
  19.5 5.5 %collective-permute-done.1 = f32[4,3,2,3,3,128]{5,2,4,3,1,0:T(2,128)S(1)} collective-permute-done((f32[4,3,2,3,3,128]{5,2,4,3,1,0:T(2,128)S(1)}, f32[4,3,2,3,3,128]{5,2,4,3,1,0:T(2,128)S(1)}, u32[]{:S(2)}, u32[]{:S(2)}) %collective-permute-start.1) | collective-permute-done | bytes 110624 | tf_op jit(solution)/shard_map/ppermute | solution.py:12
  25.3 0.9 %copy-done = f32[4,2,3,8,128]{4,3,2,1,0:T(8,128)S(1)} copy-done((f32[4,2,3,8,128]{4,3,2,1,0:T(8,128)S(1)}, f32[4,2,3,8,128]{4,3,2,1,0:T(8,128)}, u32[]{:S(2)}) %copy-start) | copy-done | bytes 98328
  26.2 0.2 fusion.47
  27.1 3.3 %collective-permute-start.6 = (f32[4,2,3,8,128]{4,3,2,0,1:T(8,128)S(1)}, f32[4,2,3,8,128]{4,3,2,0,1:T(8,128)S(1)}, u32[]{:S(2)}, u32[]{:S(2)}) collective-permute-start(f32[4,2,3,8,128]{4,3,2,0,1:T(8,128)S(1)} %copy_multiply_fusion.2), channel_id=1, source_target_pairs={{0,24},{1,25},{2,26},{3,27},{4,28},{5,29},{6,30},{7,31},{8,0},{9,1... | collective-permute-start | bytes 294920 | tf_op jit(solution)/shard_map/ppermute | solution.py:12
  30.5 3.4 %collective-permute-start.8 = (f32[1,2,3,8,128]{4,3,2,0,1:T(8,128)S(1)}, f32[1,2,3,8,128]{4,3,2,0,1:T(8,128)S(1)}, u32[]{:S(2)}, u32[]{:S(2)}) collective-permute-start(f32[1,2,3,8,128]{4,3,2,0,1:T(8,128)S(1)} %get-tuple-element.199), channel_id=1, source_target_pairs={{1,0},{2,1},{3,2},{4,3},{5,4},{6,5},{7,6},{8,7},{9,8},{10,9},{11,1... | collective-permute-start | bytes 73736 | tf_op jit(solution)/shard_map/ppermute | solution.py:18
  34.0 3.3 %collective-permute-start.9 = (f32[1,2,3,8,128]{4,3,2,0,1:T(8,128)S(1)}, f32[1,2,3,8,128]{4,3,2,0,1:T(8,128)S(1)}, u32[]{:S(2)}, u32[]{:S(2)}) collective-permute-start(f32[1,2,3,8,128]{4,3,2,0,1:T(8,128)S(1)} %get-tuple-element.200), channel_id=1, source_target_pairs={{0,1},{1,2},{2,3},{3,4},{4,5},{5,6},{6,7},{7,8},{8,9},{9,10},{10,1... | collective-permute-start | bytes 73736 | tf_op jit(solution)/shard_map/ppermute | solution.py:18
  37.3 0.1 maximum_select_fusion.1
  38.1 0.1 collective-permute-done.9
  38.6 0.2 broadcast_multiply_fusion
  39.6 3.3 %collective-permute-start.10 = (f32[4,2,3,8,128]{4,3,2,0,1:T(8,128)S(1)}, f32[4,2,3,8,128]{4,3,2,0,1:T(8,128)S(1)}, u32[]{:S(2)}, u32[]{:S(2)}) collective-permute-start(f32[4,2,3,8,128]{4,3,2,0,1:T(8,128)S(1)} %copy.66), channel_id=1, source_target_pairs={{0,24},{1,25},{2,26},{3,27},{4,28},{5,29},{6,30},{7,31},{8,0},{9,1... | collective-permute-start | bytes 294920 | tf_op jit(solution)/shard_map/ppermute | solution.py:12
  42.8 5.7 %collective-permute-start.13 = (f32[1,2,3,8,128]{4,3,2,1,0:T(8,128)S(1)}, f32[1,2,3,8,128]{4,3,2,1,0:T(8,128)S(1)}, u32[]{:S(2)}, u32[]{:S(2)}) collective-permute-start(f32[1,2,3,8,128]{4,3,2,1,0:T(8,128)S(1)} %slice.3866), channel_id=1, source_target_pairs={{0,1},{1,2},{2,3},{3,4},{4,5},{5,6},{6,7},{7,8},{8,9},{9,10},{10,1... | collective-permute-start | bytes 73736 | tf_op jit(solution)/shard_map/ppermute | solution.py:18
  48.5 1.9 %collective-permute-start.12 = (f32[1,2,3,8,128]{4,3,2,0,1:T(8,128)S(1)}, f32[1,2,3,8,128]{4,3,2,0,1:T(8,128)S(1)}, u32[]{:S(2)}, u32[]{:S(2)}) collective-permute-start(f32[1,2,3,8,128]{4,3,2,0,1:T(8,128)S(1)} %slice.3834), channel_id=1, source_target_pairs={{1,0},{2,1},{3,2},{4,3},{5,4},{6,5},{7,6},{8,7},{9,8},{10,9},{11,1... | collective-permute-start | bytes 73736 | tf_op jit(solution)/shard_map/ppermute | solution.py:18
  50.4 0.1 maximum_select_fusion.2
  51.2 3.3 %collective-permute-done.12 = f32[1,2,3,8,128]{4,3,2,0,1:T(8,128)S(1)} collective-permute-done((f32[1,2,3,8,128]{4,3,2,0,1:T(8,128)S(1)}, f32[1,2,3,8,128]{4,3,2,0,1:T(8,128)S(1)}, u32[]{:S(2)}, u32[]{:S(2)}) %collective-permute-start.12) | collective-permute-done | bytes 24608 | tf_op jit(solution)/shard_map/ppermute | solution.py:18
  54.9 0.8 %copy_add_fusion = f32[4,2,3,8,128]{4,3,2,1,0:T(8,128)} fusion(f32[4,2,3,8,128]{4,3,2,1,0:T(8,128)S(1)} %copy_subtract_fusion.1, f32[]{:T(128)} %bitcast.2, f32[4]{0:T(128)S(1)} %fusion.133, f32[4,1,3,8,128]{4,3,2,0,1:T(8,128)S(1)} %maximum_bitcast_fusion.39, f32[4,1,3,8,128]{4,3,2,0,1:T(8,128)S(1)} %maximum_bitcast_fusion.38, ...), kind=kLoop, calls=%fused_computation.102 | loop fusion | flops 688128 | bytes 1285044 | tf_op jit(solution)/shard_map/add | solution.py:100
  (291 shorter events, 5.5 us)
Async XLA Ops:
  2.3 17.2 %collective-permute-start.2 = (f32[4,2,3,8,128]{4,3,2,0,1:T(8,128)S(1)}, f32[4,2,3,8,128]{4,3,2,0,1:T(8,128)S(1)}, u32[]{:S(2)}, u32[]{:S(2)}) collective-permute-start(f32[4,2,3,8,128]{4,3,2,0,1:T(8,128)S(1)} %copy_multiply_fusion.1), channel_id=1, source_target_pairs={{0,8},{1,9},{2,10},{3,11},{4,12},{5,13},{6,14},{7,15},{8,16},{9,17... | collective-permute-start | bytes 294920 | tf_op jit(solution)/shard_map/ppermute | solution.py:12
  3.6 15.8 %collective-permute-start = (f32[4,2,3,8,128]{4,3,2,0,1:T(8,128)S(1)}, f32[4,2,3,8,128]{4,3,2,0,1:T(8,128)S(1)}, u32[]{:S(2)}, u32[]{:S(2)}) collective-permute-start(f32[4,2,3,8,128]{4,3,2,0,1:T(8,128)S(1)} %copy_multiply_fusion.1), channel_id=1, source_target_pairs={{0,24},{1,25},{2,26},{3,27},{4,28},{5,29},{6,30},{7,31},{8,0},{9,1... | collective-permute-start | bytes 294920 | tf_op jit(solution)/shard_map/ppermute | solution.py:12
  6.4 8.9 %copy-start.1 = (f32[4,3,4,2,3,3,128]{6,3,5,4,2,1,0:T(2,128)S(1)}, f32[4,3,4,2,3,3,128]{6,3,5,4,2,1,0:T(2,128)}, u32[]{:S(2)}) copy-start(f32[4,3,4,2,3,3,128]{6,3,5,4,2,1,0:T(2,128)} %param.6) | copy-start | bytes 1327108
  6.5 12.5 %collective-permute-start.4 = (f32[1,3,2,3,3,128]{5,2,4,3,1,0:T(2,128)S(1)}, f32[1,3,2,3,3,128]{5,2,4,3,1,0:T(2,128)S(1)}, u32[]{:S(2)}, u32[]{:S(2)}) collective-permute-start(f32[1,3,2,3,3,128]{5,2,4,3,1,0:T(2,128)S(1)} %slice_bitcast_fusion.46), channel_id=1, source_target_pairs={{0,1},{1,2},{2,3},{3,4},{4,5},{5,6},{6,7},{7,8},{8,9},{9,10},{10,1... | collective-permute-start | bytes 82952 | tf_op jit(solution)/shard_map/ppermute | solution.py:18
  10.7 8.0 %collective-permute-start.5 = (f32[1,2,3,8,128]{4,3,2,0,1:T(8,128)S(1)}, f32[1,2,3,8,128]{4,3,2,0,1:T(8,128)S(1)}, u32[]{:S(2)}, u32[]{:S(2)}) collective-permute-start(f32[1,2,3,8,128]{4,3,2,0,1:T(8,128)S(1)} %get-tuple-element.205), channel_id=1, source_target_pairs={{0,1},{1,2},{2,3},{3,4},{4,5},{5,6},{6,7},{7,8},{8,9},{9,10},{10,1... | collective-permute-start | bytes 73736 | tf_op jit(solution)/shard_map/ppermute | solution.py:18
  12.7 6.1 %collective-permute-start.3 = (f32[1,2,3,8,128]{4,3,2,0,1:T(8,128)S(1)}, f32[1,2,3,8,128]{4,3,2,0,1:T(8,128)S(1)}, u32[]{:S(2)}, u32[]{:S(2)}) collective-permute-start(f32[1,2,3,8,128]{4,3,2,0,1:T(8,128)S(1)} %get-tuple-element.206), channel_id=1, source_target_pairs={{1,0},{2,1},{3,2},{4,3},{5,4},{6,5},{7,6},{8,7},{9,8},{10,9},{11,1... | collective-permute-start | bytes 73736 | tf_op jit(solution)/shard_map/ppermute | solution.py:18
  18.7 6.4 %collective-permute-start.1 = (f32[4,3,2,3,3,128]{5,2,4,3,1,0:T(2,128)S(1)}, f32[4,3,2,3,3,128]{5,2,4,3,1,0:T(2,128)S(1)}, u32[]{:S(2)}, u32[]{:S(2)}) collective-permute-start(f32[4,3,2,3,3,128]{5,2,4,3,1,0:T(2,128)S(1)} %slice_bitcast_fusion.3), channel_id=1, source_target_pairs={{0,8},{1,9},{2,10},{3,11},{4,12},{5,13},{6,14},{7,15},{8,16},{9,17... | collective-permute-start | bytes 331784 | tf_op jit(solution)/shard_map/ppermute | solution.py:12
  25.3 0.9 %copy-start = (f32[4,2,3,8,128]{4,3,2,1,0:T(8,128)S(1)}, f32[4,2,3,8,128]{4,3,2,1,0:T(8,128)}, u32[]{:S(2)}) copy-start(f32[4,2,3,8,128]{4,3,2,1,0:T(8,128)} %param.5) | copy-start | bytes 294916
  27.0 11.4 %collective-permute-start.7 = (f32[4,2,3,8,128]{4,3,2,0,1:T(8,128)S(1)}, f32[4,2,3,8,128]{4,3,2,0,1:T(8,128)S(1)}, u32[]{:S(2)}, u32[]{:S(2)}) collective-permute-start(f32[4,2,3,8,128]{4,3,2,0,1:T(8,128)S(1)} %copy_multiply_fusion.2), channel_id=1, source_target_pairs={{0,8},{1,9},{2,10},{3,11},{4,12},{5,13},{6,14},{7,15},{8,16},{9,17... | collective-permute-start | bytes 294920 | tf_op jit(solution)/shard_map/ppermute | solution.py:12
  27.1 11.4 %collective-permute-start.6 = (f32[4,2,3,8,128]{4,3,2,0,1:T(8,128)S(1)}, f32[4,2,3,8,128]{4,3,2,0,1:T(8,128)S(1)}, u32[]{:S(2)}, u32[]{:S(2)}) collective-permute-start(f32[4,2,3,8,128]{4,3,2,0,1:T(8,128)S(1)} %copy_multiply_fusion.2), channel_id=1, source_target_pairs={{0,24},{1,25},{2,26},{3,27},{4,28},{5,29},{6,30},{7,31},{8,0},{9,1... | collective-permute-start | bytes 294920 | tf_op jit(solution)/shard_map/ppermute | solution.py:12
  30.5 7.5 %collective-permute-start.8 = (f32[1,2,3,8,128]{4,3,2,0,1:T(8,128)S(1)}, f32[1,2,3,8,128]{4,3,2,0,1:T(8,128)S(1)}, u32[]{:S(2)}, u32[]{:S(2)}) collective-permute-start(f32[1,2,3,8,128]{4,3,2,0,1:T(8,128)S(1)} %get-tuple-element.199), channel_id=1, source_target_pairs={{1,0},{2,1},{3,2},{4,3},{5,4},{6,5},{7,6},{8,7},{9,8},{10,9},{11,1... | collective-permute-start | bytes 73736 | tf_op jit(solution)/shard_map/ppermute | solution.py:18
  34.0 4.3 %collective-permute-start.9 = (f32[1,2,3,8,128]{4,3,2,0,1:T(8,128)S(1)}, f32[1,2,3,8,128]{4,3,2,0,1:T(8,128)S(1)}, u32[]{:S(2)}, u32[]{:S(2)}) collective-permute-start(f32[1,2,3,8,128]{4,3,2,0,1:T(8,128)S(1)} %get-tuple-element.200), channel_id=1, source_target_pairs={{0,1},{1,2},{2,3},{3,4},{4,5},{5,6},{6,7},{7,8},{8,9},{9,10},{10,1... | collective-permute-start | bytes 73736 | tf_op jit(solution)/shard_map/ppermute | solution.py:18
  39.5 15.2 %collective-permute-start.11 = (f32[4,2,3,8,128]{4,3,2,0,1:T(8,128)S(1)}, f32[4,2,3,8,128]{4,3,2,0,1:T(8,128)S(1)}, u32[]{:S(2)}, u32[]{:S(2)}) collective-permute-start(f32[4,2,3,8,128]{4,3,2,0,1:T(8,128)S(1)} %copy.66), channel_id=1, source_target_pairs={{0,8},{1,9},{2,10},{3,11},{4,12},{5,13},{6,14},{7,15},{8,16},{9,17... | collective-permute-start | bytes 294920 | tf_op jit(solution)/shard_map/ppermute | solution.py:12
  39.6 15.2 %collective-permute-start.10 = (f32[4,2,3,8,128]{4,3,2,0,1:T(8,128)S(1)}, f32[4,2,3,8,128]{4,3,2,0,1:T(8,128)S(1)}, u32[]{:S(2)}, u32[]{:S(2)}) collective-permute-start(f32[4,2,3,8,128]{4,3,2,0,1:T(8,128)S(1)} %copy.66), channel_id=1, source_target_pairs={{0,24},{1,25},{2,26},{3,27},{4,28},{5,29},{6,30},{7,31},{8,0},{9,1... | collective-permute-start | bytes 294920 | tf_op jit(solution)/shard_map/ppermute | solution.py:12
  42.8 8.3 %collective-permute-start.13 = (f32[1,2,3,8,128]{4,3,2,1,0:T(8,128)S(1)}, f32[1,2,3,8,128]{4,3,2,1,0:T(8,128)S(1)}, u32[]{:S(2)}, u32[]{:S(2)}) collective-permute-start(f32[1,2,3,8,128]{4,3,2,1,0:T(8,128)S(1)} %slice.3866), channel_id=1, source_target_pairs={{0,1},{1,2},{2,3},{3,4},{4,5},{5,6},{6,7},{7,8},{8,9},{9,10},{10,1... | collective-permute-start | bytes 73736 | tf_op jit(solution)/shard_map/ppermute | solution.py:18
  48.5 6.0 %collective-permute-start.12 = (f32[1,2,3,8,128]{4,3,2,0,1:T(8,128)S(1)}, f32[1,2,3,8,128]{4,3,2,0,1:T(8,128)S(1)}, u32[]{:S(2)}, u32[]{:S(2)}) collective-permute-start(f32[1,2,3,8,128]{4,3,2,0,1:T(8,128)S(1)} %slice.3834), channel_id=1, source_target_pairs={{1,0},{2,1},{3,2},{4,3},{5,4},{6,5},{7,6},{8,7},{9,8},{10,9},{11,1... | collective-permute-start | bytes 73736 | tf_op jit(solution)/shard_map/ppermute | solution.py:18
where the time goes:
time: 56.2 us; the launch traced here: 55.8 us
  starting transfers between devices  33 us (59%)
  waiting for transfers between devices  8.98 us (16%)
  other arithmetic  5.78 us (10%)
  between operations  4.19 us (7%)
  local copies, waits for them, and re-layouts  3.8 us (7%)
    ppermute x7, starting transfers between devices, shifted(): return lax.ppermute(array, axis, pairs)  22.9 us
    ppermute x7, starting transfers between devices, passed_along(): lax.ppermute(array, axis, [(i, (i + by) % count) for i in range(count)])  10.1 us
    ppermute x7, waiting for transfers between devices, passed_along(): lax.ppermute(array, axis, [(i, (i + by) % count) for i in range(count)])  5.56 us
    ppermute x7, waiting for transfers between devices, shifted(): return lax.ppermute(array, axis, pairs)  3.42 us
    add x72, other arithmetic, multiply(): real_sum = term_re if real_sum is None else real_sum + term_re  1.59 us
  transfers between devices with their start and end apart: 14, of which 3 were waited for; matrix products, arithmetic and copies ran while one was open for 9% of the time, Pallas kernels for 0%

commit v1 on v0

v1 whole, which is shorter than its diff:
```python
import functools

import jax
import jax.numpy as jnp
from jax import lax
from jax.experimental import pallas as pl
from jax.experimental.pallas import tpu as pltpu
from jax.sharding import PartitionSpec as P

BAND = 32
LX = 8
SETS = 3
MUS = 4
ENTRIES = 18


def load_field(ref, row):
    return [[ref[row, c, a] for a in range(3)] for c in range(2)]


def store_field(ref, row, field):
    for c in range(2):
        for a in range(3):
            ref[row, c, a] = field[c][a]


def combine(function, *fields):
    return [[function(*(f[c][a] for f in fields)) for a in range(3)] for c in range(2)]


def entry(links_ref, row, link_set, mu, a, b, c, shape):
    index = ((row * SETS + link_set) * MUS + mu) * ENTRIES + (a * 3 + b) * 2 + c
    return jnp.broadcast_to(links_ref[pl.ds(index, 1), :], shape)


def transport(links_ref, row, link_set, mu, ahead, here):
    forward = [[None] * 3, [None] * 3]
    backward = [[None] * 3, [None] * 3]
    shape = (ahead if ahead is not None else here)[0][0].shape

    def add(total, c, a, value):
        total[c][a] = value if total[c][a] is None else total[c][a] + value

    for a in range(3):
        for b in range(3):
            real = entry(links_ref, row, link_set, mu, a, b, 0, shape)
            imag = entry(links_ref, row, link_set, mu, a, b, 1, shape)
            if ahead is not None:
                add(forward, 0, a, real * ahead[0][b] - imag * ahead[1][b])
                add(forward, 1, a, real * ahead[1][b] + imag * ahead[0][b])
            if here is not None:
                add(backward, 0, b, real * here[0][a] + imag * here[1][a])
                add(backward, 1, b, real * here[1][a] - imag * here[0][a])
    return forward, backward


def roll(plane, by):
    return pltpu.roll(plane, by % plane.shape[-1], plane.ndim - 1)


def taper(scalars, row):
    source, width, steps, first = (scalars[i] for i in range(4))
    ones = jnp.ones((8, 128), jnp.float32)
    slice_pos = lax.rem(first + row, BAND)
    distance = ones * (slice_pos - source).astype(jnp.float32) / (ones * width.astype(jnp.float32))
    inside = 1.0 / (1.0 + distance * distance)
    eps = 0.25 / (ones * steps.astype(jnp.float32))
    return inside, eps


def send_parts(links_ref, link_set, row, rows, field, up_ref, first_ref, last_ref):
    _, up = transport(links_ref, row, link_set, 2, None, field)
    store_field(up_ref, row, up)

    @pl.when(row == 0)
    def _():
        store_field(first_ref, 0, field)

    @pl.when(row == rows - 1)
    def _():
        _, later = transport(links_ref, row, link_set, 3, None, field)
        store_field(last_ref, 0, later)


def begin_kernel(rows, scalars, adjoint_ref, links_ref, start_ref, up_ref, first_ref, last_ref):
    def one(row, carry):
        inside, _ = taper(scalars, row)
        start = combine(lambda v: inside * v, load_field(adjoint_ref, row))
        store_field(start_ref, row, start)
        send_parts(links_ref, 2, row, rows, start, up_ref, first_ref, last_ref)
        return carry

    lax.fori_loop(0, rows, one, 0)


def local_kernel(rows, link_set, field_ref, links_ref, sum_ref):
    shape = field_ref.shape[-2:]
    x_pos = lax.broadcasted_iota(jnp.int32, shape, 1) % LX
    at_last = x_pos == LX - 1
    at_first = x_pos == 0

    def one(row, carry):
        here = load_field(field_ref, row)
        ahead = combine(lambda v: jnp.where(at_last, roll(v, LX - 1), roll(v, -1)), here)
        ahead_x, hop = transport(links_ref, row, link_set, 0, ahead, here)
        total = combine(
            lambda v, f, h: f + jnp.where(at_first, roll(h, 1 - LX), roll(h, 1)) - 8.0 * v, here, ahead_x, hop
        )
        ahead = combine(lambda v: roll(v, -LX), here)
        ahead_y, hop = transport(links_ref, row, link_set, 1, ahead, here)
        total = combine(lambda s, f, h: s + f + roll(h, LX), total, ahead_y, hop)
        store_field(sum_ref, row, total)
        return carry

    lax.fori_loop(0, rows, one, 0)

    def between(row, carry):
        ahead_t, hop = transport(
            links_ref, row, link_set, 3, load_field(field_ref, row + 1), load_field(field_ref, row)
        )
        store_field(sum_ref, row, combine(lambda s, f: s + f, load_field(sum_ref, row), ahead_t))
        store_field(sum_ref, row + 1, combine(lambda s, h: s + h, load_field(sum_ref, row + 1), hop))
        return carry

    lax.fori_loop(0, rows - 1, between, 0)


def arrived_sum(links_ref, link_set, row, rows, sum_ref, above_ref, below_ref, later_ref, earlier_ref):
    ahead_z, _ = transport(links_ref, row, link_set, 2, load_field(above_ref, row), None)
    total = combine(lambda s, f, h: s + f + h, load_field(sum_ref, row), ahead_z, load_field(below_ref, row))
    is_first = jnp.where(row == 0, 1.0, 0.0)
    is_last = jnp.where(row == rows - 1, 1.0, 0.0)
    ahead_t, _ = transport(links_ref, row, link_set, 3, load_field(later_ref, 0), None)
    return combine(lambda s, f, h: s + is_last * f + is_first * h, total, ahead_t, load_field(earlier_ref, 0))


def third_kernel(
    rows, scalars, links_ref, sum_ref, above_ref, below_ref, later_ref, earlier_ref,
    third_ref, up_ref, first_ref, last_ref,
):
    def one(row, carry):
        inside, eps = taper(scalars, row)
        total = arrived_sum(links_ref, 2, row, rows, sum_ref, above_ref, below_ref, later_ref, earlier_ref)
        third = combine(lambda s: 0.75 * (inside * (eps * s)), total)
        store_field(third_ref, row, third)
        send_parts(links_ref, 1, row, rows, third, up_ref, first_ref, last_ref)
        return carry

    lax.fori_loop(0, rows, one, 0)


def second_kernel(
    rows, scalars, links_ref, sum_ref, above_ref, below_ref, later_ref, earlier_ref, start_ref, third_ref,
    mixed_ref, up_ref, first_ref, last_ref, base_ref,
):
    def one(row, carry):
        inside, eps = taper(scalars, row)
        total = arrived_sum(links_ref, 1, row, rows, sum_ref, above_ref, below_ref, later_ref, earlier_ref)
        third = load_field(third_ref, row)
        second = combine(lambda v, s: v + (8.0 / 9.0) * (inside * (eps * s)), load_field(start_ref, row), total)
        mixed = combine(lambda p, q: 0.25 * p - (2.0 / 9.0) * q, second, third)
        store_field(mixed_ref, row, mixed)
        store_field(base_ref, row, combine(lambda p, q: p + q, second, third))
        send_parts(links_ref, 0, row, rows, mixed, up_ref, first_ref, last_ref)
        return carry

    lax.fori_loop(0, rows, one, 0)


def last_kernel(
    rows, scalars, links_ref, sum_ref, above_ref, below_ref, later_ref, earlier_ref, base_ref, out_ref
):
    def one(row, carry):
        inside, eps = taper(scalars, row)
        total = arrived_sum(links_ref, 0, row, rows, sum_ref, above_ref, below_ref, later_ref, earlier_ref)
        store_field(out_ref, row, combine(lambda p, s: p + inside * (eps * s), load_field(base_ref, row), total))
        return carry

    lax.fori_loop(0, rows, one, 0)


def call(kernel, name, n_scalars, operands, out_shapes, matvecs):
    vmem = pl.BlockSpec(memory_space=pltpu.VMEM)
    smem = pl.BlockSpec(memory_space=pltpu.SMEM)
    return pl.pallas_call(
        kernel,
        name=name,
        out_shape=out_shapes,
        in_specs=[smem] * n_scalars + [vmem] * (len(operands) - n_scalars),
        out_specs=jax.tree.map(lambda _: vmem, out_shapes),
        cost_estimate=pl.CostEstimate(flops=matvecs * 72 * 1024, bytes_accessed=4096 * 18 * matvecs, transcendentals=0),
        compiler_params=pltpu.CompilerParams(vmem_limit_bytes=16 * 2**20),
    )(*operands)


def body(adjoint, flowed, source_slice, band_width, flow_steps):
    rows = adjoint.shape[0]
    per_plane = BAND // rows
    count = lax.axis_size("gz")
    me = lax.axis_index("gz")
    links = jnp.transpose(flowed, (0, 1, 2, 4, 5, 3, 6)).reshape(-1, flowed.shape[-1])
    scalars = jnp.concatenate(
        [source_slice, band_width, flow_steps, (me * rows).astype(jnp.int32).reshape(1)]
    )
    whole = jax.ShapeDtypeStruct(adjoint.shape, jnp.float32)
    one_row = jax.ShapeDtypeStruct((1,) + adjoint.shape[1:], jnp.float32)

    up_pairs = [(i, (i + per_plane) % count) for i in range(count)]
    down_pairs = [(j, i) for i, j in up_pairs]
    later_pairs = [(i, i + 1) for i in range(count) if (i + 1) % per_plane]
    earlier_pairs = [(j, i) for i, j in later_pairs]

    def exchange(field, up, first, last):
        later = lax.ppermute(first, "gz", earlier_pairs)
        earlier = lax.ppermute(last, "gz", later_pairs)
        above = lax.ppermute(field, "gz", down_pairs)
        below = lax.ppermute(up, "gz", up_pairs)
        return above, below, later, earlier

    def local(field, link_set):
        return call(
            functools.partial(local_kernel, rows, link_set), f"local_{link_set}", 0, (field, links), whole, 22
        )

    start, up, first, last = call(
        functools.partial(begin_kernel, rows), "begin", 1, (scalars, adjoint, links),
        (whole, whole, one_row, one_row), 5,
    )
    arrived = exchange(start, up, first, last)
    third, up, first, last = call(
        functools.partial(third_kernel, rows), "third", 1, (scalars, links, local(start, 2)) + arrived,
        (whole, whole, one_row, one_row), 10,
    )
    arrived = exchange(third, up, first, last)
    mixed, up, first, last, base = call(
        functools.partial(second_kernel, rows), "second", 1,
        (scalars, links, local(third, 1)) + arrived + (start, third),
        (whole, whole, one_row, one_row, whole), 10,
    )
    arrived = exchange(mixed, up, first, last)
    return call(
        functools.partial(last_kernel, rows), "last", 1, (scalars, links, local(mixed, 0)) + arrived + (base,),
        whole, 5,
    )


def solution(mesh):
    in_specs = (
        P(("cfg", "gz"), None, None, None, None),
        P(("cfg", "gz"), None, None, None, None, None, None),
        P("cfg"),
        P("cfg"),
        P("cfg"),
    )
    out_specs = P(("cfg", "gz"), None, None, None, None)
    return jax.shard_map(body, mesh=mesh, in_specs=in_specs, out_specs=out_specs, check_vma=False)
```

time: 56.2 us -> 43.8 us (0.78)
  the two profiles are of different devices: /device:TPU:3 before, /device:TPU:4 now
where the time goes in v1:
time: 43.8 us; the launch traced here: 43.5 us
  starting transfers between devices  24.6 us (56%)
  waiting for transfers between devices  9.78 us (22%)
  Pallas kernels  5.07 us (12%)
  between operations  2.09 us (5%)
  local copies, waits for them, and re-layouts  1.91 us (4%)
    ppermute x3, starting transfers between devices, exchange(): above = lax.ppermute(field, 'gz', down_pairs)  9.87 us
    ppermute x3, waiting for transfers between devices, exchange(): earlier = lax.ppermute(last, 'gz', later_pairs)  9.75 us
    ppermute x3, starting transfers between devices, exchange(): earlier = lax.ppermute(last, 'gz', later_pairs)  6.79 us
    ppermute x3, starting transfers between devices, exchange(): later = lax.ppermute(first, 'gz', earlier_pairs)  6.15 us
    pallas_call x7, Pallas kernels, call(): pl.pallas_call(kernel, name=name, out_shape=out_shapes, in_specs=[smem] *...  5.07 us
    unnamed x6, local copies, waits for them, and re-layouts  1.91 us
    ppermute x3, starting transfers between devices, exchange(): below = lax.ppermute(up, 'gz', up_pairs)  1.75 us
  transfers between devices with their start and end apart: 12, of which 3 were waited for; matrix products, arithmetic and copies ran while one was open for 0% of the time, Pallas kernels for 3%

profile of v1, /device:TPU:4, one launch (start us, length us, event | category | flops | bytes accessed | tf_op | source)
XLA Modules:
  0.0 43.5 jit_solution(7082937295136098520)
XLA Ops:
  1.9 0.1 pad_add_fusion.scalars
  2.0 1.0 %copy-done = f32[4,3,4,2,3,3,128]{6,3,5,4,2,1,0:T(2,128)S(1)} copy-done((f32[4,3,4,2,3,3,128]{6,3,5,4,2,1,0:T(2,128)S(1)}, f32[4,3,4,2,3,3,128]{6,3,5,4,2,1,0:T(2,128)}, u32[]{:S(2)}) %copy-start) | copy-done | bytes 442392
  3.0 0.9 %copy-done.2 = f32[4,2,3,8,128]{4,3,2,1,0:T(8,128)S(1)} copy-done((f32[4,2,3,8,128]{4,3,2,1,0:T(8,128)S(1)}, f32[4,2,3,8,128]{4,3,2,1,0:T(8,128)}, u32[]{:S(2)}) %copy-start.2) | copy-done | bytes 98328
  3.9 0.7 %begin.1 = (f32[4,2,3,8,128]{4,3,2,1,0:T(8,128)S(1)}, f32[4,2,3,8,128]{4,3,2,1,0:T(8,128)S(1)}, f32[1,2,3,8,128]{4,3,2,1,0:T(8,128)S(1)}, f32[1,2,3,8,128]{4,3,2,1,0:T(8,128)S(1)}) custom-call(s32[4]{0:T(128)S(1)} %pad_add_fusion.scalars, f32[4,2,3,8,128]{4,3,2,1,0:T(8,128)S(1)} %copy-done.2, f32[864,128]{1,0:T(8,128)S(1)} %bitcast.4), custom_call_target="tpu_custom_call" | custom-call | flops 368640 | bytes 368640 | tf_op jit(solution)/shard_map/begin/pallas_call | solution.py:185
  4.6 1.6 %collective-permute-start.1 = (f32[4,2,3,8,128]{4,3,2,1,0:T(8,128)S(1)}, f32[4,2,3,8,128]{4,3,2,1,0:T(8,128)S(1)}, u32[]{:S(2)}, u32[]{:S(2)}) collective-permute-start(f32[4,2,3,8,128]{4,3,2,1,0:T(8,128)S(1)} %get-tuple-element.19), channel_id=1, source_target_pairs={{0,8},{1,9},{2,10},{3,11},{4,12},{5,13},{6,14},{7,15},{8,16},{9,17... | collective-permute-start | bytes 294920 | tf_op jit(solution)/shard_map/ppermute | solution.py:217
  6.3 2.2 %collective-permute-start = (f32[4,2,3,8,128]{4,3,2,1,0:T(8,128)S(1)}, f32[4,2,3,8,128]{4,3,2,1,0:T(8,128)S(1)}, u32[]{:S(2)}, u32[]{:S(2)}) collective-permute-start(f32[4,2,3,8,128]{4,3,2,1,0:T(8,128)S(1)} %get-tuple-element.18.field_ref.start_ref), channel_id=1, source_target_pairs={{8,0},{9,1},{10,2},{11,3},{12,4},{13,5},{14,6},{15,7},{16,8},{17,9... | collective-permute-start | bytes 294920 | tf_op jit(solution)/shard_map/ppermute | solution.py:216
  8.5 2.3 %collective-permute-start.2 = (f32[1,2,3,8,128]{4,3,2,1,0:T(8,128)S(1)}, f32[1,2,3,8,128]{4,3,2,1,0:T(8,128)S(1)}, u32[]{:S(2)}, u32[]{:S(2)}) collective-permute-start(f32[1,2,3,8,128]{4,3,2,1,0:T(8,128)S(1)} %get-tuple-element.20), channel_id=1, source_target_pairs={{1,0},{2,1},{3,2},{4,3},{5,4},{6,5},{7,6},{9,8},{10,9},{11,10},{12... | collective-permute-start | bytes 73736 | tf_op jit(solution)/shard_map/ppermute | solution.py:214
  10.9 2.0 %collective-permute-start.3 = (f32[1,2,3,8,128]{4,3,2,1,0:T(8,128)S(1)}, f32[1,2,3,8,128]{4,3,2,1,0:T(8,128)S(1)}, u32[]{:S(2)}, u32[]{:S(2)}) collective-permute-start(f32[1,2,3,8,128]{4,3,2,1,0:T(8,128)S(1)} %get-tuple-element.21), channel_id=1, source_target_pairs={{0,1},{1,2},{2,3},{3,4},{4,5},{5,6},{6,7},{8,9},{9,10},{10,11},{11... | collective-permute-start | bytes 73736 | tf_op jit(solution)/shard_map/ppermute | solution.py:215
  12.9 0.5 %local_2.1.sum_ref = f32[4,2,3,8,128]{4,3,2,1,0:T(8,128)S(1)} custom-call(f32[4,2,3,8,128]{4,3,2,1,0:T(8,128)S(1)} %get-tuple-element.18.field_ref.start_ref, f32[864,128]{1,0:T(8,128)S(1)} %bitcast.5), custom_call_target="tpu_custom_call" | custom-call | flops 1622016 | bytes 1622016 | tf_op jit(solution)/shard_map/local_2/pallas_call | solution.py:185
  13.4 3.5 %collective-permute-done.3.earlier_ref = f32[1,2,3,8,128]{4,3,2,1,0:T(8,128)S(1)} collective-permute-done((f32[1,2,3,8,128]{4,3,2,1,0:T(8,128)S(1)}, f32[1,2,3,8,128]{4,3,2,1,0:T(8,128)S(1)}, u32[]{:S(2)}, u32[]{:S(2)}) %collective-permute-start.3) | collective-permute-done | bytes 24608 | tf_op jit(solution)/shard_map/ppermute | solution.py:215
  16.9 0.8 %third.1 = (f32[4,2,3,8,128]{4,3,2,1,0:T(8,128)S(1)}, f32[4,2,3,8,128]{4,3,2,1,0:T(8,128)S(1)}, f32[1,2,3,8,128]{4,3,2,1,0:T(8,128)S(1)}, f32[1,2,3,8,128]{4,3,2,1,0:T(8,128)S(1)}) custom-call(s32[4]{0:T(128)S(1)} %pad_add_fusion.scalars, f32[864,128]{1,0:T(8,128)S(1)} %bitcast.6, f32[4,2,3,8,128]{4,3,2,1,0:T(8,128)S(1)} %local_2.1.sum_ref, ...), custom_call_target="tpu_custom_call" | custom-call | flops 737280 | bytes 737280 | tf_op jit(solution)/shard_map/third/pallas_call | solution.py:185
  17.7 0.1 collective-permute-start.5
  17.7 3.8 %collective-permute-start.4 = (f32[4,2,3,8,128]{4,3,2,1,0:T(8,128)S(1)}, f32[4,2,3,8,128]{4,3,2,1,0:T(8,128)S(1)}, u32[]{:S(2)}, u32[]{:S(2)}) collective-permute-start(f32[4,2,3,8,128]{4,3,2,1,0:T(8,128)S(1)} %get-tuple-element.22.field_ref.third_ref), channel_id=1, source_target_pairs={{8,0},{9,1},{10,2},{11,3},{12,4},{13,5},{14,6},{15,7},{16,8},{17,9... | collective-permute-start | bytes 294920 | tf_op jit(solution)/shard_map/ppermute | solution.py:216
  21.6 1.9 %collective-permute-start.6 = (f32[1,2,3,8,128]{4,3,2,1,0:T(8,128)S(1)}, f32[1,2,3,8,128]{4,3,2,1,0:T(8,128)S(1)}, u32[]{:S(2)}, u32[]{:S(2)}) collective-permute-start(f32[1,2,3,8,128]{4,3,2,1,0:T(8,128)S(1)} %get-tuple-element.24), channel_id=1, source_target_pairs={{1,0},{2,1},{3,2},{4,3},{5,4},{6,5},{7,6},{9,8},{10,9},{11,10},{12... | collective-permute-start | bytes 73736 | tf_op jit(solution)/shard_map/ppermute | solution.py:214
  23.5 2.4 %collective-permute-start.7 = (f32[1,2,3,8,128]{4,3,2,1,0:T(8,128)S(1)}, f32[1,2,3,8,128]{4,3,2,1,0:T(8,128)S(1)}, u32[]{:S(2)}, u32[]{:S(2)}) collective-permute-start(f32[1,2,3,8,128]{4,3,2,1,0:T(8,128)S(1)} %get-tuple-element.25), channel_id=1, source_target_pairs={{0,1},{1,2},{2,3},{3,4},{4,5},{5,6},{6,7},{8,9},{9,10},{10,11},{11... | collective-permute-start | bytes 73736 | tf_op jit(solution)/shard_map/ppermute | solution.py:215
  25.9 0.5 %local_1.1.sum_ref = f32[4,2,3,8,128]{4,3,2,1,0:T(8,128)S(1)} custom-call(f32[4,2,3,8,128]{4,3,2,1,0:T(8,128)S(1)} %get-tuple-element.22.field_ref.third_ref, f32[864,128]{1,0:T(8,128)S(1)} %bitcast.7), custom_call_target="tpu_custom_call" | custom-call | flops 1622016 | bytes 1622016 | tf_op jit(solution)/shard_map/local_1/pallas_call | solution.py:185
  26.4 3.1 %collective-permute-done.7.earlier_ref = f32[1,2,3,8,128]{4,3,2,1,0:T(8,128)S(1)} collective-permute-done((f32[1,2,3,8,128]{4,3,2,1,0:T(8,128)S(1)}, f32[1,2,3,8,128]{4,3,2,1,0:T(8,128)S(1)}, u32[]{:S(2)}, u32[]{:S(2)}) %collective-permute-start.7) | collective-permute-done | bytes 24608 | tf_op jit(solution)/shard_map/ppermute | solution.py:215
  29.5 0.8 %second.1 = (f32[4,2,3,8,128]{4,3,2,1,0:T(8,128)S(1)}, f32[4,2,3,8,128]{4,3,2,1,0:T(8,128)S(1)}, f32[1,2,3,8,128]{4,3,2,1,0:T(8,128)S(1)}, f32[1,2,3,8,128]{4,3,2,1,0:T(8,128)S(1)}, f32[4,2,3,8,128]{4,3,2,1,0:T(8,128)S(1)}) custom-call(s32[4]{0:T(128)S(1)} %pad_add_fusion.scalars, f32[864,128]{1,0:T(8,128)S(1)} %bitcast.8, ...), custom_call_target="tpu_custom_call" | custom-call | flops 737280 | bytes 737280 | tf_op jit(solution)/shard_map/second/pallas_call | solution.py:185
  30.4 3.8 %collective-permute-start.8 = (f32[4,2,3,8,128]{4,3,2,1,0:T(8,128)S(1)}, f32[4,2,3,8,128]{4,3,2,1,0:T(8,128)S(1)}, u32[]{:S(2)}, u32[]{:S(2)}) collective-permute-start(f32[4,2,3,8,128]{4,3,2,1,0:T(8,128)S(1)} %get-tuple-element.26.field_ref), channel_id=1, source_target_pairs={{8,0},{9,1},{10,2},{11,3},{12,4},{13,5},{14,6},{15,7},{16,8},{17,9... | collective-permute-start | bytes 294920 | tf_op jit(solution)/shard_map/ppermute | solution.py:216
  34.2 1.9 %collective-permute-start.10 = (f32[1,2,3,8,128]{4,3,2,1,0:T(8,128)S(1)}, f32[1,2,3,8,128]{4,3,2,1,0:T(8,128)S(1)}, u32[]{:S(2)}, u32[]{:S(2)}) collective-permute-start(f32[1,2,3,8,128]{4,3,2,1,0:T(8,128)S(1)} %get-tuple-element.28), channel_id=1, source_target_pairs={{1,0},{2,1},{3,2},{4,3},{5,4},{6,5},{7,6},{9,8},{10,9},{11,10},{12... | collective-permute-start | bytes 73736 | tf_op jit(solution)/shard_map/ppermute | solution.py:214
  36.1 2.4 %collective-permute-start.11 = (f32[1,2,3,8,128]{4,3,2,1,0:T(8,128)S(1)}, f32[1,2,3,8,128]{4,3,2,1,0:T(8,128)S(1)}, u32[]{:S(2)}, u32[]{:S(2)}) collective-permute-start(f32[1,2,3,8,128]{4,3,2,1,0:T(8,128)S(1)} %get-tuple-element.29), channel_id=1, source_target_pairs={{0,1},{1,2},{2,3},{3,4},{4,5},{5,6},{6,7},{8,9},{9,10},{10,11},{11... | collective-permute-start | bytes 73736 | tf_op jit(solution)/shard_map/ppermute | solution.py:215
  38.5 0.5 %local_0.1.sum_ref = f32[4,2,3,8,128]{4,3,2,1,0:T(8,128)S(1)} custom-call(f32[4,2,3,8,128]{4,3,2,1,0:T(8,128)S(1)} %get-tuple-element.26.field_ref, f32[864,128]{1,0:T(8,128)S(1)} %bitcast.9), custom_call_target="tpu_custom_call" | custom-call | flops 1622016 | bytes 1622016 | tf_op jit(solution)/shard_map/local_0/pallas_call | solution.py:185
  39.0 3.1 %collective-permute-done.11.earlier_ref = f32[1,2,3,8,128]{4,3,2,1,0:T(8,128)S(1)} collective-permute-done((f32[1,2,3,8,128]{4,3,2,1,0:T(8,128)S(1)}, f32[1,2,3,8,128]{4,3,2,1,0:T(8,128)S(1)}, u32[]{:S(2)}, u32[]{:S(2)}) %collective-permute-start.11) | collective-permute-done | bytes 24608 | tf_op jit(solution)/shard_map/ppermute | solution.py:215
  42.1 1.3 %last.1 = f32[4,2,3,8,128]{4,3,2,1,0:T(8,128)} custom-call(s32[4]{0:T(128)S(1)} %pad_add_fusion.scalars, f32[864,128]{1,0:T(8,128)S(1)} %bitcast.10, f32[4,2,3,8,128]{4,3,2,1,0:T(8,128)S(1)} %local_0.1.sum_ref, f32[4,2,3,8,128]{4,3,2,1,0:T(8,128)S(1)} %collective-permute-done.8.above_ref, f32[4,2,3,8,128]{4,3,2,1,0:T(8,128)S(1)} %collective-permute-done.9.below_ref, ...), custom_call_target="tpu_custom_call" | custom-call | flops 368640 | bytes 368640 | tf_op jit(solution)/shard_map/last/pallas_call | solution.py:185
  (14 shorter events, 0.1 us)
Async XLA Ops:
  2.0 1.0 %copy-start = (f32[4,3,4,2,3,3,128]{6,3,5,4,2,1,0:T(2,128)S(1)}, f32[4,3,4,2,3,3,128]{6,3,5,4,2,1,0:T(2,128)}, u32[]{:S(2)}) copy-start(f32[4,3,4,2,3,3,128]{6,3,5,4,2,1,0:T(2,128)} %param.6) | copy-start | bytes 1327108
  3.0 0.9 %copy-start.2 = (f32[4,2,3,8,128]{4,3,2,1,0:T(8,128)S(1)}, f32[4,2,3,8,128]{4,3,2,1,0:T(8,128)}, u32[]{:S(2)}) copy-start(f32[4,2,3,8,128]{4,3,2,1,0:T(8,128)} %adjoint_ref.1) | copy-start | bytes 294916
  3.9 8.9 %copy-start.1 = (f32[4,3,4,2,3,3,128]{6,3,5,4,2,1,0:T(2,128)S(1)}, f32[4,3,4,2,3,3,128]{6,3,5,4,2,1,0:T(2,128)}, u32[]{:S(2)}) copy-start(f32[4,3,4,2,3,3,128]{6,3,5,4,2,1,0:T(2,128)} %param.6) | copy-start | bytes 1327108
  4.6 12.3 %collective-permute-start.1 = (f32[4,2,3,8,128]{4,3,2,1,0:T(8,128)S(1)}, f32[4,2,3,8,128]{4,3,2,1,0:T(8,128)S(1)}, u32[]{:S(2)}, u32[]{:S(2)}) collective-permute-start(f32[4,2,3,8,128]{4,3,2,1,0:T(8,128)S(1)} %get-tuple-element.19), channel_id=1, source_target_pairs={{0,8},{1,9},{2,10},{3,11},{4,12},{5,13},{6,14},{7,15},{8,16},{9,17... | collective-permute-start | bytes 294920 | tf_op jit(solution)/shard_map/ppermute | solution.py:217
  6.3 10.6 %collective-permute-start = (f32[4,2,3,8,128]{4,3,2,1,0:T(8,128)S(1)}, f32[4,2,3,8,128]{4,3,2,1,0:T(8,128)S(1)}, u32[]{:S(2)}, u32[]{:S(2)}) collective-permute-start(f32[4,2,3,8,128]{4,3,2,1,0:T(8,128)S(1)} %get-tuple-element.18.field_ref.start_ref), channel_id=1, source_target_pairs={{8,0},{9,1},{10,2},{11,3},{12,4},{13,5},{14,6},{15,7},{16,8},{17,9... | collective-permute-start | bytes 294920 | tf_op jit(solution)/shard_map/ppermute | solution.py:216
  8.5 4.9 %collective-permute-start.2 = (f32[1,2,3,8,128]{4,3,2,1,0:T(8,128)S(1)}, f32[1,2,3,8,128]{4,3,2,1,0:T(8,128)S(1)}, u32[]{:S(2)}, u32[]{:S(2)}) collective-permute-start(f32[1,2,3,8,128]{4,3,2,1,0:T(8,128)S(1)} %get-tuple-element.20), channel_id=1, source_target_pairs={{1,0},{2,1},{3,2},{4,3},{5,4},{6,5},{7,6},{9,8},{10,9},{11,10},{12... | collective-permute-start | bytes 73736 | tf_op jit(solution)/shard_map/ppermute | solution.py:214
  10.9 6.0 %collective-permute-start.3 = (f32[1,2,3,8,128]{4,3,2,1,0:T(8,128)S(1)}, f32[1,2,3,8,128]{4,3,2,1,0:T(8,128)S(1)}, u32[]{:S(2)}, u32[]{:S(2)}) collective-permute-start(f32[1,2,3,8,128]{4,3,2,1,0:T(8,128)S(1)} %get-tuple-element.21), channel_id=1, source_target_pairs={{0,1},{1,2},{2,3},{3,4},{4,5},{5,6},{6,7},{8,9},{9,10},{10,11},{11... | collective-permute-start | bytes 73736 | tf_op jit(solution)/shard_map/ppermute | solution.py:215
  17.7 11.8 %collective-permute-start.5 = (f32[4,2,3,8,128]{4,3,2,1,0:T(8,128)S(1)}, f32[4,2,3,8,128]{4,3,2,1,0:T(8,128)S(1)}, u32[]{:S(2)}, u32[]{:S(2)}) collective-permute-start(f32[4,2,3,8,128]{4,3,2,1,0:T(8,128)S(1)} %get-tuple-element.23), channel_id=1, source_target_pairs={{0,8},{1,9},{2,10},{3,11},{4,12},{5,13},{6,14},{7,15},{8,16},{9,17... | collective-permute-start | bytes 294920 | tf_op jit(solution)/shard_map/ppermute | solution.py:217
  17.7 11.8 %collective-permute-start.4 = (f32[4,2,3,8,128]{4,3,2,1,0:T(8,128)S(1)}, f32[4,2,3,8,128]{4,3,2,1,0:T(8,128)S(1)}, u32[]{:S(2)}, u32[]{:S(2)}) collective-permute-start(f32[4,2,3,8,128]{4,3,2,1,0:T(8,128)S(1)} %get-tuple-element.22.field_ref.third_ref), channel_id=1, source_target_pairs={{8,0},{9,1},{10,2},{11,3},{12,4},{13,5},{14,6},{15,7},{16,8},{17,9... | collective-permute-start | bytes 294920 | tf_op jit(solution)/shard_map/ppermute | solution.py:216
  21.6 4.8 %collective-permute-start.6 = (f32[1,2,3,8,128]{4,3,2,1,0:T(8,128)S(1)}, f32[1,2,3,8,128]{4,3,2,1,0:T(8,128)S(1)}, u32[]{:S(2)}, u32[]{:S(2)}) collective-permute-start(f32[1,2,3,8,128]{4,3,2,1,0:T(8,128)S(1)} %get-tuple-element.24), channel_id=1, source_target_pairs={{1,0},{2,1},{3,2},{4,3},{5,4},{6,5},{7,6},{9,8},{10,9},{11,10},{12... | collective-permute-start | bytes 73736 | tf_op jit(solution)/shard_map/ppermute | solution.py:214
  23.5 6.0 %collective-permute-start.7 = (f32[1,2,3,8,128]{4,3,2,1,0:T(8,128)S(1)}, f32[1,2,3,8,128]{4,3,2,1,0:T(8,128)S(1)}, u32[]{:S(2)}, u32[]{:S(2)}) collective-permute-start(f32[1,2,3,8,128]{4,3,2,1,0:T(8,128)S(1)} %get-tuple-element.25), channel_id=1, source_target_pairs={{0,1},{1,2},{2,3},{3,4},{4,5},{5,6},{6,7},{8,9},{9,10},{10,11},{11... | collective-permute-start | bytes 73736 | tf_op jit(solution)/shard_map/ppermute | solution.py:215
  30.3 11.8 %collective-permute-start.9 = (f32[4,2,3,8,128]{4,3,2,1,0:T(8,128)S(1)}, f32[4,2,3,8,128]{4,3,2,1,0:T(8,128)S(1)}, u32[]{:S(2)}, u32[]{:S(2)}) collective-permute-start(f32[4,2,3,8,128]{4,3,2,1,0:T(8,128)S(1)} %get-tuple-element.27), channel_id=1, source_target_pairs={{0,8},{1,9},{2,10},{3,11},{4,12},{5,13},{6,14},{7,15},{8,16},{9,17... | collective-permute-start | bytes 294920 | tf_op jit(solution)/shard_map/ppermute | solution.py:217
  30.4 11.8 %collective-permute-start.8 = (f32[4,2,3,8,128]{4,3,2,1,0:T(8,128)S(1)}, f32[4,2,3,8,128]{4,3,2,1,0:T(8,128)S(1)}, u32[]{:S(2)}, u32[]{:S(2)}) collective-permute-start(f32[4,2,3,8,128]{4,3,2,1,0:T(8,128)S(1)} %get-tuple-element.26.field_ref), channel_id=1, source_target_pairs={{8,0},{9,1},{10,2},{11,3},{12,4},{13,5},{14,6},{15,7},{16,8},{17,9... | collective-permute-start | bytes 294920 | tf_op jit(solution)/shard_map/ppermute | solution.py:216
  34.2 4.8 %collective-permute-start.10 = (f32[1,2,3,8,128]{4,3,2,1,0:T(8,128)S(1)}, f32[1,2,3,8,128]{4,3,2,1,0:T(8,128)S(1)}, u32[]{:S(2)}, u32[]{:S(2)}) collective-permute-start(f32[1,2,3,8,128]{4,3,2,1,0:T(8,128)S(1)} %get-tuple-element.28), channel_id=1, source_target_pairs={{1,0},{2,1},{3,2},{4,3},{5,4},{6,5},{7,6},{9,8},{10,9},{11,10},{12... | collective-permute-start | bytes 73736 | tf_op jit(solution)/shard_map/ppermute | solution.py:214
  36.1 6.0 %collective-permute-start.11 = (f32[1,2,3,8,128]{4,3,2,1,0:T(8,128)S(1)}, f32[1,2,3,8,128]{4,3,2,1,0:T(8,128)S(1)}, u32[]{:S(2)}, u32[]{:S(2)}) collective-permute-start(f32[1,2,3,8,128]{4,3,2,1,0:T(8,128)S(1)} %get-tuple-element.29), channel_id=1, source_target_pairs={{0,1},{1,2},{2,3},{3,4},{4,5},{5,6},{6,7},{8,9},{9,10},{10,11},{11... | collective-permute-start | bytes 73736 | tf_op jit(solution)/shard_map/ppermute | solution.py:215

commit v2 on v1

--- a/solution.py
+++ b/solution.py
@@ -68,10 +68,7 @@
     return inside, eps
 
 
-def send_parts(links_ref, link_set, row, rows, field, up_ref, first_ref, last_ref):
-    _, up = transport(links_ref, row, link_set, 2, None, field)
-    store_field(up_ref, row, up)
-
+def edge_parts(links_ref, link_set, row, rows, field, first_ref, last_ref):
     @pl.when(row == 0)
     def _():
         store_field(first_ref, 0, field)
@@ -82,15 +79,32 @@
         store_field(last_ref, 0, later)
 
 
-def begin_kernel(rows, scalars, adjoint_ref, links_ref, start_ref, up_ref, first_ref, last_ref):
+def begin_kernel(rows, scalars, adjoint_ref, links_ref, start_ref, first_ref, last_ref):
     def one(row, carry):
         inside, _ = taper(scalars, row)
         start = combine(lambda v: inside * v, load_field(adjoint_ref, row))
         store_field(start_ref, row, start)
-        send_parts(links_ref, 2, row, rows, start, up_ref, first_ref, last_ref)
-        return carry
-
-    lax.fori_loop(0, rows, one, 0)
+        edge_parts(links_ref, 2, row, rows, start, first_ref, last_ref)
+        return carry
+
+    lax.fori_loop(0, rows, one, 0)
+
+
+def middle_kernel(rows, link_set, scalars, field_ref, links_ref, later_ref, earlier_ref, up_ref, down_ref, edge_ref):
+    def one(row, carry):
+        field = load_field(field_ref, row)
+        store_field(down_ref, row, field)
+        _, up = transport(links_ref, row, link_set, 2, None, field)
+        store_field(up_ref, row, up)
+        return carry
+
+    lax.fori_loop(0, rows, one, 0)
+    first_pos = lax.rem(scalars[3], BAND)
+    not_first = jnp.where(first_pos != 0, 1.0, 0.0)
+    not_last = jnp.where(first_pos != BAND - rows, 1.0, 0.0)
+    store_field(edge_ref, 0, combine(lambda h: not_first * h, load_field(earlier_ref, 0)))
+    ahead_t, _ = transport(links_ref, rows - 1, link_set, 3, load_field(later_ref, 0), None)
+    store_field(edge_ref, 1, combine(lambda f: not_last * f, ahead_t))
 
 
 def local_kernel(rows, link_set, field_ref, links_ref, sum_ref):
@@ -125,54 +139,52 @@
     lax.fori_loop(0, rows - 1, between, 0)
 
 
-def arrived_sum(links_ref, link_set, row, rows, sum_ref, above_ref, below_ref, later_ref, earlier_ref):
+def arrived_sum(links_ref, link_set, row, rows, sum_ref, edge_ref, above_ref, below_ref):
     ahead_z, _ = transport(links_ref, row, link_set, 2, load_field(above_ref, row), None)
     total = combine(lambda s, f, h: s + f + h, load_field(sum_ref, row), ahead_z, load_field(below_ref, row))
     is_first = jnp.where(row == 0, 1.0, 0.0)
     is_last = jnp.where(row == rows - 1, 1.0, 0.0)
-    ahead_t, _ = transport(links_ref, row, link_set, 3, load_field(later_ref, 0), None)
-    return combine(lambda s, f, h: s + is_last * f + is_first * h, total, ahead_t, load_field(earlier_ref, 0))
+    return combine(
+        lambda s, h, f: s + is_first * h + is_last * f, total, load_field(edge_ref, 0), load_field(edge_ref, 1)
+    )
 
 
 def third_kernel(
-    rows, scalars, links_ref, sum_ref, above_ref, below_ref, later_ref, earlier_ref,
-    third_ref, up_ref, first_ref, last_ref,
+    rows, scalars, links_ref, sum_ref, edge_ref, above_ref, below_ref, third_ref, first_ref, last_ref
 ):
     def one(row, carry):
         inside, eps = taper(scalars, row)
-        total = arrived_sum(links_ref, 2, row, rows, sum_ref, above_ref, below_ref, later_ref, earlier_ref)
+        total = arrived_sum(links_ref, 2, row, rows, sum_ref, edge_ref, above_ref, below_ref)
         third = combine(lambda s: 0.75 * (inside * (eps * s)), total)
         store_field(third_ref, row, third)
-        send_parts(links_ref, 1, row, rows, third, up_ref, first_ref, last_ref)
+        edge_parts(links_ref, 1, row, rows, third, first_ref, last_ref)
         return carry
 
     lax.fori_loop(0, rows, one, 0)
 
 
 def second_kernel(
-    rows, scalars, links_ref, sum_ref, above_ref, below_ref, later_ref, earlier_ref, start_ref, third_ref,
-    mixed_ref, up_ref, first_ref, last_ref, base_ref,
+    rows, scalars, links_ref, sum_ref, edge_ref, above_ref, below_ref, start_ref, third_ref,
+    mixed_ref, first_ref, last_ref, base_ref,
 ):
     def one(row, carry):
         inside, eps = taper(scalars, row)
-        total = arrived_sum(links_ref, 1, row, rows, sum_ref, above_ref, below_ref, later_ref, earlier_ref)
+        total = arrived_sum(links_ref, 1, row, rows, sum_ref, edge_ref, above_ref, below_ref)
         third = load_field(third_ref, row)
         second = combine(lambda v, s: v + (8.0 / 9.0) * (inside * (eps * s)), load_field(start_ref, row), total)
         mixed = combine(lambda p, q: 0.25 * p - (2.0 / 9.0) * q, second, third)
         store_field(mixed_ref, row, mixed)
         store_field(base_ref, row, combine(lambda p, q: p + q, second, third))
-        send_parts(links_ref, 0, row, rows, mixed, up_ref, first_ref, last_ref)
-        return carry
-
-    lax.fori_loop(0, rows, one, 0)
-
-
-def last_kernel(
-    rows, scalars, links_ref, sum_ref, above_ref, below_ref, later_ref, earlier_ref, base_ref, out_ref
-):
+        edge_parts(links_ref, 0, row, rows, mixed, first_ref, last_ref)
+        return carry
+
+    lax.fori_loop(0, rows, one, 0)
+
+
+def last_kernel(rows, scalars, links_ref, sum_ref, edge_ref, above_ref, below_ref, base_ref, out_ref):
     def one(row, carry):
         inside, eps = taper(scalars, row)
-        total = arrived_sum(links_ref, 0, row, rows, sum_ref, above_ref, below_ref, later_ref, earlier_ref)
+        total = arrived_sum(links_ref, 0, row, rows, sum_ref, edge_ref, above_ref, below_ref)
         store_field(out_ref, row, combine(lambda p, s: p + inside * (eps * s), load_field(base_ref, row), total))
         return carry
 
@@ -204,43 +216,42 @@
     )
     whole = jax.ShapeDtypeStruct(adjoint.shape, jnp.float32)
     one_row = jax.ShapeDtypeStruct((1,) + adjoint.shape[1:], jnp.float32)
+    two_rows = jax.ShapeDtypeStruct((2,) + adjoint.shape[1:], jnp.float32)
 
     up_pairs = [(i, (i + per_plane) % count) for i in range(count)]
     down_pairs = [(j, i) for i, j in up_pairs]
-    later_pairs = [(i, i + 1) for i in range(count) if (i + 1) % per_plane]
+    later_pairs = [(i, i - i % per_plane + (i + 1) % per_plane) for i in range(count)]
     earlier_pairs = [(j, i) for i, j in later_pairs]
 
-    def exchange(field, up, first, last):
+    def gathered(link_set, field, first, last):
         later = lax.ppermute(first, "gz", earlier_pairs)
         earlier = lax.ppermute(last, "gz", later_pairs)
-        above = lax.ppermute(field, "gz", down_pairs)
+        up, down, edge = call(
+            functools.partial(middle_kernel, rows, link_set), f"middle_{link_set}", 1,
+            (scalars, field, links, later, earlier), (whole, whole, two_rows), 5,
+        )
+        above = lax.ppermute(down, "gz", down_pairs)
         below = lax.ppermute(up, "gz", up_pairs)
-        return above, below, later, earlier
-
-    def local(field, link_set):
-        return call(
+        total = call(
             functools.partial(local_kernel, rows, link_set), f"local_{link_set}", 0, (field, links), whole, 22
         )
-
-    start, up, first, last = call(
-        functools.partial(begin_kernel, rows), "begin", 1, (scalars, adjoint, links),
-        (whole, whole, one_row, one_row), 5,
-    )
-    arrived = exchange(start, up, first, last)
-    third, up, first, last = call(
-        functools.partial(third_kernel, rows), "third", 1, (scalars, links, local(start, 2)) + arrived,
-        (whole, whole, one_row, one_row), 10,
-    )
-    arrived = exchange(third, up, first, last)
-    mixed, up, first, last, base = call(
+        return total, edge, above, below
+
+    start, first, last = call(
+        functools.partial(begin_kernel, rows), "begin", 1, (scalars, adjoint, links), (whole, one_row, one_row), 1
+    )
+    third, first, last = call(
+        functools.partial(third_kernel, rows), "third", 1, (scalars, links) + gathered(2, start, first, last),
+        (whole, one_row, one_row), 5,
+    )
+    mixed, first, last, base = call(
         functools.partial(second_kernel, rows), "second", 1,
-        (scalars, links, local(third, 1)) + arrived + (start, third),
-        (whole, whole, one_row, one_row, whole), 10,
-    )
-    arrived = exchange(mixed, up, first, last)
+        (scalars, links) + gathered(1, third, first, last) + (start, third),
+        (whole, one_row, one_row, whole), 5,
+    )
     return call(
-        functools.partial(last_kernel, rows), "last", 1, (scalars, links, local(mixed, 0)) + arrived + (base,),
-        whole, 5,
+        functools.partial(last_kernel, rows), "last", 1,
+        (scalars, links) + gathered(0, mixed, first, last) + (base,), whole, 4,
     )
 
 

time: 43.8 us -> 49.5 us (1.13)
  the two profiles are of different devices: /device:TPU:4 before, /device:TPU:0 now
where the time goes in v2:
time: 49.5 us; the launch traced here: 49.3 us
  waiting for transfers between devices  26.3 us (53%)
  starting transfers between devices  12.3 us (25%)
  Pallas kernels  6.7 us (14%)
  between operations  2.03 us (4%)
  local copies, waits for them, and re-layouts  1.91 us (4%)
    ppermute x3, waiting for transfers between devices, gathered(): below = lax.ppermute(up, 'gz', up_pairs)  8.26 us
    ppermute x3, waiting for transfers between devices, gathered(): earlier = lax.ppermute(last, 'gz', later_pairs)  7.95 us
    pallas_call x10, Pallas kernels, call(): pl.pallas_call(kernel, name=name, out_shape=out_shapes, in_specs=[smem] *...  6.7 us
    ppermute x3, waiting for transfers between devices, gathered(): above = lax.ppermute(down, 'gz', down_pairs)  6.06 us
    ppermute x3, starting transfers between devices, gathered(): above = lax.ppermute(down, 'gz', down_pairs)  4.35 us
    ppermute x3, waiting for transfers between devices, gathered(): later = lax.ppermute(first, 'gz', earlier_pairs)  4.01 us
    ppermute x3, starting transfers between devices, gathered(): later = lax.ppermute(first, 'gz', earlier_pairs)  3.96 us
    ppermute x3, starting transfers between devices, gathered(): below = lax.ppermute(up, 'gz', up_pairs)  3.45 us
  transfers between devices with their start and end apart: 12, of which 12 were waited for; matrix products, arithmetic and copies ran while one was open for 0% of the time, Pallas kernels for 3%

profile of v2, /device:TPU:0, one launch (start us, length us, event | category | flops | bytes accessed | tf_op | source)
XLA Modules:
  0.0 49.3 jit_solution(13361105408233615459)
XLA Ops:
  2.0 1.0 %copy-done = f32[4,3,4,2,3,3,128]{6,3,5,4,2,1,0:T(2,128)S(1)} copy-done((f32[4,3,4,2,3,3,128]{6,3,5,4,2,1,0:T(2,128)S(1)}, f32[4,3,4,2,3,3,128]{6,3,5,4,2,1,0:T(2,128)}, u32[]{:S(2)}) %copy-start) | copy-done | bytes 442392
  3.0 0.9 %copy-done.2 = f32[4,2,3,8,128]{4,3,2,1,0:T(8,128)S(1)} copy-done((f32[4,2,3,8,128]{4,3,2,1,0:T(8,128)S(1)}, f32[4,2,3,8,128]{4,3,2,1,0:T(8,128)}, u32[]{:S(2)}) %copy-start.2) | copy-done | bytes 98328
  3.9 0.7 %begin.1 = (f32[4,2,3,8,128]{4,3,2,1,0:T(8,128)S(1)}, f32[1,2,3,8,128]{4,3,2,1,0:T(8,128)S(1)}, f32[1,2,3,8,128]{4,3,2,1,0:T(8,128)S(1)}) custom-call(s32[4]{0:T(128)S(1)} %pad_add_fusion.scalars, f32[4,2,3,8,128]{4,3,2,1,0:T(8,128)S(1)} %copy-done.2, f32[864,128]{1,0:T(8,128)S(1)} %bitcast.4), custom_call_target="tpu_custom_call" | custom-call | flops 73728 | bytes 73728 | tf_op jit(solution)/shard_map/begin/pallas_call | solution.py:197
  4.6 3.4 %collective-permute-start = (f32[1,2,3,8,128]{4,3,2,1,0:T(8,128)S(1)}, f32[1,2,3,8,128]{4,3,2,1,0:T(8,128)S(1)}, u32[]{:S(2)}, u32[]{:S(2)}) collective-permute-start(f32[1,2,3,8,128]{4,3,2,1,0:T(8,128)S(1)} %get-tuple-element.25), channel_id=1, source_target_pairs={{1,0},{2,1},{3,2},{4,3},{5,4},{6,5},{7,6},{0,7},{9,8},{10,9},{11,1... | collective-permute-start | bytes 73736 | tf_op jit(solution)/shard_map/ppermute | solution.py:227
  8.0 1.5 %collective-permute-done.later_ref = f32[1,2,3,8,128]{4,3,2,1,0:T(8,128)S(1)} collective-permute-done((f32[1,2,3,8,128]{4,3,2,1,0:T(8,128)S(1)}, f32[1,2,3,8,128]{4,3,2,1,0:T(8,128)S(1)}, u32[]{:S(2)}, u32[]{:S(2)}) %collective-permute-start) | collective-permute-done | bytes 24608 | tf_op jit(solution)/shard_map/ppermute | solution.py:227
  9.5 2.6 %collective-permute-done.1.earlier_ref = f32[1,2,3,8,128]{4,3,2,1,0:T(8,128)S(1)} collective-permute-done((f32[1,2,3,8,128]{4,3,2,1,0:T(8,128)S(1)}, f32[1,2,3,8,128]{4,3,2,1,0:T(8,128)S(1)}, u32[]{:S(2)}, u32[]{:S(2)}) %collective-permute-start.1) | collective-permute-done | bytes 24608 | tf_op jit(solution)/shard_map/ppermute | solution.py:228
  12.1 0.6 %middle_2.1 = (f32[4,2,3,8,128]{4,3,2,1,0:T(8,128)S(1)}, f32[4,2,3,8,128]{4,3,2,1,0:T(8,128)S(1)}, f32[2,2,3,8,128]{4,3,2,1,0:T(8,128)S(1)}) custom-call(s32[4]{0:T(128)S(1)} %pad_add_fusion.scalars, f32[4,2,3,8,128]{4,3,2,1,0:T(8,128)S(1)} %get-tuple-element.24.field_ref.start_ref, f32[864,128]{1,0:T(8,128)S(1)} %bitcast.5, ...), custom_call_target="tpu_custom_call" | custom-call | flops 368640 | bytes 368640 | tf_op jit(solution)/shard_map/middle_2/pallas_call | solution.py:197
  12.8 3.7 %collective-permute-start.2 = (f32[4,2,3,8,128]{4,3,2,1,0:T(8,128)S(1)}, f32[4,2,3,8,128]{4,3,2,1,0:T(8,128)S(1)}, u32[]{:S(2)}, u32[]{:S(2)}) collective-permute-start(f32[4,2,3,8,128]{4,3,2,1,0:T(8,128)S(1)} %get-tuple-element.28), channel_id=1, source_target_pairs={{8,0},{9,1},{10,2},{11,3},{12,4},{13,5},{14,6},{15,7},{16,8},{17,9... | collective-permute-start | bytes 294920 | tf_op jit(solution)/shard_map/ppermute | solution.py:233
  16.9 1.7 %collective-permute-done.2.above_ref = f32[4,2,3,8,128]{4,3,2,1,0:T(8,128)S(1)} collective-permute-done((f32[4,2,3,8,128]{4,3,2,1,0:T(8,128)S(1)}, f32[4,2,3,8,128]{4,3,2,1,0:T(8,128)S(1)}, u32[]{:S(2)}, u32[]{:S(2)}) %collective-permute-start.2) | collective-permute-done | bytes 98336 | tf_op jit(solution)/shard_map/ppermute | solution.py:233
  18.6 4.2 %collective-permute-done.3.below_ref = f32[4,2,3,8,128]{4,3,2,1,0:T(8,128)S(1)} collective-permute-done((f32[4,2,3,8,128]{4,3,2,1,0:T(8,128)S(1)}, f32[4,2,3,8,128]{4,3,2,1,0:T(8,128)S(1)}, u32[]{:S(2)}, u32[]{:S(2)}) %collective-permute-start.3) | collective-permute-done | bytes 98336 | tf_op jit(solution)/shard_map/ppermute | solution.py:234
  22.8 0.7 %third.1 = (f32[4,2,3,8,128]{4,3,2,1,0:T(8,128)S(1)}, f32[1,2,3,8,128]{4,3,2,1,0:T(8,128)S(1)}, f32[1,2,3,8,128]{4,3,2,1,0:T(8,128)S(1)}) custom-call(s32[4]{0:T(128)S(1)} %pad_add_fusion.scalars, f32[864,128]{1,0:T(8,128)S(1)} %bitcast.7, f32[4,2,3,8,128]{4,3,2,1,0:T(8,128)S(1)} %local_2.1.sum_ref, f32[2,2,3,8,128]{4,3,2,1,0:T(8,128)S(1)} %get-tuple-element.27.edge_ref, ...), custom_call_target="tpu_custom_call" | custom-call | flops 368640 | bytes 368640 | tf_op jit(solution)/shard_map/third/pallas_call | solution.py:197
  24.1 1.0 %collective-permute-done.4.later_ref = f32[1,2,3,8,128]{4,3,2,1,0:T(8,128)S(1)} collective-permute-done((f32[1,2,3,8,128]{4,3,2,1,0:T(8,128)S(1)}, f32[1,2,3,8,128]{4,3,2,1,0:T(8,128)S(1)}, u32[]{:S(2)}, u32[]{:S(2)}) %collective-permute-start.4) | collective-permute-done | bytes 24608 | tf_op jit(solution)/shard_map/ppermute | solution.py:227
  25.1 2.7 %collective-permute-done.5.earlier_ref = f32[1,2,3,8,128]{4,3,2,1,0:T(8,128)S(1)} collective-permute-done((f32[1,2,3,8,128]{4,3,2,1,0:T(8,128)S(1)}, f32[1,2,3,8,128]{4,3,2,1,0:T(8,128)S(1)}, u32[]{:S(2)}, u32[]{:S(2)}) %collective-permute-start.5) | collective-permute-done | bytes 24608 | tf_op jit(solution)/shard_map/ppermute | solution.py:228
  28.5 2.0 %collective-permute-start.7 = (f32[4,2,3,8,128]{4,3,2,1,0:T(8,128)S(1)}, f32[4,2,3,8,128]{4,3,2,1,0:T(8,128)S(1)}, u32[]{:S(2)}, u32[]{:S(2)}) collective-permute-start(f32[4,2,3,8,128]{4,3,2,1,0:T(8,128)S(1)} %get-tuple-element.35), channel_id=1, source_target_pairs={{0,8},{1,9},{2,10},{3,11},{4,12},{5,13},{6,14},{7,15},{8,16},{9,17... | collective-permute-start | bytes 294920 | tf_op jit(solution)/shard_map/ppermute | solution.py:234
  31.0 2.3 %collective-permute-done.6.above_ref = f32[4,2,3,8,128]{4,3,2,1,0:T(8,128)S(1)} collective-permute-done((f32[4,2,3,8,128]{4,3,2,1,0:T(8,128)S(1)}, f32[4,2,3,8,128]{4,3,2,1,0:T(8,128)S(1)}, u32[]{:S(2)}, u32[]{:S(2)}) %collective-permute-start.6) | collective-permute-done | bytes 98336 | tf_op jit(solution)/shard_map/ppermute | solution.py:233
  33.3 1.7 %collective-permute-done.7.below_ref = f32[4,2,3,8,128]{4,3,2,1,0:T(8,128)S(1)} collective-permute-done((f32[4,2,3,8,128]{4,3,2,1,0:T(8,128)S(1)}, f32[4,2,3,8,128]{4,3,2,1,0:T(8,128)S(1)}, u32[]{:S(2)}, u32[]{:S(2)}) %collective-permute-start.7) | collective-permute-done | bytes 98336 | tf_op jit(solution)/shard_map/ppermute | solution.py:234
  35.0 0.7 %second.1 = (f32[4,2,3,8,128]{4,3,2,1,0:T(8,128)S(1)}, f32[1,2,3,8,128]{4,3,2,1,0:T(8,128)S(1)}, f32[1,2,3,8,128]{4,3,2,1,0:T(8,128)S(1)}, f32[4,2,3,8,128]{4,3,2,1,0:T(8,128)S(1)}) custom-call(s32[4]{0:T(128)S(1)} %pad_add_fusion.scalars, f32[864,128]{1,0:T(8,128)S(1)} %bitcast.10, f32[4,2,3,8,128]{4,3,2,1,0:T(8,128)S(1)} %local_1.1.sum_ref, ...), custom_call_target="tpu_custom_call" | custom-call | flops 368640 | bytes 368640 | tf_op jit(solution)/shard_map/second/pallas_call | solution.py:197
  36.2 1.5 %collective-permute-done.8.later_ref = f32[1,2,3,8,128]{4,3,2,1,0:T(8,128)S(1)} collective-permute-done((f32[1,2,3,8,128]{4,3,2,1,0:T(8,128)S(1)}, f32[1,2,3,8,128]{4,3,2,1,0:T(8,128)S(1)}, u32[]{:S(2)}, u32[]{:S(2)}) %collective-permute-start.8) | collective-permute-done | bytes 24608 | tf_op jit(solution)/shard_map/ppermute | solution.py:227
  37.7 2.6 %collective-permute-done.9.earlier_ref = f32[1,2,3,8,128]{4,3,2,1,0:T(8,128)S(1)} collective-permute-done((f32[1,2,3,8,128]{4,3,2,1,0:T(8,128)S(1)}, f32[1,2,3,8,128]{4,3,2,1,0:T(8,128)S(1)}, u32[]{:S(2)}, u32[]{:S(2)}) %collective-permute-start.9) | collective-permute-done | bytes 24608 | tf_op jit(solution)/shard_map/ppermute | solution.py:228
  41.0 0.6 %collective-permute-start.10 = (f32[4,2,3,8,128]{4,3,2,1,0:T(8,128)S(1)}, f32[4,2,3,8,128]{4,3,2,1,0:T(8,128)S(1)}, u32[]{:S(2)}, u32[]{:S(2)}) collective-permute-start(f32[4,2,3,8,128]{4,3,2,1,0:T(8,128)S(1)} %get-tuple-element.40), channel_id=1, source_target_pairs={{8,0},{9,1},{10,2},{11,3},{12,4},{13,5},{14,6},{15,7},{16,8},{17,9... | collective-permute-start | bytes 294920 | tf_op jit(solution)/shard_map/ppermute | solution.py:233
  41.6 1.4 %collective-permute-start.11 = (f32[4,2,3,8,128]{4,3,2,1,0:T(8,128)S(1)}, f32[4,2,3,8,128]{4,3,2,1,0:T(8,128)S(1)}, u32[]{:S(2)}, u32[]{:S(2)}) collective-permute-start(f32[4,2,3,8,128]{4,3,2,1,0:T(8,128)S(1)} %get-tuple-element.41), channel_id=1, source_target_pairs={{0,8},{1,9},{2,10},{3,11},{4,12},{5,13},{6,14},{7,15},{8,16},{9,17... | collective-permute-start | bytes 294920 | tf_op jit(solution)/shard_map/ppermute | solution.py:234
  43.5 2.1 %collective-permute-done.10.above_ref = f32[4,2,3,8,128]{4,3,2,1,0:T(8,128)S(1)} collective-permute-done((f32[4,2,3,8,128]{4,3,2,1,0:T(8,128)S(1)}, f32[4,2,3,8,128]{4,3,2,1,0:T(8,128)S(1)}, u32[]{:S(2)}, u32[]{:S(2)}) %collective-permute-start.10) | collective-permute-done | bytes 98336 | tf_op jit(solution)/shard_map/ppermute | solution.py:233
  45.6 2.4 %collective-permute-done.11.below_ref = f32[4,2,3,8,128]{4,3,2,1,0:T(8,128)S(1)} collective-permute-done((f32[4,2,3,8,128]{4,3,2,1,0:T(8,128)S(1)}, f32[4,2,3,8,128]{4,3,2,1,0:T(8,128)S(1)}, u32[]{:S(2)}, u32[]{:S(2)}) %collective-permute-start.11) | collective-permute-done | bytes 98336 | tf_op jit(solution)/shard_map/ppermute | solution.py:234
  48.0 1.3 %last.1 = f32[4,2,3,8,128]{4,3,2,1,0:T(8,128)} custom-call(s32[4]{0:T(128)S(1)} %pad_add_fusion.scalars, f32[864,128]{1,0:T(8,128)S(1)} %bitcast.13, f32[4,2,3,8,128]{4,3,2,1,0:T(8,128)S(1)} %local_0.1.sum_ref, f32[2,2,3,8,128]{4,3,2,1,0:T(8,128)S(1)} %get-tuple-element.39.edge_ref, f32[4,2,3,8,128]{4,3,2,1,0:T(8,128)S(1)} %collective-permute-done.10.above_ref, ...), custom_call_target="tpu_custom_call" | custom-call | flops 294912 | bytes 294912 | tf_op jit(solution)/shard_map/last/pallas_call | solution.py:197
  (17 shorter events, 4.0 us)
Async XLA Ops:
  2.0 1.0 %copy-start = (f32[4,3,4,2,3,3,128]{6,3,5,4,2,1,0:T(2,128)S(1)}, f32[4,3,4,2,3,3,128]{6,3,5,4,2,1,0:T(2,128)}, u32[]{:S(2)}) copy-start(f32[4,3,4,2,3,3,128]{6,3,5,4,2,1,0:T(2,128)} %param.6) | copy-start | bytes 1327108
  3.0 0.9 %copy-start.2 = (f32[4,2,3,8,128]{4,3,2,1,0:T(8,128)S(1)}, f32[4,2,3,8,128]{4,3,2,1,0:T(8,128)}, u32[]{:S(2)}) copy-start(f32[4,2,3,8,128]{4,3,2,1,0:T(8,128)} %adjoint_ref.1) | copy-start | bytes 294916
  3.9 8.2 %copy-start.1 = (f32[4,3,4,2,3,3,128]{6,3,5,4,2,1,0:T(2,128)S(1)}, f32[4,3,4,2,3,3,128]{6,3,5,4,2,1,0:T(2,128)}, u32[]{:S(2)}) copy-start(f32[4,3,4,2,3,3,128]{6,3,5,4,2,1,0:T(2,128)} %param.6) | copy-start | bytes 1327108
  4.6 4.9 %collective-permute-start = (f32[1,2,3,8,128]{4,3,2,1,0:T(8,128)S(1)}, f32[1,2,3,8,128]{4,3,2,1,0:T(8,128)S(1)}, u32[]{:S(2)}, u32[]{:S(2)}) collective-permute-start(f32[1,2,3,8,128]{4,3,2,1,0:T(8,128)S(1)} %get-tuple-element.25), channel_id=1, source_target_pairs={{1,0},{2,1},{3,2},{4,3},{5,4},{6,5},{7,6},{0,7},{9,8},{10,9},{11,1... | collective-permute-start | bytes 73736 | tf_op jit(solution)/shard_map/ppermute | solution.py:227
  8.0 4.2 %collective-permute-start.1 = (f32[1,2,3,8,128]{4,3,2,1,0:T(8,128)S(1)}, f32[1,2,3,8,128]{4,3,2,1,0:T(8,128)S(1)}, u32[]{:S(2)}, u32[]{:S(2)}) collective-permute-start(f32[1,2,3,8,128]{4,3,2,1,0:T(8,128)S(1)} %get-tuple-element.26), channel_id=1, source_target_pairs={{0,1},{1,2},{2,3},{3,4},{4,5},{5,6},{6,7},{7,0},{8,9},{9,10},{10,1... | collective-permute-start | bytes 73736 | tf_op jit(solution)/shard_map/ppermute | solution.py:228
  12.8 5.9 %collective-permute-start.2 = (f32[4,2,3,8,128]{4,3,2,1,0:T(8,128)S(1)}, f32[4,2,3,8,128]{4,3,2,1,0:T(8,128)S(1)}, u32[]{:S(2)}, u32[]{:S(2)}) collective-permute-start(f32[4,2,3,8,128]{4,3,2,1,0:T(8,128)S(1)} %get-tuple-element.28), channel_id=1, source_target_pairs={{8,0},{9,1},{10,2},{11,3},{12,4},{13,5},{14,6},{15,7},{16,8},{17,9... | collective-permute-start | bytes 294920 | tf_op jit(solution)/shard_map/ppermute | solution.py:233
  16.4 6.4 %collective-permute-start.3 = (f32[4,2,3,8,128]{4,3,2,1,0:T(8,128)S(1)}, f32[4,2,3,8,128]{4,3,2,1,0:T(8,128)S(1)}, u32[]{:S(2)}, u32[]{:S(2)}) collective-permute-start(f32[4,2,3,8,128]{4,3,2,1,0:T(8,128)S(1)} %get-tuple-element.29), channel_id=1, source_target_pairs={{0,8},{1,9},{2,10},{3,11},{4,12},{5,13},{6,14},{7,15},{8,16},{9,17... | collective-permute-start | bytes 294920 | tf_op jit(solution)/shard_map/ppermute | solution.py:234
  23.5 1.6 %collective-permute-start.4 = (f32[1,2,3,8,128]{4,3,2,1,0:T(8,128)S(1)}, f32[1,2,3,8,128]{4,3,2,1,0:T(8,128)S(1)}, u32[]{:S(2)}, u32[]{:S(2)}) collective-permute-start(f32[1,2,3,8,128]{4,3,2,1,0:T(8,128)S(1)} %get-tuple-element.31), channel_id=1, source_target_pairs={{1,0},{2,1},{3,2},{4,3},{5,4},{6,5},{7,6},{0,7},{9,8},{10,9},{11,1... | collective-permute-start | bytes 73736 | tf_op jit(solution)/shard_map/ppermute | solution.py:227
  23.6 4.2 %collective-permute-start.5 = (f32[1,2,3,8,128]{4,3,2,1,0:T(8,128)S(1)}, f32[1,2,3,8,128]{4,3,2,1,0:T(8,128)S(1)}, u32[]{:S(2)}, u32[]{:S(2)}) collective-permute-start(f32[1,2,3,8,128]{4,3,2,1,0:T(8,128)S(1)} %get-tuple-element.32), channel_id=1, source_target_pairs={{0,1},{1,2},{2,3},{3,4},{4,5},{5,6},{6,7},{7,0},{8,9},{9,10},{10,1... | collective-permute-start | bytes 73736 | tf_op jit(solution)/shard_map/ppermute | solution.py:228
  28.4 4.9 %collective-permute-start.6 = (f32[4,2,3,8,128]{4,3,2,1,0:T(8,128)S(1)}, f32[4,2,3,8,128]{4,3,2,1,0:T(8,128)S(1)}, u32[]{:S(2)}, u32[]{:S(2)}) collective-permute-start(f32[4,2,3,8,128]{4,3,2,1,0:T(8,128)S(1)} %get-tuple-element.34), channel_id=1, source_target_pairs={{8,0},{9,1},{10,2},{11,3},{12,4},{13,5},{14,6},{15,7},{16,8},{17,9... | collective-permute-start | bytes 294920 | tf_op jit(solution)/shard_map/ppermute | solution.py:233
  28.5 6.5 %collective-permute-start.7 = (f32[4,2,3,8,128]{4,3,2,1,0:T(8,128)S(1)}, f32[4,2,3,8,128]{4,3,2,1,0:T(8,128)S(1)}, u32[]{:S(2)}, u32[]{:S(2)}) collective-permute-start(f32[4,2,3,8,128]{4,3,2,1,0:T(8,128)S(1)} %get-tuple-element.35), channel_id=1, source_target_pairs={{0,8},{1,9},{2,10},{3,11},{4,12},{5,13},{6,14},{7,15},{8,16},{9,17... | collective-permute-start | bytes 294920 | tf_op jit(solution)/shard_map/ppermute | solution.py:234
  35.7 2.0 %collective-permute-start.8 = (f32[1,2,3,8,128]{4,3,2,1,0:T(8,128)S(1)}, f32[1,2,3,8,128]{4,3,2,1,0:T(8,128)S(1)}, u32[]{:S(2)}, u32[]{:S(2)}) collective-permute-start(f32[1,2,3,8,128]{4,3,2,1,0:T(8,128)S(1)} %get-tuple-element.37), channel_id=1, source_target_pairs={{1,0},{2,1},{3,2},{4,3},{5,4},{6,5},{7,6},{0,7},{9,8},{10,9},{11,1... | collective-permute-start | bytes 73736 | tf_op jit(solution)/shard_map/ppermute | solution.py:227
  36.2 4.2 %collective-permute-start.9 = (f32[1,2,3,8,128]{4,3,2,1,0:T(8,128)S(1)}, f32[1,2,3,8,128]{4,3,2,1,0:T(8,128)S(1)}, u32[]{:S(2)}, u32[]{:S(2)}) collective-permute-start(f32[1,2,3,8,128]{4,3,2,1,0:T(8,128)S(1)} %get-tuple-element.38), channel_id=1, source_target_pairs={{0,1},{1,2},{2,3},{3,4},{4,5},{5,6},{6,7},{7,0},{8,9},{9,10},{10,1... | collective-permute-start | bytes 73736 | tf_op jit(solution)/shard_map/ppermute | solution.py:228
  41.0 4.7 %collective-permute-start.10 = (f32[4,2,3,8,128]{4,3,2,1,0:T(8,128)S(1)}, f32[4,2,3,8,128]{4,3,2,1,0:T(8,128)S(1)}, u32[]{:S(2)}, u32[]{:S(2)}) collective-permute-start(f32[4,2,3,8,128]{4,3,2,1,0:T(8,128)S(1)} %get-tuple-element.40), channel_id=1, source_target_pairs={{8,0},{9,1},{10,2},{11,3},{12,4},{13,5},{14,6},{15,7},{16,8},{17,9... | collective-permute-start | bytes 294920 | tf_op jit(solution)/shard_map/ppermute | solution.py:233
  41.6 6.4 %collective-permute-start.11 = (f32[4,2,3,8,128]{4,3,2,1,0:T(8,128)S(1)}, f32[4,2,3,8,128]{4,3,2,1,0:T(8,128)S(1)}, u32[]{:S(2)}, u32[]{:S(2)}) collective-permute-start(f32[4,2,3,8,128]{4,3,2,1,0:T(8,128)S(1)} %get-tuple-element.41), channel_id=1, source_target_pairs={{0,8},{1,9},{2,10},{3,11},{4,12},{5,13},{6,14},{7,15},{8,16},{9,17... | collective-permute-start | bytes 294920 | tf_op jit(solution)/shard_map/ppermute | solution.py:234

commit v3 on v2

--- a/solution.py
+++ b/solution.py
@@ -28,12 +28,12 @@
     return [[function(*(f[c][a] for f in fields)) for a in range(3)] for c in range(2)]
 
 
-def entry(links_ref, row, link_set, mu, a, b, c, shape):
-    index = ((row * SETS + link_set) * MUS + mu) * ENTRIES + (a * 3 + b) * 2 + c
+def entry(links_ref, row, link_set, mu, a, b, c, shape, mus=MUS):
+    index = ((row * SETS + link_set) * mus + mu) * ENTRIES + (a * 3 + b) * 2 + c
     return jnp.broadcast_to(links_ref[pl.ds(index, 1), :], shape)
 
 
-def transport(links_ref, row, link_set, mu, ahead, here):
+def transport(links_ref, row, link_set, mu, ahead, here, mus=MUS):
     forward = [[None] * 3, [None] * 3]
     backward = [[None] * 3, [None] * 3]
     shape = (ahead if ahead is not None else here)[0][0].shape
@@ -43,8 +43,8 @@
 
     for a in range(3):
         for b in range(3):
-            real = entry(links_ref, row, link_set, mu, a, b, 0, shape)
-            imag = entry(links_ref, row, link_set, mu, a, b, 1, shape)
+            real = entry(links_ref, row, link_set, mu, a, b, 0, shape, mus)
+            imag = entry(links_ref, row, link_set, mu, a, b, 1, shape, mus)
             if ahead is not None:
                 add(forward, 0, a, real * ahead[0][b] - imag * ahead[1][b])
                 add(forward, 1, a, real * ahead[1][b] + imag * ahead[0][b])
@@ -90,23 +90,6 @@
     lax.fori_loop(0, rows, one, 0)
 
 
-def middle_kernel(rows, link_set, scalars, field_ref, links_ref, later_ref, earlier_ref, up_ref, down_ref, edge_ref):
-    def one(row, carry):
-        field = load_field(field_ref, row)
-        store_field(down_ref, row, field)
-        _, up = transport(links_ref, row, link_set, 2, None, field)
-        store_field(up_ref, row, up)
-        return carry
-
-    lax.fori_loop(0, rows, one, 0)
-    first_pos = lax.rem(scalars[3], BAND)
-    not_first = jnp.where(first_pos != 0, 1.0, 0.0)
-    not_last = jnp.where(first_pos != BAND - rows, 1.0, 0.0)
-    store_field(edge_ref, 0, combine(lambda h: not_first * h, load_field(earlier_ref, 0)))
-    ahead_t, _ = transport(links_ref, rows - 1, link_set, 3, load_field(later_ref, 0), None)
-    store_field(edge_ref, 1, combine(lambda f: not_last * f, ahead_t))
-
-
 def local_kernel(rows, link_set, field_ref, links_ref, sum_ref):
     shape = field_ref.shape[-2:]
     x_pos = lax.broadcasted_iota(jnp.int32, shape, 1) % LX
@@ -139,22 +122,31 @@
     lax.fori_loop(0, rows - 1, between, 0)
 
 
-def arrived_sum(links_ref, link_set, row, rows, sum_ref, edge_ref, above_ref, below_ref):
-    ahead_z, _ = transport(links_ref, row, link_set, 2, load_field(above_ref, row), None)
-    total = combine(lambda s, f, h: s + f + h, load_field(sum_ref, row), ahead_z, load_field(below_ref, row))
-    is_first = jnp.where(row == 0, 1.0, 0.0)
-    is_last = jnp.where(row == rows - 1, 1.0, 0.0)
-    return combine(
-        lambda s, h, f: s + is_first * h + is_last * f, total, load_field(edge_ref, 0), load_field(edge_ref, 1)
-    )
+def arrived_sum(
+    links_ref, link_set, row, rows, scalars, planes, sum_ref, lower_links_ref, gathered_ref, later_ref, earlier_ref
+):
+    first_pos = lax.rem(scalars[3], BAND)
+    plane = scalars[3] // BAND
+    above = lax.rem(plane + 1, planes)
+    below = lax.rem(plane + planes - 1, planes)
+    ahead_z, _ = transport(links_ref, row, link_set, 2, load_field(gathered_ref.at[above], row), None)
+    _, behind_z = transport(lower_links_ref, row, link_set, 0, None, load_field(gathered_ref.at[below], row), 1)
+    total = combine(lambda s, f, h: s + f + h, load_field(sum_ref, row), ahead_z, behind_z)
+    is_first = jnp.where((row == 0) & (first_pos != 0), 1.0, 0.0)
+    is_last = jnp.where((row == rows - 1) & (first_pos != BAND - rows), 1.0, 0.0)
+    ahead_t, _ = transport(links_ref, row, link_set, 3, load_field(later_ref, 0), None)
+    return combine(lambda s, f, h: s + is_last * f + is_first * h, total, ahead_t, load_field(earlier_ref, 0))
 
 
 def third_kernel(
-    rows, scalars, links_ref, sum_ref, edge_ref, above_ref, below_ref, third_ref, first_ref, last_ref
+    rows, planes, scalars, links_ref, sum_ref, lower_links_ref, gathered_ref, later_ref, earlier_ref,
+    third_ref, first_ref, last_ref,
 ):
     def one(row, carry):
         inside, eps = taper(scalars, row)
-        total = arrived_sum(links_ref, 2, row, rows, sum_ref, edge_ref, above_ref, below_ref)
+        total = arrived_sum(
+            links_ref, 2, row, rows, scalars, planes, sum_ref, lower_links_ref, gathered_ref, later_ref, earlier_ref
+        )
         third = combine(lambda s: 0.75 * (inside * (eps * s)), total)
         store_field(third_ref, row, third)
         edge_parts(links_ref, 1, row, rows, third, first_ref, last_ref)
@@ -164,12 +156,14 @@
 
 
 def second_kernel(
-    rows, scalars, links_ref, sum_ref, edge_ref, above_ref, below_ref, start_ref, third_ref,
-    mixed_ref, first_ref, last_ref, base_ref,
+    rows, planes, scalars, links_ref, sum_ref, lower_links_ref, gathered_ref, later_ref, earlier_ref, start_ref,
+    third_ref, mixed_ref, first_ref, last_ref, base_ref,
 ):
     def one(row, carry):
         inside, eps = taper(scalars, row)
-        total = arrived_sum(links_ref, 1, row, rows, sum_ref, edge_ref, above_ref, below_ref)
+        total = arrived_sum(
+            links_ref, 1, row, rows, scalars, planes, sum_ref, lower_links_ref, gathered_ref, later_ref, earlier_ref
+        )
         third = load_field(third_ref, row)
         second = combine(lambda v, s: v + (8.0 / 9.0) * (inside * (eps * s)), load_field(start_ref, row), total)
         mixed = combine(lambda p, q: 0.25 * p - (2.0 / 9.0) * q, second, third)
@@ -181,10 +175,14 @@
     lax.fori_loop(0, rows, one, 0)
 
 
-def last_kernel(rows, scalars, links_ref, sum_ref, edge_ref, above_ref, below_ref, base_ref, out_ref):
+def last_kernel(
+    rows, planes, scalars, links_ref, sum_ref, lower_links_ref, gathered_ref, later_ref, earlier_ref, base_ref, out_ref
+):
     def one(row, carry):
         inside, eps = taper(scalars, row)
-        total = arrived_sum(links_ref, 0, row, rows, sum_ref, edge_ref, above_ref, below_ref)
+        total = arrived_sum(
+            links_ref, 0, row, rows, scalars, planes, sum_ref, lower_links_ref, gathered_ref, later_ref, earlier_ref
+        )
         store_field(out_ref, row, combine(lambda p, s: p + inside * (eps * s), load_field(base_ref, row), total))
         return carry
 
@@ -210,48 +208,45 @@
     per_plane = BAND // rows
     count = lax.axis_size("gz")
     me = lax.axis_index("gz")
-    links = jnp.transpose(flowed, (0, 1, 2, 4, 5, 3, 6)).reshape(-1, flowed.shape[-1])
+    planes = count // per_plane
+    by_entry = jnp.transpose(flowed, (0, 1, 2, 4, 5, 3, 6))
+    links = by_entry.reshape(-1, flowed.shape[-1])
     scalars = jnp.concatenate(
         [source_slice, band_width, flow_steps, (me * rows).astype(jnp.int32).reshape(1)]
     )
     whole = jax.ShapeDtypeStruct(adjoint.shape, jnp.float32)
     one_row = jax.ShapeDtypeStruct((1,) + adjoint.shape[1:], jnp.float32)
-    two_rows = jax.ShapeDtypeStruct((2,) + adjoint.shape[1:], jnp.float32)
 
     up_pairs = [(i, (i + per_plane) % count) for i in range(count)]
-    down_pairs = [(j, i) for i, j in up_pairs]
     later_pairs = [(i, i - i % per_plane + (i + 1) % per_plane) for i in range(count)]
     earlier_pairs = [(j, i) for i, j in later_pairs]
-
-    def gathered(link_set, field, first, last):
+    z_lines = [[t + z * per_plane for z in range(planes)] for t in range(per_plane)]
+    lower_links = lax.ppermute(by_entry[:, :, 2], "gz", up_pairs).reshape(-1, flowed.shape[-1])
+
+    def arrivals(link_set, field, first, last):
+        gathered = lax.all_gather(field, "gz", axis_index_groups=z_lines)
         later = lax.ppermute(first, "gz", earlier_pairs)
         earlier = lax.ppermute(last, "gz", later_pairs)
-        up, down, edge = call(
-            functools.partial(middle_kernel, rows, link_set), f"middle_{link_set}", 1,
-            (scalars, field, links, later, earlier), (whole, whole, two_rows), 5,
-        )
-        above = lax.ppermute(down, "gz", down_pairs)
-        below = lax.ppermute(up, "gz", up_pairs)
         total = call(
             functools.partial(local_kernel, rows, link_set), f"local_{link_set}", 0, (field, links), whole, 22
         )
-        return total, edge, above, below
+        return total, lower_links, gathered, later, earlier
 
     start, first, last = call(
         functools.partial(begin_kernel, rows), "begin", 1, (scalars, adjoint, links), (whole, one_row, one_row), 1
     )
     third, first, last = call(
-        functools.partial(third_kernel, rows), "third", 1, (scalars, links) + gathered(2, start, first, last),
-        (whole, one_row, one_row), 5,
+        functools.partial(third_kernel, rows, planes), "third", 1, (scalars, links) + arrivals(2, start, first, last),
+        (whole, one_row, one_row), 13,
     )
     mixed, first, last, base = call(
-        functools.partial(second_kernel, rows), "second", 1,
-        (scalars, links) + gathered(1, third, first, last) + (start, third),
-        (whole, one_row, one_row, whole), 5,
+        functools.partial(second_kernel, rows, planes), "second", 1,
+        (scalars, links) + arrivals(1, third, first, last) + (start, third),
+        (whole, one_row, one_row, whole), 13,
     )
     return call(
-        functools.partial(last_kernel, rows), "last", 1,
-        (scalars, links) + gathered(0, mixed, first, last) + (base,), whole, 4,
+        functools.partial(last_kernel, rows, planes), "last", 1,
+        (scalars, links) + arrivals(0, mixed, first, last) + (base,), whole, 12,
     )
 
 

time: 49.5 us -> 60.8 us (1.23)
  blocking collectives: 0 us -> 43.5 us
  waiting for transfers between devices: 26.3 us -> 0.02 us
  starting transfers between devices: 12.3 us -> 7.69 us
  Pallas kernels: 6.7 us -> 5.19 us
    all_gather x0 -> x3, blocking collectives: none -> 43.5 us  [arrivals(): gathered = lax.all_gather(field, 'gz', axis_index_groups=z_lines)]
    ppermute x12 -> x7, waiting for transfers between devices: 26.3 us -> 0.02 us  [the longest x3 0.01 us: arrivals(): earlier = lax.ppermute(last, 'gz', later_pairs)]
    ppermute x12 -> x7, starting transfers between devices: 12.3 us -> 7.69 us  [the longest x3 4.6 us: arrivals(): later = lax.ppermute(first, 'gz', earlier_pairs)]
    pallas_call x10 -> x7, Pallas kernels: 6.7 us -> 5.19 us  [call(): pl.pallas_call(kernel, name=name, out_shape=out_shapes, in_specs=[smem] *...]
    squeeze x0 -> x1, local copies, waits for them, and re-layouts: none -> 0.96 us  [body(): by_entry[:, :, 2]]
    unnamed x6, local copies, waits for them, and re-layouts: 1.91 us -> 1.02 us
  transfers between devices with their start and end apart: 12 -> 7, of which waited for: 12 -> 0; matrix products, arithmetic and copies ran while one was open for 0% -> 0% of each run, Pallas kernels for 3% -> 4%
where the time goes in v3:
time: 60.8 us; the launch traced here: 60.5 us
  blocking collectives  43.5 us (72%)
  starting transfers between devices  7.69 us (13%)
  Pallas kernels  5.19 us (9%)
  between operations  2.06 us (3%)
  local copies, waits for them, and re-layouts  1.98 us (3%)
    all_gather x3, blocking collectives, arrivals(): gathered = lax.all_gather(field, 'gz', axis_index_groups=z_lines)  43.5 us
    pallas_call x7, Pallas kernels, call(): pl.pallas_call(kernel, name=name, out_shape=out_shapes, in_specs=[smem] *...  5.19 us
    ppermute x3, starting transfers between devices, arrivals(): later = lax.ppermute(first, 'gz', earlier_pairs)  4.6 us
    ppermute x1, starting transfers between devices, body(): lax.ppermute(by_entry[:, :, 2], 'gz', up_pairs)  3.08 us
  transfers between devices with their start and end apart: 7, of which 0 were waited for; matrix products, arithmetic and copies ran while one was open for 0% of the time, Pallas kernels for 4%

profile of v3, /device:TPU:0, one launch (start us, length us, event | category | flops | bytes accessed | tf_op | source)
XLA Modules:
  0.0 60.5 jit_solution(15672862946388321447)
XLA Ops:
  0.0 1.0 %slice_bitcast_fusion = f32[4,3,3,3,2,128]{5,4,3,2,1,0:T(2,128)S(1)} fusion(f32[4,3,4,3,3,2,128]{6,5,4,3,2,1,0:T(2,128)} %bitcast.10), kind=kLoop, calls=%fused_computation | loop fusion | bytes 221184 | tf_op jit(solution)/shard_map/squeeze | solution.py:224
  1.0 3.1 %collective-permute-start = (f32[4,3,3,3,2,128]{5,4,3,2,1,0:T(2,128)S(1)}, f32[4,3,3,3,2,128]{5,4,3,2,1,0:T(2,128)S(1)}, u32[]{:S(2)}, u32[]{:S(2)}) collective-permute-start(f32[4,3,3,3,2,128]{5,4,3,2,1,0:T(2,128)S(1)} %slice_bitcast_fusion), channel_id=1, source_target_pairs={{0,8},{1,9},{2,10},{3,11},{4,12},{5,13},{6,14},{7,15},{8,16},{9,17... | collective-permute-start | bytes 331784 | tf_op jit(solution)/shard_map/ppermute | solution.py:224
  6.0 0.1 pad_add_fusion.scalars
  6.1 1.0 %copy-done = f32[4,3,4,2,3,3,128]{6,3,5,4,2,1,0:T(2,128)S(1)} copy-done((f32[4,3,4,2,3,3,128]{6,3,5,4,2,1,0:T(2,128)S(1)}, f32[4,3,4,2,3,3,128]{6,3,5,4,2,1,0:T(2,128)}, u32[]{:S(2)}) %copy-start) | copy-done | bytes 442392
  7.1 0.7 %begin.1 = (f32[4,2,3,8,128]{4,3,2,1,0:T(8,128)S(1)}, f32[1,2,3,8,128]{4,3,2,1,0:T(8,128)S(1)}, f32[1,2,3,8,128]{4,3,2,1,0:T(8,128)S(1)}) custom-call(s32[4]{0:T(128)S(1)} %pad_add_fusion.scalars, f32[4,2,3,8,128]{4,3,2,1,0:T(8,128)S(1)} %copy-done.2, f32[864,128]{1,0:T(8,128)S(1)} %bitcast.11), custom_call_target="tpu_custom_call" | custom-call | flops 73728 | bytes 73728 | tf_op jit(solution)/shard_map/begin/pallas_call | solution.py:195
  7.7 1.7 %collective-permute-start.1 = (f32[1,2,3,8,128]{4,3,2,1,0:T(8,128)S(1)}, f32[1,2,3,8,128]{4,3,2,1,0:T(8,128)S(1)}, u32[]{:S(2)}, u32[]{:S(2)}) collective-permute-start(f32[1,2,3,8,128]{4,3,2,1,0:T(8,128)S(1)} %get-tuple-element.16), channel_id=1, source_target_pairs={{1,0},{2,1},{3,2},{4,3},{5,4},{6,5},{7,6},{0,7},{9,8},{10,9},{11,1... | collective-permute-start | bytes 73736 | tf_op jit(solution)/shard_map/ppermute | solution.py:228
  9.4 0.0 collective-permute-start.2
  9.4 14.6 %all-gather = f32[16,2,3,8,128]{4,3,2,1,0:T(8,128)S(1)} all-gather(f32[4,2,3,8,128]{4,3,2,1,0:T(8,128)S(1)} %get-tuple-element.15.field_ref.start_ref), channel_id=2, replica_groups={{0,8,16,24},{1,9,17,25},{2,10,18,26},{3,11,19,27},{4,12,20,28},{5,13,21..., dimensions={0}, use_global_device_ids=true | all-gather | bytes 491520 | tf_op jit(solution)/shard_map/all_gather | solution.py:227
  24.0 0.5 local_2.1.sum_ref
  24.5 0.0 collective-permute-done.1.later_ref
  24.5 0.0 collective-permute-done.2.earlier_ref
  24.5 0.0 collective-permute-done
  24.6 0.8 %third.1 = (f32[4,2,3,8,128]{4,3,2,1,0:T(8,128)S(1)}, f32[1,2,3,8,128]{4,3,2,1,0:T(8,128)S(1)}, f32[1,2,3,8,128]{4,3,2,1,0:T(8,128)S(1)}) custom-call(s32[4]{0:T(128)S(1)} %pad_add_fusion.scalars, f32[864,128]{1,0:T(8,128)S(1)} %bitcast.13, f32[4,2,3,8,128]{4,3,2,1,0:T(8,128)S(1)} %local_2.1.sum_ref, f32[216,128]{1,0:T(8,128)S(1)} %bitcast.21, ...), custom_call_target="tpu_custom_call" | custom-call | flops 958464 | bytes 958464 | tf_op jit(solution)/shard_map/third/pallas_call | solution.py:195
  25.4 1.6 %collective-permute-start.3 = (f32[1,2,3,8,128]{4,3,2,1,0:T(8,128)S(1)}, f32[1,2,3,8,128]{4,3,2,1,0:T(8,128)S(1)}, u32[]{:S(2)}, u32[]{:S(2)}) collective-permute-start(f32[1,2,3,8,128]{4,3,2,1,0:T(8,128)S(1)} %get-tuple-element.19), channel_id=1, source_target_pairs={{1,0},{2,1},{3,2},{4,3},{5,4},{6,5},{7,6},{0,7},{9,8},{10,9},{11,1... | collective-permute-start | bytes 73736 | tf_op jit(solution)/shard_map/ppermute | solution.py:228
  26.9 14.6 %all-gather.1 = f32[16,2,3,8,128]{4,3,2,1,0:T(8,128)S(1)} all-gather(f32[4,2,3,8,128]{4,3,2,1,0:T(8,128)S(1)} %get-tuple-element.18.field_ref.third_ref), channel_id=3, replica_groups={{0,8,16,24},{1,9,17,25},{2,10,18,26},{3,11,19,27},{4,12,20,28},{5,13,21..., dimensions={0}, use_global_device_ids=true | all-gather | bytes 491520 | tf_op jit(solution)/shard_map/all_gather | solution.py:227
  41.5 0.5 local_1.1.sum_ref
  42.0 0.0 collective-permute-done.3.later_ref
  42.0 0.8 %second.1 = (f32[4,2,3,8,128]{4,3,2,1,0:T(8,128)S(1)}, f32[1,2,3,8,128]{4,3,2,1,0:T(8,128)S(1)}, f32[1,2,3,8,128]{4,3,2,1,0:T(8,128)S(1)}, f32[4,2,3,8,128]{4,3,2,1,0:T(8,128)S(1)}) custom-call(s32[4]{0:T(128)S(1)} %pad_add_fusion.scalars, f32[864,128]{1,0:T(8,128)S(1)} %bitcast.15, f32[4,2,3,8,128]{4,3,2,1,0:T(8,128)S(1)} %local_1.1.sum_ref, ...), custom_call_target="tpu_custom_call" | custom-call | flops 958464 | bytes 958464 | tf_op jit(solution)/shard_map/second/pallas_call | solution.py:195
  42.9 1.4 %collective-permute-start.5 = (f32[1,2,3,8,128]{4,3,2,1,0:T(8,128)S(1)}, f32[1,2,3,8,128]{4,3,2,1,0:T(8,128)S(1)}, u32[]{:S(2)}, u32[]{:S(2)}) collective-permute-start(f32[1,2,3,8,128]{4,3,2,1,0:T(8,128)S(1)} %get-tuple-element.22), channel_id=1, source_target_pairs={{1,0},{2,1},{3,2},{4,3},{5,4},{6,5},{7,6},{0,7},{9,8},{10,9},{11,1... | collective-permute-start | bytes 73736 | tf_op jit(solution)/shard_map/ppermute | solution.py:228
  44.3 0.0 collective-permute-start.6
  44.3 14.3 %all-gather.2 = f32[16,2,3,8,128]{4,3,2,1,0:T(8,128)S(1)} all-gather(f32[4,2,3,8,128]{4,3,2,1,0:T(8,128)S(1)} %get-tuple-element.21.field_ref), channel_id=4, replica_groups={{0,8,16,24},{1,9,17,25},{2,10,18,26},{3,11,19,27},{4,12,20,28},{5,13,21..., dimensions={0}, use_global_device_ids=true | all-gather | bytes 491520 | tf_op jit(solution)/shard_map/all_gather | solution.py:227
  58.6 0.5 local_0.1.sum_ref
  59.1 0.0 collective-permute-done.6.earlier_ref
  59.1 1.4 %last.1 = f32[4,2,3,8,128]{4,3,2,1,0:T(8,128)} custom-call(s32[4]{0:T(128)S(1)} %pad_add_fusion.scalars, f32[864,128]{1,0:T(8,128)S(1)} %bitcast.17, f32[4,2,3,8,128]{4,3,2,1,0:T(8,128)S(1)} %local_0.1.sum_ref, f32[216,128]{1,0:T(8,128)S(1)} %bitcast.23, f32[4,4,2,3,8,128]{5,4,3,2,1,0:T(8,128)S(1)} %bitcast.20, ...), custom_call_target="tpu_custom_call" | custom-call | flops 884736 | bytes 884736 | tf_op jit(solution)/shard_map/last/pallas_call | solution.py:195
  (8 shorter events, 0.0 us)
Async XLA Ops:
  0.0 6.1 %copy-start.2 = (f32[4,2,3,8,128]{4,3,2,1,0:T(8,128)S(1)}, f32[4,2,3,8,128]{4,3,2,1,0:T(8,128)}, u32[]{:S(2)}) copy-start(f32[4,2,3,8,128]{4,3,2,1,0:T(8,128)} %adjoint_ref.1) | copy-start | bytes 294916
  1.0 23.6 %collective-permute-start = (f32[4,3,3,3,2,128]{5,4,3,2,1,0:T(2,128)S(1)}, f32[4,3,3,3,2,128]{5,4,3,2,1,0:T(2,128)S(1)}, u32[]{:S(2)}, u32[]{:S(2)}) collective-permute-start(f32[4,3,3,3,2,128]{5,4,3,2,1,0:T(2,128)S(1)} %slice_bitcast_fusion), channel_id=1, source_target_pairs={{0,8},{1,9},{2,10},{3,11},{4,12},{5,13},{6,14},{7,15},{8,16},{9,17... | collective-permute-start | bytes 331784 | tf_op jit(solution)/shard_map/ppermute | solution.py:224
  6.1 1.0 %copy-start = (f32[4,3,4,2,3,3,128]{6,3,5,4,2,1,0:T(2,128)S(1)}, f32[4,3,4,2,3,3,128]{6,3,5,4,2,1,0:T(2,128)}, u32[]{:S(2)}) copy-start(f32[4,3,4,2,3,3,128]{6,3,5,4,2,1,0:T(2,128)} %param.6) | copy-start | bytes 1327108
  7.1 16.9 %copy-start.1 = (f32[4,3,4,2,3,3,128]{6,3,5,4,2,1,0:T(2,128)S(1)}, f32[4,3,4,2,3,3,128]{6,3,5,4,2,1,0:T(2,128)}, u32[]{:S(2)}) copy-start(f32[4,3,4,2,3,3,128]{6,3,5,4,2,1,0:T(2,128)} %param.6) | copy-start | bytes 1327108
  7.7 16.8 %collective-permute-start.1 = (f32[1,2,3,8,128]{4,3,2,1,0:T(8,128)S(1)}, f32[1,2,3,8,128]{4,3,2,1,0:T(8,128)S(1)}, u32[]{:S(2)}, u32[]{:S(2)}) collective-permute-start(f32[1,2,3,8,128]{4,3,2,1,0:T(8,128)S(1)} %get-tuple-element.16), channel_id=1, source_target_pairs={{1,0},{2,1},{3,2},{4,3},{5,4},{6,5},{7,6},{0,7},{9,8},{10,9},{11,1... | collective-permute-start | bytes 73736 | tf_op jit(solution)/shard_map/ppermute | solution.py:228
  9.4 15.1 %collective-permute-start.2 = (f32[1,2,3,8,128]{4,3,2,1,0:T(8,128)S(1)}, f32[1,2,3,8,128]{4,3,2,1,0:T(8,128)S(1)}, u32[]{:S(2)}, u32[]{:S(2)}) collective-permute-start(f32[1,2,3,8,128]{4,3,2,1,0:T(8,128)S(1)} %get-tuple-element.17), channel_id=1, source_target_pairs={{0,1},{1,2},{2,3},{3,4},{4,5},{5,6},{6,7},{7,0},{8,9},{9,10},{10,1... | collective-permute-start | bytes 73736 | tf_op jit(solution)/shard_map/ppermute | solution.py:229
  25.4 16.6 %collective-permute-start.3 = (f32[1,2,3,8,128]{4,3,2,1,0:T(8,128)S(1)}, f32[1,2,3,8,128]{4,3,2,1,0:T(8,128)S(1)}, u32[]{:S(2)}, u32[]{:S(2)}) collective-permute-start(f32[1,2,3,8,128]{4,3,2,1,0:T(8,128)S(1)} %get-tuple-element.19), channel_id=1, source_target_pairs={{1,0},{2,1},{3,2},{4,3},{5,4},{6,5},{7,6},{0,7},{9,8},{10,9},{11,1... | collective-permute-start | bytes 73736 | tf_op jit(solution)/shard_map/ppermute | solution.py:228
  26.9 15.1 %collective-permute-start.4 = (f32[1,2,3,8,128]{4,3,2,1,0:T(8,128)S(1)}, f32[1,2,3,8,128]{4,3,2,1,0:T(8,128)S(1)}, u32[]{:S(2)}, u32[]{:S(2)}) collective-permute-start(f32[1,2,3,8,128]{4,3,2,1,0:T(8,128)S(1)} %get-tuple-element.20), channel_id=1, source_target_pairs={{0,1},{1,2},{2,3},{3,4},{4,5},{5,6},{6,7},{7,0},{8,9},{9,10},{10,1... | collective-permute-start | bytes 73736 | tf_op jit(solution)/shard_map/ppermute | solution.py:229
  42.9 16.2 %collective-permute-start.5 = (f32[1,2,3,8,128]{4,3,2,1,0:T(8,128)S(1)}, f32[1,2,3,8,128]{4,3,2,1,0:T(8,128)S(1)}, u32[]{:S(2)}, u32[]{:S(2)}) collective-permute-start(f32[1,2,3,8,128]{4,3,2,1,0:T(8,128)S(1)} %get-tuple-element.22), channel_id=1, source_target_pairs={{1,0},{2,1},{3,2},{4,3},{5,4},{6,5},{7,6},{0,7},{9,8},{10,9},{11,1... | collective-permute-start | bytes 73736 | tf_op jit(solution)/shard_map/ppermute | solution.py:228
  44.3 14.9 %collective-permute-start.6 = (f32[1,2,3,8,128]{4,3,2,1,0:T(8,128)S(1)}, f32[1,2,3,8,128]{4,3,2,1,0:T(8,128)S(1)}, u32[]{:S(2)}, u32[]{:S(2)}) collective-permute-start(f32[1,2,3,8,128]{4,3,2,1,0:T(8,128)S(1)} %get-tuple-element.23), channel_id=1, source_target_pairs={{0,1},{1,2},{2,3},{3,4},{4,5},{5,6},{6,7},{7,0},{8,9},{9,10},{10,1... | collective-permute-start | bytes 73736 | tf_op jit(solution)/shard_map/ppermute | solution.py:229

commit v4 on v1

--- a/solution.py
+++ b/solution.py
@@ -58,39 +58,40 @@
     return pltpu.roll(plane, by % plane.shape[-1], plane.ndim - 1)
 
 
+def place(scalars, rows):
+    first_pos = lax.rem(scalars[3], BAND)
+    return first_pos, lax.rem(first_pos // rows, 2) == 1
+
+
 def taper(scalars, row):
-    source, width, steps, first = (scalars[i] for i in range(4))
     ones = jnp.ones((8, 128), jnp.float32)
-    slice_pos = lax.rem(first + row, BAND)
-    distance = ones * (slice_pos - source).astype(jnp.float32) / (ones * width.astype(jnp.float32))
+    slice_pos = lax.rem(scalars[3] + row, BAND)
+    distance = ones * (slice_pos - scalars[0]).astype(jnp.float32) / (ones * scalars[1].astype(jnp.float32))
     inside = 1.0 / (1.0 + distance * distance)
-    eps = 0.25 / (ones * steps.astype(jnp.float32))
+    eps = 0.25 / (ones * scalars[2].astype(jnp.float32))
     return inside, eps
 
 
-def send_parts(links_ref, link_set, row, rows, field, up_ref, first_ref, last_ref):
+def store_edges(scalars, links_ref, link_set, rows, field_ref, outer_ref, inner_ref):
+    _, is_odd = place(scalars, rows)
+    first = load_field(field_ref, 0)
+    _, last = transport(links_ref, rows - 1, link_set, 3, None, load_field(field_ref, rows - 1))
+    store_field(outer_ref, 0, combine(lambda p, q: jnp.where(is_odd, q, p), first, last))
+    store_field(inner_ref, 0, combine(lambda p, q: jnp.where(is_odd, p, q), first, last))
+
+
+def store_up(links_ref, link_set, row, field, up_ref):
     _, up = transport(links_ref, row, link_set, 2, None, field)
     store_field(up_ref, row, up)
 
-    @pl.when(row == 0)
-    def _():
-        store_field(first_ref, 0, field)
-
-    @pl.when(row == rows - 1)
-    def _():
-        _, later = transport(links_ref, row, link_set, 3, None, field)
-        store_field(last_ref, 0, later)
-
-
-def begin_kernel(rows, scalars, adjoint_ref, links_ref, start_ref, up_ref, first_ref, last_ref):
-    def one(row, carry):
+
+def begin_kernel(rows, scalars, adjoint_ref, links_ref, start_ref, up_ref, outer_ref, inner_ref):
+    for row in range(rows):
         inside, _ = taper(scalars, row)
         start = combine(lambda v: inside * v, load_field(adjoint_ref, row))
         store_field(start_ref, row, start)
-        send_parts(links_ref, 2, row, rows, start, up_ref, first_ref, last_ref)
-        return carry
-
-    lax.fori_loop(0, rows, one, 0)
+        store_up(links_ref, 2, row, start, up_ref)
+    store_edges(scalars, links_ref, 2, rows, start_ref, outer_ref, inner_ref)
 
 
 def local_kernel(rows, link_set, field_ref, links_ref, sum_ref):
@@ -125,58 +126,57 @@
     lax.fori_loop(0, rows - 1, between, 0)
 
 
-def arrived_sum(links_ref, link_set, row, rows, sum_ref, above_ref, below_ref, later_ref, earlier_ref):
-    ahead_z, _ = transport(links_ref, row, link_set, 2, load_field(above_ref, row), None)
+def arrived_sum(scalars, links_ref, link_set, row, rows, arrivals, scale=None):
+    sum_ref, above_ref, below_ref, outer_ref, inner_ref = arrivals
+    first_pos, is_odd = place(scalars, rows)
+    above = load_field(above_ref, row)
+    if scale is not None:
+        above = combine(lambda v: scale * v, above)
+    ahead_z, _ = transport(links_ref, row, link_set, 2, above, None)
     total = combine(lambda s, f, h: s + f + h, load_field(sum_ref, row), ahead_z, load_field(below_ref, row))
-    is_first = jnp.where(row == 0, 1.0, 0.0)
-    is_last = jnp.where(row == rows - 1, 1.0, 0.0)
-    ahead_t, _ = transport(links_ref, row, link_set, 3, load_field(later_ref, 0), None)
-    return combine(lambda s, f, h: s + is_last * f + is_first * h, total, ahead_t, load_field(earlier_ref, 0))
-
-
-def third_kernel(
-    rows, scalars, links_ref, sum_ref, above_ref, below_ref, later_ref, earlier_ref,
-    third_ref, up_ref, first_ref, last_ref,
-):
-    def one(row, carry):
+    outer, inner = load_field(outer_ref, 0), load_field(inner_ref, 0)
+    if row == 0:
+        exists = jnp.where(first_pos != 0, 1.0, 0.0)
+        total = combine(lambda s, p, q: s + exists * jnp.where(is_odd, q, p), total, outer, inner)
+    if row == rows - 1:
+        exists = jnp.where(first_pos != BAND - rows, 1.0, 0.0)
+        later = combine(lambda p, q: exists * jnp.where(is_odd, p, q), outer, inner)
+        ahead_t, _ = transport(links_ref, row, link_set, 3, later, None)
+        total = combine(lambda s, f: s + f, total, ahead_t)
+    return total
+
+
+def third_kernel(rows, scalars, links_ref, *refs):
+    arrivals, (third_ref, up_ref, outer_ref, inner_ref) = refs[:5], refs[5:]
+    for row in range(rows):
         inside, eps = taper(scalars, row)
-        total = arrived_sum(links_ref, 2, row, rows, sum_ref, above_ref, below_ref, later_ref, earlier_ref)
+        total = arrived_sum(scalars, links_ref, 2, row, rows, arrivals, inside)
         third = combine(lambda s: 0.75 * (inside * (eps * s)), total)
         store_field(third_ref, row, third)
-        send_parts(links_ref, 1, row, rows, third, up_ref, first_ref, last_ref)
-        return carry
-
-    lax.fori_loop(0, rows, one, 0)
-
-
-def second_kernel(
-    rows, scalars, links_ref, sum_ref, above_ref, below_ref, later_ref, earlier_ref, start_ref, third_ref,
-    mixed_ref, up_ref, first_ref, last_ref, base_ref,
-):
-    def one(row, carry):
+        store_up(links_ref, 1, row, third, up_ref)
+    store_edges(scalars, links_ref, 1, rows, third_ref, outer_ref, inner_ref)
+
+
+def second_kernel(rows, scalars, links_ref, *refs):
+    arrivals, (start_ref, third_ref, mixed_ref, up_ref, outer_ref, inner_ref, base_ref) = refs[:5], refs[5:]
+    for row in range(rows):
         inside, eps = taper(scalars, row)
-        total = arrived_sum(links_ref, 1, row, rows, sum_ref, above_ref, below_ref, later_ref, earlier_ref)
+        total = arrived_sum(scalars, links_ref, 1, row, rows, arrivals)
         third = load_field(third_ref, row)
         second = combine(lambda v, s: v + (8.0 / 9.0) * (inside * (eps * s)), load_field(start_ref, row), total)
         mixed = combine(lambda p, q: 0.25 * p - (2.0 / 9.0) * q, second, third)
         store_field(mixed_ref, row, mixed)
         store_field(base_ref, row, combine(lambda p, q: p + q, second, third))
-        send_parts(links_ref, 0, row, rows, mixed, up_ref, first_ref, last_ref)
-        return carry
-
-    lax.fori_loop(0, rows, one, 0)
-
-
-def last_kernel(
-    rows, scalars, links_ref, sum_ref, above_ref, below_ref, later_ref, earlier_ref, base_ref, out_ref
-):
-    def one(row, carry):
+        store_up(links_ref, 0, row, mixed, up_ref)
+    store_edges(scalars, links_ref, 0, rows, mixed_ref, outer_ref, inner_ref)
+
+
+def last_kernel(rows, scalars, links_ref, *refs):
+    arrivals, (base_ref, out_ref) = refs[:5], refs[5:]
+    for row in range(rows):
         inside, eps = taper(scalars, row)
-        total = arrived_sum(links_ref, 0, row, rows, sum_ref, above_ref, below_ref, later_ref, earlier_ref)
+        total = arrived_sum(scalars, links_ref, 0, row, rows, arrivals)
         store_field(out_ref, row, combine(lambda p, s: p + inside * (eps * s), load_field(base_ref, row), total))
-        return carry
-
-    lax.fori_loop(0, rows, one, 0)
 
 
 def call(kernel, name, n_scalars, operands, out_shapes, matvecs):
@@ -207,40 +207,41 @@
 
     up_pairs = [(i, (i + per_plane) % count) for i in range(count)]
     down_pairs = [(j, i) for i, j in up_pairs]
-    later_pairs = [(i, i + 1) for i in range(count) if (i + 1) % per_plane]
-    earlier_pairs = [(j, i) for i, j in later_pairs]
-
-    def exchange(field, up, first, last):
-        later = lax.ppermute(first, "gz", earlier_pairs)
-        earlier = lax.ppermute(last, "gz", later_pairs)
-        above = lax.ppermute(field, "gz", down_pairs)
-        below = lax.ppermute(up, "gz", up_pairs)
-        return above, below, later, earlier
+
+    def in_plane(i, by):
+        return i - i % per_plane + (i + by) % per_plane
+
+    outer_pairs = [(i, in_plane(i, 1 if i % 2 else -1)) for i in range(count)]
+    inner_pairs = [(i, in_plane(i, -1 if i % 2 else 1)) for i in range(count)]
 
     def local(field, link_set):
         return call(
             functools.partial(local_kernel, rows, link_set), f"local_{link_set}", 0, (field, links), whole, 22
         )
 
-    start, up, first, last = call(
+    def arrivals(link_set, field, sent_down, up, outer, inner):
+        above = lax.ppermute(sent_down, "gz", down_pairs)
+        below = lax.ppermute(up, "gz", up_pairs)
+        outer = lax.ppermute(outer, "gz", outer_pairs)
+        inner = lax.ppermute(inner, "gz", inner_pairs)
+        return local(field, link_set), above, below, outer, inner
+
+    start, up, outer, inner = call(
         functools.partial(begin_kernel, rows), "begin", 1, (scalars, adjoint, links),
         (whole, whole, one_row, one_row), 5,
     )
-    arrived = exchange(start, up, first, last)
-    third, up, first, last = call(
-        functools.partial(third_kernel, rows), "third", 1, (scalars, links, local(start, 2)) + arrived,
-        (whole, whole, one_row, one_row), 10,
-    )
-    arrived = exchange(third, up, first, last)
-    mixed, up, first, last, base = call(
+    third, up, outer, inner = call(
+        functools.partial(third_kernel, rows), "third", 1,
+        (scalars, links) + arrivals(2, start, adjoint, up, outer, inner), (whole, whole, one_row, one_row), 10,
+    )
+    mixed, up, outer, inner, base = call(
         functools.partial(second_kernel, rows), "second", 1,
-        (scalars, links, local(third, 1)) + arrived + (start, third),
+        (scalars, links) + arrivals(1, third, third, up, outer, inner) + (start, third),
         (whole, whole, one_row, one_row, whole), 10,
     )
-    arrived = exchange(mixed, up, first, last)
     return call(
-        functools.partial(last_kernel, rows), "last", 1, (scalars, links, local(mixed, 0)) + arrived + (base,),
-        whole, 5,
+        functools.partial(last_kernel, rows), "last", 1,
+        (scalars, links) + arrivals(0, mixed, mixed, up, outer, inner) + (base,), whole, 5,
     )
 
 

time: 43.8 us -> 35.2 us (0.80)
  the two profiles are of different devices: /device:TPU:4 before, /device:TPU:0 now
where the time goes in v4:
time: 35.2 us; the launch traced here: 35 us
  starting transfers between devices  16.7 us (47%)
  waiting for transfers between devices  9.52 us (27%)
  Pallas kernels  4.73 us (13%)
  between operations  2.03 us (6%)
  local copies, waits for them, and re-layouts  1.91 us (5%)
    ppermute x3, starting transfers between devices, arrivals(): above = lax.ppermute(sent_down, 'gz', down_pairs)  12.7 us
    ppermute x3, waiting for transfers between devices, arrivals(): outer = lax.ppermute(outer, 'gz', outer_pairs)  7.48 us
    pallas_call x7, Pallas kernels, call(): pl.pallas_call(kernel, name=name, out_shape=out_shapes, in_specs=[smem] *...  4.73 us
    ppermute x3, starting transfers between devices, arrivals(): inner = lax.ppermute(inner, 'gz', inner_pairs)  2.15 us
    ppermute x3, waiting for transfers between devices, arrivals(): below = lax.ppermute(up, 'gz', up_pairs)  2.02 us
    unnamed x6, local copies, waits for them, and re-layouts  1.91 us
    ppermute x3, starting transfers between devices, arrivals(): outer = lax.ppermute(outer, 'gz', outer_pairs)  1.68 us
  transfers between devices with their start and end apart: 12, of which 4 were waited for; matrix products, arithmetic and copies ran while one was open for 0% of the time, Pallas kernels for 6%

profile of v4, /device:TPU:0, one launch (start us, length us, event | category | flops | bytes accessed | tf_op | source)
XLA Modules:
  0.0 35.0 jit_solution(12402504135630114007)
XLA Ops:
  0.0 5.0 %collective-permute-start = (f32[4,2,3,8,128]{4,3,2,1,0:T(8,128)}, f32[4,2,3,8,128]{4,3,2,1,0:T(8,128)S(1)}, u32[]{:S(2)}, u32[]{:S(2)}) collective-permute-start(f32[4,2,3,8,128]{4,3,2,1,0:T(8,128)} %adjoint_ref.1), channel_id=1, source_target_pairs={{8,0},{9,1},{10,2},{11,3},{12,4},{13,5},{14,6},{15,7},{16,8},{17,9... | collective-permute-start | bytes 294920 | tf_op jit(solution)/shard_map/ppermute | solution.py:223
  7.0 0.1 pad_add_fusion.scalars
  7.1 1.0 %copy-done = f32[4,3,4,2,3,3,128]{6,3,5,4,2,1,0:T(2,128)S(1)} copy-done((f32[4,3,4,2,3,3,128]{6,3,5,4,2,1,0:T(2,128)S(1)}, f32[4,3,4,2,3,3,128]{6,3,5,4,2,1,0:T(2,128)}, u32[]{:S(2)}) %copy-start) | copy-done | bytes 442392
  8.1 0.9 %copy-done.2 = f32[4,2,3,8,128]{4,3,2,1,0:T(8,128)S(1)} copy-done((f32[4,2,3,8,128]{4,3,2,1,0:T(8,128)S(1)}, f32[4,2,3,8,128]{4,3,2,1,0:T(8,128)}, u32[]{:S(2)}) %copy-start.2) | copy-done | bytes 98328
  9.0 0.6 %begin.1 = (f32[4,2,3,8,128]{4,3,2,1,0:T(8,128)S(1)}, f32[4,2,3,8,128]{4,3,2,1,0:T(8,128)S(1)}, f32[1,2,3,8,128]{4,3,2,1,0:T(8,128)S(1)}, f32[1,2,3,8,128]{4,3,2,1,0:T(8,128)S(1)}) custom-call(s32[4]{0:T(128)S(1)} %pad_add_fusion.scalars, f32[4,2,3,8,128]{4,3,2,1,0:T(8,128)S(1)} %copy-done.2, f32[864,128]{1,0:T(8,128)S(1)} %bitcast.4), custom_call_target="tpu_custom_call" | custom-call | flops 368640 | bytes 368640 | tf_op jit(solution)/shard_map/begin/pallas_call | solution.py:185
  9.6 0.1 collective-permute-start.1
  9.7 1.7 %collective-permute-start.2 = (f32[1,2,3,8,128]{4,3,2,1,0:T(8,128)S(1)}, f32[1,2,3,8,128]{4,3,2,1,0:T(8,128)S(1)}, u32[]{:S(2)}, u32[]{:S(2)}) collective-permute-start(f32[1,2,3,8,128]{4,3,2,1,0:T(8,128)S(1)} %get-tuple-element.20), channel_id=1, source_target_pairs={{0,7},{1,2},{2,1},{3,4},{4,3},{5,6},{6,5},{7,0},{8,15},{9,10},{10,... | collective-permute-start | bytes 73736 | tf_op jit(solution)/shard_map/ppermute | solution.py:225
  11.3 0.0 collective-permute-start.3
  11.3 0.5 %local_2.1.refs_0_ = f32[4,2,3,8,128]{4,3,2,1,0:T(8,128)S(1)} custom-call(f32[4,2,3,8,128]{4,3,2,1,0:T(8,128)S(1)} %get-tuple-element.18.field_ref.refs_5_, f32[864,128]{1,0:T(8,128)S(1)} %bitcast.5), custom_call_target="tpu_custom_call" | custom-call | flops 1622016 | bytes 1622016 | tf_op jit(solution)/shard_map/local_2/pallas_call | solution.py:185
  11.9 2.2 %collective-permute-done.2.refs_3_ = f32[1,2,3,8,128]{4,3,2,1,0:T(8,128)S(1)} collective-permute-done((f32[1,2,3,8,128]{4,3,2,1,0:T(8,128)S(1)}, f32[1,2,3,8,128]{4,3,2,1,0:T(8,128)S(1)}, u32[]{:S(2)}, u32[]{:S(2)}) %collective-permute-start.2) | collective-permute-done | bytes 24608 | tf_op jit(solution)/shard_map/ppermute | solution.py:225
  14.1 2.0 %collective-permute-done.1.refs_2_ = f32[4,2,3,8,128]{4,3,2,1,0:T(8,128)S(1)} collective-permute-done((f32[4,2,3,8,128]{4,3,2,1,0:T(8,128)S(1)}, f32[4,2,3,8,128]{4,3,2,1,0:T(8,128)S(1)}, u32[]{:S(2)}, u32[]{:S(2)}) %collective-permute-start.1) | collective-permute-done | bytes 98336 | tf_op jit(solution)/shard_map/ppermute | solution.py:224
  16.1 0.7 %third.1 = (f32[4,2,3,8,128]{4,3,2,1,0:T(8,128)S(1)}, f32[4,2,3,8,128]{4,3,2,1,0:T(8,128)S(1)}, f32[1,2,3,8,128]{4,3,2,1,0:T(8,128)S(1)}, f32[1,2,3,8,128]{4,3,2,1,0:T(8,128)S(1)}) custom-call(s32[4]{0:T(128)S(1)} %pad_add_fusion.scalars, f32[864,128]{1,0:T(8,128)S(1)} %bitcast.6, f32[4,2,3,8,128]{4,3,2,1,0:T(8,128)S(1)} %local_2.1.refs_0_, ...), custom_call_target="tpu_custom_call" | custom-call | flops 737280 | bytes 737280 | tf_op jit(solution)/shard_map/third/pallas_call | solution.py:185
  16.8 0.1 collective-permute-start.5
  16.8 3.8 %collective-permute-start.4 = (f32[4,2,3,8,128]{4,3,2,1,0:T(8,128)S(1)}, f32[4,2,3,8,128]{4,3,2,1,0:T(8,128)S(1)}, u32[]{:S(2)}, u32[]{:S(2)}) collective-permute-start(f32[4,2,3,8,128]{4,3,2,1,0:T(8,128)S(1)} %get-tuple-element.22.field_ref.refs_6_), channel_id=1, source_target_pairs={{8,0},{9,1},{10,2},{11,3},{12,4},{13,5},{14,6},{15,7},{16,8},{17,9... | collective-permute-start | bytes 294920 | tf_op jit(solution)/shard_map/ppermute | solution.py:223
  20.6 1.6 %collective-permute-start.7 = (f32[1,2,3,8,128]{4,3,2,1,0:T(8,128)S(1)}, f32[1,2,3,8,128]{4,3,2,1,0:T(8,128)S(1)}, u32[]{:S(2)}, u32[]{:S(2)}) collective-permute-start(f32[1,2,3,8,128]{4,3,2,1,0:T(8,128)S(1)} %get-tuple-element.25), channel_id=1, source_target_pairs={{0,1},{1,0},{2,3},{3,2},{4,5},{5,4},{6,7},{7,6},{8,9},{9,8},{10,11... | collective-permute-start | bytes 73736 | tf_op jit(solution)/shard_map/ppermute | solution.py:226
  22.2 0.5 %local_1.1.refs_0_ = f32[4,2,3,8,128]{4,3,2,1,0:T(8,128)S(1)} custom-call(f32[4,2,3,8,128]{4,3,2,1,0:T(8,128)S(1)} %get-tuple-element.22.field_ref.refs_6_, f32[864,128]{1,0:T(8,128)S(1)} %bitcast.7), custom_call_target="tpu_custom_call" | custom-call | flops 1622016 | bytes 1622016 | tf_op jit(solution)/shard_map/local_1/pallas_call | solution.py:185
  22.7 2.2 %collective-permute-done.6.refs_3_ = f32[1,2,3,8,128]{4,3,2,1,0:T(8,128)S(1)} collective-permute-done((f32[1,2,3,8,128]{4,3,2,1,0:T(8,128)S(1)}, f32[1,2,3,8,128]{4,3,2,1,0:T(8,128)S(1)}, u32[]{:S(2)}, u32[]{:S(2)}) %collective-permute-start.6) | collective-permute-done | bytes 24608 | tf_op jit(solution)/shard_map/ppermute | solution.py:225
  25.0 0.7 %second.1 = (f32[4,2,3,8,128]{4,3,2,1,0:T(8,128)S(1)}, f32[4,2,3,8,128]{4,3,2,1,0:T(8,128)S(1)}, f32[1,2,3,8,128]{4,3,2,1,0:T(8,128)S(1)}, f32[1,2,3,8,128]{4,3,2,1,0:T(8,128)S(1)}, f32[4,2,3,8,128]{4,3,2,1,0:T(8,128)S(1)}) custom-call(s32[4]{0:T(128)S(1)} %pad_add_fusion.scalars, f32[864,128]{1,0:T(8,128)S(1)} %bitcast.8, ...), custom_call_target="tpu_custom_call" | custom-call | flops 737280 | bytes 737280 | tf_op jit(solution)/shard_map/second/pallas_call | solution.py:185
  25.6 0.1 collective-permute-start.9
  25.7 3.8 %collective-permute-start.8 = (f32[4,2,3,8,128]{4,3,2,1,0:T(8,128)S(1)}, f32[4,2,3,8,128]{4,3,2,1,0:T(8,128)S(1)}, u32[]{:S(2)}, u32[]{:S(2)}) collective-permute-start(f32[4,2,3,8,128]{4,3,2,1,0:T(8,128)S(1)} %get-tuple-element.26.field_ref), channel_id=1, source_target_pairs={{8,0},{9,1},{10,2},{11,3},{12,4},{13,5},{14,6},{15,7},{16,8},{17,9... | collective-permute-start | bytes 294920 | tf_op jit(solution)/shard_map/ppermute | solution.py:223
  29.5 0.5 %collective-permute-start.11 = (f32[1,2,3,8,128]{4,3,2,1,0:T(8,128)S(1)}, f32[1,2,3,8,128]{4,3,2,1,0:T(8,128)S(1)}, u32[]{:S(2)}, u32[]{:S(2)}) collective-permute-start(f32[1,2,3,8,128]{4,3,2,1,0:T(8,128)S(1)} %get-tuple-element.29), channel_id=1, source_target_pairs={{0,1},{1,0},{2,3},{3,2},{4,5},{5,4},{6,7},{7,6},{8,9},{9,8},{10,11... | collective-permute-start | bytes 73736 | tf_op jit(solution)/shard_map/ppermute | solution.py:226
  30.1 0.5 %local_0.1.refs_0_ = f32[4,2,3,8,128]{4,3,2,1,0:T(8,128)S(1)} custom-call(f32[4,2,3,8,128]{4,3,2,1,0:T(8,128)S(1)} %get-tuple-element.26.field_ref, f32[864,128]{1,0:T(8,128)S(1)} %bitcast.9), custom_call_target="tpu_custom_call" | custom-call | flops 1622016 | bytes 1622016 | tf_op jit(solution)/shard_map/local_0/pallas_call | solution.py:185
  30.6 3.1 %collective-permute-done.10.refs_3_ = f32[1,2,3,8,128]{4,3,2,1,0:T(8,128)S(1)} collective-permute-done((f32[1,2,3,8,128]{4,3,2,1,0:T(8,128)S(1)}, f32[1,2,3,8,128]{4,3,2,1,0:T(8,128)S(1)}, u32[]{:S(2)}, u32[]{:S(2)}) %collective-permute-start.10) | collective-permute-done | bytes 24608 | tf_op jit(solution)/shard_map/ppermute | solution.py:225
  33.7 1.3 %last.1 = f32[4,2,3,8,128]{4,3,2,1,0:T(8,128)} custom-call(s32[4]{0:T(128)S(1)} %pad_add_fusion.scalars, f32[864,128]{1,0:T(8,128)S(1)} %bitcast.10, f32[4,2,3,8,128]{4,3,2,1,0:T(8,128)S(1)} %local_0.1.refs_0_, f32[4,2,3,8,128]{4,3,2,1,0:T(8,128)S(1)} %collective-permute-done.8.refs_1_, f32[4,2,3,8,128]{4,3,2,1,0:T(8,128)S(1)} %collective-permute-done.9.refs_2_, ...), custom_call_target="tpu_custom_call" | custom-call | flops 368640 | bytes 368640 | tf_op jit(solution)/shard_map/last/pallas_call | solution.py:185
  (14 shorter events, 0.0 us)
Async XLA Ops:
  0.0 14.1 %collective-permute-start = (f32[4,2,3,8,128]{4,3,2,1,0:T(8,128)}, f32[4,2,3,8,128]{4,3,2,1,0:T(8,128)S(1)}, u32[]{:S(2)}, u32[]{:S(2)}) collective-permute-start(f32[4,2,3,8,128]{4,3,2,1,0:T(8,128)} %adjoint_ref.1), channel_id=1, source_target_pairs={{8,0},{9,1},{10,2},{11,3},{12,4},{13,5},{14,6},{15,7},{16,8},{17,9... | collective-permute-start | bytes 294920 | tf_op jit(solution)/shard_map/ppermute | solution.py:223
  7.1 1.0 %copy-start = (f32[4,3,4,2,3,3,128]{6,3,5,4,2,1,0:T(2,128)S(1)}, f32[4,3,4,2,3,3,128]{6,3,5,4,2,1,0:T(2,128)}, u32[]{:S(2)}) copy-start(f32[4,3,4,2,3,3,128]{6,3,5,4,2,1,0:T(2,128)} %param.6) | copy-start | bytes 1327108
  8.1 0.9 %copy-start.2 = (f32[4,2,3,8,128]{4,3,2,1,0:T(8,128)S(1)}, f32[4,2,3,8,128]{4,3,2,1,0:T(8,128)}, u32[]{:S(2)}) copy-start(f32[4,2,3,8,128]{4,3,2,1,0:T(8,128)} %adjoint_ref.1) | copy-start | bytes 294916
  9.0 2.4 %copy-start.1 = (f32[4,3,4,2,3,3,128]{6,3,5,4,2,1,0:T(2,128)S(1)}, f32[4,3,4,2,3,3,128]{6,3,5,4,2,1,0:T(2,128)}, u32[]{:S(2)}) copy-start(f32[4,3,4,2,3,3,128]{6,3,5,4,2,1,0:T(2,128)} %param.6) | copy-start | bytes 1327108
  9.6 6.5 %collective-permute-start.1 = (f32[4,2,3,8,128]{4,3,2,1,0:T(8,128)S(1)}, f32[4,2,3,8,128]{4,3,2,1,0:T(8,128)S(1)}, u32[]{:S(2)}, u32[]{:S(2)}) collective-permute-start(f32[4,2,3,8,128]{4,3,2,1,0:T(8,128)S(1)} %get-tuple-element.19), channel_id=1, source_target_pairs={{0,8},{1,9},{2,10},{3,11},{4,12},{5,13},{6,14},{7,15},{8,16},{9,17... | collective-permute-start | bytes 294920 | tf_op jit(solution)/shard_map/ppermute | solution.py:224
  9.7 4.4 %collective-permute-start.2 = (f32[1,2,3,8,128]{4,3,2,1,0:T(8,128)S(1)}, f32[1,2,3,8,128]{4,3,2,1,0:T(8,128)S(1)}, u32[]{:S(2)}, u32[]{:S(2)}) collective-permute-start(f32[1,2,3,8,128]{4,3,2,1,0:T(8,128)S(1)} %get-tuple-element.20), channel_id=1, source_target_pairs={{0,7},{1,2},{2,1},{3,4},{4,3},{5,6},{6,5},{7,0},{8,15},{9,10},{10,... | collective-permute-start | bytes 73736 | tf_op jit(solution)/shard_map/ppermute | solution.py:225
  11.3 2.7 %collective-permute-start.3 = (f32[1,2,3,8,128]{4,3,2,1,0:T(8,128)S(1)}, f32[1,2,3,8,128]{4,3,2,1,0:T(8,128)S(1)}, u32[]{:S(2)}, u32[]{:S(2)}) collective-permute-start(f32[1,2,3,8,128]{4,3,2,1,0:T(8,128)S(1)} %get-tuple-element.21), channel_id=1, source_target_pairs={{0,1},{1,0},{2,3},{3,2},{4,5},{5,4},{6,7},{7,6},{8,9},{9,8},{10,11... | collective-permute-start | bytes 73736 | tf_op jit(solution)/shard_map/ppermute | solution.py:226
  16.8 8.2 %collective-permute-start.5 = (f32[4,2,3,8,128]{4,3,2,1,0:T(8,128)S(1)}, f32[4,2,3,8,128]{4,3,2,1,0:T(8,128)S(1)}, u32[]{:S(2)}, u32[]{:S(2)}) collective-permute-start(f32[4,2,3,8,128]{4,3,2,1,0:T(8,128)S(1)} %get-tuple-element.23), channel_id=1, source_target_pairs={{0,8},{1,9},{2,10},{3,11},{4,12},{5,13},{6,14},{7,15},{8,16},{9,17... | collective-permute-start | bytes 294920 | tf_op jit(solution)/shard_map/ppermute | solution.py:224
  16.8 8.1 %collective-permute-start.4 = (f32[4,2,3,8,128]{4,3,2,1,0:T(8,128)S(1)}, f32[4,2,3,8,128]{4,3,2,1,0:T(8,128)S(1)}, u32[]{:S(2)}, u32[]{:S(2)}) collective-permute-start(f32[4,2,3,8,128]{4,3,2,1,0:T(8,128)S(1)} %get-tuple-element.22.field_ref.refs_6_), channel_id=1, source_target_pairs={{8,0},{9,1},{10,2},{11,3},{12,4},{13,5},{14,6},{15,7},{16,8},{17,9... | collective-permute-start | bytes 294920 | tf_op jit(solution)/shard_map/ppermute | solution.py:223
  20.6 4.3 %collective-permute-start.6 = (f32[1,2,3,8,128]{4,3,2,1,0:T(8,128)S(1)}, f32[1,2,3,8,128]{4,3,2,1,0:T(8,128)S(1)}, u32[]{:S(2)}, u32[]{:S(2)}) collective-permute-start(f32[1,2,3,8,128]{4,3,2,1,0:T(8,128)S(1)} %get-tuple-element.24), channel_id=1, source_target_pairs={{0,7},{1,2},{2,1},{3,4},{4,3},{5,6},{6,5},{7,0},{8,15},{9,10},{10,... | collective-permute-start | bytes 73736 | tf_op jit(solution)/shard_map/ppermute | solution.py:225
  20.6 4.3 %collective-permute-start.7 = (f32[1,2,3,8,128]{4,3,2,1,0:T(8,128)S(1)}, f32[1,2,3,8,128]{4,3,2,1,0:T(8,128)S(1)}, u32[]{:S(2)}, u32[]{:S(2)}) collective-permute-start(f32[1,2,3,8,128]{4,3,2,1,0:T(8,128)S(1)} %get-tuple-element.25), channel_id=1, source_target_pairs={{0,1},{1,0},{2,3},{3,2},{4,5},{5,4},{6,7},{7,6},{8,9},{9,8},{10,11... | collective-permute-start | bytes 73736 | tf_op jit(solution)/shard_map/ppermute | solution.py:226
  25.6 8.0 %collective-permute-start.9 = (f32[4,2,3,8,128]{4,3,2,1,0:T(8,128)S(1)}, f32[4,2,3,8,128]{4,3,2,1,0:T(8,128)S(1)}, u32[]{:S(2)}, u32[]{:S(2)}) collective-permute-start(f32[4,2,3,8,128]{4,3,2,1,0:T(8,128)S(1)} %get-tuple-element.27), channel_id=1, source_target_pairs={{0,8},{1,9},{2,10},{3,11},{4,12},{5,13},{6,14},{7,15},{8,16},{9,17... | collective-permute-start | bytes 294920 | tf_op jit(solution)/shard_map/ppermute | solution.py:224
  25.7 8.0 %collective-permute-start.8 = (f32[4,2,3,8,128]{4,3,2,1,0:T(8,128)S(1)}, f32[4,2,3,8,128]{4,3,2,1,0:T(8,128)S(1)}, u32[]{:S(2)}, u32[]{:S(2)}) collective-permute-start(f32[4,2,3,8,128]{4,3,2,1,0:T(8,128)S(1)} %get-tuple-element.26.field_ref), channel_id=1, source_target_pairs={{8,0},{9,1},{10,2},{11,3},{12,4},{13,5},{14,6},{15,7},{16,8},{17,9... | collective-permute-start | bytes 294920 | tf_op jit(solution)/shard_map/ppermute | solution.py:223
  29.5 4.2 %collective-permute-start.10 = (f32[1,2,3,8,128]{4,3,2,1,0:T(8,128)S(1)}, f32[1,2,3,8,128]{4,3,2,1,0:T(8,128)S(1)}, u32[]{:S(2)}, u32[]{:S(2)}) collective-permute-start(f32[1,2,3,8,128]{4,3,2,1,0:T(8,128)S(1)} %get-tuple-element.28), channel_id=1, source_target_pairs={{0,7},{1,2},{2,1},{3,4},{4,3},{5,6},{6,5},{7,0},{8,15},{9,10},{10,... | collective-permute-start | bytes 73736 | tf_op jit(solution)/shard_map/ppermute | solution.py:225
  29.5 4.2 %collective-permute-start.11 = (f32[1,2,3,8,128]{4,3,2,1,0:T(8,128)S(1)}, f32[1,2,3,8,128]{4,3,2,1,0:T(8,128)S(1)}, u32[]{:S(2)}, u32[]{:S(2)}) collective-permute-start(f32[1,2,3,8,128]{4,3,2,1,0:T(8,128)S(1)} %get-tuple-element.29), channel_id=1, source_target_pairs={{0,1},{1,0},{2,3},{3,2},{4,5},{5,4},{6,7},{7,6},{8,9},{9,8},{10,11... | collective-permute-start | bytes 73736 | tf_op jit(solution)/shard_map/ppermute | solution.py:226

commit v5 on v4

v5 whole, which is shorter than its diff:
```python
import functools

import jax
import jax.numpy as jnp
from jax import lax
from jax.experimental import pallas as pl
from jax.experimental.pallas import tpu as pltpu
from jax.sharding import PartitionSpec as P

BAND = 32
LX = 8
SETS = 3
MUS = 4
ENTRIES = 18


def load_field(ref, row):
    return [[ref[row, c, a] for a in range(3)] for c in range(2)]


def store_field(ref, row, field):
    for c in range(2):
        for a in range(3):
            ref[row, c, a] = field[c][a]


def combine(function, *fields):
    return [[function(*(f[c][a] for f in fields)) for a in range(3)] for c in range(2)]


def links_at(links_ref, row, link_set, mu):
    return links_ref, ((row * SETS + link_set) * MUS + mu) * ENTRIES


def entry(matrices, a, b, c, shape):
    ref, base = matrices
    return jnp.broadcast_to(ref[pl.ds(base + (a * 3 + b) * 2 + c, 1), :], shape)


def transport(matrices, ahead, here):
    forward = [[None] * 3, [None] * 3]
    backward = [[None] * 3, [None] * 3]
    shape = (ahead if ahead is not None else here)[0][0].shape

    def add(total, c, a, value):
        total[c][a] = value if total[c][a] is None else total[c][a] + value

    for a in range(3):
        for b in range(3):
            real = entry(matrices, a, b, 0, shape)
            imag = entry(matrices, a, b, 1, shape)
            if ahead is not None:
                add(forward, 0, a, real * ahead[0][b] - imag * ahead[1][b])
                add(forward, 1, a, real * ahead[1][b] + imag * ahead[0][b])
            if here is not None:
                add(backward, 0, b, real * here[0][a] + imag * here[1][a])
                add(backward, 1, b, real * here[1][a] - imag * here[0][a])
    return forward, backward


def roll(plane, by):
    return pltpu.roll(plane, by % plane.shape[-1], plane.ndim - 1)


def place(rows):
    first = lax.axis_index("gz") * rows
    plane, first_pos = first // BAND, lax.rem(first, BAND)
    return plane, first_pos, lax.rem(plane, 2) == 1, lax.rem(first_pos // rows, 2) == 1


def taper(first_pos, row, source, width):
    ones = jnp.ones((8, 128), jnp.float32)
    distance = ones * (first_pos + row - source).astype(jnp.float32) / (ones * width.astype(jnp.float32))
    return 1.0 / (1.0 + distance * distance)


def store_z(rows, matrices, row, field, far_ref, near_ref):
    _, _, odd_plane, _ = place(rows)
    _, up = transport(matrices, None, field)
    store_field(far_ref, row, combine(lambda v, h: jnp.where(odd_plane, h, v), field, up))
    store_field(near_ref, row, combine(lambda v, h: jnp.where(odd_plane, v, h), field, up))


def store_t(rows, matrices, field_ref, outer_ref, inner_ref):
    _, _, _, odd_block = place(rows)
    first = load_field(field_ref, 0)
    _, last = transport(matrices, None, load_field(field_ref, rows - 1))
    store_field(outer_ref, 0, combine(lambda p, q: jnp.where(odd_block, q, p), first, last))
    store_field(inner_ref, 0, combine(lambda p, q: jnp.where(odd_block, p, q), first, last))


def begin_kernel(
    rows, source_hbm, width_hbm, steps_hbm, adjoint_hbm, links_hbm,
    start_ref, far_ref, near_ref, outer_ref, inner_ref, coefs_ref,
    source_ref, width_ref, steps_ref, adjoint_ref, links_ref, sems,
):
    row_entries = SETS * MUS * ENTRIES
    z_first = (2 * MUS + 2) * ENTRIES
    aligned = z_first // 8 * 8
    pairs = [(source_hbm, source_ref), (width_hbm, width_ref), (steps_hbm, steps_ref), (adjoint_hbm, adjoint_ref)]
    for row in range(rows):
        part = links_hbm.at[pl.ds(row * row_entries + aligned, row_entries - aligned), :]
        pairs.append((part, links_ref.at[row]))
    copies = [pltpu.make_async_copy(p, q, sems.at[i]) for i, (p, q) in enumerate(pairs)]
    for copy in copies:
        copy.start()
    for copy in copies:
        copy.wait()
    _, first_pos, _, _ = place(rows)
    for row in range(rows):
        inside = taper(first_pos, row, source_ref[0], width_ref[0])
        coefs_ref[row] = inside
        start = combine(lambda v: inside * v, load_field(adjoint_ref, row))
        store_field(start_ref, row, start)
        store_z(rows, (links_ref.at[row], z_first - aligned), row, start, far_ref, near_ref)
    coefs_ref[rows] = 0.25 / (jnp.ones((8, 128), jnp.float32) * steps_ref[0].astype(jnp.float32))
    store_t(rows, (links_ref.at[rows - 1], z_first + ENTRIES - aligned), start_ref, outer_ref, inner_ref)


def local_kernel(rows, link_set, field_ref, links_ref, sum_ref):
    shape = field_ref.shape[-2:]
    x_pos = lax.broadcasted_iota(jnp.int32, shape, 1) % LX
    at_last = x_pos == LX - 1
    at_first = x_pos == 0

    def one(row, carry):
        here = load_field(field_ref, row)
        ahead = combine(lambda v: jnp.where(at_last, roll(v, LX - 1), roll(v, -1)), here)
        ahead_x, hop = transport(links_at(links_ref, row, link_set, 0), ahead, here)
        total = combine(
            lambda v, f, h: f + jnp.where(at_first, roll(h, 1 - LX), roll(h, 1)) - 8.0 * v, here, ahead_x, hop
        )
        ahead = combine(lambda v: roll(v, -LX), here)
        ahead_y, hop = transport(links_at(links_ref, row, link_set, 1), ahead, here)
        total = combine(lambda s, f, h: s + f + roll(h, LX), total, ahead_y, hop)
        store_field(sum_ref, row, total)
        return carry

    lax.fori_loop(0, rows, one, 0)

    def between(row, carry):
        ahead_t, hop = transport(
            links_at(links_ref, row, link_set, 3), load_field(field_ref, row + 1), load_field(field_ref, row)
        )
        store_field(sum_ref, row, combine(lambda s, f: s + f, load_field(sum_ref, row), ahead_t))
        store_field(sum_ref, row + 1, combine(lambda s, h: s + h, load_field(sum_ref, row + 1), hop))
        return carry

    lax.fori_loop(0, rows - 1, between, 0)


def arrived_sum(links_ref, link_set, row, rows, arrivals):
    sum_ref, far_ref, near_ref, outer_ref, inner_ref = arrivals
    _, first_pos, odd_plane, odd_block = place(rows)
    far, near = load_field(far_ref, row), load_field(near_ref, row)
    above = combine(lambda p, q: jnp.where(odd_plane, p, q), far, near)
    ahead_z, _ = transport(links_at(links_ref, row, link_set, 2), above, None)
    total = combine(
        lambda s, f, p, q: s + f + jnp.where(odd_plane, q, p), load_field(sum_ref, row), ahead_z, far, near
    )
    outer, inner = load_field(outer_ref, 0), load_field(inner_ref, 0)
    if row == 0:
        exists = jnp.where(first_pos != 0, 1.0, 0.0)
        total = combine(lambda s, p, q: s + exists * jnp.where(odd_block, q, p), total, outer, inner)
    if row == rows - 1:
        exists = jnp.where(first_pos != BAND - rows, 1.0, 0.0)
        later = combine(lambda p, q: exists * jnp.where(odd_block, p, q), outer, inner)
        ahead_t, _ = transport(links_at(links_ref, row, link_set, 3), later, None)
        total = combine(lambda s, f: s + f, total, ahead_t)
    return total


def third_kernel(rows, coefs_ref, links_ref, *refs):
    arrivals, (third_ref, far_ref, near_ref, outer_ref, inner_ref) = refs[:5], refs[5:]
    for row in range(rows):
        inside, eps = coefs_ref[row], coefs_ref[rows]
        total = arrived_sum(links_ref, 2, row, rows, arrivals)
        third = combine(lambda s: 0.75 * (inside * (eps * s)), total)
        store_field(third_ref, row, third)
        store_z(rows, links_at(links_ref, row, 1, 2), row, third, far_ref, near_ref)
    store_t(rows, links_at(links_ref, rows - 1, 1, 3), third_ref, outer_ref, inner_ref)


def second_kernel(rows, coefs_ref, links_ref, *refs):
    arrivals, (start_ref, third_ref, mixed_ref, far_ref, near_ref, outer_ref, inner_ref, base_ref) = refs[:5], refs[5:]
    for row in range(rows):
        inside, eps = coefs_ref[row], coefs_ref[rows]
        total = arrived_sum(links_ref, 1, row, rows, arrivals)
        third = load_field(third_ref, row)
        second = combine(lambda v, s: v + (8.0 / 9.0) * (inside * (eps * s)), load_field(start_ref, row), total)
        mixed = combine(lambda p, q: 0.25 * p - (2.0 / 9.0) * q, second, third)
        store_field(mixed_ref, row, mixed)
        store_field(base_ref, row, combine(lambda p, q: p + q, second, third))
        store_z(rows, links_at(links_ref, row, 0, 2), row, mixed, far_ref, near_ref)
    store_t(rows, links_at(links_ref, rows - 1, 0, 3), mixed_ref, outer_ref, inner_ref)


def last_kernel(rows, coefs_ref, links_ref, *refs):
    arrivals, (base_ref, out_ref) = refs[:5], refs[5:]
    for row in range(rows):
        inside, eps = coefs_ref[row], coefs_ref[rows]
        total = arrived_sum(links_ref, 0, row, rows, arrivals)
        store_field(out_ref, row, combine(lambda p, s: p + inside * (eps * s), load_field(base_ref, row), total))


def call(kernel, name, operands, out_shapes, matvecs, space=pltpu.VMEM, scratch=()):
    vmem = pl.BlockSpec(memory_space=pltpu.VMEM)
    return pl.pallas_call(
        kernel,
        name=name,
        out_shape=out_shapes,
        in_specs=[pl.BlockSpec(memory_space=space)] * len(operands),
        out_specs=jax.tree.map(lambda _: vmem, out_shapes),
        scratch_shapes=scratch,
        cost_estimate=pl.CostEstimate(flops=matvecs * 72 * 1024, bytes_accessed=4096 * 18 * matvecs, transcendentals=0),
        compiler_params=pltpu.CompilerParams(vmem_limit_bytes=16 * 2**20),
    )(*operands)


def body(adjoint, flowed, source_slice, band_width, flow_steps):
    rows = adjoint.shape[0]
    per_plane = BAND // rows
    count = lax.axis_size("gz")
    links = jnp.transpose(flowed, (0, 1, 2, 4, 5, 3, 6)).reshape(-1, flowed.shape[-1])
    whole = jax.ShapeDtypeStruct(adjoint.shape, jnp.float32)
    one_row = jax.ShapeDtypeStruct((1,) + adjoint.shape[1:], jnp.float32)
    coefs = jax.ShapeDtypeStruct((rows + 1,) + adjoint.shape[3:], jnp.float32)

    def in_plane(i, by):
        return i - i % per_plane + (i + by) % per_plane

    def in_line(i, by):
        return (i + by * per_plane) % count

    far_pairs = [(i, in_line(i, 1 if i // per_plane % 2 else -1)) for i in range(count)]
    near_pairs = [(i, in_line(i, -1 if i // per_plane % 2 else 1)) for i in range(count)]
    outer_pairs = [(i, in_plane(i, 1 if i % 2 else -1)) for i in range(count)]
    inner_pairs = [(i, in_plane(i, -1 if i % 2 else 1)) for i in range(count)]

    def arrivals(link_set, field, far, near, outer, inner):
        far = lax.ppermute(far, "gz", far_pairs)
        near = lax.ppermute(near, "gz", near_pairs)
        outer = lax.ppermute(outer, "gz", outer_pairs)
        inner = lax.ppermute(inner, "gz", inner_pairs)
        total = call(functools.partial(local_kernel, rows, link_set), f"local_{link_set}", (field, links), whole, 22)
        return total, far, near, outer, inner

    sent = (whole, whole, one_row, one_row)
    copied = SETS * MUS * ENTRIES - (2 * MUS + 2) * ENTRIES // 8 * 8
    start, far, near, outer, inner, coefs = call(
        functools.partial(begin_kernel, rows), "begin", (source_slice, band_width, flow_steps, adjoint, links),
        (whole,) + sent + (coefs,), 5, pltpu.HBM,
        [pltpu.SMEM((1,), jnp.int32)] * 3
        + [
            pltpu.VMEM(adjoint.shape, jnp.float32),
            pltpu.VMEM((rows, copied, flowed.shape[-1]), jnp.float32),
            pltpu.SemaphoreType.DMA((4 + rows,)),
        ],
    )
    third, far, near, outer, inner = call(
        functools.partial(third_kernel, rows), "third",
        (coefs, links) + arrivals(2, start, far, near, outer, inner), (whole,) + sent, 10,
    )
    mixed, far, near, outer, inner, base = call(
        functools.partial(second_kernel, rows), "second",
        (coefs, links) + arrivals(1, third, far, near, outer, inner) + (start, third),
        (whole,) + sent + (whole,), 10,
    )
    return call(
        functools.partial(last_kernel, rows), "last",
        (coefs, links) + arrivals(0, mixed, far, near, outer, inner) + (base,), whole, 5,
    )


def solution(mesh):
    in_specs = (
        P(("cfg", "gz"), None, None, None, None),
        P(("cfg", "gz"), None, None, None, None, None, None),
        P("cfg"),
        P("cfg"),
        P("cfg"),
    )
    out_specs = P(("cfg", "gz"), None, None, None, None)
    return jax.shard_map(body, mesh=mesh, in_specs=in_specs, out_specs=out_specs, check_vma=False)
```

time: 35.2 us -> 31.2 us (0.89)
  starting transfers between devices: 16.7 us -> 14.3 us
  Pallas kernels: 4.73 us -> 3.24 us
    ppermute x6, starting transfers between devices: 12.8 us -> 9.36 us  [the longest x3 9.35 us: arrivals(): far = lax.ppermute(far, 'gz', far_pairs)]
    pallas_call x7, Pallas kernels: 4.73 us -> 3.24 us  [call(): pl.pallas_call(kernel, name=name, out_shape=out_shapes, in_specs=[pl.Bloc...]
    ppermute x6, waiting for transfers between devices: 2.03 us -> 3.22 us  [the longest x3 2.33 us: arrivals(): near = lax.ppermute(near, 'gz', near_pairs)]
    ppermute x3, waiting for transfers between devices: 7.48 us -> 6.39 us  [arrivals(): outer = lax.ppermute(outer, 'gz', outer_pairs)]
    ppermute x3, starting transfers between devices: 2.15 us -> 3.11 us  [arrivals(): inner = lax.ppermute(inner, 'gz', inner_pairs)]
  transfers between devices with their start and end apart: 12 -> 12, of which waited for: 4 -> 8; matrix products, arithmetic and copies ran while one was open for 0% -> 0% of each run, Pallas kernels for 6% -> 5%
where the time goes in v5:
time: 31.2 us; the launch traced here: 31 us
  starting transfers between devices  14.3 us (46%)
  waiting for transfers between devices  9.62 us (31%)
  Pallas kernels  3.24 us (10%)
  between operations  2 us (6%)
  local copies, waits for them, and re-layouts  1.9 us (6%)
    ppermute x3, starting transfers between devices, arrivals(): far = lax.ppermute(far, 'gz', far_pairs)  9.35 us
    ppermute x3, waiting for transfers between devices, arrivals(): outer = lax.ppermute(outer, 'gz', outer_pairs)  6.39 us
    pallas_call x7, Pallas kernels, call(): pl.pallas_call(kernel, name=name, out_shape=out_shapes, in_specs=[pl.Bloc...  3.24 us
    ppermute x3, starting transfers between devices, arrivals(): inner = lax.ppermute(inner, 'gz', inner_pairs)  3.11 us
    ppermute x3, waiting for transfers between devices, arrivals(): near = lax.ppermute(near, 'gz', near_pairs)  2.33 us
    unnamed x6, local copies, waits for them, and re-layouts  1.9 us
    ppermute x3, starting transfers between devices, arrivals(): outer = lax.ppermute(outer, 'gz', outer_pairs)  1.81 us
    ppermute x3, waiting for transfers between devices, arrivals(): far = lax.ppermute(far, 'gz', far_pairs)  0.89 us
  transfers between devices with their start and end apart: 12, of which 8 were waited for; matrix products, arithmetic and copies ran while one was open for 0% of the time, Pallas kernels for 5%

profile of v5, /device:TPU:0, one launch (start us, length us, event | category | flops | bytes accessed | tf_op | source)
XLA Modules:
  0.0 31.0 jit_solution(16512871542399146769)
XLA Ops:
  2.0 1.0 %copy-done = f32[4,3,4,2,3,3,128]{6,3,5,4,2,1,0:T(2,128)S(1)} copy-done((f32[4,3,4,2,3,3,128]{6,3,5,4,2,1,0:T(2,128)S(1)}, f32[4,3,4,2,3,3,128]{6,3,5,4,2,1,0:T(2,128)}, u32[]{:S(2)}) %copy-start) | copy-done | bytes 442392
  3.0 0.9 %copy-done.2 = f32[4,2,3,8,128]{4,3,2,1,0:T(8,128)S(1)} copy-done((f32[4,2,3,8,128]{4,3,2,1,0:T(8,128)S(1)}, f32[4,2,3,8,128]{4,3,2,1,0:T(8,128)}, u32[]{:S(2)}) %copy-start.2) | copy-done | bytes 98328
  3.9 0.7 %begin.1 = (f32[4,2,3,8,128]{4,3,2,1,0:T(8,128)S(1)}, f32[4,2,3,8,128]{4,3,2,1,0:T(8,128)S(1)}, f32[4,2,3,8,128]{4,3,2,1,0:T(8,128)S(1)}, f32[1,2,3,8,128]{4,3,2...) custom-call(s32[1]{0:T(128)S(6)} %copy.6.source_hbm, s32[1]{0:T(128)S(6)} %copy.7.width_hbm, ...), custom_call_target="tpu_custom_call" | custom-call | flops 368640 | bytes 368640 | tf_op jit(solution)/shard_map/begin/pallas_call | solution.py:208
  4.6 5.1 %collective-permute-start = (f32[4,2,3,8,128]{4,3,2,1,0:T(8,128)S(1)}, f32[4,2,3,8,128]{4,3,2,1,0:T(8,128)S(1)}, u32[]{:S(2)}, u32[]{:S(2)}) collective-permute-start(f32[4,2,3,8,128]{4,3,2,1,0:T(8,128)S(1)} %get-tuple-element.24), channel_id=1, source_target_pairs={{0,24},{1,25},{2,26},{3,27},{4,28},{5,29},{6,30},{7,31},{8,16},{9,... | collective-permute-start | bytes 294920 | tf_op jit(solution)/shard_map/ppermute | solution.py:241
  9.7 1.6 %collective-permute-start.2 = (f32[1,2,3,8,128]{4,3,2,1,0:T(8,128)S(1)}, f32[1,2,3,8,128]{4,3,2,1,0:T(8,128)S(1)}, u32[]{:S(2)}, u32[]{:S(2)}) collective-permute-start(f32[1,2,3,8,128]{4,3,2,1,0:T(8,128)S(1)} %get-tuple-element.26), channel_id=1, source_target_pairs={{0,7},{1,2},{2,1},{3,4},{4,3},{5,6},{6,5},{7,0},{8,15},{9,10},{10,... | collective-permute-start | bytes 73736 | tf_op jit(solution)/shard_map/ppermute | solution.py:243
  11.3 0.5 %local_2.1.refs_0_ = f32[4,2,3,8,128]{4,3,2,1,0:T(8,128)S(1)} custom-call(f32[4,2,3,8,128]{4,3,2,1,0:T(8,128)S(1)} %get-tuple-element.23.field_ref.refs_5_, f32[864,128]{1,0:T(8,128)S(1)} %bitcast.4), custom_call_target="tpu_custom_call" | custom-call | flops 1622016 | bytes 1622016 | tf_op jit(solution)/shard_map/local_2/pallas_call | solution.py:208
  11.8 2.2 %collective-permute-done.2.refs_3_ = f32[1,2,3,8,128]{4,3,2,1,0:T(8,128)S(1)} collective-permute-done((f32[1,2,3,8,128]{4,3,2,1,0:T(8,128)S(1)}, f32[1,2,3,8,128]{4,3,2,1,0:T(8,128)S(1)}, u32[]{:S(2)}, u32[]{:S(2)}) %collective-permute-start.2) | collective-permute-done | bytes 24608 | tf_op jit(solution)/shard_map/ppermute | solution.py:243
  14.0 0.7 %collective-permute-done.1.refs_2_ = f32[4,2,3,8,128]{4,3,2,1,0:T(8,128)S(1)} collective-permute-done((f32[4,2,3,8,128]{4,3,2,1,0:T(8,128)S(1)}, f32[4,2,3,8,128]{4,3,2,1,0:T(8,128)S(1)}, u32[]{:S(2)}, u32[]{:S(2)}) %collective-permute-start.1) | collective-permute-done | bytes 98336 | tf_op jit(solution)/shard_map/ppermute | solution.py:242
  14.7 0.1 third.1
  14.9 2.5 %collective-permute-start.4 = (f32[4,2,3,8,128]{4,3,2,1,0:T(8,128)S(1)}, f32[4,2,3,8,128]{4,3,2,1,0:T(8,128)S(1)}, u32[]{:S(2)}, u32[]{:S(2)}) collective-permute-start(f32[4,2,3,8,128]{4,3,2,1,0:T(8,128)S(1)} %get-tuple-element.29), channel_id=1, source_target_pairs={{0,24},{1,25},{2,26},{3,27},{4,28},{5,29},{6,30},{7,31},{8,16},{9,... | collective-permute-start | bytes 294920 | tf_op jit(solution)/shard_map/ppermute | solution.py:241
  17.4 1.6 %collective-permute-start.7 = (f32[1,2,3,8,128]{4,3,2,1,0:T(8,128)S(1)}, f32[1,2,3,8,128]{4,3,2,1,0:T(8,128)S(1)}, u32[]{:S(2)}, u32[]{:S(2)}) collective-permute-start(f32[1,2,3,8,128]{4,3,2,1,0:T(8,128)S(1)} %get-tuple-element.32), channel_id=1, source_target_pairs={{0,1},{1,0},{2,3},{3,2},{4,5},{5,4},{6,7},{7,6},{8,9},{9,8},{10,11... | collective-permute-start | bytes 73736 | tf_op jit(solution)/shard_map/ppermute | solution.py:244
  19.0 0.5 %local_1.1.refs_0_ = f32[4,2,3,8,128]{4,3,2,1,0:T(8,128)S(1)} custom-call(f32[4,2,3,8,128]{4,3,2,1,0:T(8,128)S(1)} %get-tuple-element.28.field_ref.refs_6_, f32[864,128]{1,0:T(8,128)S(1)} %bitcast.6), custom_call_target="tpu_custom_call" | custom-call | flops 1622016 | bytes 1622016 | tf_op jit(solution)/shard_map/local_1/pallas_call | solution.py:208
  19.5 2.2 %collective-permute-done.6.refs_3_ = f32[1,2,3,8,128]{4,3,2,1,0:T(8,128)S(1)} collective-permute-done((f32[1,2,3,8,128]{4,3,2,1,0:T(8,128)S(1)}, f32[1,2,3,8,128]{4,3,2,1,0:T(8,128)S(1)}, u32[]{:S(2)}, u32[]{:S(2)}) %collective-permute-start.6) | collective-permute-done | bytes 24608 | tf_op jit(solution)/shard_map/ppermute | solution.py:243
  21.7 0.3 collective-permute-done.4.refs_1_
  21.9 0.8 %collective-permute-done.5.refs_2_ = f32[4,2,3,8,128]{4,3,2,1,0:T(8,128)S(1)} collective-permute-done((f32[4,2,3,8,128]{4,3,2,1,0:T(8,128)S(1)}, f32[4,2,3,8,128]{4,3,2,1,0:T(8,128)S(1)}, u32[]{:S(2)}, u32[]{:S(2)}) %collective-permute-start.5) | collective-permute-done | bytes 98336 | tf_op jit(solution)/shard_map/ppermute | solution.py:242
  22.7 0.2 second.1
  22.9 1.7 %collective-permute-start.8 = (f32[4,2,3,8,128]{4,3,2,1,0:T(8,128)S(1)}, f32[4,2,3,8,128]{4,3,2,1,0:T(8,128)S(1)}, u32[]{:S(2)}, u32[]{:S(2)}) collective-permute-start(f32[4,2,3,8,128]{4,3,2,1,0:T(8,128)S(1)} %get-tuple-element.34), channel_id=1, source_target_pairs={{0,24},{1,25},{2,26},{3,27},{4,28},{5,29},{6,30},{7,31},{8,16},{9,... | collective-permute-start | bytes 294920 | tf_op jit(solution)/shard_map/ppermute | solution.py:241
  24.6 0.2 collective-permute-start.10
  24.9 1.5 %collective-permute-start.11 = (f32[1,2,3,8,128]{4,3,2,1,0:T(8,128)S(1)}, f32[1,2,3,8,128]{4,3,2,1,0:T(8,128)S(1)}, u32[]{:S(2)}, u32[]{:S(2)}) collective-permute-start(f32[1,2,3,8,128]{4,3,2,1,0:T(8,128)S(1)} %get-tuple-element.37), channel_id=1, source_target_pairs={{0,1},{1,0},{2,3},{3,2},{4,5},{5,4},{6,7},{7,6},{8,9},{9,8},{10,11... | collective-permute-start | bytes 73736 | tf_op jit(solution)/shard_map/ppermute | solution.py:244
  26.4 0.5 %local_0.1.refs_0_ = f32[4,2,3,8,128]{4,3,2,1,0:T(8,128)S(1)} custom-call(f32[4,2,3,8,128]{4,3,2,1,0:T(8,128)S(1)} %get-tuple-element.33.field_ref, f32[864,128]{1,0:T(8,128)S(1)} %bitcast.8), custom_call_target="tpu_custom_call" | custom-call | flops 1622016 | bytes 1622016 | tf_op jit(solution)/shard_map/local_0/pallas_call | solution.py:208
  26.9 2.0 %collective-permute-done.10.refs_3_ = f32[1,2,3,8,128]{4,3,2,1,0:T(8,128)S(1)} collective-permute-done((f32[1,2,3,8,128]{4,3,2,1,0:T(8,128)S(1)}, f32[1,2,3,8,128]{4,3,2,1,0:T(8,128)S(1)}, u32[]{:S(2)}, u32[]{:S(2)}) %collective-permute-start.10) | collective-permute-done | bytes 24608 | tf_op jit(solution)/shard_map/ppermute | solution.py:243
  28.9 0.6 %collective-permute-done.8.refs_1_ = f32[4,2,3,8,128]{4,3,2,1,0:T(8,128)S(1)} collective-permute-done((f32[4,2,3,8,128]{4,3,2,1,0:T(8,128)S(1)}, f32[4,2,3,8,128]{4,3,2,1,0:T(8,128)S(1)}, u32[]{:S(2)}, u32[]{:S(2)}) %collective-permute-start.8) | collective-permute-done | bytes 98336 | tf_op jit(solution)/shard_map/ppermute | solution.py:241
  29.5 0.8 %collective-permute-done.9.refs_2_ = f32[4,2,3,8,128]{4,3,2,1,0:T(8,128)S(1)} collective-permute-done((f32[4,2,3,8,128]{4,3,2,1,0:T(8,128)S(1)}, f32[4,2,3,8,128]{4,3,2,1,0:T(8,128)S(1)}, u32[]{:S(2)}, u32[]{:S(2)}) %collective-permute-start.9) | collective-permute-done | bytes 98336 | tf_op jit(solution)/shard_map/ppermute | solution.py:242
  30.3 0.7 %last.1 = f32[4,2,3,8,128]{4,3,2,1,0:T(8,128)} custom-call(f32[5,8,128]{2,1,0:T(8,128)S(1)} %get-tuple-element.22.coefs_ref, f32[864,128]{1,0:T(8,128)S(1)} %bitcast.9, f32[4,2,3,8,128]{4,3,2,1,0:T(8,128)S(1)} %local_0.1.refs_0_, f32[4,2,3,8,128]{4,3,2,1,0:T(8,128)S(1)} %collective-permute-done.8.refs_1_, ...), custom_call_target="tpu_custom_call" | custom-call | flops 368640 | bytes 368640 | tf_op jit(solution)/shard_map/last/pallas_call | solution.py:208
  (13 shorter events, 0.0 us)
Async XLA Ops:
  1.9 1.0 %copy-start = (f32[4,3,4,2,3,3,128]{6,3,5,4,2,1,0:T(2,128)S(1)}, f32[4,3,4,2,3,3,128]{6,3,5,4,2,1,0:T(2,128)}, u32[]{:S(2)}) copy-start(f32[4,3,4,2,3,3,128]{6,3,5,4,2,1,0:T(2,128)} %param.6) | copy-start | bytes 1327108
  3.0 0.9 %copy-start.2 = (f32[4,2,3,8,128]{4,3,2,1,0:T(8,128)S(1)}, f32[4,2,3,8,128]{4,3,2,1,0:T(8,128)}, u32[]{:S(2)}) copy-start(f32[4,2,3,8,128]{4,3,2,1,0:T(8,128)} %adjoint_hbm.1) | copy-start | bytes 294916
  3.8 7.5 %copy-start.1 = (f32[4,3,4,2,3,3,128]{6,3,5,4,2,1,0:T(2,128)S(1)}, f32[4,3,4,2,3,3,128]{6,3,5,4,2,1,0:T(2,128)}, u32[]{:S(2)}) copy-start(f32[4,3,4,2,3,3,128]{6,3,5,4,2,1,0:T(2,128)} %param.6) | copy-start | bytes 1327108
  4.6 9.4 %collective-permute-start = (f32[4,2,3,8,128]{4,3,2,1,0:T(8,128)S(1)}, f32[4,2,3,8,128]{4,3,2,1,0:T(8,128)S(1)}, u32[]{:S(2)}, u32[]{:S(2)}) collective-permute-start(f32[4,2,3,8,128]{4,3,2,1,0:T(8,128)S(1)} %get-tuple-element.24), channel_id=1, source_target_pairs={{0,24},{1,25},{2,26},{3,27},{4,28},{5,29},{6,30},{7,31},{8,16},{9,... | collective-permute-start | bytes 294920 | tf_op jit(solution)/shard_map/ppermute | solution.py:241
  9.7 5.0 %collective-permute-start.1 = (f32[4,2,3,8,128]{4,3,2,1,0:T(8,128)S(1)}, f32[4,2,3,8,128]{4,3,2,1,0:T(8,128)S(1)}, u32[]{:S(2)}, u32[]{:S(2)}) collective-permute-start(f32[4,2,3,8,128]{4,3,2,1,0:T(8,128)S(1)} %get-tuple-element.25), channel_id=1, source_target_pairs={{0,8},{1,9},{2,10},{3,11},{4,12},{5,13},{6,14},{7,15},{8,0},{9,1},... | collective-permute-start | bytes 294920 | tf_op jit(solution)/shard_map/ppermute | solution.py:242
  9.7 4.3 %collective-permute-start.2 = (f32[1,2,3,8,128]{4,3,2,1,0:T(8,128)S(1)}, f32[1,2,3,8,128]{4,3,2,1,0:T(8,128)S(1)}, u32[]{:S(2)}, u32[]{:S(2)}) collective-permute-start(f32[1,2,3,8,128]{4,3,2,1,0:T(8,128)S(1)} %get-tuple-element.26), channel_id=1, source_target_pairs={{0,7},{1,2},{2,1},{3,4},{4,3},{5,6},{6,5},{7,0},{8,15},{9,10},{10,... | collective-permute-start | bytes 73736 | tf_op jit(solution)/shard_map/ppermute | solution.py:243
  11.3 2.7 %collective-permute-start.3 = (f32[1,2,3,8,128]{4,3,2,1,0:T(8,128)S(1)}, f32[1,2,3,8,128]{4,3,2,1,0:T(8,128)S(1)}, u32[]{:S(2)}, u32[]{:S(2)}) collective-permute-start(f32[1,2,3,8,128]{4,3,2,1,0:T(8,128)S(1)} %get-tuple-element.27), channel_id=1, source_target_pairs={{0,1},{1,0},{2,3},{3,2},{4,5},{5,4},{6,7},{7,6},{8,9},{9,8},{10,11... | collective-permute-start | bytes 73736 | tf_op jit(solution)/shard_map/ppermute | solution.py:244
  14.9 7.1 %collective-permute-start.4 = (f32[4,2,3,8,128]{4,3,2,1,0:T(8,128)S(1)}, f32[4,2,3,8,128]{4,3,2,1,0:T(8,128)S(1)}, u32[]{:S(2)}, u32[]{:S(2)}) collective-permute-start(f32[4,2,3,8,128]{4,3,2,1,0:T(8,128)S(1)} %get-tuple-element.29), channel_id=1, source_target_pairs={{0,24},{1,25},{2,26},{3,27},{4,28},{5,29},{6,30},{7,31},{8,16},{9,... | collective-permute-start | bytes 294920 | tf_op jit(solution)/shard_map/ppermute | solution.py:241
  17.3 5.4 %collective-permute-start.5 = (f32[4,2,3,8,128]{4,3,2,1,0:T(8,128)S(1)}, f32[4,2,3,8,128]{4,3,2,1,0:T(8,128)S(1)}, u32[]{:S(2)}, u32[]{:S(2)}) collective-permute-start(f32[4,2,3,8,128]{4,3,2,1,0:T(8,128)S(1)} %get-tuple-element.30), channel_id=1, source_target_pairs={{0,8},{1,9},{2,10},{3,11},{4,12},{5,13},{6,14},{7,15},{8,0},{9,1},... | collective-permute-start | bytes 294920 | tf_op jit(solution)/shard_map/ppermute | solution.py:242
  17.4 4.3 %collective-permute-start.6 = (f32[1,2,3,8,128]{4,3,2,1,0:T(8,128)S(1)}, f32[1,2,3,8,128]{4,3,2,1,0:T(8,128)S(1)}, u32[]{:S(2)}, u32[]{:S(2)}) collective-permute-start(f32[1,2,3,8,128]{4,3,2,1,0:T(8,128)S(1)} %get-tuple-element.31), channel_id=1, source_target_pairs={{0,7},{1,2},{2,1},{3,4},{4,3},{5,6},{6,5},{7,0},{8,15},{9,10},{10,... | collective-permute-start | bytes 73736 | tf_op jit(solution)/shard_map/ppermute | solution.py:243
  17.4 4.3 %collective-permute-start.7 = (f32[1,2,3,8,128]{4,3,2,1,0:T(8,128)S(1)}, f32[1,2,3,8,128]{4,3,2,1,0:T(8,128)S(1)}, u32[]{:S(2)}, u32[]{:S(2)}) collective-permute-start(f32[1,2,3,8,128]{4,3,2,1,0:T(8,128)S(1)} %get-tuple-element.32), channel_id=1, source_target_pairs={{0,1},{1,0},{2,3},{3,2},{4,5},{5,4},{6,7},{7,6},{8,9},{9,8},{10,11... | collective-permute-start | bytes 73736 | tf_op jit(solution)/shard_map/ppermute | solution.py:244
  22.9 6.6 %collective-permute-start.8 = (f32[4,2,3,8,128]{4,3,2,1,0:T(8,128)S(1)}, f32[4,2,3,8,128]{4,3,2,1,0:T(8,128)S(1)}, u32[]{:S(2)}, u32[]{:S(2)}) collective-permute-start(f32[4,2,3,8,128]{4,3,2,1,0:T(8,128)S(1)} %get-tuple-element.34), channel_id=1, source_target_pairs={{0,24},{1,25},{2,26},{3,27},{4,28},{5,29},{6,30},{7,31},{8,16},{9,... | collective-permute-start | bytes 294920 | tf_op jit(solution)/shard_map/ppermute | solution.py:241
  24.6 5.7 %collective-permute-start.9 = (f32[4,2,3,8,128]{4,3,2,1,0:T(8,128)S(1)}, f32[4,2,3,8,128]{4,3,2,1,0:T(8,128)S(1)}, u32[]{:S(2)}, u32[]{:S(2)}) collective-permute-start(f32[4,2,3,8,128]{4,3,2,1,0:T(8,128)S(1)} %get-tuple-element.35), channel_id=1, source_target_pairs={{0,8},{1,9},{2,10},{3,11},{4,12},{5,13},{6,14},{7,15},{8,0},{9,1},... | collective-permute-start | bytes 294920 | tf_op jit(solution)/shard_map/ppermute | solution.py:242
  24.6 4.2 %collective-permute-start.10 = (f32[1,2,3,8,128]{4,3,2,1,0:T(8,128)S(1)}, f32[1,2,3,8,128]{4,3,2,1,0:T(8,128)S(1)}, u32[]{:S(2)}, u32[]{:S(2)}) collective-permute-start(f32[1,2,3,8,128]{4,3,2,1,0:T(8,128)S(1)} %get-tuple-element.36), channel_id=1, source_target_pairs={{0,7},{1,2},{2,1},{3,4},{4,3},{5,6},{6,5},{7,0},{8,15},{9,10},{10,... | collective-permute-start | bytes 73736 | tf_op jit(solution)/shard_map/ppermute | solution.py:243
  24.9 4.0 %collective-permute-start.11 = (f32[1,2,3,8,128]{4,3,2,1,0:T(8,128)S(1)}, f32[1,2,3,8,128]{4,3,2,1,0:T(8,128)S(1)}, u32[]{:S(2)}, u32[]{:S(2)}) collective-permute-start(f32[1,2,3,8,128]{4,3,2,1,0:T(8,128)S(1)} %get-tuple-element.37), channel_id=1, source_target_pairs={{0,1},{1,0},{2,3},{3,2},{4,5},{5,4},{6,7},{7,6},{8,9},{9,8},{10,11... | collective-permute-start | bytes 73736 | tf_op jit(solution)/shard_map/ppermute | solution.py:244

commit v6 on v5

--- a/solution.py
+++ b/solution.py
@@ -68,10 +68,14 @@
     return plane, first_pos, lax.rem(plane, 2) == 1, lax.rem(first_pos // rows, 2) == 1
 
 
-def taper(first_pos, row, source, width):
+def taper_kernel(rows, source_ref, width_ref, steps_ref, coefs_ref):
+    _, first_pos, _, _ = place(rows)
     ones = jnp.ones((8, 128), jnp.float32)
-    distance = ones * (first_pos + row - source).astype(jnp.float32) / (ones * width.astype(jnp.float32))
-    return 1.0 / (1.0 + distance * distance)
+    per_width = ones * width_ref[0].astype(jnp.float32)
+    for i in range(rows + 2):
+        distance = ones * (first_pos + i - 1 - source_ref[0]).astype(jnp.float32) / per_width
+        coefs_ref[i] = 1.0 / (1.0 + distance * distance)
+    coefs_ref[rows + 2] = 0.25 / (ones * steps_ref[0].astype(jnp.float32))
 
 
 def store_z(rows, matrices, row, field, far_ref, near_ref):
@@ -90,31 +94,30 @@
 
 
 def begin_kernel(
-    rows, source_hbm, width_hbm, steps_hbm, adjoint_hbm, links_hbm,
-    start_ref, far_ref, near_ref, outer_ref, inner_ref, coefs_ref,
-    source_ref, width_ref, steps_ref, adjoint_ref, links_ref, sems,
+    rows, adjoint_hbm, links_hbm, far_ref, near_ref, outer_ref, inner_ref, adjoint_ref, links_ref, sems
 ):
     row_entries = SETS * MUS * ENTRIES
     z_first = (2 * MUS + 2) * ENTRIES
     aligned = z_first // 8 * 8
-    pairs = [(source_hbm, source_ref), (width_hbm, width_ref), (steps_hbm, steps_ref), (adjoint_hbm, adjoint_ref)]
+    copies = [pltpu.make_async_copy(adjoint_hbm, adjoint_ref, sems.at[rows])]
     for row in range(rows):
         part = links_hbm.at[pl.ds(row * row_entries + aligned, row_entries - aligned), :]
-        pairs.append((part, links_ref.at[row]))
-    copies = [pltpu.make_async_copy(p, q, sems.at[i]) for i, (p, q) in enumerate(pairs)]
+        copies.append(pltpu.make_async_copy(part, links_ref.at[row], sems.at[row]))
     for copy in copies:
         copy.start()
     for copy in copies:
         copy.wait()
-    _, first_pos, _, _ = place(rows)
-    for row in range(rows):
-        inside = taper(first_pos, row, source_ref[0], width_ref[0])
-        coefs_ref[row] = inside
-        start = combine(lambda v: inside * v, load_field(adjoint_ref, row))
-        store_field(start_ref, row, start)
-        store_z(rows, (links_ref.at[row], z_first - aligned), row, start, far_ref, near_ref)
-    coefs_ref[rows] = 0.25 / (jnp.ones((8, 128), jnp.float32) * steps_ref[0].astype(jnp.float32))
-    store_t(rows, (links_ref.at[rows - 1], z_first + ENTRIES - aligned), start_ref, outer_ref, inner_ref)
+    for row in range(rows):
+        matrices = links_ref.at[row], z_first - aligned
+        store_z(rows, matrices, row, load_field(adjoint_ref, row), far_ref, near_ref)
+    store_t(rows, (links_ref.at[rows - 1], z_first + ENTRIES - aligned), adjoint_ref, outer_ref, inner_ref)
+
+
+def start_kernel(rows, link_set, coefs_ref, adjoint_ref, links_ref, sum_ref, start_ref):
+    for row in range(rows):
+        inside = coefs_ref[row + 1]
+        store_field(start_ref, row, combine(lambda v: inside * v, load_field(adjoint_ref, row)))
+    local_kernel(rows, link_set, start_ref, links_ref, sum_ref)
 
 
 def local_kernel(rows, link_set, field_ref, links_ref, sum_ref):
@@ -149,10 +152,12 @@
     lax.fori_loop(0, rows - 1, between, 0)
 
 
-def arrived_sum(links_ref, link_set, row, rows, arrivals):
+def arrived_sum(links_ref, link_set, row, rows, arrivals, coefs_ref=None):
     sum_ref, far_ref, near_ref, outer_ref, inner_ref = arrivals
     _, first_pos, odd_plane, odd_block = place(rows)
     far, near = load_field(far_ref, row), load_field(near_ref, row)
+    if coefs_ref is not None:
+        far, near = (combine(lambda v: coefs_ref[row + 1] * v, f) for f in (far, near))
     above = combine(lambda p, q: jnp.where(odd_plane, p, q), far, near)
     ahead_z, _ = transport(links_at(links_ref, row, link_set, 2), above, None)
     total = combine(
@@ -161,9 +166,13 @@
     outer, inner = load_field(outer_ref, 0), load_field(inner_ref, 0)
     if row == 0:
         exists = jnp.where(first_pos != 0, 1.0, 0.0)
+        if coefs_ref is not None:
+            exists = exists * coefs_ref[0]
         total = combine(lambda s, p, q: s + exists * jnp.where(odd_block, q, p), total, outer, inner)
     if row == rows - 1:
         exists = jnp.where(first_pos != BAND - rows, 1.0, 0.0)
+        if coefs_ref is not None:
+            exists = exists * coefs_ref[rows + 1]
         later = combine(lambda p, q: exists * jnp.where(odd_block, p, q), outer, inner)
         ahead_t, _ = transport(links_at(links_ref, row, link_set, 3), later, None)
         total = combine(lambda s, f: s + f, total, ahead_t)
@@ -173,8 +182,8 @@
 def third_kernel(rows, coefs_ref, links_ref, *refs):
     arrivals, (third_ref, far_ref, near_ref, outer_ref, inner_ref) = refs[:5], refs[5:]
     for row in range(rows):
-        inside, eps = coefs_ref[row], coefs_ref[rows]
-        total = arrived_sum(links_ref, 2, row, rows, arrivals)
+        inside, eps = coefs_ref[row + 1], coefs_ref[rows + 2]
+        total = arrived_sum(links_ref, 2, row, rows, arrivals, coefs_ref)
         third = combine(lambda s: 0.75 * (inside * (eps * s)), total)
         store_field(third_ref, row, third)
         store_z(rows, links_at(links_ref, row, 1, 2), row, third, far_ref, near_ref)
@@ -184,7 +193,7 @@
 def second_kernel(rows, coefs_ref, links_ref, *refs):
     arrivals, (start_ref, third_ref, mixed_ref, far_ref, near_ref, outer_ref, inner_ref, base_ref) = refs[:5], refs[5:]
     for row in range(rows):
-        inside, eps = coefs_ref[row], coefs_ref[rows]
+        inside, eps = coefs_ref[row + 1], coefs_ref[rows + 2]
         total = arrived_sum(links_ref, 1, row, rows, arrivals)
         third = load_field(third_ref, row)
         second = combine(lambda v, s: v + (8.0 / 9.0) * (inside * (eps * s)), load_field(start_ref, row), total)
@@ -198,7 +207,7 @@
 def last_kernel(rows, coefs_ref, links_ref, *refs):
     arrivals, (base_ref, out_ref) = refs[:5], refs[5:]
     for row in range(rows):
-        inside, eps = coefs_ref[row], coefs_ref[rows]
+        inside, eps = coefs_ref[row + 1], coefs_ref[rows + 2]
         total = arrived_sum(links_ref, 0, row, rows, arrivals)
         store_field(out_ref, row, combine(lambda p, s: p + inside * (eps * s), load_field(base_ref, row), total))
 
@@ -224,7 +233,7 @@
     links = jnp.transpose(flowed, (0, 1, 2, 4, 5, 3, 6)).reshape(-1, flowed.shape[-1])
     whole = jax.ShapeDtypeStruct(adjoint.shape, jnp.float32)
     one_row = jax.ShapeDtypeStruct((1,) + adjoint.shape[1:], jnp.float32)
-    coefs = jax.ShapeDtypeStruct((rows + 1,) + adjoint.shape[3:], jnp.float32)
+    coefs_shape = jax.ShapeDtypeStruct((rows + 3,) + adjoint.shape[3:], jnp.float32)
 
     def in_plane(i, by):
         return i - i % per_plane + (i + by) % per_plane
@@ -237,38 +246,47 @@
     outer_pairs = [(i, in_plane(i, 1 if i % 2 else -1)) for i in range(count)]
     inner_pairs = [(i, in_plane(i, -1 if i % 2 else 1)) for i in range(count)]
 
-    def arrivals(link_set, field, far, near, outer, inner):
-        far = lax.ppermute(far, "gz", far_pairs)
-        near = lax.ppermute(near, "gz", near_pairs)
-        outer = lax.ppermute(outer, "gz", outer_pairs)
-        inner = lax.ppermute(inner, "gz", inner_pairs)
-        total = call(functools.partial(local_kernel, rows, link_set), f"local_{link_set}", (field, links), whole, 22)
-        return total, far, near, outer, inner
+    def sent_on(far, near, outer, inner):
+        return (
+            lax.ppermute(far, "gz", far_pairs),
+            lax.ppermute(near, "gz", near_pairs),
+            lax.ppermute(outer, "gz", outer_pairs),
+            lax.ppermute(inner, "gz", inner_pairs),
+        )
+
+    def local(link_set, field):
+        return call(functools.partial(local_kernel, rows, link_set), f"local_{link_set}", (field, links), whole, 22)
 
     sent = (whole, whole, one_row, one_row)
     copied = SETS * MUS * ENTRIES - (2 * MUS + 2) * ENTRIES // 8 * 8
-    start, far, near, outer, inner, coefs = call(
-        functools.partial(begin_kernel, rows), "begin", (source_slice, band_width, flow_steps, adjoint, links),
-        (whole,) + sent + (coefs,), 5, pltpu.HBM,
-        [pltpu.SMEM((1,), jnp.int32)] * 3
-        + [
+    sending = call(
+        functools.partial(begin_kernel, rows), "begin",
+        tuple(pltpu.with_memory_space_constraint(a, pltpu.HBM) for a in (adjoint, links)), sent, 5, pltpu.HBM,
+        [
             pltpu.VMEM(adjoint.shape, jnp.float32),
             pltpu.VMEM((rows, copied, flowed.shape[-1]), jnp.float32),
-            pltpu.SemaphoreType.DMA((4 + rows,)),
+            pltpu.SemaphoreType.DMA((rows + 1,)),
         ],
     )
-    third, far, near, outer, inner = call(
-        functools.partial(third_kernel, rows), "third",
-        (coefs, links) + arrivals(2, start, far, near, outer, inner), (whole,) + sent, 10,
-    )
-    mixed, far, near, outer, inner, base = call(
-        functools.partial(second_kernel, rows), "second",
-        (coefs, links) + arrivals(1, third, far, near, outer, inner) + (start, third),
+    arrived = sent_on(*sending)
+    coefs = call(
+        functools.partial(taper_kernel, rows), "tapers", (source_slice, band_width, flow_steps), coefs_shape, 1,
+        pltpu.SMEM,
+    )
+    total, start = call(
+        functools.partial(start_kernel, rows, 2), "start", (coefs, adjoint, links), (whole, whole), 22
+    )
+    third, *sending = call(
+        functools.partial(third_kernel, rows), "third", (coefs, links, total) + arrived, (whole,) + sent, 10
+    )
+    arrived = sent_on(*sending)
+    mixed, *sending, base = call(
+        functools.partial(second_kernel, rows), "second", (coefs, links, local(1, third)) + arrived + (start, third),
         (whole,) + sent + (whole,), 10,
     )
+    arrived = sent_on(*sending)
     return call(
-        functools.partial(last_kernel, rows), "last",
-        (coefs, links) + arrivals(0, mixed, far, near, outer, inner) + (base,), whole, 5,
+        functools.partial(last_kernel, rows), "last", (coefs, links, local(0, mixed)) + arrived + (base,), whole, 5
     )
 
 

time: 31.2 us -> 27.7 us (0.89)
  waiting for transfers between devices: 9.62 us -> 7.6 us
  local copies, waits for them, and re-layouts: 1.9 us -> 0.01 us
  Pallas kernels: 3.24 us -> 3.64 us
    ppermute x12, waiting for transfers between devices: 9.62 us -> 7.6 us  [the longest x3 4.38 us: sent_on(): lax.ppermute(outer, 'gz', outer_pairs)]
    unnamed x6 -> x4, local copies, waits for them, and re-layouts: 1.9 us -> 0.01 us
    pallas_call x7 -> x8, Pallas kernels: 3.24 us -> 3.64 us  [call(): pl.pallas_call(kernel, name=name, out_shape=out_shapes, in_specs=[pl.Bloc...]
  transfers between devices with their start and end apart: 12 -> 12, of which waited for: 8 -> 8; matrix products, arithmetic and copies ran while one was open for 0% -> 0% of each run, Pallas kernels for 5% -> 6%
where the time goes in v6:
time: 27.7 us; the launch traced here: 27.6 us
  starting transfers between devices  14.3 us (52%)
  waiting for transfers between devices  7.6 us (27%)
  Pallas kernels  3.64 us (13%)
  between operations  2.02 us (7%)
    ppermute x3, starting transfers between devices, sent_on(): lax.ppermute(far, 'gz', far_pairs)  9.36 us
    ppermute x3, waiting for transfers between devices, sent_on(): lax.ppermute(outer, 'gz', outer_pairs)  4.38 us
    pallas_call x8, Pallas kernels, call(): pl.pallas_call(kernel, name=name, out_shape=out_shapes, in_specs=[pl.Bloc...  3.64 us
    ppermute x3, starting transfers between devices, sent_on(): lax.ppermute(inner, 'gz', inner_pairs)  3.11 us
    ppermute x3, waiting for transfers between devices, sent_on(): lax.ppermute(near, 'gz', near_pairs)  1.96 us
    ppermute x3, starting transfers between devices, sent_on(): lax.ppermute(outer, 'gz', outer_pairs)  1.81 us
    ppermute x3, waiting for transfers between devices, sent_on(): lax.ppermute(far, 'gz', far_pairs)  1.25 us
  transfers between devices with their start and end apart: 12, of which 8 were waited for; matrix products, arithmetic and copies ran while one was open for 0% of the time, Pallas kernels for 6%

profile of v6, /device:TPU:0, one launch (start us, length us, event | category | flops | bytes accessed | tf_op | source)
XLA Modules:
  0.0 27.6 jit_solution(3271509344034863555)
XLA Ops:
  0.0 1.1 %begin.1 = (f32[4,2,3,8,128]{4,3,2,1,0:T(8,128)S(1)}, f32[4,2,3,8,128]{4,3,2,1,0:T(8,128)S(1)}, f32[1,2,3,8,128]{4,3,2,1,0:T(8,128)S(1)}, f32[1,2,3,8,128]{4,3,2,1,0:T(8,128)S(1)}) custom-call(f32[4,2,3,8,128]{4,3,2,1,0:T(8,128)} %adjoint_hbm.1, f32[864,128]{1,0:T(8,128)} %bitcast.3), custom_call_target="tpu_custom_call" | custom-call | flops 368640 | bytes 368640 | tf_op jit(solution)/shard_map/begin/pallas_call | solution.py:217
  1.1 5.1 %collective-permute-start = (f32[4,2,3,8,128]{4,3,2,1,0:T(8,128)S(1)}, f32[4,2,3,8,128]{4,3,2,1,0:T(8,128)S(1)}, u32[]{:S(2)}, u32[]{:S(2)}) collective-permute-start(f32[4,2,3,8,128]{4,3,2,1,0:T(8,128)S(1)} %get-tuple-element.23), channel_id=1, source_target_pairs={{0,24},{1,25},{2,26},{3,27},{4,28},{5,29},{6,30},{7,31},{8,16},{9,... | collective-permute-start | bytes 294920 | tf_op jit(solution)/shard_map/ppermute | solution.py:251
  6.2 0.0 collective-permute-start.1
  6.2 1.6 %collective-permute-start.2 = (f32[1,2,3,8,128]{4,3,2,1,0:T(8,128)S(1)}, f32[1,2,3,8,128]{4,3,2,1,0:T(8,128)S(1)}, u32[]{:S(2)}, u32[]{:S(2)}) collective-permute-start(f32[1,2,3,8,128]{4,3,2,1,0:T(8,128)S(1)} %get-tuple-element.25), channel_id=1, source_target_pairs={{0,7},{1,2},{2,1},{3,4},{4,3},{5,6},{6,5},{7,0},{8,15},{9,10},{10,... | collective-permute-start | bytes 73736 | tf_op jit(solution)/shard_map/ppermute | solution.py:253
  7.8 0.0 collective-permute-start.3
  9.8 0.5 %start.1 = (f32[4,2,3,8,128]{4,3,2,1,0:T(8,128)S(1)}, f32[4,2,3,8,128]{4,3,2,1,0:T(8,128)S(1)}) custom-call(f32[7,8,128]{2,1,0:T(8,128)S(1)} %tapers.1.coefs_ref, f32[4,2,3,8,128]{4,3,2,1,0:T(8,128)S(1)} %copy-done.1, f32[864,128]{1,0:T(8,128)S(1)} %bitcast.4), custom_call_target="tpu_custom_call" | custom-call | flops 1622016 | bytes 1622016 | tf_op jit(solution)/shard_map/start/pallas_call | solution.py:217
  10.3 0.2 collective-permute-done.2.refs_3_
  10.5 0.7 %collective-permute-done.1.refs_2_ = f32[4,2,3,8,128]{4,3,2,1,0:T(8,128)S(1)} collective-permute-done((f32[4,2,3,8,128]{4,3,2,1,0:T(8,128)S(1)}, f32[4,2,3,8,128]{4,3,2,1,0:T(8,128)S(1)}, u32[]{:S(2)}, u32[]{:S(2)}) %collective-permute-start.1) | collective-permute-done | bytes 98336 | tf_op jit(solution)/shard_map/ppermute | solution.py:252
  11.2 0.2 third.1
  11.4 2.5 %collective-permute-start.4 = (f32[4,2,3,8,128]{4,3,2,1,0:T(8,128)S(1)}, f32[4,2,3,8,128]{4,3,2,1,0:T(8,128)S(1)}, u32[]{:S(2)}, u32[]{:S(2)}) collective-permute-start(f32[4,2,3,8,128]{4,3,2,1,0:T(8,128)S(1)} %get-tuple-element.28), channel_id=1, source_target_pairs={{0,24},{1,25},{2,26},{3,27},{4,28},{5,29},{6,30},{7,31},{8,16},{9,... | collective-permute-start | bytes 294920 | tf_op jit(solution)/shard_map/ppermute | solution.py:251
  13.9 1.6 %collective-permute-start.7 = (f32[1,2,3,8,128]{4,3,2,1,0:T(8,128)S(1)}, f32[1,2,3,8,128]{4,3,2,1,0:T(8,128)S(1)}, u32[]{:S(2)}, u32[]{:S(2)}) collective-permute-start(f32[1,2,3,8,128]{4,3,2,1,0:T(8,128)S(1)} %get-tuple-element.31), channel_id=1, source_target_pairs={{0,1},{1,0},{2,3},{3,2},{4,5},{5,4},{6,7},{7,6},{8,9},{9,8},{10,11... | collective-permute-start | bytes 73736 | tf_op jit(solution)/shard_map/ppermute | solution.py:254
  15.5 0.5 %local_1.1.refs_0_ = f32[4,2,3,8,128]{4,3,2,1,0:T(8,128)S(1)} custom-call(f32[4,2,3,8,128]{4,3,2,1,0:T(8,128)S(1)} %get-tuple-element.27.field_ref.refs_6_, f32[864,128]{1,0:T(8,128)S(1)} %bitcast.6), custom_call_target="tpu_custom_call" | custom-call | flops 1622016 | bytes 1622016 | tf_op jit(solution)/shard_map/local_1/pallas_call | solution.py:217
  16.0 2.2 %collective-permute-done.6.refs_3_ = f32[1,2,3,8,128]{4,3,2,1,0:T(8,128)S(1)} collective-permute-done((f32[1,2,3,8,128]{4,3,2,1,0:T(8,128)S(1)}, f32[1,2,3,8,128]{4,3,2,1,0:T(8,128)S(1)}, u32[]{:S(2)}, u32[]{:S(2)}) %collective-permute-start.6) | collective-permute-done | bytes 24608 | tf_op jit(solution)/shard_map/ppermute | solution.py:253
  18.2 0.6 %collective-permute-done.4.refs_1_ = f32[4,2,3,8,128]{4,3,2,1,0:T(8,128)S(1)} collective-permute-done((f32[4,2,3,8,128]{4,3,2,1,0:T(8,128)S(1)}, f32[4,2,3,8,128]{4,3,2,1,0:T(8,128)S(1)}, u32[]{:S(2)}, u32[]{:S(2)}) %collective-permute-start.4) | collective-permute-done | bytes 98336 | tf_op jit(solution)/shard_map/ppermute | solution.py:251
  18.8 0.4 %collective-permute-done.5.refs_2_ = f32[4,2,3,8,128]{4,3,2,1,0:T(8,128)S(1)} collective-permute-done((f32[4,2,3,8,128]{4,3,2,1,0:T(8,128)S(1)}, f32[4,2,3,8,128]{4,3,2,1,0:T(8,128)S(1)}, u32[]{:S(2)}, u32[]{:S(2)}) %collective-permute-start.5) | collective-permute-done | bytes 98336 | tf_op jit(solution)/shard_map/ppermute | solution.py:252
  19.2 0.2 second.1
  19.4 1.8 %collective-permute-start.8 = (f32[4,2,3,8,128]{4,3,2,1,0:T(8,128)S(1)}, f32[4,2,3,8,128]{4,3,2,1,0:T(8,128)S(1)}, u32[]{:S(2)}, u32[]{:S(2)}) collective-permute-start(f32[4,2,3,8,128]{4,3,2,1,0:T(8,128)S(1)} %get-tuple-element.34), channel_id=1, source_target_pairs={{0,24},{1,25},{2,26},{3,27},{4,28},{5,29},{6,30},{7,31},{8,16},{9,... | collective-permute-start | bytes 294920 | tf_op jit(solution)/shard_map/ppermute | solution.py:251
  21.2 0.2 collective-permute-start.10
  21.4 1.5 %collective-permute-start.11 = (f32[1,2,3,8,128]{4,3,2,1,0:T(8,128)S(1)}, f32[1,2,3,8,128]{4,3,2,1,0:T(8,128)S(1)}, u32[]{:S(2)}, u32[]{:S(2)}) collective-permute-start(f32[1,2,3,8,128]{4,3,2,1,0:T(8,128)S(1)} %get-tuple-element.37), channel_id=1, source_target_pairs={{0,1},{1,0},{2,3},{3,2},{4,5},{5,4},{6,7},{7,6},{8,9},{9,8},{10,11... | collective-permute-start | bytes 73736 | tf_op jit(solution)/shard_map/ppermute | solution.py:254
  22.9 0.5 %local_0.1.refs_0_ = f32[4,2,3,8,128]{4,3,2,1,0:T(8,128)S(1)} custom-call(f32[4,2,3,8,128]{4,3,2,1,0:T(8,128)S(1)} %get-tuple-element.33.field_ref, f32[864,128]{1,0:T(8,128)S(1)} %bitcast.8), custom_call_target="tpu_custom_call" | custom-call | flops 1622016 | bytes 1622016 | tf_op jit(solution)/shard_map/local_0/pallas_call | solution.py:217
  23.4 2.0 %collective-permute-done.10.refs_3_ = f32[1,2,3,8,128]{4,3,2,1,0:T(8,128)S(1)} collective-permute-done((f32[1,2,3,8,128]{4,3,2,1,0:T(8,128)S(1)}, f32[1,2,3,8,128]{4,3,2,1,0:T(8,128)S(1)}, u32[]{:S(2)}, u32[]{:S(2)}) %collective-permute-start.10) | collective-permute-done | bytes 24608 | tf_op jit(solution)/shard_map/ppermute | solution.py:253
  25.4 0.6 %collective-permute-done.8.refs_1_ = f32[4,2,3,8,128]{4,3,2,1,0:T(8,128)S(1)} collective-permute-done((f32[4,2,3,8,128]{4,3,2,1,0:T(8,128)S(1)}, f32[4,2,3,8,128]{4,3,2,1,0:T(8,128)S(1)}, u32[]{:S(2)}, u32[]{:S(2)}) %collective-permute-start.8) | collective-permute-done | bytes 98336 | tf_op jit(solution)/shard_map/ppermute | solution.py:251
  26.0 0.8 %collective-permute-done.9.refs_2_ = f32[4,2,3,8,128]{4,3,2,1,0:T(8,128)S(1)} collective-permute-done((f32[4,2,3,8,128]{4,3,2,1,0:T(8,128)S(1)}, f32[4,2,3,8,128]{4,3,2,1,0:T(8,128)S(1)}, u32[]{:S(2)}, u32[]{:S(2)}) %collective-permute-start.9) | collective-permute-done | bytes 98336 | tf_op jit(solution)/shard_map/ppermute | solution.py:252
  26.8 0.7 %last.1 = f32[4,2,3,8,128]{4,3,2,1,0:T(8,128)} custom-call(f32[7,8,128]{2,1,0:T(8,128)S(1)} %tapers.1.coefs_ref, f32[864,128]{1,0:T(8,128)S(1)} %bitcast.9, f32[4,2,3,8,128]{4,3,2,1,0:T(8,128)S(1)} %local_0.1.refs_0_, f32[4,2,3,8,128]{4,3,2,1,0:T(8,128)S(1)} %collective-permute-done.8.refs_1_, f32[4,2,3,8,128]{4,3,2,1,0:T(8,128)S(1)} %collective-permute-done.9.refs_2_, ...), custom_call_target="tpu_custom_call" | custom-call | flops 368640 | bytes 368640 | tf_op jit(solution)/shard_map/last/pallas_call | solution.py:217
  (12 shorter events, 0.1 us)
Async XLA Ops:
  0.0 9.8 %copy-start = (f32[4,3,4,2,3,3,128]{6,3,5,4,2,1,0:T(2,128)S(1)}, f32[4,3,4,2,3,3,128]{6,3,5,4,2,1,0:T(2,128)}, u32[]{:S(2)}) copy-start(f32[4,3,4,2,3,3,128]{6,3,5,4,2,1,0:T(2,128)} %param.6) | copy-start | bytes 1327108
  0.0 9.8 %copy-start.1 = (f32[4,2,3,8,128]{4,3,2,1,0:T(8,128)S(1)}, f32[4,2,3,8,128]{4,3,2,1,0:T(8,128)}, u32[]{:S(2)}) copy-start(f32[4,2,3,8,128]{4,3,2,1,0:T(8,128)} %adjoint_hbm.1) | copy-start | bytes 294916
  1.1 9.4 %collective-permute-start = (f32[4,2,3,8,128]{4,3,2,1,0:T(8,128)S(1)}, f32[4,2,3,8,128]{4,3,2,1,0:T(8,128)S(1)}, u32[]{:S(2)}, u32[]{:S(2)}) collective-permute-start(f32[4,2,3,8,128]{4,3,2,1,0:T(8,128)S(1)} %get-tuple-element.23), channel_id=1, source_target_pairs={{0,24},{1,25},{2,26},{3,27},{4,28},{5,29},{6,30},{7,31},{8,16},{9,... | collective-permute-start | bytes 294920 | tf_op jit(solution)/shard_map/ppermute | solution.py:251
  6.2 5.0 %collective-permute-start.1 = (f32[4,2,3,8,128]{4,3,2,1,0:T(8,128)S(1)}, f32[4,2,3,8,128]{4,3,2,1,0:T(8,128)S(1)}, u32[]{:S(2)}, u32[]{:S(2)}) collective-permute-start(f32[4,2,3,8,128]{4,3,2,1,0:T(8,128)S(1)} %get-tuple-element.24), channel_id=1, source_target_pairs={{0,8},{1,9},{2,10},{3,11},{4,12},{5,13},{6,14},{7,15},{8,0},{9,1},... | collective-permute-start | bytes 294920 | tf_op jit(solution)/shard_map/ppermute | solution.py:252
  6.2 4.3 %collective-permute-start.2 = (f32[1,2,3,8,128]{4,3,2,1,0:T(8,128)S(1)}, f32[1,2,3,8,128]{4,3,2,1,0:T(8,128)S(1)}, u32[]{:S(2)}, u32[]{:S(2)}) collective-permute-start(f32[1,2,3,8,128]{4,3,2,1,0:T(8,128)S(1)} %get-tuple-element.25), channel_id=1, source_target_pairs={{0,7},{1,2},{2,1},{3,4},{4,3},{5,6},{6,5},{7,0},{8,15},{9,10},{10,... | collective-permute-start | bytes 73736 | tf_op jit(solution)/shard_map/ppermute | solution.py:253
  7.8 2.7 %collective-permute-start.3 = (f32[1,2,3,8,128]{4,3,2,1,0:T(8,128)S(1)}, f32[1,2,3,8,128]{4,3,2,1,0:T(8,128)S(1)}, u32[]{:S(2)}, u32[]{:S(2)}) collective-permute-start(f32[1,2,3,8,128]{4,3,2,1,0:T(8,128)S(1)} %get-tuple-element.26), channel_id=1, source_target_pairs={{0,1},{1,0},{2,3},{3,2},{4,5},{5,4},{6,7},{7,6},{8,9},{9,8},{10,11... | collective-permute-start | bytes 73736 | tf_op jit(solution)/shard_map/ppermute | solution.py:254
  11.4 7.4 %collective-permute-start.4 = (f32[4,2,3,8,128]{4,3,2,1,0:T(8,128)S(1)}, f32[4,2,3,8,128]{4,3,2,1,0:T(8,128)S(1)}, u32[]{:S(2)}, u32[]{:S(2)}) collective-permute-start(f32[4,2,3,8,128]{4,3,2,1,0:T(8,128)S(1)} %get-tuple-element.28), channel_id=1, source_target_pairs={{0,24},{1,25},{2,26},{3,27},{4,28},{5,29},{6,30},{7,31},{8,16},{9,... | collective-permute-start | bytes 294920 | tf_op jit(solution)/shard_map/ppermute | solution.py:251
  13.9 5.4 %collective-permute-start.5 = (f32[4,2,3,8,128]{4,3,2,1,0:T(8,128)S(1)}, f32[4,2,3,8,128]{4,3,2,1,0:T(8,128)S(1)}, u32[]{:S(2)}, u32[]{:S(2)}) collective-permute-start(f32[4,2,3,8,128]{4,3,2,1,0:T(8,128)S(1)} %get-tuple-element.29), channel_id=1, source_target_pairs={{0,8},{1,9},{2,10},{3,11},{4,12},{5,13},{6,14},{7,15},{8,0},{9,1},... | collective-permute-start | bytes 294920 | tf_op jit(solution)/shard_map/ppermute | solution.py:252
  13.9 4.3 %collective-permute-start.6 = (f32[1,2,3,8,128]{4,3,2,1,0:T(8,128)S(1)}, f32[1,2,3,8,128]{4,3,2,1,0:T(8,128)S(1)}, u32[]{:S(2)}, u32[]{:S(2)}) collective-permute-start(f32[1,2,3,8,128]{4,3,2,1,0:T(8,128)S(1)} %get-tuple-element.30), channel_id=1, source_target_pairs={{0,7},{1,2},{2,1},{3,4},{4,3},{5,6},{6,5},{7,0},{8,15},{9,10},{10,... | collective-permute-start | bytes 73736 | tf_op jit(solution)/shard_map/ppermute | solution.py:253
  13.9 4.3 %collective-permute-start.7 = (f32[1,2,3,8,128]{4,3,2,1,0:T(8,128)S(1)}, f32[1,2,3,8,128]{4,3,2,1,0:T(8,128)S(1)}, u32[]{:S(2)}, u32[]{:S(2)}) collective-permute-start(f32[1,2,3,8,128]{4,3,2,1,0:T(8,128)S(1)} %get-tuple-element.31), channel_id=1, source_target_pairs={{0,1},{1,0},{2,3},{3,2},{4,5},{5,4},{6,7},{7,6},{8,9},{9,8},{10,11... | collective-permute-start | bytes 73736 | tf_op jit(solution)/shard_map/ppermute | solution.py:254
  19.4 6.6 %collective-permute-start.8 = (f32[4,2,3,8,128]{4,3,2,1,0:T(8,128)S(1)}, f32[4,2,3,8,128]{4,3,2,1,0:T(8,128)S(1)}, u32[]{:S(2)}, u32[]{:S(2)}) collective-permute-start(f32[4,2,3,8,128]{4,3,2,1,0:T(8,128)S(1)} %get-tuple-element.34), channel_id=1, source_target_pairs={{0,24},{1,25},{2,26},{3,27},{4,28},{5,29},{6,30},{7,31},{8,16},{9,... | collective-permute-start | bytes 294920 | tf_op jit(solution)/shard_map/ppermute | solution.py:251
  21.2 5.7 %collective-permute-start.9 = (f32[4,2,3,8,128]{4,3,2,1,0:T(8,128)S(1)}, f32[4,2,3,8,128]{4,3,2,1,0:T(8,128)S(1)}, u32[]{:S(2)}, u32[]{:S(2)}) collective-permute-start(f32[4,2,3,8,128]{4,3,2,1,0:T(8,128)S(1)} %get-tuple-element.35), channel_id=1, source_target_pairs={{0,8},{1,9},{2,10},{3,11},{4,12},{5,13},{6,14},{7,15},{8,0},{9,1},... | collective-permute-start | bytes 294920 | tf_op jit(solution)/shard_map/ppermute | solution.py:252
  21.2 4.2 %collective-permute-start.10 = (f32[1,2,3,8,128]{4,3,2,1,0:T(8,128)S(1)}, f32[1,2,3,8,128]{4,3,2,1,0:T(8,128)S(1)}, u32[]{:S(2)}, u32[]{:S(2)}) collective-permute-start(f32[1,2,3,8,128]{4,3,2,1,0:T(8,128)S(1)} %get-tuple-element.36), channel_id=1, source_target_pairs={{0,7},{1,2},{2,1},{3,4},{4,3},{5,6},{6,5},{7,0},{8,15},{9,10},{10,... | collective-permute-start | bytes 73736 | tf_op jit(solution)/shard_map/ppermute | solution.py:253
  21.4 4.0 %collective-permute-start.11 = (f32[1,2,3,8,128]{4,3,2,1,0:T(8,128)S(1)}, f32[1,2,3,8,128]{4,3,2,1,0:T(8,128)S(1)}, u32[]{:S(2)}, u32[]{:S(2)}) collective-permute-start(f32[1,2,3,8,128]{4,3,2,1,0:T(8,128)S(1)} %get-tuple-element.37), channel_id=1, source_target_pairs={{0,1},{1,0},{2,3},{3,2},{4,5},{5,4},{6,7},{7,6},{8,9},{9,8},{10,11... | collective-permute-start | bytes 73736 | tf_op jit(solution)/shard_map/ppermute | solution.py:254

commit v7 on v6

--- a/solution.py
+++ b/solution.py
@@ -247,12 +247,11 @@
     inner_pairs = [(i, in_plane(i, -1 if i % 2 else 1)) for i in range(count)]
 
     def sent_on(far, near, outer, inner):
-        return (
-            lax.ppermute(far, "gz", far_pairs),
-            lax.ppermute(near, "gz", near_pairs),
-            lax.ppermute(outer, "gz", outer_pairs),
-            lax.ppermute(inner, "gz", inner_pairs),
-        )
+        near = lax.ppermute(near, "gz", near_pairs)
+        far = lax.ppermute(far, "gz", far_pairs)
+        outer = lax.ppermute(outer, "gz", outer_pairs)
+        inner = lax.ppermute(inner, "gz", inner_pairs)
+        return far, near, outer, inner
 
     def local(link_set, field):
         return call(functools.partial(local_kernel, rows, link_set), f"local_{link_set}", (field, links), whole, 22)

time: 27.7 us -> 27.7 us (level)
  no operation moved by 1% of the time
where the time goes in v7:
time: 27.7 us; the launch traced here: 27.6 us
  starting transfers between devices  14.3 us (52%)
  waiting for transfers between devices  7.6 us (27%)
  Pallas kernels  3.64 us (13%)
  between operations  2.02 us (7%)
    ppermute x3, starting transfers between devices, sent_on(): far = lax.ppermute(far, 'gz', far_pairs)  9.36 us
    ppermute x3, waiting for transfers between devices, sent_on(): outer = lax.ppermute(outer, 'gz', outer_pairs)  4.38 us
    pallas_call x8, Pallas kernels, call(): pl.pallas_call(kernel, name=name, out_shape=out_shapes, in_specs=[pl.Bloc...  3.64 us
    ppermute x3, starting transfers between devices, sent_on(): inner = lax.ppermute(inner, 'gz', inner_pairs)  3.11 us
    ppermute x3, waiting for transfers between devices, sent_on(): near = lax.ppermute(near, 'gz', near_pairs)  1.96 us
    ppermute x3, starting transfers between devices, sent_on(): outer = lax.ppermute(outer, 'gz', outer_pairs)  1.81 us
    ppermute x3, waiting for transfers between devices, sent_on(): far = lax.ppermute(far, 'gz', far_pairs)  1.25 us
  transfers between devices with their start and end apart: 12, of which 8 were waited for; matrix products, arithmetic and copies ran while one was open for 0% of the time, Pallas kernels for 6%

profile of v7, /device:TPU:0, one launch (start us, length us, event | category | flops | bytes accessed | tf_op | source)
XLA Modules:
  0.0 27.6 jit_solution(3271509344034863555)
XLA Ops:
  0.0 1.1 %begin.1 = (f32[4,2,3,8,128]{4,3,2,1,0:T(8,128)S(1)}, f32[4,2,3,8,128]{4,3,2,1,0:T(8,128)S(1)}, f32[1,2,3,8,128]{4,3,2,1,0:T(8,128)S(1)}, f32[1,2,3,8,128]{4,3,2,1,0:T(8,128)S(1)}) custom-call(f32[4,2,3,8,128]{4,3,2,1,0:T(8,128)} %adjoint_hbm.1, f32[864,128]{1,0:T(8,128)} %bitcast.3), custom_call_target="tpu_custom_call" | custom-call | flops 368640 | bytes 368640 | tf_op jit(solution)/shard_map/begin/pallas_call | solution.py:217
  1.1 5.1 %collective-permute-start = (f32[4,2,3,8,128]{4,3,2,1,0:T(8,128)S(1)}, f32[4,2,3,8,128]{4,3,2,1,0:T(8,128)S(1)}, u32[]{:S(2)}, u32[]{:S(2)}) collective-permute-start(f32[4,2,3,8,128]{4,3,2,1,0:T(8,128)S(1)} %get-tuple-element.23), channel_id=1, source_target_pairs={{0,24},{1,25},{2,26},{3,27},{4,28},{5,29},{6,30},{7,31},{8,16},{9,... | collective-permute-start | bytes 294920 | tf_op jit(solution)/shard_map/ppermute | solution.py:251
  6.2 0.0 collective-permute-start.1
  6.2 1.6 %collective-permute-start.2 = (f32[1,2,3,8,128]{4,3,2,1,0:T(8,128)S(1)}, f32[1,2,3,8,128]{4,3,2,1,0:T(8,128)S(1)}, u32[]{:S(2)}, u32[]{:S(2)}) collective-permute-start(f32[1,2,3,8,128]{4,3,2,1,0:T(8,128)S(1)} %get-tuple-element.25), channel_id=1, source_target_pairs={{0,7},{1,2},{2,1},{3,4},{4,3},{5,6},{6,5},{7,0},{8,15},{9,10},{10,... | collective-permute-start | bytes 73736 | tf_op jit(solution)/shard_map/ppermute | solution.py:252
  7.8 0.0 collective-permute-start.3
  9.8 0.5 %start.1 = (f32[4,2,3,8,128]{4,3,2,1,0:T(8,128)S(1)}, f32[4,2,3,8,128]{4,3,2,1,0:T(8,128)S(1)}) custom-call(f32[7,8,128]{2,1,0:T(8,128)S(1)} %tapers.1.coefs_ref, f32[4,2,3,8,128]{4,3,2,1,0:T(8,128)S(1)} %copy-done.1, f32[864,128]{1,0:T(8,128)S(1)} %bitcast.4), custom_call_target="tpu_custom_call" | custom-call | flops 1622016 | bytes 1622016 | tf_op jit(solution)/shard_map/start/pallas_call | solution.py:217
  10.3 0.2 collective-permute-done.2.refs_3_
  10.5 0.7 %collective-permute-done.1.refs_2_ = f32[4,2,3,8,128]{4,3,2,1,0:T(8,128)S(1)} collective-permute-done((f32[4,2,3,8,128]{4,3,2,1,0:T(8,128)S(1)}, f32[4,2,3,8,128]{4,3,2,1,0:T(8,128)S(1)}, u32[]{:S(2)}, u32[]{:S(2)}) %collective-permute-start.1) | collective-permute-done | bytes 98336 | tf_op jit(solution)/shard_map/ppermute | solution.py:250
  11.2 0.2 third.1
  11.4 2.5 %collective-permute-start.4 = (f32[4,2,3,8,128]{4,3,2,1,0:T(8,128)S(1)}, f32[4,2,3,8,128]{4,3,2,1,0:T(8,128)S(1)}, u32[]{:S(2)}, u32[]{:S(2)}) collective-permute-start(f32[4,2,3,8,128]{4,3,2,1,0:T(8,128)S(1)} %get-tuple-element.28), channel_id=1, source_target_pairs={{0,24},{1,25},{2,26},{3,27},{4,28},{5,29},{6,30},{7,31},{8,16},{9,... | collective-permute-start | bytes 294920 | tf_op jit(solution)/shard_map/ppermute | solution.py:251
  13.9 1.6 %collective-permute-start.7 = (f32[1,2,3,8,128]{4,3,2,1,0:T(8,128)S(1)}, f32[1,2,3,8,128]{4,3,2,1,0:T(8,128)S(1)}, u32[]{:S(2)}, u32[]{:S(2)}) collective-permute-start(f32[1,2,3,8,128]{4,3,2,1,0:T(8,128)S(1)} %get-tuple-element.31), channel_id=1, source_target_pairs={{0,1},{1,0},{2,3},{3,2},{4,5},{5,4},{6,7},{7,6},{8,9},{9,8},{10,11... | collective-permute-start | bytes 73736 | tf_op jit(solution)/shard_map/ppermute | solution.py:253
  15.5 0.5 %local_1.1.refs_0_ = f32[4,2,3,8,128]{4,3,2,1,0:T(8,128)S(1)} custom-call(f32[4,2,3,8,128]{4,3,2,1,0:T(8,128)S(1)} %get-tuple-element.27.field_ref.refs_6_, f32[864,128]{1,0:T(8,128)S(1)} %bitcast.6), custom_call_target="tpu_custom_call" | custom-call | flops 1622016 | bytes 1622016 | tf_op jit(solution)/shard_map/local_1/pallas_call | solution.py:217
  16.0 2.2 %collective-permute-done.6.refs_3_ = f32[1,2,3,8,128]{4,3,2,1,0:T(8,128)S(1)} collective-permute-done((f32[1,2,3,8,128]{4,3,2,1,0:T(8,128)S(1)}, f32[1,2,3,8,128]{4,3,2,1,0:T(8,128)S(1)}, u32[]{:S(2)}, u32[]{:S(2)}) %collective-permute-start.6) | collective-permute-done | bytes 24608 | tf_op jit(solution)/shard_map/ppermute | solution.py:252
  18.2 0.6 %collective-permute-done.4.refs_1_ = f32[4,2,3,8,128]{4,3,2,1,0:T(8,128)S(1)} collective-permute-done((f32[4,2,3,8,128]{4,3,2,1,0:T(8,128)S(1)}, f32[4,2,3,8,128]{4,3,2,1,0:T(8,128)S(1)}, u32[]{:S(2)}, u32[]{:S(2)}) %collective-permute-start.4) | collective-permute-done | bytes 98336 | tf_op jit(solution)/shard_map/ppermute | solution.py:251
  18.8 0.4 %collective-permute-done.5.refs_2_ = f32[4,2,3,8,128]{4,3,2,1,0:T(8,128)S(1)} collective-permute-done((f32[4,2,3,8,128]{4,3,2,1,0:T(8,128)S(1)}, f32[4,2,3,8,128]{4,3,2,1,0:T(8,128)S(1)}, u32[]{:S(2)}, u32[]{:S(2)}) %collective-permute-start.5) | collective-permute-done | bytes 98336 | tf_op jit(solution)/shard_map/ppermute | solution.py:250
  19.2 0.2 second.1
  19.4 1.8 %collective-permute-start.8 = (f32[4,2,3,8,128]{4,3,2,1,0:T(8,128)S(1)}, f32[4,2,3,8,128]{4,3,2,1,0:T(8,128)S(1)}, u32[]{:S(2)}, u32[]{:S(2)}) collective-permute-start(f32[4,2,3,8,128]{4,3,2,1,0:T(8,128)S(1)} %get-tuple-element.34), channel_id=1, source_target_pairs={{0,24},{1,25},{2,26},{3,27},{4,28},{5,29},{6,30},{7,31},{8,16},{9,... | collective-permute-start | bytes 294920 | tf_op jit(solution)/shard_map/ppermute | solution.py:251
  21.2 0.2 collective-permute-start.10
  21.4 1.5 %collective-permute-start.11 = (f32[1,2,3,8,128]{4,3,2,1,0:T(8,128)S(1)}, f32[1,2,3,8,128]{4,3,2,1,0:T(8,128)S(1)}, u32[]{:S(2)}, u32[]{:S(2)}) collective-permute-start(f32[1,2,3,8,128]{4,3,2,1,0:T(8,128)S(1)} %get-tuple-element.37), channel_id=1, source_target_pairs={{0,1},{1,0},{2,3},{3,2},{4,5},{5,4},{6,7},{7,6},{8,9},{9,8},{10,11... | collective-permute-start | bytes 73736 | tf_op jit(solution)/shard_map/ppermute | solution.py:253
  22.9 0.5 %local_0.1.refs_0_ = f32[4,2,3,8,128]{4,3,2,1,0:T(8,128)S(1)} custom-call(f32[4,2,3,8,128]{4,3,2,1,0:T(8,128)S(1)} %get-tuple-element.33.field_ref, f32[864,128]{1,0:T(8,128)S(1)} %bitcast.8), custom_call_target="tpu_custom_call" | custom-call | flops 1622016 | bytes 1622016 | tf_op jit(solution)/shard_map/local_0/pallas_call | solution.py:217
  23.4 2.0 %collective-permute-done.10.refs_3_ = f32[1,2,3,8,128]{4,3,2,1,0:T(8,128)S(1)} collective-permute-done((f32[1,2,3,8,128]{4,3,2,1,0:T(8,128)S(1)}, f32[1,2,3,8,128]{4,3,2,1,0:T(8,128)S(1)}, u32[]{:S(2)}, u32[]{:S(2)}) %collective-permute-start.10) | collective-permute-done | bytes 24608 | tf_op jit(solution)/shard_map/ppermute | solution.py:252
  25.4 0.6 %collective-permute-done.8.refs_1_ = f32[4,2,3,8,128]{4,3,2,1,0:T(8,128)S(1)} collective-permute-done((f32[4,2,3,8,128]{4,3,2,1,0:T(8,128)S(1)}, f32[4,2,3,8,128]{4,3,2,1,0:T(8,128)S(1)}, u32[]{:S(2)}, u32[]{:S(2)}) %collective-permute-start.8) | collective-permute-done | bytes 98336 | tf_op jit(solution)/shard_map/ppermute | solution.py:251
  26.0 0.8 %collective-permute-done.9.refs_2_ = f32[4,2,3,8,128]{4,3,2,1,0:T(8,128)S(1)} collective-permute-done((f32[4,2,3,8,128]{4,3,2,1,0:T(8,128)S(1)}, f32[4,2,3,8,128]{4,3,2,1,0:T(8,128)S(1)}, u32[]{:S(2)}, u32[]{:S(2)}) %collective-permute-start.9) | collective-permute-done | bytes 98336 | tf_op jit(solution)/shard_map/ppermute | solution.py:250
  26.8 0.7 %last.1 = f32[4,2,3,8,128]{4,3,2,1,0:T(8,128)} custom-call(f32[7,8,128]{2,1,0:T(8,128)S(1)} %tapers.1.coefs_ref, f32[864,128]{1,0:T(8,128)S(1)} %bitcast.9, f32[4,2,3,8,128]{4,3,2,1,0:T(8,128)S(1)} %local_0.1.refs_0_, f32[4,2,3,8,128]{4,3,2,1,0:T(8,128)S(1)} %collective-permute-done.8.refs_1_, f32[4,2,3,8,128]{4,3,2,1,0:T(8,128)S(1)} %collective-permute-done.9.refs_2_, ...), custom_call_target="tpu_custom_call" | custom-call | flops 368640 | bytes 368640 | tf_op jit(solution)/shard_map/last/pallas_call | solution.py:217
  (12 shorter events, 0.1 us)
Async XLA Ops:
  0.0 9.8 %copy-start = (f32[4,3,4,2,3,3,128]{6,3,5,4,2,1,0:T(2,128)S(1)}, f32[4,3,4,2,3,3,128]{6,3,5,4,2,1,0:T(2,128)}, u32[]{:S(2)}) copy-start(f32[4,3,4,2,3,3,128]{6,3,5,4,2,1,0:T(2,128)} %param.6) | copy-start | bytes 1327108
  0.0 9.8 %copy-start.1 = (f32[4,2,3,8,128]{4,3,2,1,0:T(8,128)S(1)}, f32[4,2,3,8,128]{4,3,2,1,0:T(8,128)}, u32[]{:S(2)}) copy-start(f32[4,2,3,8,128]{4,3,2,1,0:T(8,128)} %adjoint_hbm.1) | copy-start | bytes 294916
  1.1 9.4 %collective-permute-start = (f32[4,2,3,8,128]{4,3,2,1,0:T(8,128)S(1)}, f32[4,2,3,8,128]{4,3,2,1,0:T(8,128)S(1)}, u32[]{:S(2)}, u32[]{:S(2)}) collective-permute-start(f32[4,2,3,8,128]{4,3,2,1,0:T(8,128)S(1)} %get-tuple-element.23), channel_id=1, source_target_pairs={{0,24},{1,25},{2,26},{3,27},{4,28},{5,29},{6,30},{7,31},{8,16},{9,... | collective-permute-start | bytes 294920 | tf_op jit(solution)/shard_map/ppermute | solution.py:251
  6.2 5.0 %collective-permute-start.1 = (f32[4,2,3,8,128]{4,3,2,1,0:T(8,128)S(1)}, f32[4,2,3,8,128]{4,3,2,1,0:T(8,128)S(1)}, u32[]{:S(2)}, u32[]{:S(2)}) collective-permute-start(f32[4,2,3,8,128]{4,3,2,1,0:T(8,128)S(1)} %get-tuple-element.24), channel_id=1, source_target_pairs={{0,8},{1,9},{2,10},{3,11},{4,12},{5,13},{6,14},{7,15},{8,0},{9,1},... | collective-permute-start | bytes 294920 | tf_op jit(solution)/shard_map/ppermute | solution.py:250
  6.2 4.3 %collective-permute-start.2 = (f32[1,2,3,8,128]{4,3,2,1,0:T(8,128)S(1)}, f32[1,2,3,8,128]{4,3,2,1,0:T(8,128)S(1)}, u32[]{:S(2)}, u32[]{:S(2)}) collective-permute-start(f32[1,2,3,8,128]{4,3,2,1,0:T(8,128)S(1)} %get-tuple-element.25), channel_id=1, source_target_pairs={{0,7},{1,2},{2,1},{3,4},{4,3},{5,6},{6,5},{7,0},{8,15},{9,10},{10,... | collective-permute-start | bytes 73736 | tf_op jit(solution)/shard_map/ppermute | solution.py:252
  7.8 2.7 %collective-permute-start.3 = (f32[1,2,3,8,128]{4,3,2,1,0:T(8,128)S(1)}, f32[1,2,3,8,128]{4,3,2,1,0:T(8,128)S(1)}, u32[]{:S(2)}, u32[]{:S(2)}) collective-permute-start(f32[1,2,3,8,128]{4,3,2,1,0:T(8,128)S(1)} %get-tuple-element.26), channel_id=1, source_target_pairs={{0,1},{1,0},{2,3},{3,2},{4,5},{5,4},{6,7},{7,6},{8,9},{9,8},{10,11... | collective-permute-start | bytes 73736 | tf_op jit(solution)/shard_map/ppermute | solution.py:253
  11.4 7.4 %collective-permute-start.4 = (f32[4,2,3,8,128]{4,3,2,1,0:T(8,128)S(1)}, f32[4,2,3,8,128]{4,3,2,1,0:T(8,128)S(1)}, u32[]{:S(2)}, u32[]{:S(2)}) collective-permute-start(f32[4,2,3,8,128]{4,3,2,1,0:T(8,128)S(1)} %get-tuple-element.28), channel_id=1, source_target_pairs={{0,24},{1,25},{2,26},{3,27},{4,28},{5,29},{6,30},{7,31},{8,16},{9,... | collective-permute-start | bytes 294920 | tf_op jit(solution)/shard_map/ppermute | solution.py:251
  13.9 5.4 %collective-permute-start.5 = (f32[4,2,3,8,128]{4,3,2,1,0:T(8,128)S(1)}, f32[4,2,3,8,128]{4,3,2,1,0:T(8,128)S(1)}, u32[]{:S(2)}, u32[]{:S(2)}) collective-permute-start(f32[4,2,3,8,128]{4,3,2,1,0:T(8,128)S(1)} %get-tuple-element.29), channel_id=1, source_target_pairs={{0,8},{1,9},{2,10},{3,11},{4,12},{5,13},{6,14},{7,15},{8,0},{9,1},... | collective-permute-start | bytes 294920 | tf_op jit(solution)/shard_map/ppermute | solution.py:250
  13.9 4.3 %collective-permute-start.6 = (f32[1,2,3,8,128]{4,3,2,1,0:T(8,128)S(1)}, f32[1,2,3,8,128]{4,3,2,1,0:T(8,128)S(1)}, u32[]{:S(2)}, u32[]{:S(2)}) collective-permute-start(f32[1,2,3,8,128]{4,3,2,1,0:T(8,128)S(1)} %get-tuple-element.30), channel_id=1, source_target_pairs={{0,7},{1,2},{2,1},{3,4},{4,3},{5,6},{6,5},{7,0},{8,15},{9,10},{10,... | collective-permute-start | bytes 73736 | tf_op jit(solution)/shard_map/ppermute | solution.py:252
  13.9 4.3 %collective-permute-start.7 = (f32[1,2,3,8,128]{4,3,2,1,0:T(8,128)S(1)}, f32[1,2,3,8,128]{4,3,2,1,0:T(8,128)S(1)}, u32[]{:S(2)}, u32[]{:S(2)}) collective-permute-start(f32[1,2,3,8,128]{4,3,2,1,0:T(8,128)S(1)} %get-tuple-element.31), channel_id=1, source_target_pairs={{0,1},{1,0},{2,3},{3,2},{4,5},{5,4},{6,7},{7,6},{8,9},{9,8},{10,11... | collective-permute-start | bytes 73736 | tf_op jit(solution)/shard_map/ppermute | solution.py:253
  19.4 6.6 %collective-permute-start.8 = (f32[4,2,3,8,128]{4,3,2,1,0:T(8,128)S(1)}, f32[4,2,3,8,128]{4,3,2,1,0:T(8,128)S(1)}, u32[]{:S(2)}, u32[]{:S(2)}) collective-permute-start(f32[4,2,3,8,128]{4,3,2,1,0:T(8,128)S(1)} %get-tuple-element.34), channel_id=1, source_target_pairs={{0,24},{1,25},{2,26},{3,27},{4,28},{5,29},{6,30},{7,31},{8,16},{9,... | collective-permute-start | bytes 294920 | tf_op jit(solution)/shard_map/ppermute | solution.py:251
  21.2 5.7 %collective-permute-start.9 = (f32[4,2,3,8,128]{4,3,2,1,0:T(8,128)S(1)}, f32[4,2,3,8,128]{4,3,2,1,0:T(8,128)S(1)}, u32[]{:S(2)}, u32[]{:S(2)}) collective-permute-start(f32[4,2,3,8,128]{4,3,2,1,0:T(8,128)S(1)} %get-tuple-element.35), channel_id=1, source_target_pairs={{0,8},{1,9},{2,10},{3,11},{4,12},{5,13},{6,14},{7,15},{8,0},{9,1},... | collective-permute-start | bytes 294920 | tf_op jit(solution)/shard_map/ppermute | solution.py:250
  21.2 4.2 %collective-permute-start.10 = (f32[1,2,3,8,128]{4,3,2,1,0:T(8,128)S(1)}, f32[1,2,3,8,128]{4,3,2,1,0:T(8,128)S(1)}, u32[]{:S(2)}, u32[]{:S(2)}) collective-permute-start(f32[1,2,3,8,128]{4,3,2,1,0:T(8,128)S(1)} %get-tuple-element.36), channel_id=1, source_target_pairs={{0,7},{1,2},{2,1},{3,4},{4,3},{5,6},{6,5},{7,0},{8,15},{9,10},{10,... | collective-permute-start | bytes 73736 | tf_op jit(solution)/shard_map/ppermute | solution.py:252
  21.4 4.0 %collective-permute-start.11 = (f32[1,2,3,8,128]{4,3,2,1,0:T(8,128)S(1)}, f32[1,2,3,8,128]{4,3,2,1,0:T(8,128)S(1)}, u32[]{:S(2)}, u32[]{:S(2)}) collective-permute-start(f32[1,2,3,8,128]{4,3,2,1,0:T(8,128)S(1)} %get-tuple-element.37), channel_id=1, source_target_pairs={{0,1},{1,0},{2,3},{3,2},{4,5},{5,4},{6,7},{7,6},{8,9},{9,8},{10,11... | collective-permute-start | bytes 73736 | tf_op jit(solution)/shard_map/ppermute | solution.py:253

commit v8 on v7

--- a/solution.py
+++ b/solution.py
@@ -153,7 +153,7 @@
 
 
 def arrived_sum(links_ref, link_set, row, rows, arrivals, coefs_ref=None):
-    sum_ref, far_ref, near_ref, outer_ref, inner_ref = arrivals
+    sum_ref, near_ref, far_ref, outer_ref, inner_ref = arrivals
     _, first_pos, odd_plane, odd_block = place(rows)
     far, near = load_field(far_ref, row), load_field(near_ref, row)
     if coefs_ref is not None:
@@ -251,7 +251,7 @@
         far = lax.ppermute(far, "gz", far_pairs)
         outer = lax.ppermute(outer, "gz", outer_pairs)
         inner = lax.ppermute(inner, "gz", inner_pairs)
-        return far, near, outer, inner
+        return near, far, outer, inner
 
     def local(link_set, field):
         return call(functools.partial(local_kernel, rows, link_set), f"local_{link_set}", (field, links), whole, 22)

time: 27.7 us -> 27.5 us (level)
  waiting for transfers between devices: 7.6 us -> 5.92 us
  starting transfers between devices: 14.3 us -> 15.8 us
    ppermute x3, starting transfers between devices: 0.01 us -> 4.45 us  [sent_on(): near = lax.ppermute(near, 'gz', near_pairs)]
    ppermute x3, starting transfers between devices: 9.36 us -> 6.51 us  [sent_on(): far = lax.ppermute(far, 'gz', far_pairs)]
    ppermute x3, waiting for transfers between devices: 1.96 us -> 0.01 us  [sent_on(): near = lax.ppermute(near, 'gz', near_pairs)]
    ppermute x3, starting transfers between devices: 1.81 us -> 1.33 us  [sent_on(): outer = lax.ppermute(outer, 'gz', outer_pairs)]
    ppermute x3, starting transfers between devices: 3.11 us -> 3.49 us  [sent_on(): inner = lax.ppermute(inner, 'gz', inner_pairs)]
  transfers between devices with their start and end apart: 12 -> 12, of which waited for: 8 -> 6; matrix products, arithmetic and copies ran while one was open for 0% -> 0% of each run, Pallas kernels for 6% -> 6%
where the time goes in v8:
time: 27.5 us; the launch traced here: 27.4 us
  starting transfers between devices  15.8 us (57%)
  waiting for transfers between devices  5.92 us (22%)
  Pallas kernels  3.64 us (13%)
  between operations  2.02 us (7%)
    ppermute x3, starting transfers between devices, sent_on(): far = lax.ppermute(far, 'gz', far_pairs)  6.51 us
    ppermute x3, waiting for transfers between devices, sent_on(): outer = lax.ppermute(outer, 'gz', outer_pairs)  4.58 us
    ppermute x3, starting transfers between devices, sent_on(): near = lax.ppermute(near, 'gz', near_pairs)  4.45 us
    pallas_call x8, Pallas kernels, call(): pl.pallas_call(kernel, name=name, out_shape=out_shapes, in_specs=[pl.Bloc...  3.64 us
    ppermute x3, starting transfers between devices, sent_on(): inner = lax.ppermute(inner, 'gz', inner_pairs)  3.49 us
    ppermute x3, starting transfers between devices, sent_on(): outer = lax.ppermute(outer, 'gz', outer_pairs)  1.33 us
    ppermute x3, waiting for transfers between devices, sent_on(): far = lax.ppermute(far, 'gz', far_pairs)  1.33 us
  transfers between devices with their start and end apart: 12, of which 6 were waited for; matrix products, arithmetic and copies ran while one was open for 0% of the time, Pallas kernels for 6%

profile of v8, /device:TPU:0, one launch (start us, length us, event | category | flops | bytes accessed | tf_op | source)
XLA Modules:
  0.0 27.4 jit_solution(15230204210970023193)
XLA Ops:
  0.0 1.1 %begin.1 = (f32[4,2,3,8,128]{4,3,2,1,0:T(8,128)S(1)}, f32[4,2,3,8,128]{4,3,2,1,0:T(8,128)S(1)}, f32[1,2,3,8,128]{4,3,2,1,0:T(8,128)S(1)}, f32[1,2,3,8,128]{4,3,2,1,0:T(8,128)S(1)}) custom-call(f32[4,2,3,8,128]{4,3,2,1,0:T(8,128)} %adjoint_hbm.1, f32[864,128]{1,0:T(8,128)} %bitcast.3), custom_call_target="tpu_custom_call" | custom-call | flops 368640 | bytes 368640 | tf_op jit(solution)/shard_map/begin/pallas_call | solution.py:217
  1.1 3.1 %collective-permute-start = (f32[4,2,3,8,128]{4,3,2,1,0:T(8,128)S(1)}, f32[4,2,3,8,128]{4,3,2,1,0:T(8,128)S(1)}, u32[]{:S(2)}, u32[]{:S(2)}) collective-permute-start(f32[4,2,3,8,128]{4,3,2,1,0:T(8,128)S(1)} %get-tuple-element.23), channel_id=1, source_target_pairs={{0,8},{1,9},{2,10},{3,11},{4,12},{5,13},{6,14},{7,15},{8,0},{9,1},... | collective-permute-start | bytes 294920 | tf_op jit(solution)/shard_map/ppermute | solution.py:250
  4.2 2.5 %collective-permute-start.1 = (f32[4,2,3,8,128]{4,3,2,1,0:T(8,128)S(1)}, f32[4,2,3,8,128]{4,3,2,1,0:T(8,128)S(1)}, u32[]{:S(2)}, u32[]{:S(2)}) collective-permute-start(f32[4,2,3,8,128]{4,3,2,1,0:T(8,128)S(1)} %get-tuple-element.24), channel_id=1, source_target_pairs={{0,24},{1,25},{2,26},{3,27},{4,28},{5,29},{6,30},{7,31},{8,16},{9,... | collective-permute-start | bytes 294920 | tf_op jit(solution)/shard_map/ppermute | solution.py:251
  6.7 1.3 %collective-permute-start.2 = (f32[1,2,3,8,128]{4,3,2,1,0:T(8,128)S(1)}, f32[1,2,3,8,128]{4,3,2,1,0:T(8,128)S(1)}, u32[]{:S(2)}, u32[]{:S(2)}) collective-permute-start(f32[1,2,3,8,128]{4,3,2,1,0:T(8,128)S(1)} %get-tuple-element.25), channel_id=1, source_target_pairs={{0,7},{1,2},{2,1},{3,4},{4,3},{5,6},{6,5},{7,0},{8,15},{9,10},{10,... | collective-permute-start | bytes 73736 | tf_op jit(solution)/shard_map/ppermute | solution.py:252
  8.0 0.3 %collective-permute-start.3 = (f32[1,2,3,8,128]{4,3,2,1,0:T(8,128)S(1)}, f32[1,2,3,8,128]{4,3,2,1,0:T(8,128)S(1)}, u32[]{:S(2)}, u32[]{:S(2)}) collective-permute-start(f32[1,2,3,8,128]{4,3,2,1,0:T(8,128)S(1)} %get-tuple-element.26), channel_id=1, source_target_pairs={{0,1},{1,0},{2,3},{3,2},{4,5},{5,4},{6,7},{7,6},{8,9},{9,8},{10,11... | collective-permute-start | bytes 73736 | tf_op jit(solution)/shard_map/ppermute | solution.py:253
  10.3 0.5 %start.1 = (f32[4,2,3,8,128]{4,3,2,1,0:T(8,128)S(1)}, f32[4,2,3,8,128]{4,3,2,1,0:T(8,128)S(1)}) custom-call(f32[7,8,128]{2,1,0:T(8,128)S(1)} %tapers.1.coefs_ref, f32[4,2,3,8,128]{4,3,2,1,0:T(8,128)S(1)} %copy-done.1, f32[864,128]{1,0:T(8,128)S(1)} %bitcast.4), custom_call_target="tpu_custom_call" | custom-call | flops 1622016 | bytes 1622016 | tf_op jit(solution)/shard_map/start/pallas_call | solution.py:217
  10.8 0.2 collective-permute-done.2.refs_3_
  11.0 0.0 collective-permute-done.3.refs_4_
  11.0 0.4 %collective-permute-done.1.refs_2_ = f32[4,2,3,8,128]{4,3,2,1,0:T(8,128)S(1)} collective-permute-done((f32[4,2,3,8,128]{4,3,2,1,0:T(8,128)S(1)}, f32[4,2,3,8,128]{4,3,2,1,0:T(8,128)S(1)}, u32[]{:S(2)}, u32[]{:S(2)}) %collective-permute-start.1) | collective-permute-done | bytes 98336 | tf_op jit(solution)/shard_map/ppermute | solution.py:251
  11.3 0.2 third.1
  11.5 0.7 %collective-permute-start.4 = (f32[4,2,3,8,128]{4,3,2,1,0:T(8,128)S(1)}, f32[4,2,3,8,128]{4,3,2,1,0:T(8,128)S(1)}, u32[]{:S(2)}, u32[]{:S(2)}) collective-permute-start(f32[4,2,3,8,128]{4,3,2,1,0:T(8,128)S(1)} %get-tuple-element.28), channel_id=1, source_target_pairs={{0,8},{1,9},{2,10},{3,11},{4,12},{5,13},{6,14},{7,15},{8,0},{9,1},... | collective-permute-start | bytes 294920 | tf_op jit(solution)/shard_map/ppermute | solution.py:250
  12.2 2.6 %collective-permute-start.5 = (f32[4,2,3,8,128]{4,3,2,1,0:T(8,128)S(1)}, f32[4,2,3,8,128]{4,3,2,1,0:T(8,128)S(1)}, u32[]{:S(2)}, u32[]{:S(2)}) collective-permute-start(f32[4,2,3,8,128]{4,3,2,1,0:T(8,128)S(1)} %get-tuple-element.29), channel_id=1, source_target_pairs={{0,24},{1,25},{2,26},{3,27},{4,28},{5,29},{6,30},{7,31},{8,16},{9,... | collective-permute-start | bytes 294920 | tf_op jit(solution)/shard_map/ppermute | solution.py:251
  14.8 1.6 %collective-permute-start.7 = (f32[1,2,3,8,128]{4,3,2,1,0:T(8,128)S(1)}, f32[1,2,3,8,128]{4,3,2,1,0:T(8,128)S(1)}, u32[]{:S(2)}, u32[]{:S(2)}) collective-permute-start(f32[1,2,3,8,128]{4,3,2,1,0:T(8,128)S(1)} %get-tuple-element.31), channel_id=1, source_target_pairs={{0,1},{1,0},{2,3},{3,2},{4,5},{5,4},{6,7},{7,6},{8,9},{9,8},{10,11... | collective-permute-start | bytes 73736 | tf_op jit(solution)/shard_map/ppermute | solution.py:253
  16.4 0.5 %local_1.1.refs_0_ = f32[4,2,3,8,128]{4,3,2,1,0:T(8,128)S(1)} custom-call(f32[4,2,3,8,128]{4,3,2,1,0:T(8,128)S(1)} %get-tuple-element.27.field_ref.refs_6_, f32[864,128]{1,0:T(8,128)S(1)} %bitcast.6), custom_call_target="tpu_custom_call" | custom-call | flops 1622016 | bytes 1622016 | tf_op jit(solution)/shard_map/local_1/pallas_call | solution.py:217
  16.9 2.2 %collective-permute-done.6.refs_3_ = f32[1,2,3,8,128]{4,3,2,1,0:T(8,128)S(1)} collective-permute-done((f32[1,2,3,8,128]{4,3,2,1,0:T(8,128)S(1)}, f32[1,2,3,8,128]{4,3,2,1,0:T(8,128)S(1)}, u32[]{:S(2)}, u32[]{:S(2)}) %collective-permute-start.6) | collective-permute-done | bytes 24608 | tf_op jit(solution)/shard_map/ppermute | solution.py:252
  19.1 0.2 collective-permute-done.5.refs_2_
  19.3 0.2 second.1
  19.4 0.7 %collective-permute-start.8 = (f32[4,2,3,8,128]{4,3,2,1,0:T(8,128)S(1)}, f32[4,2,3,8,128]{4,3,2,1,0:T(8,128)S(1)}, u32[]{:S(2)}, u32[]{:S(2)}) collective-permute-start(f32[4,2,3,8,128]{4,3,2,1,0:T(8,128)S(1)} %get-tuple-element.34), channel_id=1, source_target_pairs={{0,8},{1,9},{2,10},{3,11},{4,12},{5,13},{6,14},{7,15},{8,0},{9,1},... | collective-permute-start | bytes 294920 | tf_op jit(solution)/shard_map/ppermute | solution.py:250
  20.1 1.4 %collective-permute-start.9 = (f32[4,2,3,8,128]{4,3,2,1,0:T(8,128)S(1)}, f32[4,2,3,8,128]{4,3,2,1,0:T(8,128)S(1)}, u32[]{:S(2)}, u32[]{:S(2)}) collective-permute-start(f32[4,2,3,8,128]{4,3,2,1,0:T(8,128)S(1)} %get-tuple-element.35), channel_id=1, source_target_pairs={{0,24},{1,25},{2,26},{3,27},{4,28},{5,29},{6,30},{7,31},{8,16},{9,... | collective-permute-start | bytes 294920 | tf_op jit(solution)/shard_map/ppermute | solution.py:251
  21.5 1.6 %collective-permute-start.11 = (f32[1,2,3,8,128]{4,3,2,1,0:T(8,128)S(1)}, f32[1,2,3,8,128]{4,3,2,1,0:T(8,128)S(1)}, u32[]{:S(2)}, u32[]{:S(2)}) collective-permute-start(f32[1,2,3,8,128]{4,3,2,1,0:T(8,128)S(1)} %get-tuple-element.37), channel_id=1, source_target_pairs={{0,1},{1,0},{2,3},{3,2},{4,5},{5,4},{6,7},{7,6},{8,9},{9,8},{10,11... | collective-permute-start | bytes 73736 | tf_op jit(solution)/shard_map/ppermute | solution.py:253
  23.1 0.5 %local_0.1.refs_0_ = f32[4,2,3,8,128]{4,3,2,1,0:T(8,128)S(1)} custom-call(f32[4,2,3,8,128]{4,3,2,1,0:T(8,128)S(1)} %get-tuple-element.33.field_ref, f32[864,128]{1,0:T(8,128)S(1)} %bitcast.8), custom_call_target="tpu_custom_call" | custom-call | flops 1622016 | bytes 1622016 | tf_op jit(solution)/shard_map/local_0/pallas_call | solution.py:217
  23.6 2.2 %collective-permute-done.10.refs_3_ = f32[1,2,3,8,128]{4,3,2,1,0:T(8,128)S(1)} collective-permute-done((f32[1,2,3,8,128]{4,3,2,1,0:T(8,128)S(1)}, f32[1,2,3,8,128]{4,3,2,1,0:T(8,128)S(1)}, u32[]{:S(2)}, u32[]{:S(2)}) %collective-permute-start.10) | collective-permute-done | bytes 24608 | tf_op jit(solution)/shard_map/ppermute | solution.py:252
  25.8 0.8 %collective-permute-done.9.refs_2_ = f32[4,2,3,8,128]{4,3,2,1,0:T(8,128)S(1)} collective-permute-done((f32[4,2,3,8,128]{4,3,2,1,0:T(8,128)S(1)}, f32[4,2,3,8,128]{4,3,2,1,0:T(8,128)S(1)}, u32[]{:S(2)}, u32[]{:S(2)}) %collective-permute-start.9) | collective-permute-done | bytes 98336 | tf_op jit(solution)/shard_map/ppermute | solution.py:251
  26.6 0.7 %last.1 = f32[4,2,3,8,128]{4,3,2,1,0:T(8,128)} custom-call(f32[7,8,128]{2,1,0:T(8,128)S(1)} %tapers.1.coefs_ref, f32[864,128]{1,0:T(8,128)S(1)} %bitcast.9, f32[4,2,3,8,128]{4,3,2,1,0:T(8,128)S(1)} %local_0.1.refs_0_, f32[4,2,3,8,128]{4,3,2,1,0:T(8,128)S(1)} %collective-permute-done.8.refs_1_, f32[4,2,3,8,128]{4,3,2,1,0:T(8,128)S(1)} %collective-permute-done.9.refs_2_, ...), custom_call_target="tpu_custom_call" | custom-call | flops 368640 | bytes 368640 | tf_op jit(solution)/shard_map/last/pallas_call | solution.py:217
  (12 shorter events, 0.1 us)
Async XLA Ops:
  0.0 10.2 %copy-start = (f32[4,3,4,2,3,3,128]{6,3,5,4,2,1,0:T(2,128)S(1)}, f32[4,3,4,2,3,3,128]{6,3,5,4,2,1,0:T(2,128)}, u32[]{:S(2)}) copy-start(f32[4,3,4,2,3,3,128]{6,3,5,4,2,1,0:T(2,128)} %param.6) | copy-start | bytes 1327108
  0.0 10.2 %copy-start.1 = (f32[4,2,3,8,128]{4,3,2,1,0:T(8,128)S(1)}, f32[4,2,3,8,128]{4,3,2,1,0:T(8,128)}, u32[]{:S(2)}) copy-start(f32[4,2,3,8,128]{4,3,2,1,0:T(8,128)} %adjoint_hbm.1) | copy-start | bytes 294916
  1.1 9.9 %collective-permute-start = (f32[4,2,3,8,128]{4,3,2,1,0:T(8,128)S(1)}, f32[4,2,3,8,128]{4,3,2,1,0:T(8,128)S(1)}, u32[]{:S(2)}, u32[]{:S(2)}) collective-permute-start(f32[4,2,3,8,128]{4,3,2,1,0:T(8,128)S(1)} %get-tuple-element.23), channel_id=1, source_target_pairs={{0,8},{1,9},{2,10},{3,11},{4,12},{5,13},{6,14},{7,15},{8,0},{9,1},... | collective-permute-start | bytes 294920 | tf_op jit(solution)/shard_map/ppermute | solution.py:250
  4.2 7.2 %collective-permute-start.1 = (f32[4,2,3,8,128]{4,3,2,1,0:T(8,128)S(1)}, f32[4,2,3,8,128]{4,3,2,1,0:T(8,128)S(1)}, u32[]{:S(2)}, u32[]{:S(2)}) collective-permute-start(f32[4,2,3,8,128]{4,3,2,1,0:T(8,128)S(1)} %get-tuple-element.24), channel_id=1, source_target_pairs={{0,24},{1,25},{2,26},{3,27},{4,28},{5,29},{6,30},{7,31},{8,16},{9,... | collective-permute-start | bytes 294920 | tf_op jit(solution)/shard_map/ppermute | solution.py:251
  6.7 4.3 %collective-permute-start.2 = (f32[1,2,3,8,128]{4,3,2,1,0:T(8,128)S(1)}, f32[1,2,3,8,128]{4,3,2,1,0:T(8,128)S(1)}, u32[]{:S(2)}, u32[]{:S(2)}) collective-permute-start(f32[1,2,3,8,128]{4,3,2,1,0:T(8,128)S(1)} %get-tuple-element.25), channel_id=1, source_target_pairs={{0,7},{1,2},{2,1},{3,4},{4,3},{5,6},{6,5},{7,0},{8,15},{9,10},{10,... | collective-permute-start | bytes 73736 | tf_op jit(solution)/shard_map/ppermute | solution.py:252
  8.0 3.0 %collective-permute-start.3 = (f32[1,2,3,8,128]{4,3,2,1,0:T(8,128)S(1)}, f32[1,2,3,8,128]{4,3,2,1,0:T(8,128)S(1)}, u32[]{:S(2)}, u32[]{:S(2)}) collective-permute-start(f32[1,2,3,8,128]{4,3,2,1,0:T(8,128)S(1)} %get-tuple-element.26), channel_id=1, source_target_pairs={{0,1},{1,0},{2,3},{3,2},{4,5},{5,4},{6,7},{7,6},{8,9},{9,8},{10,11... | collective-permute-start | bytes 73736 | tf_op jit(solution)/shard_map/ppermute | solution.py:253
  11.5 7.6 %collective-permute-start.4 = (f32[4,2,3,8,128]{4,3,2,1,0:T(8,128)S(1)}, f32[4,2,3,8,128]{4,3,2,1,0:T(8,128)S(1)}, u32[]{:S(2)}, u32[]{:S(2)}) collective-permute-start(f32[4,2,3,8,128]{4,3,2,1,0:T(8,128)S(1)} %get-tuple-element.28), channel_id=1, source_target_pairs={{0,8},{1,9},{2,10},{3,11},{4,12},{5,13},{6,14},{7,15},{8,0},{9,1},... | collective-permute-start | bytes 294920 | tf_op jit(solution)/shard_map/ppermute | solution.py:250
  12.2 7.1 %collective-permute-start.5 = (f32[4,2,3,8,128]{4,3,2,1,0:T(8,128)S(1)}, f32[4,2,3,8,128]{4,3,2,1,0:T(8,128)S(1)}, u32[]{:S(2)}, u32[]{:S(2)}) collective-permute-start(f32[4,2,3,8,128]{4,3,2,1,0:T(8,128)S(1)} %get-tuple-element.29), channel_id=1, source_target_pairs={{0,24},{1,25},{2,26},{3,27},{4,28},{5,29},{6,30},{7,31},{8,16},{9,... | collective-permute-start | bytes 294920 | tf_op jit(solution)/shard_map/ppermute | solution.py:251
  14.8 4.3 %collective-permute-start.6 = (f32[1,2,3,8,128]{4,3,2,1,0:T(8,128)S(1)}, f32[1,2,3,8,128]{4,3,2,1,0:T(8,128)S(1)}, u32[]{:S(2)}, u32[]{:S(2)}) collective-permute-start(f32[1,2,3,8,128]{4,3,2,1,0:T(8,128)S(1)} %get-tuple-element.30), channel_id=1, source_target_pairs={{0,7},{1,2},{2,1},{3,4},{4,3},{5,6},{6,5},{7,0},{8,15},{9,10},{10,... | collective-permute-start | bytes 73736 | tf_op jit(solution)/shard_map/ppermute | solution.py:252
  14.8 4.3 %collective-permute-start.7 = (f32[1,2,3,8,128]{4,3,2,1,0:T(8,128)S(1)}, f32[1,2,3,8,128]{4,3,2,1,0:T(8,128)S(1)}, u32[]{:S(2)}, u32[]{:S(2)}) collective-permute-start(f32[1,2,3,8,128]{4,3,2,1,0:T(8,128)S(1)} %get-tuple-element.31), channel_id=1, source_target_pairs={{0,1},{1,0},{2,3},{3,2},{4,5},{5,4},{6,7},{7,6},{8,9},{9,8},{10,11... | collective-permute-start | bytes 73736 | tf_op jit(solution)/shard_map/ppermute | solution.py:253
  19.4 6.4 %collective-permute-start.8 = (f32[4,2,3,8,128]{4,3,2,1,0:T(8,128)S(1)}, f32[4,2,3,8,128]{4,3,2,1,0:T(8,128)S(1)}, u32[]{:S(2)}, u32[]{:S(2)}) collective-permute-start(f32[4,2,3,8,128]{4,3,2,1,0:T(8,128)S(1)} %get-tuple-element.34), channel_id=1, source_target_pairs={{0,8},{1,9},{2,10},{3,11},{4,12},{5,13},{6,14},{7,15},{8,0},{9,1},... | collective-permute-start | bytes 294920 | tf_op jit(solution)/shard_map/ppermute | solution.py:250
  20.1 6.5 %collective-permute-start.9 = (f32[4,2,3,8,128]{4,3,2,1,0:T(8,128)S(1)}, f32[4,2,3,8,128]{4,3,2,1,0:T(8,128)S(1)}, u32[]{:S(2)}, u32[]{:S(2)}) collective-permute-start(f32[4,2,3,8,128]{4,3,2,1,0:T(8,128)S(1)} %get-tuple-element.35), channel_id=1, source_target_pairs={{0,24},{1,25},{2,26},{3,27},{4,28},{5,29},{6,30},{7,31},{8,16},{9,... | collective-permute-start | bytes 294920 | tf_op jit(solution)/shard_map/ppermute | solution.py:251
  21.5 4.3 %collective-permute-start.10 = (f32[1,2,3,8,128]{4,3,2,1,0:T(8,128)S(1)}, f32[1,2,3,8,128]{4,3,2,1,0:T(8,128)S(1)}, u32[]{:S(2)}, u32[]{:S(2)}) collective-permute-start(f32[1,2,3,8,128]{4,3,2,1,0:T(8,128)S(1)} %get-tuple-element.36), channel_id=1, source_target_pairs={{0,7},{1,2},{2,1},{3,4},{4,3},{5,6},{6,5},{7,0},{8,15},{9,10},{10,... | collective-permute-start | bytes 73736 | tf_op jit(solution)/shard_map/ppermute | solution.py:252
  21.5 4.3 %collective-permute-start.11 = (f32[1,2,3,8,128]{4,3,2,1,0:T(8,128)S(1)}, f32[1,2,3,8,128]{4,3,2,1,0:T(8,128)S(1)}, u32[]{:S(2)}, u32[]{:S(2)}) collective-permute-start(f32[1,2,3,8,128]{4,3,2,1,0:T(8,128)S(1)} %get-tuple-element.37), channel_id=1, source_target_pairs={{0,1},{1,0},{2,3},{3,2},{4,5},{5,4},{6,7},{7,6},{8,9},{9,8},{10,11... | collective-permute-start | bytes 73736 | tf_op jit(solution)/shard_map/ppermute | solution.py:253

commit v9 on v8

--- a/solution.py
+++ b/solution.py
@@ -65,11 +65,12 @@
 def place(rows):
     first = lax.axis_index("gz") * rows
     plane, first_pos = first // BAND, lax.rem(first, BAND)
-    return plane, first_pos, lax.rem(plane, 2) == 1, lax.rem(first_pos // rows, 2) == 1
+    block = first_pos // rows
+    return first_pos, lax.rem(plane + block, 2) == 1, lax.rem(block, 2) == 1
 
 
 def taper_kernel(rows, source_ref, width_ref, steps_ref, coefs_ref):
-    _, first_pos, _, _ = place(rows)
+    first_pos, _, _ = place(rows)
     ones = jnp.ones((8, 128), jnp.float32)
     per_width = ones * width_ref[0].astype(jnp.float32)
     for i in range(rows + 2):
@@ -78,15 +79,15 @@
     coefs_ref[rows + 2] = 0.25 / (ones * steps_ref[0].astype(jnp.float32))
 
 
-def store_z(rows, matrices, row, field, far_ref, near_ref):
-    _, _, odd_plane, _ = place(rows)
+def store_z(rows, matrices, row, field, one_ref, two_ref):
+    _, above_first, _ = place(rows)
     _, up = transport(matrices, None, field)
-    store_field(far_ref, row, combine(lambda v, h: jnp.where(odd_plane, h, v), field, up))
-    store_field(near_ref, row, combine(lambda v, h: jnp.where(odd_plane, v, h), field, up))
+    store_field(one_ref, row, combine(lambda v, h: jnp.where(above_first, h, v), field, up))
+    store_field(two_ref, row, combine(lambda v, h: jnp.where(above_first, v, h), field, up))
 
 
 def store_t(rows, matrices, field_ref, outer_ref, inner_ref):
-    _, _, _, odd_block = place(rows)
+    _, _, odd_block = place(rows)
     first = load_field(field_ref, 0)
     _, last = transport(matrices, None, load_field(field_ref, rows - 1))
     store_field(outer_ref, 0, combine(lambda p, q: jnp.where(odd_block, q, p), first, last))
@@ -94,7 +95,7 @@
 
 
 def begin_kernel(
-    rows, adjoint_hbm, links_hbm, far_ref, near_ref, outer_ref, inner_ref, adjoint_ref, links_ref, sems
+    rows, adjoint_hbm, links_hbm, one_ref, two_ref, outer_ref, inner_ref, adjoint_ref, links_ref, sems
 ):
     row_entries = SETS * MUS * ENTRIES
     z_first = (2 * MUS + 2) * ENTRIES
@@ -109,7 +110,7 @@
         copy.wait()
     for row in range(rows):
         matrices = links_ref.at[row], z_first - aligned
-        store_z(rows, matrices, row, load_field(adjoint_ref, row), far_ref, near_ref)
+        store_z(rows, matrices, row, load_field(adjoint_ref, row), one_ref, two_ref)
     store_t(rows, (links_ref.at[rows - 1], z_first + ENTRIES - aligned), adjoint_ref, outer_ref, inner_ref)
 
 
@@ -153,15 +154,15 @@
 
 
 def arrived_sum(links_ref, link_set, row, rows, arrivals, coefs_ref=None):
-    sum_ref, near_ref, far_ref, outer_ref, inner_ref = arrivals
-    _, first_pos, odd_plane, odd_block = place(rows)
-    far, near = load_field(far_ref, row), load_field(near_ref, row)
+    sum_ref, one_ref, two_ref, outer_ref, inner_ref = arrivals
+    first_pos, above_first, odd_block = place(rows)
+    one, two = load_field(one_ref, row), load_field(two_ref, row)
     if coefs_ref is not None:
-        far, near = (combine(lambda v: coefs_ref[row + 1] * v, f) for f in (far, near))
-    above = combine(lambda p, q: jnp.where(odd_plane, p, q), far, near)
+        one, two = (combine(lambda v: coefs_ref[row + 1] * v, f) for f in (one, two))
+    above = combine(lambda p, q: jnp.where(above_first, p, q), one, two)
     ahead_z, _ = transport(links_at(links_ref, row, link_set, 2), above, None)
     total = combine(
-        lambda s, f, p, q: s + f + jnp.where(odd_plane, q, p), load_field(sum_ref, row), ahead_z, far, near
+        lambda s, f, p, q: s + f + jnp.where(above_first, q, p), load_field(sum_ref, row), ahead_z, one, two
     )
     outer, inner = load_field(outer_ref, 0), load_field(inner_ref, 0)
     if row == 0:
@@ -180,18 +181,18 @@
 
 
 def third_kernel(rows, coefs_ref, links_ref, *refs):
-    arrivals, (third_ref, far_ref, near_ref, outer_ref, inner_ref) = refs[:5], refs[5:]
+    arrivals, (third_ref, one_ref, two_ref, outer_ref, inner_ref) = refs[:5], refs[5:]
     for row in range(rows):
         inside, eps = coefs_ref[row + 1], coefs_ref[rows + 2]
         total = arrived_sum(links_ref, 2, row, rows, arrivals, coefs_ref)
         third = combine(lambda s: 0.75 * (inside * (eps * s)), total)
         store_field(third_ref, row, third)
-        store_z(rows, links_at(links_ref, row, 1, 2), row, third, far_ref, near_ref)
+        store_z(rows, links_at(links_ref, row, 1, 2), row, third, one_ref, two_ref)
     store_t(rows, links_at(links_ref, rows - 1, 1, 3), third_ref, outer_ref, inner_ref)
 
 
 def second_kernel(rows, coefs_ref, links_ref, *refs):
-    arrivals, (start_ref, third_ref, mixed_ref, far_ref, near_ref, outer_ref, inner_ref, base_ref) = refs[:5], refs[5:]
+    arrivals, (start_ref, third_ref, mixed_ref, one_ref, two_ref, outer_ref, inner_ref, base_ref) = refs[:5], refs[5:]
     for row in range(rows):
         inside, eps = coefs_ref[row + 1], coefs_ref[rows + 2]
         total = arrived_sum(links_ref, 1, row, rows, arrivals)
@@ -200,7 +201,7 @@
         mixed = combine(lambda p, q: 0.25 * p - (2.0 / 9.0) * q, second, third)
         store_field(mixed_ref, row, mixed)
         store_field(base_ref, row, combine(lambda p, q: p + q, second, third))
-        store_z(rows, links_at(links_ref, row, 0, 2), row, mixed, far_ref, near_ref)
+        store_z(rows, links_at(links_ref, row, 0, 2), row, mixed, one_ref, two_ref)
     store_t(rows, links_at(links_ref, rows - 1, 0, 3), mixed_ref, outer_ref, inner_ref)
 
 
@@ -241,17 +242,17 @@
     def in_line(i, by):
         return (i + by * per_plane) % count
 
-    far_pairs = [(i, in_line(i, 1 if i // per_plane % 2 else -1)) for i in range(count)]
-    near_pairs = [(i, in_line(i, -1 if i // per_plane % 2 else 1)) for i in range(count)]
+    one_pairs = [(i, in_line(i, 1 if (i // per_plane + i) % 2 else -1)) for i in range(count)]
+    two_pairs = [(i, in_line(i, -1 if (i // per_plane + i) % 2 else 1)) for i in range(count)]
     outer_pairs = [(i, in_plane(i, 1 if i % 2 else -1)) for i in range(count)]
     inner_pairs = [(i, in_plane(i, -1 if i % 2 else 1)) for i in range(count)]
 
-    def sent_on(far, near, outer, inner):
-        near = lax.ppermute(near, "gz", near_pairs)
-        far = lax.ppermute(far, "gz", far_pairs)
+    def sent_on(one, two, outer, inner):
+        one = lax.ppermute(one, "gz", one_pairs)
+        two = lax.ppermute(two, "gz", two_pairs)
         outer = lax.ppermute(outer, "gz", outer_pairs)
         inner = lax.ppermute(inner, "gz", inner_pairs)
-        return near, far, outer, inner
+        return one, two, outer, inner
 
     def local(link_set, field):
         return call(functools.partial(local_kernel, rows, link_set), f"local_{link_set}", (field, links), whole, 22)

time: 27.5 us -> 28.6 us (1.040)
  waiting for transfers between devices: 5.92 us -> 7.55 us
  starting transfers between devices: 15.8 us -> 15.2 us
    ppermute x3, starting transfers between devices: 1.33 us -> 5.23 us  [sent_on(): outer = lax.ppermute(outer, 'gz', outer_pairs)]
    ppermute x6, waiting for transfers between devices: 1.33 us -> 4.45 us  [the longest x3 2.61 us: sent_on(): two = lax.ppermute(two, 'gz', two_pairs)]
    ppermute x3, starting transfers between devices: 3.49 us -> 0.78 us  [sent_on(): inner = lax.ppermute(inner, 'gz', inner_pairs)]
    ppermute x6, starting transfers between devices: 11 us -> 9.21 us  [the longest x3 8.84 us: sent_on(): one = lax.ppermute(one, 'gz', one_pairs)]
    ppermute x3, waiting for transfers between devices: 4.58 us -> 3.1 us  [sent_on(): outer = lax.ppermute(outer, 'gz', outer_pairs)]
  transfers between devices with their start and end apart: 12 -> 12, of which waited for: 6 -> 7; matrix products, arithmetic and copies ran while one was open for 0% -> 0% of each run, Pallas kernels for 6% -> 5%
where the time goes in v9:
time: 28.6 us; the launch traced here: 28.5 us
  starting transfers between devices  15.2 us (53%)
  waiting for transfers between devices  7.55 us (26%)
  Pallas kernels  3.65 us (13%)
  between operations  2.03 us (7%)
    ppermute x3, starting transfers between devices, sent_on(): one = lax.ppermute(one, 'gz', one_pairs)  8.84 us
    ppermute x3, starting transfers between devices, sent_on(): outer = lax.ppermute(outer, 'gz', outer_pairs)  5.23 us
    pallas_call x8, Pallas kernels, call(): pl.pallas_call(kernel, name=name, out_shape=out_shapes, in_specs=[pl.Bloc...  3.65 us
    ppermute x3, waiting for transfers between devices, sent_on(): outer = lax.ppermute(outer, 'gz', outer_pairs)  3.1 us
    ppermute x3, waiting for transfers between devices, sent_on(): two = lax.ppermute(two, 'gz', two_pairs)  2.61 us
    ppermute x3, waiting for transfers between devices, sent_on(): one = lax.ppermute(one, 'gz', one_pairs)  1.84 us
    ppermute x3, starting transfers between devices, sent_on(): inner = lax.ppermute(inner, 'gz', inner_pairs)  0.78 us
  transfers between devices with their start and end apart: 12, of which 7 were waited for; matrix products, arithmetic and copies ran while one was open for 0% of the time, Pallas kernels for 5%

profile of v9, /device:TPU:0, one launch (start us, length us, event | category | flops | bytes accessed | tf_op | source)
XLA Modules:
  0.0 28.5 jit_solution(4644065561993316368)
XLA Ops:
  0.0 1.1 %begin.1 = (f32[4,2,3,8,128]{4,3,2,1,0:T(8,128)S(1)}, f32[4,2,3,8,128]{4,3,2,1,0:T(8,128)S(1)}, f32[1,2,3,8,128]{4,3,2,1,0:T(8,128)S(1)}, f32[1,2,3,8,128]{4,3,2,1,0:T(8,128)S(1)}) custom-call(f32[4,2,3,8,128]{4,3,2,1,0:T(8,128)} %adjoint_hbm.1, f32[864,128]{1,0:T(8,128)} %bitcast.3), custom_call_target="tpu_custom_call" | custom-call | flops 368640 | bytes 368640 | tf_op jit(solution)/shard_map/begin/pallas_call | solution.py:218
  1.1 5.1 %collective-permute-start = (f32[4,2,3,8,128]{4,3,2,1,0:T(8,128)S(1)}, f32[4,2,3,8,128]{4,3,2,1,0:T(8,128)S(1)}, u32[]{:S(2)}, u32[]{:S(2)}) collective-permute-start(f32[4,2,3,8,128]{4,3,2,1,0:T(8,128)S(1)} %get-tuple-element.23), channel_id=1, source_target_pairs={{0,24},{1,9},{2,26},{3,11},{4,28},{5,13},{6,30},{7,15},{8,16},{9,1... | collective-permute-start | bytes 294920 | tf_op jit(solution)/shard_map/ppermute | solution.py:251
  6.2 0.0 collective-permute-start.1
  6.2 1.8 %collective-permute-start.2 = (f32[1,2,3,8,128]{4,3,2,1,0:T(8,128)S(1)}, f32[1,2,3,8,128]{4,3,2,1,0:T(8,128)S(1)}, u32[]{:S(2)}, u32[]{:S(2)}) collective-permute-start(f32[1,2,3,8,128]{4,3,2,1,0:T(8,128)S(1)} %get-tuple-element.25), channel_id=1, source_target_pairs={{0,7},{1,2},{2,1},{3,4},{4,3},{5,6},{6,5},{7,0},{8,15},{9,10},{10,... | collective-permute-start | bytes 73736 | tf_op jit(solution)/shard_map/ppermute | solution.py:253
  10.0 0.5 %start.1 = (f32[4,2,3,8,128]{4,3,2,1,0:T(8,128)S(1)}, f32[4,2,3,8,128]{4,3,2,1,0:T(8,128)S(1)}) custom-call(f32[7,8,128]{2,1,0:T(8,128)S(1)} %tapers.1.coefs_ref, f32[4,2,3,8,128]{4,3,2,1,0:T(8,128)S(1)} %copy-done.1, f32[864,128]{1,0:T(8,128)S(1)} %bitcast.4), custom_call_target="tpu_custom_call" | custom-call | flops 1622016 | bytes 1622016 | tf_op jit(solution)/shard_map/start/pallas_call | solution.py:218
  10.5 0.0 collective-permute-done.2.refs_3_
  10.5 0.8 %collective-permute-done.1.refs_2_ = f32[4,2,3,8,128]{4,3,2,1,0:T(8,128)S(1)} collective-permute-done((f32[4,2,3,8,128]{4,3,2,1,0:T(8,128)S(1)}, f32[4,2,3,8,128]{4,3,2,1,0:T(8,128)S(1)}, u32[]{:S(2)}, u32[]{:S(2)}) %collective-permute-start.1) | collective-permute-done | bytes 98336 | tf_op jit(solution)/shard_map/ppermute | solution.py:252
  11.3 0.2 third.1
  11.5 1.8 %collective-permute-start.4 = (f32[4,2,3,8,128]{4,3,2,1,0:T(8,128)S(1)}, f32[4,2,3,8,128]{4,3,2,1,0:T(8,128)S(1)}, u32[]{:S(2)}, u32[]{:S(2)}) collective-permute-start(f32[4,2,3,8,128]{4,3,2,1,0:T(8,128)S(1)} %get-tuple-element.28), channel_id=1, source_target_pairs={{0,24},{1,9},{2,26},{3,11},{4,28},{5,13},{6,30},{7,15},{8,16},{9,1... | collective-permute-start | bytes 294920 | tf_op jit(solution)/shard_map/ppermute | solution.py:251
  13.2 0.4 %collective-permute-start.5 = (f32[4,2,3,8,128]{4,3,2,1,0:T(8,128)S(1)}, f32[4,2,3,8,128]{4,3,2,1,0:T(8,128)S(1)}, u32[]{:S(2)}, u32[]{:S(2)}) collective-permute-start(f32[4,2,3,8,128]{4,3,2,1,0:T(8,128)S(1)} %get-tuple-element.29), channel_id=1, source_target_pairs={{0,8},{1,25},{2,10},{3,27},{4,12},{5,29},{6,14},{7,31},{8,0},{9,17... | collective-permute-start | bytes 294920 | tf_op jit(solution)/shard_map/ppermute | solution.py:252
  13.6 2.5 %collective-permute-start.6 = (f32[1,2,3,8,128]{4,3,2,1,0:T(8,128)S(1)}, f32[1,2,3,8,128]{4,3,2,1,0:T(8,128)S(1)}, u32[]{:S(2)}, u32[]{:S(2)}) collective-permute-start(f32[1,2,3,8,128]{4,3,2,1,0:T(8,128)S(1)} %get-tuple-element.30), channel_id=1, source_target_pairs={{0,7},{1,2},{2,1},{3,4},{4,3},{5,6},{6,5},{7,0},{8,15},{9,10},{10,... | collective-permute-start | bytes 73736 | tf_op jit(solution)/shard_map/ppermute | solution.py:253
  16.1 0.5 %local_1.1.refs_0_ = f32[4,2,3,8,128]{4,3,2,1,0:T(8,128)S(1)} custom-call(f32[4,2,3,8,128]{4,3,2,1,0:T(8,128)S(1)} %get-tuple-element.27.field_ref.refs_6_, f32[864,128]{1,0:T(8,128)S(1)} %bitcast.6), custom_call_target="tpu_custom_call" | custom-call | flops 1622016 | bytes 1622016 | tf_op jit(solution)/shard_map/local_1/pallas_call | solution.py:218
  16.6 1.1 %collective-permute-done.6.refs_3_ = f32[1,2,3,8,128]{4,3,2,1,0:T(8,128)S(1)} collective-permute-done((f32[1,2,3,8,128]{4,3,2,1,0:T(8,128)S(1)}, f32[1,2,3,8,128]{4,3,2,1,0:T(8,128)S(1)}, u32[]{:S(2)}, u32[]{:S(2)}) %collective-permute-start.6) | collective-permute-done | bytes 24608 | tf_op jit(solution)/shard_map/ppermute | solution.py:253
  17.7 1.3 %collective-permute-done.4.refs_1_ = f32[4,2,3,8,128]{4,3,2,1,0:T(8,128)S(1)} collective-permute-done((f32[4,2,3,8,128]{4,3,2,1,0:T(8,128)S(1)}, f32[4,2,3,8,128]{4,3,2,1,0:T(8,128)S(1)}, u32[]{:S(2)}, u32[]{:S(2)}) %collective-permute-start.4) | collective-permute-done | bytes 98336 | tf_op jit(solution)/shard_map/ppermute | solution.py:251
  19.1 0.9 %collective-permute-done.5.refs_2_ = f32[4,2,3,8,128]{4,3,2,1,0:T(8,128)S(1)} collective-permute-done((f32[4,2,3,8,128]{4,3,2,1,0:T(8,128)S(1)}, f32[4,2,3,8,128]{4,3,2,1,0:T(8,128)S(1)}, u32[]{:S(2)}, u32[]{:S(2)}) %collective-permute-start.5) | collective-permute-done | bytes 98336 | tf_op jit(solution)/shard_map/ppermute | solution.py:252
  19.9 0.2 second.1
  20.1 2.0 %collective-permute-start.8 = (f32[4,2,3,8,128]{4,3,2,1,0:T(8,128)S(1)}, f32[4,2,3,8,128]{4,3,2,1,0:T(8,128)S(1)}, u32[]{:S(2)}, u32[]{:S(2)}) collective-permute-start(f32[4,2,3,8,128]{4,3,2,1,0:T(8,128)S(1)} %get-tuple-element.34), channel_id=1, source_target_pairs={{0,24},{1,9},{2,26},{3,11},{4,28},{5,13},{6,30},{7,15},{8,16},{9,1... | collective-permute-start | bytes 294920 | tf_op jit(solution)/shard_map/ppermute | solution.py:251
  22.1 1.0 %collective-permute-start.10 = (f32[1,2,3,8,128]{4,3,2,1,0:T(8,128)S(1)}, f32[1,2,3,8,128]{4,3,2,1,0:T(8,128)S(1)}, u32[]{:S(2)}, u32[]{:S(2)}) collective-permute-start(f32[1,2,3,8,128]{4,3,2,1,0:T(8,128)S(1)} %get-tuple-element.36), channel_id=1, source_target_pairs={{0,7},{1,2},{2,1},{3,4},{4,3},{5,6},{6,5},{7,0},{8,15},{9,10},{10,... | collective-permute-start | bytes 73736 | tf_op jit(solution)/shard_map/ppermute | solution.py:253
  23.0 0.8 %collective-permute-start.11 = (f32[1,2,3,8,128]{4,3,2,1,0:T(8,128)S(1)}, f32[1,2,3,8,128]{4,3,2,1,0:T(8,128)S(1)}, u32[]{:S(2)}, u32[]{:S(2)}) collective-permute-start(f32[1,2,3,8,128]{4,3,2,1,0:T(8,128)S(1)} %get-tuple-element.37), channel_id=1, source_target_pairs={{0,1},{1,0},{2,3},{3,2},{4,5},{5,4},{6,7},{7,6},{8,9},{9,8},{10,11... | collective-permute-start | bytes 73736 | tf_op jit(solution)/shard_map/ppermute | solution.py:254
  23.8 0.5 %local_0.1.refs_0_ = f32[4,2,3,8,128]{4,3,2,1,0:T(8,128)S(1)} custom-call(f32[4,2,3,8,128]{4,3,2,1,0:T(8,128)S(1)} %get-tuple-element.33.field_ref, f32[864,128]{1,0:T(8,128)S(1)} %bitcast.8), custom_call_target="tpu_custom_call" | custom-call | flops 1622016 | bytes 1622016 | tf_op jit(solution)/shard_map/local_0/pallas_call | solution.py:218
  24.3 1.9 %collective-permute-done.10.refs_3_ = f32[1,2,3,8,128]{4,3,2,1,0:T(8,128)S(1)} collective-permute-done((f32[1,2,3,8,128]{4,3,2,1,0:T(8,128)S(1)}, f32[1,2,3,8,128]{4,3,2,1,0:T(8,128)S(1)}, u32[]{:S(2)}, u32[]{:S(2)}) %collective-permute-start.10) | collective-permute-done | bytes 24608 | tf_op jit(solution)/shard_map/ppermute | solution.py:253
  26.3 0.5 %collective-permute-done.8.refs_1_ = f32[4,2,3,8,128]{4,3,2,1,0:T(8,128)S(1)} collective-permute-done((f32[4,2,3,8,128]{4,3,2,1,0:T(8,128)S(1)}, f32[4,2,3,8,128]{4,3,2,1,0:T(8,128)S(1)}, u32[]{:S(2)}, u32[]{:S(2)}) %collective-permute-start.8) | collective-permute-done | bytes 98336 | tf_op jit(solution)/shard_map/ppermute | solution.py:251
  26.8 0.9 %collective-permute-done.9.refs_2_ = f32[4,2,3,8,128]{4,3,2,1,0:T(8,128)S(1)} collective-permute-done((f32[4,2,3,8,128]{4,3,2,1,0:T(8,128)S(1)}, f32[4,2,3,8,128]{4,3,2,1,0:T(8,128)S(1)}, u32[]{:S(2)}, u32[]{:S(2)}) %collective-permute-start.9) | collective-permute-done | bytes 98336 | tf_op jit(solution)/shard_map/ppermute | solution.py:252
  27.7 0.7 %last.1 = f32[4,2,3,8,128]{4,3,2,1,0:T(8,128)} custom-call(f32[7,8,128]{2,1,0:T(8,128)S(1)} %tapers.1.coefs_ref, f32[864,128]{1,0:T(8,128)S(1)} %bitcast.9, f32[4,2,3,8,128]{4,3,2,1,0:T(8,128)S(1)} %local_0.1.refs_0_, f32[4,2,3,8,128]{4,3,2,1,0:T(8,128)S(1)} %collective-permute-done.8.refs_1_, f32[4,2,3,8,128]{4,3,2,1,0:T(8,128)S(1)} %collective-permute-done.9.refs_2_, ...), custom_call_target="tpu_custom_call" | custom-call | flops 368640 | bytes 368640 | tf_op jit(solution)/shard_map/last/pallas_call | solution.py:218
  (12 shorter events, 0.1 us)
Async XLA Ops:
  0.0 10.0 %copy-start = (f32[4,3,4,2,3,3,128]{6,3,5,4,2,1,0:T(2,128)S(1)}, f32[4,3,4,2,3,3,128]{6,3,5,4,2,1,0:T(2,128)}, u32[]{:S(2)}) copy-start(f32[4,3,4,2,3,3,128]{6,3,5,4,2,1,0:T(2,128)} %param.6) | copy-start | bytes 1327108
  0.0 10.0 %copy-start.1 = (f32[4,2,3,8,128]{4,3,2,1,0:T(8,128)S(1)}, f32[4,2,3,8,128]{4,3,2,1,0:T(8,128)}, u32[]{:S(2)}) copy-start(f32[4,2,3,8,128]{4,3,2,1,0:T(8,128)} %adjoint_hbm.1) | copy-start | bytes 294916
  1.1 9.4 %collective-permute-start = (f32[4,2,3,8,128]{4,3,2,1,0:T(8,128)S(1)}, f32[4,2,3,8,128]{4,3,2,1,0:T(8,128)S(1)}, u32[]{:S(2)}, u32[]{:S(2)}) collective-permute-start(f32[4,2,3,8,128]{4,3,2,1,0:T(8,128)S(1)} %get-tuple-element.23), channel_id=1, source_target_pairs={{0,24},{1,9},{2,26},{3,11},{4,28},{5,13},{6,30},{7,15},{8,16},{9,1... | collective-permute-start | bytes 294920 | tf_op jit(solution)/shard_map/ppermute | solution.py:251
  6.2 5.1 %collective-permute-start.1 = (f32[4,2,3,8,128]{4,3,2,1,0:T(8,128)S(1)}, f32[4,2,3,8,128]{4,3,2,1,0:T(8,128)S(1)}, u32[]{:S(2)}, u32[]{:S(2)}) collective-permute-start(f32[4,2,3,8,128]{4,3,2,1,0:T(8,128)S(1)} %get-tuple-element.24), channel_id=1, source_target_pairs={{0,8},{1,25},{2,10},{3,27},{4,12},{5,29},{6,14},{7,31},{8,0},{9,17... | collective-permute-start | bytes 294920 | tf_op jit(solution)/shard_map/ppermute | solution.py:252
  6.2 4.3 %collective-permute-start.2 = (f32[1,2,3,8,128]{4,3,2,1,0:T(8,128)S(1)}, f32[1,2,3,8,128]{4,3,2,1,0:T(8,128)S(1)}, u32[]{:S(2)}, u32[]{:S(2)}) collective-permute-start(f32[1,2,3,8,128]{4,3,2,1,0:T(8,128)S(1)} %get-tuple-element.25), channel_id=1, source_target_pairs={{0,7},{1,2},{2,1},{3,4},{4,3},{5,6},{6,5},{7,0},{8,15},{9,10},{10,... | collective-permute-start | bytes 73736 | tf_op jit(solution)/shard_map/ppermute | solution.py:253
  8.0 2.5 %collective-permute-start.3 = (f32[1,2,3,8,128]{4,3,2,1,0:T(8,128)S(1)}, f32[1,2,3,8,128]{4,3,2,1,0:T(8,128)S(1)}, u32[]{:S(2)}, u32[]{:S(2)}) collective-permute-start(f32[1,2,3,8,128]{4,3,2,1,0:T(8,128)S(1)} %get-tuple-element.26), channel_id=1, source_target_pairs={{0,1},{1,0},{2,3},{3,2},{4,5},{5,4},{6,7},{7,6},{8,9},{9,8},{10,11... | collective-permute-start | bytes 73736 | tf_op jit(solution)/shard_map/ppermute | solution.py:254
  11.5 7.6 %collective-permute-start.4 = (f32[4,2,3,8,128]{4,3,2,1,0:T(8,128)S(1)}, f32[4,2,3,8,128]{4,3,2,1,0:T(8,128)S(1)}, u32[]{:S(2)}, u32[]{:S(2)}) collective-permute-start(f32[4,2,3,8,128]{4,3,2,1,0:T(8,128)S(1)} %get-tuple-element.28), channel_id=1, source_target_pairs={{0,24},{1,9},{2,26},{3,11},{4,28},{5,13},{6,30},{7,15},{8,16},{9,1... | collective-permute-start | bytes 294920 | tf_op jit(solution)/shard_map/ppermute | solution.py:251
  13.2 6.7 %collective-permute-start.5 = (f32[4,2,3,8,128]{4,3,2,1,0:T(8,128)S(1)}, f32[4,2,3,8,128]{4,3,2,1,0:T(8,128)S(1)}, u32[]{:S(2)}, u32[]{:S(2)}) collective-permute-start(f32[4,2,3,8,128]{4,3,2,1,0:T(8,128)S(1)} %get-tuple-element.29), channel_id=1, source_target_pairs={{0,8},{1,25},{2,10},{3,27},{4,12},{5,29},{6,14},{7,31},{8,0},{9,17... | collective-permute-start | bytes 294920 | tf_op jit(solution)/shard_map/ppermute | solution.py:252
  13.6 4.2 %collective-permute-start.6 = (f32[1,2,3,8,128]{4,3,2,1,0:T(8,128)S(1)}, f32[1,2,3,8,128]{4,3,2,1,0:T(8,128)S(1)}, u32[]{:S(2)}, u32[]{:S(2)}) collective-permute-start(f32[1,2,3,8,128]{4,3,2,1,0:T(8,128)S(1)} %get-tuple-element.30), channel_id=1, source_target_pairs={{0,7},{1,2},{2,1},{3,4},{4,3},{5,6},{6,5},{7,0},{8,15},{9,10},{10,... | collective-permute-start | bytes 73736 | tf_op jit(solution)/shard_map/ppermute | solution.py:253
  16.1 1.7 %collective-permute-start.7 = (f32[1,2,3,8,128]{4,3,2,1,0:T(8,128)S(1)}, f32[1,2,3,8,128]{4,3,2,1,0:T(8,128)S(1)}, u32[]{:S(2)}, u32[]{:S(2)}) collective-permute-start(f32[1,2,3,8,128]{4,3,2,1,0:T(8,128)S(1)} %get-tuple-element.31), channel_id=1, source_target_pairs={{0,1},{1,0},{2,3},{3,2},{4,5},{5,4},{6,7},{7,6},{8,9},{9,8},{10,11... | collective-permute-start | bytes 73736 | tf_op jit(solution)/shard_map/ppermute | solution.py:254
  20.1 6.7 %collective-permute-start.8 = (f32[4,2,3,8,128]{4,3,2,1,0:T(8,128)S(1)}, f32[4,2,3,8,128]{4,3,2,1,0:T(8,128)S(1)}, u32[]{:S(2)}, u32[]{:S(2)}) collective-permute-start(f32[4,2,3,8,128]{4,3,2,1,0:T(8,128)S(1)} %get-tuple-element.34), channel_id=1, source_target_pairs={{0,24},{1,9},{2,26},{3,11},{4,28},{5,13},{6,30},{7,15},{8,16},{9,1... | collective-permute-start | bytes 294920 | tf_op jit(solution)/shard_map/ppermute | solution.py:251
  22.1 5.7 %collective-permute-start.9 = (f32[4,2,3,8,128]{4,3,2,1,0:T(8,128)S(1)}, f32[4,2,3,8,128]{4,3,2,1,0:T(8,128)S(1)}, u32[]{:S(2)}, u32[]{:S(2)}) collective-permute-start(f32[4,2,3,8,128]{4,3,2,1,0:T(8,128)S(1)} %get-tuple-element.35), channel_id=1, source_target_pairs={{0,8},{1,25},{2,10},{3,27},{4,12},{5,29},{6,14},{7,31},{8,0},{9,17... | collective-permute-start | bytes 294920 | tf_op jit(solution)/shard_map/ppermute | solution.py:252
  22.1 4.2 %collective-permute-start.10 = (f32[1,2,3,8,128]{4,3,2,1,0:T(8,128)S(1)}, f32[1,2,3,8,128]{4,3,2,1,0:T(8,128)S(1)}, u32[]{:S(2)}, u32[]{:S(2)}) collective-permute-start(f32[1,2,3,8,128]{4,3,2,1,0:T(8,128)S(1)} %get-tuple-element.36), channel_id=1, source_target_pairs={{0,7},{1,2},{2,1},{3,4},{4,3},{5,6},{6,5},{7,0},{8,15},{9,10},{10,... | collective-permute-start | bytes 73736 | tf_op jit(solution)/shard_map/ppermute | solution.py:253
  23.0 3.2 %collective-permute-start.11 = (f32[1,2,3,8,128]{4,3,2,1,0:T(8,128)S(1)}, f32[1,2,3,8,128]{4,3,2,1,0:T(8,128)S(1)}, u32[]{:S(2)}, u32[]{:S(2)}) collective-permute-start(f32[1,2,3,8,128]{4,3,2,1,0:T(8,128)S(1)} %get-tuple-element.37), channel_id=1, source_target_pairs={{0,1},{1,0},{2,3},{3,2},{4,5},{5,4},{6,7},{7,6},{8,9},{9,8},{10,11... | collective-permute-start | bytes 73736 | tf_op jit(solution)/shard_map/ppermute | solution.py:254

commit v10 on v9

--- a/solution.py
+++ b/solution.py
@@ -66,7 +66,7 @@
     first = lax.axis_index("gz") * rows
     plane, first_pos = first // BAND, lax.rem(first, BAND)
     block = first_pos // rows
-    return first_pos, lax.rem(plane + block, 2) == 1, lax.rem(block, 2) == 1
+    return first_pos, lax.rem(plane + block, 2) == 0, lax.rem(block, 2) == 1
 
 
 def taper_kernel(rows, source_ref, width_ref, steps_ref, coefs_ref):
@@ -242,8 +242,8 @@
     def in_line(i, by):
         return (i + by * per_plane) % count
 
-    one_pairs = [(i, in_line(i, 1 if (i // per_plane + i) % 2 else -1)) for i in range(count)]
-    two_pairs = [(i, in_line(i, -1 if (i // per_plane + i) % 2 else 1)) for i in range(count)]
+    one_pairs = [(i, in_line(i, -1 if (i // per_plane + i) % 2 else 1)) for i in range(count)]
+    two_pairs = [(i, in_line(i, 1 if (i // per_plane + i) % 2 else -1)) for i in range(count)]
     outer_pairs = [(i, in_plane(i, 1 if i % 2 else -1)) for i in range(count)]
     inner_pairs = [(i, in_plane(i, -1 if i % 2 else 1)) for i in range(count)]
 

time: 28.6 us -> 27.6 us (0.965)
  starting transfers between devices: 15.2 us -> 14.7 us
  waiting for transfers between devices: 7.55 us -> 7.05 us
    ppermute x3, starting transfers between devices: 0.37 us -> 5.68 us  [sent_on(): two = lax.ppermute(two, 'gz', two_pairs)]
    ppermute x3, starting transfers between devices: 8.84 us -> 4.2 us  [sent_on(): one = lax.ppermute(one, 'gz', one_pairs)]
    ppermute x3, starting transfers between devices: 5.23 us -> 1.16 us  [sent_on(): outer = lax.ppermute(outer, 'gz', outer_pairs)]
    ppermute x3, starting transfers between devices: 0.78 us -> 3.65 us  [sent_on(): inner = lax.ppermute(inner, 'gz', inner_pairs)]
    ppermute x3, waiting for transfers between devices: 1.84 us -> 0.08 us  [sent_on(): one = lax.ppermute(one, 'gz', one_pairs)]
    ppermute x3, waiting for transfers between devices: 3.1 us -> 4.42 us  [sent_on(): outer = lax.ppermute(outer, 'gz', outer_pairs)]
  transfers between devices with their start and end apart: 12 -> 12, of which waited for: 7 -> 7; matrix products, arithmetic and copies ran while one was open for 0% -> 0% of each run, Pallas kernels for 5% -> 6%
where the time goes in v10:
time: 27.6 us; the launch traced here: 27.4 us
  starting transfers between devices  14.7 us (53%)
  waiting for transfers between devices  7.05 us (26%)
  Pallas kernels  3.65 us (13%)
  between operations  2.03 us (7%)
    ppermute x3, starting transfers between devices, sent_on(): two = lax.ppermute(two, 'gz', two_pairs)  5.68 us
    ppermute x3, waiting for transfers between devices, sent_on(): outer = lax.ppermute(outer, 'gz', outer_pairs)  4.42 us
    ppermute x3, starting transfers between devices, sent_on(): one = lax.ppermute(one, 'gz', one_pairs)  4.2 us
    ppermute x3, starting transfers between devices, sent_on(): inner = lax.ppermute(inner, 'gz', inner_pairs)  3.65 us
    pallas_call x8, Pallas kernels, call(): pl.pallas_call(kernel, name=name, out_shape=out_shapes, in_specs=[pl.Bloc...  3.65 us
    ppermute x3, waiting for transfers between devices, sent_on(): two = lax.ppermute(two, 'gz', two_pairs)  2.55 us
    ppermute x3, starting transfers between devices, sent_on(): outer = lax.ppermute(outer, 'gz', outer_pairs)  1.16 us
  transfers between devices with their start and end apart: 12, of which 7 were waited for; matrix products, arithmetic and copies ran while one was open for 0% of the time, Pallas kernels for 6%

profile of v10, /device:TPU:0, one launch (start us, length us, event | category | flops | bytes accessed | tf_op | source)
XLA Modules:
  0.0 27.4 jit_solution(6934757903061764118)
XLA Ops:
  0.0 1.1 %begin.1 = (f32[4,2,3,8,128]{4,3,2,1,0:T(8,128)S(1)}, f32[4,2,3,8,128]{4,3,2,1,0:T(8,128)S(1)}, f32[1,2,3,8,128]{4,3,2,1,0:T(8,128)S(1)}, f32[1,2,3,8,128]{4,3,2,1,0:T(8,128)S(1)}) custom-call(f32[4,2,3,8,128]{4,3,2,1,0:T(8,128)} %adjoint_hbm.1, f32[864,128]{1,0:T(8,128)} %bitcast.3), custom_call_target="tpu_custom_call" | custom-call | flops 368640 | bytes 368640 | tf_op jit(solution)/shard_map/begin/pallas_call | solution.py:218
  1.1 3.1 %collective-permute-start = (f32[4,2,3,8,128]{4,3,2,1,0:T(8,128)S(1)}, f32[4,2,3,8,128]{4,3,2,1,0:T(8,128)S(1)}, u32[]{:S(2)}, u32[]{:S(2)}) collective-permute-start(f32[4,2,3,8,128]{4,3,2,1,0:T(8,128)S(1)} %get-tuple-element.23), channel_id=1, source_target_pairs={{0,8},{1,25},{2,10},{3,27},{4,12},{5,29},{6,14},{7,31},{8,0},{9,17... | collective-permute-start | bytes 294920 | tf_op jit(solution)/shard_map/ppermute | solution.py:251
  4.2 2.5 %collective-permute-start.1 = (f32[4,2,3,8,128]{4,3,2,1,0:T(8,128)S(1)}, f32[4,2,3,8,128]{4,3,2,1,0:T(8,128)S(1)}, u32[]{:S(2)}, u32[]{:S(2)}) collective-permute-start(f32[4,2,3,8,128]{4,3,2,1,0:T(8,128)S(1)} %get-tuple-element.24), channel_id=1, source_target_pairs={{0,24},{1,9},{2,26},{3,11},{4,28},{5,13},{6,30},{7,15},{8,16},{9,1... | collective-permute-start | bytes 294920 | tf_op jit(solution)/shard_map/ppermute | solution.py:252
  6.7 1.2 %collective-permute-start.2 = (f32[1,2,3,8,128]{4,3,2,1,0:T(8,128)S(1)}, f32[1,2,3,8,128]{4,3,2,1,0:T(8,128)S(1)}, u32[]{:S(2)}, u32[]{:S(2)}) collective-permute-start(f32[1,2,3,8,128]{4,3,2,1,0:T(8,128)S(1)} %get-tuple-element.25), channel_id=1, source_target_pairs={{0,7},{1,2},{2,1},{3,4},{4,3},{5,6},{6,5},{7,0},{8,15},{9,10},{10,... | collective-permute-start | bytes 73736 | tf_op jit(solution)/shard_map/ppermute | solution.py:253
  7.8 0.4 %collective-permute-start.3 = (f32[1,2,3,8,128]{4,3,2,1,0:T(8,128)S(1)}, f32[1,2,3,8,128]{4,3,2,1,0:T(8,128)S(1)}, u32[]{:S(2)}, u32[]{:S(2)}) collective-permute-start(f32[1,2,3,8,128]{4,3,2,1,0:T(8,128)S(1)} %get-tuple-element.26), channel_id=1, source_target_pairs={{0,1},{1,0},{2,3},{3,2},{4,5},{5,4},{6,7},{7,6},{8,9},{9,8},{10,11... | collective-permute-start | bytes 73736 | tf_op jit(solution)/shard_map/ppermute | solution.py:254
  10.3 0.5 %start.1 = (f32[4,2,3,8,128]{4,3,2,1,0:T(8,128)S(1)}, f32[4,2,3,8,128]{4,3,2,1,0:T(8,128)S(1)}) custom-call(f32[7,8,128]{2,1,0:T(8,128)S(1)} %tapers.1.coefs_ref, f32[4,2,3,8,128]{4,3,2,1,0:T(8,128)S(1)} %copy-done.1, f32[864,128]{1,0:T(8,128)S(1)} %bitcast.4), custom_call_target="tpu_custom_call" | custom-call | flops 1622016 | bytes 1622016 | tf_op jit(solution)/shard_map/start/pallas_call | solution.py:218
  10.8 0.2 collective-permute-done.2.refs_3_
  11.0 0.2 collective-permute-done.1.refs_2_
  11.1 0.2 third.1
  11.3 1.0 %collective-permute-start.4 = (f32[4,2,3,8,128]{4,3,2,1,0:T(8,128)S(1)}, f32[4,2,3,8,128]{4,3,2,1,0:T(8,128)S(1)}, u32[]{:S(2)}, u32[]{:S(2)}) collective-permute-start(f32[4,2,3,8,128]{4,3,2,1,0:T(8,128)S(1)} %get-tuple-element.28), channel_id=1, source_target_pairs={{0,8},{1,25},{2,10},{3,27},{4,12},{5,29},{6,14},{7,31},{8,0},{9,17... | collective-permute-start | bytes 294920 | tf_op jit(solution)/shard_map/ppermute | solution.py:251
  12.4 1.7 %collective-permute-start.5 = (f32[4,2,3,8,128]{4,3,2,1,0:T(8,128)S(1)}, f32[4,2,3,8,128]{4,3,2,1,0:T(8,128)S(1)}, u32[]{:S(2)}, u32[]{:S(2)}) collective-permute-start(f32[4,2,3,8,128]{4,3,2,1,0:T(8,128)S(1)} %get-tuple-element.29), channel_id=1, source_target_pairs={{0,24},{1,9},{2,26},{3,11},{4,28},{5,13},{6,30},{7,15},{8,16},{9,1... | collective-permute-start | bytes 294920 | tf_op jit(solution)/shard_map/ppermute | solution.py:252
  14.1 1.6 %collective-permute-start.7 = (f32[1,2,3,8,128]{4,3,2,1,0:T(8,128)S(1)}, f32[1,2,3,8,128]{4,3,2,1,0:T(8,128)S(1)}, u32[]{:S(2)}, u32[]{:S(2)}) collective-permute-start(f32[1,2,3,8,128]{4,3,2,1,0:T(8,128)S(1)} %get-tuple-element.31), channel_id=1, source_target_pairs={{0,1},{1,0},{2,3},{3,2},{4,5},{5,4},{6,7},{7,6},{8,9},{9,8},{10,11... | collective-permute-start | bytes 73736 | tf_op jit(solution)/shard_map/ppermute | solution.py:254
  15.7 0.5 %local_1.1.refs_0_ = f32[4,2,3,8,128]{4,3,2,1,0:T(8,128)S(1)} custom-call(f32[4,2,3,8,128]{4,3,2,1,0:T(8,128)S(1)} %get-tuple-element.27.field_ref.refs_6_, f32[864,128]{1,0:T(8,128)S(1)} %bitcast.6), custom_call_target="tpu_custom_call" | custom-call | flops 1622016 | bytes 1622016 | tf_op jit(solution)/shard_map/local_1/pallas_call | solution.py:218
  16.2 2.2 %collective-permute-done.6.refs_3_ = f32[1,2,3,8,128]{4,3,2,1,0:T(8,128)S(1)} collective-permute-done((f32[1,2,3,8,128]{4,3,2,1,0:T(8,128)S(1)}, f32[1,2,3,8,128]{4,3,2,1,0:T(8,128)S(1)}, u32[]{:S(2)}, u32[]{:S(2)}) %collective-permute-start.6) | collective-permute-done | bytes 24608 | tf_op jit(solution)/shard_map/ppermute | solution.py:253
  18.4 1.3 %collective-permute-done.5.refs_2_ = f32[4,2,3,8,128]{4,3,2,1,0:T(8,128)S(1)} collective-permute-done((f32[4,2,3,8,128]{4,3,2,1,0:T(8,128)S(1)}, f32[4,2,3,8,128]{4,3,2,1,0:T(8,128)S(1)}, u32[]{:S(2)}, u32[]{:S(2)}) %collective-permute-start.5) | collective-permute-done | bytes 98336 | tf_op jit(solution)/shard_map/ppermute | solution.py:252
  19.7 0.2 second.1
  19.9 0.1 collective-permute-start.8
  20.0 1.5 %collective-permute-start.9 = (f32[4,2,3,8,128]{4,3,2,1,0:T(8,128)S(1)}, f32[4,2,3,8,128]{4,3,2,1,0:T(8,128)S(1)}, u32[]{:S(2)}, u32[]{:S(2)}) collective-permute-start(f32[4,2,3,8,128]{4,3,2,1,0:T(8,128)S(1)} %get-tuple-element.35), channel_id=1, source_target_pairs={{0,24},{1,9},{2,26},{3,11},{4,28},{5,13},{6,30},{7,15},{8,16},{9,1... | collective-permute-start | bytes 294920 | tf_op jit(solution)/shard_map/ppermute | solution.py:252
  21.4 1.6 %collective-permute-start.11 = (f32[1,2,3,8,128]{4,3,2,1,0:T(8,128)S(1)}, f32[1,2,3,8,128]{4,3,2,1,0:T(8,128)S(1)}, u32[]{:S(2)}, u32[]{:S(2)}) collective-permute-start(f32[1,2,3,8,128]{4,3,2,1,0:T(8,128)S(1)} %get-tuple-element.37), channel_id=1, source_target_pairs={{0,1},{1,0},{2,3},{3,2},{4,5},{5,4},{6,7},{7,6},{8,9},{9,8},{10,11... | collective-permute-start | bytes 73736 | tf_op jit(solution)/shard_map/ppermute | solution.py:254
  23.0 0.5 %local_0.1.refs_0_ = f32[4,2,3,8,128]{4,3,2,1,0:T(8,128)S(1)} custom-call(f32[4,2,3,8,128]{4,3,2,1,0:T(8,128)S(1)} %get-tuple-element.33.field_ref, f32[864,128]{1,0:T(8,128)S(1)} %bitcast.8), custom_call_target="tpu_custom_call" | custom-call | flops 1622016 | bytes 1622016 | tf_op jit(solution)/shard_map/local_0/pallas_call | solution.py:218
  23.5 2.0 %collective-permute-done.10.refs_3_ = f32[1,2,3,8,128]{4,3,2,1,0:T(8,128)S(1)} collective-permute-done((f32[1,2,3,8,128]{4,3,2,1,0:T(8,128)S(1)}, f32[1,2,3,8,128]{4,3,2,1,0:T(8,128)S(1)}, u32[]{:S(2)}, u32[]{:S(2)}) %collective-permute-start.10) | collective-permute-done | bytes 24608 | tf_op jit(solution)/shard_map/ppermute | solution.py:253
  25.6 0.1 collective-permute-done.8.refs_1_
  25.6 1.1 %collective-permute-done.9.refs_2_ = f32[4,2,3,8,128]{4,3,2,1,0:T(8,128)S(1)} collective-permute-done((f32[4,2,3,8,128]{4,3,2,1,0:T(8,128)S(1)}, f32[4,2,3,8,128]{4,3,2,1,0:T(8,128)S(1)}, u32[]{:S(2)}, u32[]{:S(2)}) %collective-permute-start.9) | collective-permute-done | bytes 98336 | tf_op jit(solution)/shard_map/ppermute | solution.py:252
  26.7 0.7 %last.1 = f32[4,2,3,8,128]{4,3,2,1,0:T(8,128)} custom-call(f32[7,8,128]{2,1,0:T(8,128)S(1)} %tapers.1.coefs_ref, f32[864,128]{1,0:T(8,128)S(1)} %bitcast.9, f32[4,2,3,8,128]{4,3,2,1,0:T(8,128)S(1)} %local_0.1.refs_0_, f32[4,2,3,8,128]{4,3,2,1,0:T(8,128)S(1)} %collective-permute-done.8.refs_1_, f32[4,2,3,8,128]{4,3,2,1,0:T(8,128)S(1)} %collective-permute-done.9.refs_2_, ...), custom_call_target="tpu_custom_call" | custom-call | flops 368640 | bytes 368640 | tf_op jit(solution)/shard_map/last/pallas_call | solution.py:218
  (12 shorter events, 0.1 us)
Async XLA Ops:
  0.0 10.2 %copy-start = (f32[4,3,4,2,3,3,128]{6,3,5,4,2,1,0:T(2,128)S(1)}, f32[4,3,4,2,3,3,128]{6,3,5,4,2,1,0:T(2,128)}, u32[]{:S(2)}) copy-start(f32[4,3,4,2,3,3,128]{6,3,5,4,2,1,0:T(2,128)} %param.6) | copy-start | bytes 1327108
  0.0 10.2 %copy-start.1 = (f32[4,2,3,8,128]{4,3,2,1,0:T(8,128)S(1)}, f32[4,2,3,8,128]{4,3,2,1,0:T(8,128)}, u32[]{:S(2)}) copy-start(f32[4,2,3,8,128]{4,3,2,1,0:T(8,128)} %adjoint_hbm.1) | copy-start | bytes 294916
  1.1 9.9 %collective-permute-start = (f32[4,2,3,8,128]{4,3,2,1,0:T(8,128)S(1)}, f32[4,2,3,8,128]{4,3,2,1,0:T(8,128)S(1)}, u32[]{:S(2)}, u32[]{:S(2)}) collective-permute-start(f32[4,2,3,8,128]{4,3,2,1,0:T(8,128)S(1)} %get-tuple-element.23), channel_id=1, source_target_pairs={{0,8},{1,25},{2,10},{3,27},{4,12},{5,29},{6,14},{7,31},{8,0},{9,17... | collective-permute-start | bytes 294920 | tf_op jit(solution)/shard_map/ppermute | solution.py:251
  4.2 7.0 %collective-permute-start.1 = (f32[4,2,3,8,128]{4,3,2,1,0:T(8,128)S(1)}, f32[4,2,3,8,128]{4,3,2,1,0:T(8,128)S(1)}, u32[]{:S(2)}, u32[]{:S(2)}) collective-permute-start(f32[4,2,3,8,128]{4,3,2,1,0:T(8,128)S(1)} %get-tuple-element.24), channel_id=1, source_target_pairs={{0,24},{1,9},{2,26},{3,11},{4,28},{5,13},{6,30},{7,15},{8,16},{9,1... | collective-permute-start | bytes 294920 | tf_op jit(solution)/shard_map/ppermute | solution.py:252
  6.7 4.3 %collective-permute-start.2 = (f32[1,2,3,8,128]{4,3,2,1,0:T(8,128)S(1)}, f32[1,2,3,8,128]{4,3,2,1,0:T(8,128)S(1)}, u32[]{:S(2)}, u32[]{:S(2)}) collective-permute-start(f32[1,2,3,8,128]{4,3,2,1,0:T(8,128)S(1)} %get-tuple-element.25), channel_id=1, source_target_pairs={{0,7},{1,2},{2,1},{3,4},{4,3},{5,6},{6,5},{7,0},{8,15},{9,10},{10,... | collective-permute-start | bytes 73736 | tf_op jit(solution)/shard_map/ppermute | solution.py:253
  7.8 3.2 %collective-permute-start.3 = (f32[1,2,3,8,128]{4,3,2,1,0:T(8,128)S(1)}, f32[1,2,3,8,128]{4,3,2,1,0:T(8,128)S(1)}, u32[]{:S(2)}, u32[]{:S(2)}) collective-permute-start(f32[1,2,3,8,128]{4,3,2,1,0:T(8,128)S(1)} %get-tuple-element.26), channel_id=1, source_target_pairs={{0,1},{1,0},{2,3},{3,2},{4,5},{5,4},{6,7},{7,6},{8,9},{9,8},{10,11... | collective-permute-start | bytes 73736 | tf_op jit(solution)/shard_map/ppermute | solution.py:254
  11.3 7.1 %collective-permute-start.4 = (f32[4,2,3,8,128]{4,3,2,1,0:T(8,128)S(1)}, f32[4,2,3,8,128]{4,3,2,1,0:T(8,128)S(1)}, u32[]{:S(2)}, u32[]{:S(2)}) collective-permute-start(f32[4,2,3,8,128]{4,3,2,1,0:T(8,128)S(1)} %get-tuple-element.28), channel_id=1, source_target_pairs={{0,8},{1,25},{2,10},{3,27},{4,12},{5,29},{6,14},{7,31},{8,0},{9,17... | collective-permute-start | bytes 294920 | tf_op jit(solution)/shard_map/ppermute | solution.py:251
  12.4 7.4 %collective-permute-start.5 = (f32[4,2,3,8,128]{4,3,2,1,0:T(8,128)S(1)}, f32[4,2,3,8,128]{4,3,2,1,0:T(8,128)S(1)}, u32[]{:S(2)}, u32[]{:S(2)}) collective-permute-start(f32[4,2,3,8,128]{4,3,2,1,0:T(8,128)S(1)} %get-tuple-element.29), channel_id=1, source_target_pairs={{0,24},{1,9},{2,26},{3,11},{4,28},{5,13},{6,30},{7,15},{8,16},{9,1... | collective-permute-start | bytes 294920 | tf_op jit(solution)/shard_map/ppermute | solution.py:252
  14.1 4.3 %collective-permute-start.6 = (f32[1,2,3,8,128]{4,3,2,1,0:T(8,128)S(1)}, f32[1,2,3,8,128]{4,3,2,1,0:T(8,128)S(1)}, u32[]{:S(2)}, u32[]{:S(2)}) collective-permute-start(f32[1,2,3,8,128]{4,3,2,1,0:T(8,128)S(1)} %get-tuple-element.30), channel_id=1, source_target_pairs={{0,7},{1,2},{2,1},{3,4},{4,3},{5,6},{6,5},{7,0},{8,15},{9,10},{10,... | collective-permute-start | bytes 73736 | tf_op jit(solution)/shard_map/ppermute | solution.py:253
  14.1 4.3 %collective-permute-start.7 = (f32[1,2,3,8,128]{4,3,2,1,0:T(8,128)S(1)}, f32[1,2,3,8,128]{4,3,2,1,0:T(8,128)S(1)}, u32[]{:S(2)}, u32[]{:S(2)}) collective-permute-start(f32[1,2,3,8,128]{4,3,2,1,0:T(8,128)S(1)} %get-tuple-element.31), channel_id=1, source_target_pairs={{0,1},{1,0},{2,3},{3,2},{4,5},{5,4},{6,7},{7,6},{8,9},{9,8},{10,11... | collective-permute-start | bytes 73736 | tf_op jit(solution)/shard_map/ppermute | solution.py:254
  19.9 5.8 %collective-permute-start.8 = (f32[4,2,3,8,128]{4,3,2,1,0:T(8,128)S(1)}, f32[4,2,3,8,128]{4,3,2,1,0:T(8,128)S(1)}, u32[]{:S(2)}, u32[]{:S(2)}) collective-permute-start(f32[4,2,3,8,128]{4,3,2,1,0:T(8,128)S(1)} %get-tuple-element.34), channel_id=1, source_target_pairs={{0,8},{1,25},{2,10},{3,27},{4,12},{5,29},{6,14},{7,31},{8,0},{9,17... | collective-permute-start | bytes 294920 | tf_op jit(solution)/shard_map/ppermute | solution.py:251
  20.0 6.8 %collective-permute-start.9 = (f32[4,2,3,8,128]{4,3,2,1,0:T(8,128)S(1)}, f32[4,2,3,8,128]{4,3,2,1,0:T(8,128)S(1)}, u32[]{:S(2)}, u32[]{:S(2)}) collective-permute-start(f32[4,2,3,8,128]{4,3,2,1,0:T(8,128)S(1)} %get-tuple-element.35), channel_id=1, source_target_pairs={{0,24},{1,9},{2,26},{3,11},{4,28},{5,13},{6,30},{7,15},{8,16},{9,1... | collective-permute-start | bytes 294920 | tf_op jit(solution)/shard_map/ppermute | solution.py:252
  21.4 4.2 %collective-permute-start.10 = (f32[1,2,3,8,128]{4,3,2,1,0:T(8,128)S(1)}, f32[1,2,3,8,128]{4,3,2,1,0:T(8,128)S(1)}, u32[]{:S(2)}, u32[]{:S(2)}) collective-permute-start(f32[1,2,3,8,128]{4,3,2,1,0:T(8,128)S(1)} %get-tuple-element.36), channel_id=1, source_target_pairs={{0,7},{1,2},{2,1},{3,4},{4,3},{5,6},{6,5},{7,0},{8,15},{9,10},{10,... | collective-permute-start | bytes 73736 | tf_op jit(solution)/shard_map/ppermute | solution.py:253
  21.4 4.2 %collective-permute-start.11 = (f32[1,2,3,8,128]{4,3,2,1,0:T(8,128)S(1)}, f32[1,2,3,8,128]{4,3,2,1,0:T(8,128)S(1)}, u32[]{:S(2)}, u32[]{:S(2)}) collective-permute-start(f32[1,2,3,8,128]{4,3,2,1,0:T(8,128)S(1)} %get-tuple-element.37), channel_id=1, source_target_pairs={{0,1},{1,0},{2,3},{3,2},{4,5},{5,4},{6,7},{7,6},{8,9},{9,8},{10,11... | collective-permute-start | bytes 73736 | tf_op jit(solution)/shard_map/ppermute | solution.py:254

commit v11 on v8

--- a/solution.py
+++ b/solution.py
@@ -78,10 +78,12 @@
     coefs_ref[rows + 2] = 0.25 / (ones * steps_ref[0].astype(jnp.float32))
 
 
-def store_z(rows, matrices, row, field, far_ref, near_ref):
+def store_z(rows, matrices, row, field, middle_ref, near_ref, wrap_ref):
     _, _, odd_plane, _ = place(rows)
     _, up = transport(matrices, None, field)
-    store_field(far_ref, row, combine(lambda v, h: jnp.where(odd_plane, h, v), field, up))
+    far = combine(lambda v, h: jnp.where(odd_plane, h, v), field, up)
+    store_field(middle_ref, row, far)
+    store_field(wrap_ref, row, far)
     store_field(near_ref, row, combine(lambda v, h: jnp.where(odd_plane, v, h), field, up))
 
 
@@ -94,7 +96,7 @@
 
 
 def begin_kernel(
-    rows, adjoint_hbm, links_hbm, far_ref, near_ref, outer_ref, inner_ref, adjoint_ref, links_ref, sems
+    rows, adjoint_hbm, links_hbm, middle_ref, near_ref, wrap_ref, outer_ref, inner_ref, adjoint_ref, links_ref, sems
 ):
     row_entries = SETS * MUS * ENTRIES
     z_first = (2 * MUS + 2) * ENTRIES
@@ -109,7 +111,7 @@
         copy.wait()
     for row in range(rows):
         matrices = links_ref.at[row], z_first - aligned
-        store_z(rows, matrices, row, load_field(adjoint_ref, row), far_ref, near_ref)
+        store_z(rows, matrices, row, load_field(adjoint_ref, row), middle_ref, near_ref, wrap_ref)
     store_t(rows, (links_ref.at[rows - 1], z_first + ENTRIES - aligned), adjoint_ref, outer_ref, inner_ref)
 
 
@@ -153,9 +155,11 @@
 
 
 def arrived_sum(links_ref, link_set, row, rows, arrivals, coefs_ref=None):
-    sum_ref, near_ref, far_ref, outer_ref, inner_ref = arrivals
-    _, first_pos, odd_plane, odd_block = place(rows)
-    far, near = load_field(far_ref, row), load_field(near_ref, row)
+    sum_ref, middle_ref, near_ref, wrap_ref, outer_ref, inner_ref = arrivals
+    plane, first_pos, odd_plane, odd_block = place(rows)
+    at_wrap = (plane == 0) | (plane == lax.axis_size("gz") * rows // BAND - 1)
+    near = load_field(near_ref, row)
+    far = combine(lambda p, q: jnp.where(at_wrap, q, p), load_field(middle_ref, row), load_field(wrap_ref, row))
     if coefs_ref is not None:
         far, near = (combine(lambda v: coefs_ref[row + 1] * v, f) for f in (far, near))
     above = combine(lambda p, q: jnp.where(odd_plane, p, q), far, near)
@@ -180,18 +184,19 @@
 
 
 def third_kernel(rows, coefs_ref, links_ref, *refs):
-    arrivals, (third_ref, far_ref, near_ref, outer_ref, inner_ref) = refs[:5], refs[5:]
+    arrivals, (third_ref, middle_ref, near_ref, wrap_ref, outer_ref, inner_ref) = refs[:6], refs[6:]
     for row in range(rows):
         inside, eps = coefs_ref[row + 1], coefs_ref[rows + 2]
         total = arrived_sum(links_ref, 2, row, rows, arrivals, coefs_ref)
         third = combine(lambda s: 0.75 * (inside * (eps * s)), total)
         store_field(third_ref, row, third)
-        store_z(rows, links_at(links_ref, row, 1, 2), row, third, far_ref, near_ref)
+        store_z(rows, links_at(links_ref, row, 1, 2), row, third, middle_ref, near_ref, wrap_ref)
     store_t(rows, links_at(links_ref, rows - 1, 1, 3), third_ref, outer_ref, inner_ref)
 
 
 def second_kernel(rows, coefs_ref, links_ref, *refs):
-    arrivals, (start_ref, third_ref, mixed_ref, far_ref, near_ref, outer_ref, inner_ref, base_ref) = refs[:5], refs[5:]
+    arrivals, (start_ref, third_ref, mixed_ref, *sent, base_ref) = refs[:6], refs[6:]
+    middle_ref, near_ref, wrap_ref, outer_ref, inner_ref = sent
     for row in range(rows):
         inside, eps = coefs_ref[row + 1], coefs_ref[rows + 2]
         total = arrived_sum(links_ref, 1, row, rows, arrivals)
@@ -200,12 +205,12 @@
         mixed = combine(lambda p, q: 0.25 * p - (2.0 / 9.0) * q, second, third)
         store_field(mixed_ref, row, mixed)
         store_field(base_ref, row, combine(lambda p, q: p + q, second, third))
-        store_z(rows, links_at(links_ref, row, 0, 2), row, mixed, far_ref, near_ref)
+        store_z(rows, links_at(links_ref, row, 0, 2), row, mixed, middle_ref, near_ref, wrap_ref)
     store_t(rows, links_at(links_ref, rows - 1, 0, 3), mixed_ref, outer_ref, inner_ref)
 
 
 def last_kernel(rows, coefs_ref, links_ref, *refs):
-    arrivals, (base_ref, out_ref) = refs[:5], refs[5:]
+    arrivals, (base_ref, out_ref) = refs[:6], refs[6:]
     for row in range(rows):
         inside, eps = coefs_ref[row + 1], coefs_ref[rows + 2]
         total = arrived_sum(links_ref, 0, row, rows, arrivals)
@@ -241,22 +246,32 @@
     def in_line(i, by):
         return (i + by * per_plane) % count
 
-    far_pairs = [(i, in_line(i, 1 if i // per_plane % 2 else -1)) for i in range(count)]
+    planes = count // per_plane
+
+    def far_partner(i, over_wrap):
+        plane = i // per_plane
+        if (plane in (0, planes - 1)) != over_wrap:
+            return i
+        return in_line(i, 1 if plane % 2 else -1)
+
+    middle_pairs = [(i, far_partner(i, False)) for i in range(count)]
+    wrap_pairs = [(i, far_partner(i, True)) for i in range(count)]
     near_pairs = [(i, in_line(i, -1 if i // per_plane % 2 else 1)) for i in range(count)]
     outer_pairs = [(i, in_plane(i, 1 if i % 2 else -1)) for i in range(count)]
     inner_pairs = [(i, in_plane(i, -1 if i % 2 else 1)) for i in range(count)]
 
-    def sent_on(far, near, outer, inner):
+    def sent_on(middle, near, wrap, outer, inner):
+        middle = lax.ppermute(middle, "gz", middle_pairs)
         near = lax.ppermute(near, "gz", near_pairs)
-        far = lax.ppermute(far, "gz", far_pairs)
+        wrap = lax.ppermute(wrap, "gz", wrap_pairs)
         outer = lax.ppermute(outer, "gz", outer_pairs)
         inner = lax.ppermute(inner, "gz", inner_pairs)
-        return near, far, outer, inner
+        return middle, near, wrap, outer, inner
 
     def local(link_set, field):
         return call(functools.partial(local_kernel, rows, link_set), f"local_{link_set}", (field, links), whole, 22)
 
-    sent = (whole, whole, one_row, one_row)
+    sent = (whole, whole, whole, one_row, one_row)
     copied = SETS * MUS * ENTRIES - (2 * MUS + 2) * ENTRIES // 8 * 8
     sending = call(
         functools.partial(begin_kernel, rows), "begin",

time: 27.5 us -> 36.3 us (1.32)
  starting transfers between devices: 15.8 us -> 23.7 us
  waiting for transfers between devices: 5.92 us -> 6.57 us
    ppermute x3 -> x6, starting transfers between devices: 6.51 us -> 13 us  [the longest x3 11 us: sent_on(): wrap = lax.ppermute(wrap, 'gz', wrap_pairs)]
    ppermute x3, starting transfers between devices: 4.45 us -> 6.92 us  [sent_on(): near = lax.ppermute(near, 'gz', near_pairs)]
    ppermute x3, starting transfers between devices: 3.49 us -> 1.51 us  [sent_on(): inner = lax.ppermute(inner, 'gz', inner_pairs)]
    ppermute x3, waiting for transfers between devices: 4.58 us -> 5.54 us  [sent_on(): outer = lax.ppermute(outer, 'gz', outer_pairs)]
    ppermute x3, starting transfers between devices: 1.33 us -> 2.28 us  [sent_on(): outer = lax.ppermute(outer, 'gz', outer_pairs)]
    ppermute x3 -> x6, waiting for transfers between devices: 1.33 us -> 1.01 us  [the longest x3 1 us: sent_on(): wrap = lax.ppermute(wrap, 'gz', wrap_pairs)]
  transfers between devices with their start and end apart: 12 -> 15, of which waited for: 6 -> 6; matrix products, arithmetic and copies ran while one was open for 0% -> 0% of each run, Pallas kernels for 6% -> 4%
where the time goes in v11:
time: 36.3 us; the launch traced here: 36 us
  starting transfers between devices  23.7 us (65%)
  waiting for transfers between devices  6.57 us (18%)
  Pallas kernels  3.65 us (10%)
  between operations  2.09 us (6%)
    ppermute x3, starting transfers between devices, sent_on(): wrap = lax.ppermute(wrap, 'gz', wrap_pairs)  11 us
    ppermute x3, starting transfers between devices, sent_on(): near = lax.ppermute(near, 'gz', near_pairs)  6.92 us
    ppermute x3, waiting for transfers between devices, sent_on(): outer = lax.ppermute(outer, 'gz', outer_pairs)  5.54 us
    pallas_call x8, Pallas kernels, call(): pl.pallas_call(kernel, name=name, out_shape=out_shapes, in_specs=[pl.Bloc...  3.65 us
    ppermute x3, starting transfers between devices, sent_on(): outer = lax.ppermute(outer, 'gz', outer_pairs)  2.28 us
    ppermute x3, starting transfers between devices, sent_on(): middle = lax.ppermute(middle, 'gz', middle_pairs)  2 us
    ppermute x3, starting transfers between devices, sent_on(): inner = lax.ppermute(inner, 'gz', inner_pairs)  1.51 us
    ppermute x3, waiting for transfers between devices, sent_on(): wrap = lax.ppermute(wrap, 'gz', wrap_pairs)  1 us
  transfers between devices with their start and end apart: 15, of which 6 were waited for; matrix products, arithmetic and copies ran while one was open for 0% of the time, Pallas kernels for 4%

profile of v11, /device:TPU:0, one launch (start us, length us, event | category | flops | bytes accessed | tf_op | source)
XLA Modules:
  0.0 36.0 jit_solution(11383383335493780806)
XLA Ops:
  0.0 1.1 %begin.1 = (f32[4,2,3,8,128]{4,3,2,1,0:T(8,128)S(1)}, f32[4,2,3,8,128]{4,3,2,1,0:T(8,128)S(1)}, f32[4,2,3,8,128]{4,3,2,1,0:T(8,128)S(1)}, f32[1,2,3,8,128]{4,3,2,1,0:T(8,128)S(1)}, f32[1,2,3,8,128]{4,3,2,1,0:T(8,128)S(1)}) custom-call(f32[4,2,3,8,128]{4,3,2,1,0:T(8,128)} %adjoint_hbm.1, f32[864,128]{1,0:T(8,128)} %bitcast.3), custom_call_target="tpu_custom_call" | custom-call | flops 368640 | bytes 368640 | tf_op jit(solution)/shard_map/begin/pallas_call | solution.py:222
  1.1 0.7 %collective-permute-start = (f32[4,2,3,8,128]{4,3,2,1,0:T(8,128)S(1)}, f32[4,2,3,8,128]{4,3,2,1,0:T(8,128)S(1)}, u32[]{:S(2)}, u32[]{:S(2)}) collective-permute-start(f32[4,2,3,8,128]{4,3,2,1,0:T(8,128)S(1)} %get-tuple-element.26), channel_id=1, source_target_pairs={{0,0},{1,1},{2,2},{3,3},{4,4},{5,5},{6,6},{7,7},{8,16},{9,17},{10,... | collective-permute-start | bytes 294920 | tf_op jit(solution)/shard_map/ppermute | solution.py:264
  1.8 5.9 %collective-permute-start.1 = (f32[4,2,3,8,128]{4,3,2,1,0:T(8,128)S(1)}, f32[4,2,3,8,128]{4,3,2,1,0:T(8,128)S(1)}, u32[]{:S(2)}, u32[]{:S(2)}) collective-permute-start(f32[4,2,3,8,128]{4,3,2,1,0:T(8,128)S(1)} %get-tuple-element.27), channel_id=1, source_target_pairs={{0,8},{1,9},{2,10},{3,11},{4,12},{5,13},{6,14},{7,15},{8,0},{9,1},... | collective-permute-start | bytes 294920 | tf_op jit(solution)/shard_map/ppermute | solution.py:265
  7.7 3.2 %collective-permute-start.2 = (f32[4,2,3,8,128]{4,3,2,1,0:T(8,128)S(1)}, f32[4,2,3,8,128]{4,3,2,1,0:T(8,128)S(1)}, u32[]{:S(2)}, u32[]{:S(2)}) collective-permute-start(f32[4,2,3,8,128]{4,3,2,1,0:T(8,128)S(1)} %get-tuple-element.28), channel_id=1, source_target_pairs={{0,24},{1,25},{2,26},{3,27},{4,28},{5,29},{6,30},{7,31},{8,8},{9,9... | collective-permute-start | bytes 294920 | tf_op jit(solution)/shard_map/ppermute | solution.py:266
  10.9 1.1 %collective-permute-start.3 = (f32[1,2,3,8,128]{4,3,2,1,0:T(8,128)S(1)}, f32[1,2,3,8,128]{4,3,2,1,0:T(8,128)S(1)}, u32[]{:S(2)}, u32[]{:S(2)}) collective-permute-start(f32[1,2,3,8,128]{4,3,2,1,0:T(8,128)S(1)} %get-tuple-element.29), channel_id=1, source_target_pairs={{0,7},{1,2},{2,1},{3,4},{4,3},{5,6},{6,5},{7,0},{8,15},{9,10},{10,... | collective-permute-start | bytes 73736 | tf_op jit(solution)/shard_map/ppermute | solution.py:267
  12.0 0.6 %collective-permute-start.4 = (f32[1,2,3,8,128]{4,3,2,1,0:T(8,128)S(1)}, f32[1,2,3,8,128]{4,3,2,1,0:T(8,128)S(1)}, u32[]{:S(2)}, u32[]{:S(2)}) collective-permute-start(f32[1,2,3,8,128]{4,3,2,1,0:T(8,128)S(1)} %get-tuple-element.30), channel_id=1, source_target_pairs={{0,1},{1,0},{2,3},{3,2},{4,5},{5,4},{6,7},{7,6},{8,9},{9,8},{10,11... | collective-permute-start | bytes 73736 | tf_op jit(solution)/shard_map/ppermute | solution.py:268
  14.6 0.5 %start.1 = (f32[4,2,3,8,128]{4,3,2,1,0:T(8,128)S(1)}, f32[4,2,3,8,128]{4,3,2,1,0:T(8,128)S(1)}) custom-call(f32[7,8,128]{2,1,0:T(8,128)S(1)} %tapers.1.coefs_ref, f32[4,2,3,8,128]{4,3,2,1,0:T(8,128)S(1)} %copy-done.1, f32[864,128]{1,0:T(8,128)S(1)} %bitcast.4), custom_call_target="tpu_custom_call" | custom-call | flops 1622016 | bytes 1622016 | tf_op jit(solution)/shard_map/start/pallas_call | solution.py:222
  15.1 0.2 collective-permute-done.3.refs_4_
  15.3 0.7 %collective-permute-done.2.refs_3_ = f32[4,2,3,8,128]{4,3,2,1,0:T(8,128)S(1)} collective-permute-done((f32[4,2,3,8,128]{4,3,2,1,0:T(8,128)S(1)}, f32[4,2,3,8,128]{4,3,2,1,0:T(8,128)S(1)}, u32[]{:S(2)}, u32[]{:S(2)}) %collective-permute-start.2) | collective-permute-done | bytes 98336 | tf_op jit(solution)/shard_map/ppermute | solution.py:266
  16.1 0.7 %collective-permute-start.5 = (f32[4,2,3,8,128]{4,3,2,1,0:T(8,128)S(1)}, f32[4,2,3,8,128]{4,3,2,1,0:T(8,128)S(1)}, u32[]{:S(2)}, u32[]{:S(2)}) collective-permute-start(f32[4,2,3,8,128]{4,3,2,1,0:T(8,128)S(1)} %get-tuple-element.32), channel_id=1, source_target_pairs={{0,0},{1,1},{2,2},{3,3},{4,4},{5,5},{6,6},{7,7},{8,16},{9,17},{10,... | collective-permute-start | bytes 294920 | tf_op jit(solution)/shard_map/ppermute | solution.py:264
  16.9 3.8 %collective-permute-start.7 = (f32[4,2,3,8,128]{4,3,2,1,0:T(8,128)S(1)}, f32[4,2,3,8,128]{4,3,2,1,0:T(8,128)S(1)}, u32[]{:S(2)}, u32[]{:S(2)}) collective-permute-start(f32[4,2,3,8,128]{4,3,2,1,0:T(8,128)S(1)} %get-tuple-element.34), channel_id=1, source_target_pairs={{0,24},{1,25},{2,26},{3,27},{4,28},{5,29},{6,30},{7,31},{8,8},{9,9... | collective-permute-start | bytes 294920 | tf_op jit(solution)/shard_map/ppermute | solution.py:266
  20.6 1.1 %collective-permute-start.8 = (f32[1,2,3,8,128]{4,3,2,1,0:T(8,128)S(1)}, f32[1,2,3,8,128]{4,3,2,1,0:T(8,128)S(1)}, u32[]{:S(2)}, u32[]{:S(2)}) collective-permute-start(f32[1,2,3,8,128]{4,3,2,1,0:T(8,128)S(1)} %get-tuple-element.35), channel_id=1, source_target_pairs={{0,7},{1,2},{2,1},{3,4},{4,3},{5,6},{6,5},{7,0},{8,15},{9,10},{10,... | collective-permute-start | bytes 73736 | tf_op jit(solution)/shard_map/ppermute | solution.py:267
  21.7 0.4 %collective-permute-start.9 = (f32[1,2,3,8,128]{4,3,2,1,0:T(8,128)S(1)}, f32[1,2,3,8,128]{4,3,2,1,0:T(8,128)S(1)}, u32[]{:S(2)}, u32[]{:S(2)}) collective-permute-start(f32[1,2,3,8,128]{4,3,2,1,0:T(8,128)S(1)} %get-tuple-element.36), channel_id=1, source_target_pairs={{0,1},{1,0},{2,3},{3,2},{4,5},{5,4},{6,7},{7,6},{8,9},{9,8},{10,11... | collective-permute-start | bytes 73736 | tf_op jit(solution)/shard_map/ppermute | solution.py:268
  22.2 0.5 %local_1.1.refs_0_ = f32[4,2,3,8,128]{4,3,2,1,0:T(8,128)S(1)} custom-call(f32[4,2,3,8,128]{4,3,2,1,0:T(8,128)S(1)} %get-tuple-element.31.field_ref.refs_7_, f32[864,128]{1,0:T(8,128)S(1)} %bitcast.6), custom_call_target="tpu_custom_call" | custom-call | flops 1622016 | bytes 1622016 | tf_op jit(solution)/shard_map/local_1/pallas_call | solution.py:222
  22.7 2.3 %collective-permute-done.8.refs_4_ = f32[1,2,3,8,128]{4,3,2,1,0:T(8,128)S(1)} collective-permute-done((f32[1,2,3,8,128]{4,3,2,1,0:T(8,128)S(1)}, f32[1,2,3,8,128]{4,3,2,1,0:T(8,128)S(1)}, u32[]{:S(2)}, u32[]{:S(2)}) %collective-permute-start.8) | collective-permute-done | bytes 24608 | tf_op jit(solution)/shard_map/ppermute | solution.py:267
  24.9 0.2 collective-permute-done.7.refs_3_
  25.2 0.2 second.1
  25.3 0.7 %collective-permute-start.10 = (f32[4,2,3,8,128]{4,3,2,1,0:T(8,128)S(1)}, f32[4,2,3,8,128]{4,3,2,1,0:T(8,128)S(1)}, u32[]{:S(2)}, u32[]{:S(2)}) collective-permute-start(f32[4,2,3,8,128]{4,3,2,1,0:T(8,128)S(1)} %get-tuple-element.39), channel_id=1, source_target_pairs={{0,0},{1,1},{2,2},{3,3},{4,4},{5,5},{6,6},{7,7},{8,16},{9,17},{10,... | collective-permute-start | bytes 294920 | tf_op jit(solution)/shard_map/ppermute | solution.py:264
  26.0 0.9 %collective-permute-start.11 = (f32[4,2,3,8,128]{4,3,2,1,0:T(8,128)S(1)}, f32[4,2,3,8,128]{4,3,2,1,0:T(8,128)S(1)}, u32[]{:S(2)}, u32[]{:S(2)}) collective-permute-start(f32[4,2,3,8,128]{4,3,2,1,0:T(8,128)S(1)} %get-tuple-element.40), channel_id=1, source_target_pairs={{0,8},{1,9},{2,10},{3,11},{4,12},{5,13},{6,14},{7,15},{8,0},{9,1},... | collective-permute-start | bytes 294920 | tf_op jit(solution)/shard_map/ppermute | solution.py:265
  27.0 4.0 %collective-permute-start.12 = (f32[4,2,3,8,128]{4,3,2,1,0:T(8,128)S(1)}, f32[4,2,3,8,128]{4,3,2,1,0:T(8,128)S(1)}, u32[]{:S(2)}, u32[]{:S(2)}) collective-permute-start(f32[4,2,3,8,128]{4,3,2,1,0:T(8,128)S(1)} %get-tuple-element.41), channel_id=1, source_target_pairs={{0,24},{1,25},{2,26},{3,27},{4,28},{5,29},{6,30},{7,31},{8,8},{9,9... | collective-permute-start | bytes 294920 | tf_op jit(solution)/shard_map/ppermute | solution.py:266
  31.0 0.5 %collective-permute-start.14 = (f32[1,2,3,8,128]{4,3,2,1,0:T(8,128)S(1)}, f32[1,2,3,8,128]{4,3,2,1,0:T(8,128)S(1)}, u32[]{:S(2)}, u32[]{:S(2)}) collective-permute-start(f32[1,2,3,8,128]{4,3,2,1,0:T(8,128)S(1)} %get-tuple-element.43), channel_id=1, source_target_pairs={{0,1},{1,0},{2,3},{3,2},{4,5},{5,4},{6,7},{7,6},{8,9},{9,8},{10,11... | collective-permute-start | bytes 73736 | tf_op jit(solution)/shard_map/ppermute | solution.py:268
  31.6 0.5 %local_0.1.refs_0_ = f32[4,2,3,8,128]{4,3,2,1,0:T(8,128)S(1)} custom-call(f32[4,2,3,8,128]{4,3,2,1,0:T(8,128)S(1)} %get-tuple-element.38.field_ref, f32[864,128]{1,0:T(8,128)S(1)} %bitcast.8), custom_call_target="tpu_custom_call" | custom-call | flops 1622016 | bytes 1622016 | tf_op jit(solution)/shard_map/local_0/pallas_call | solution.py:222
  32.1 3.1 %collective-permute-done.13.refs_4_ = f32[1,2,3,8,128]{4,3,2,1,0:T(8,128)S(1)} collective-permute-done((f32[1,2,3,8,128]{4,3,2,1,0:T(8,128)S(1)}, f32[1,2,3,8,128]{4,3,2,1,0:T(8,128)S(1)}, u32[]{:S(2)}, u32[]{:S(2)}) %collective-permute-start.13) | collective-permute-done | bytes 24608 | tf_op jit(solution)/shard_map/ppermute | solution.py:267
  35.3 0.7 %last.1 = f32[4,2,3,8,128]{4,3,2,1,0:T(8,128)} custom-call(f32[7,8,128]{2,1,0:T(8,128)S(1)} %tapers.1.coefs_ref, f32[864,128]{1,0:T(8,128)S(1)} %bitcast.9, f32[4,2,3,8,128]{4,3,2,1,0:T(8,128)S(1)} %local_0.1.refs_0_, f32[4,2,3,8,128]{4,3,2,1,0:T(8,128)S(1)} %collective-permute-done.10.refs_1_, f32[4,2,3,8,128]{4,3,2,1,0:T(8,128)S(1)} %collective-permute-done.11.refs_2_, ...), custom_call_target="tpu_custom_call" | custom-call | flops 368640 | bytes 368640 | tf_op jit(solution)/shard_map/last/pallas_call | solution.py:222
  (18 shorter events, 0.4 us)
Async XLA Ops:
  0.0 14.6 %copy-start = (f32[4,3,4,2,3,3,128]{6,3,5,4,2,1,0:T(2,128)S(1)}, f32[4,3,4,2,3,3,128]{6,3,5,4,2,1,0:T(2,128)}, u32[]{:S(2)}) copy-start(f32[4,3,4,2,3,3,128]{6,3,5,4,2,1,0:T(2,128)} %param.6) | copy-start | bytes 1327108
  0.0 14.6 %copy-start.1 = (f32[4,2,3,8,128]{4,3,2,1,0:T(8,128)S(1)}, f32[4,2,3,8,128]{4,3,2,1,0:T(8,128)}, u32[]{:S(2)}) copy-start(f32[4,2,3,8,128]{4,3,2,1,0:T(8,128)} %adjoint_hbm.1) | copy-start | bytes 294916
  1.1 14.2 %collective-permute-start = (f32[4,2,3,8,128]{4,3,2,1,0:T(8,128)S(1)}, f32[4,2,3,8,128]{4,3,2,1,0:T(8,128)S(1)}, u32[]{:S(2)}, u32[]{:S(2)}) collective-permute-start(f32[4,2,3,8,128]{4,3,2,1,0:T(8,128)S(1)} %get-tuple-element.26), channel_id=1, source_target_pairs={{0,0},{1,1},{2,2},{3,3},{4,4},{5,5},{6,6},{7,7},{8,16},{9,17},{10,... | collective-permute-start | bytes 294920 | tf_op jit(solution)/shard_map/ppermute | solution.py:264
  1.8 13.5 %collective-permute-start.1 = (f32[4,2,3,8,128]{4,3,2,1,0:T(8,128)S(1)}, f32[4,2,3,8,128]{4,3,2,1,0:T(8,128)S(1)}, u32[]{:S(2)}, u32[]{:S(2)}) collective-permute-start(f32[4,2,3,8,128]{4,3,2,1,0:T(8,128)S(1)} %get-tuple-element.27), channel_id=1, source_target_pairs={{0,8},{1,9},{2,10},{3,11},{4,12},{5,13},{6,14},{7,15},{8,0},{9,1},... | collective-permute-start | bytes 294920 | tf_op jit(solution)/shard_map/ppermute | solution.py:265
  7.7 8.3 %collective-permute-start.2 = (f32[4,2,3,8,128]{4,3,2,1,0:T(8,128)S(1)}, f32[4,2,3,8,128]{4,3,2,1,0:T(8,128)S(1)}, u32[]{:S(2)}, u32[]{:S(2)}) collective-permute-start(f32[4,2,3,8,128]{4,3,2,1,0:T(8,128)S(1)} %get-tuple-element.28), channel_id=1, source_target_pairs={{0,24},{1,25},{2,26},{3,27},{4,28},{5,29},{6,30},{7,31},{8,8},{9,9... | collective-permute-start | bytes 294920 | tf_op jit(solution)/shard_map/ppermute | solution.py:266
  10.9 4.4 %collective-permute-start.3 = (f32[1,2,3,8,128]{4,3,2,1,0:T(8,128)S(1)}, f32[1,2,3,8,128]{4,3,2,1,0:T(8,128)S(1)}, u32[]{:S(2)}, u32[]{:S(2)}) collective-permute-start(f32[1,2,3,8,128]{4,3,2,1,0:T(8,128)S(1)} %get-tuple-element.29), channel_id=1, source_target_pairs={{0,7},{1,2},{2,1},{3,4},{4,3},{5,6},{6,5},{7,0},{8,15},{9,10},{10,... | collective-permute-start | bytes 73736 | tf_op jit(solution)/shard_map/ppermute | solution.py:267
  12.0 3.3 %collective-permute-start.4 = (f32[1,2,3,8,128]{4,3,2,1,0:T(8,128)S(1)}, f32[1,2,3,8,128]{4,3,2,1,0:T(8,128)S(1)}, u32[]{:S(2)}, u32[]{:S(2)}) collective-permute-start(f32[1,2,3,8,128]{4,3,2,1,0:T(8,128)S(1)} %get-tuple-element.30), channel_id=1, source_target_pairs={{0,1},{1,0},{2,3},{3,2},{4,5},{5,4},{6,7},{7,6},{8,9},{9,8},{10,11... | collective-permute-start | bytes 73736 | tf_op jit(solution)/shard_map/ppermute | solution.py:268
  16.1 8.8 %collective-permute-start.5 = (f32[4,2,3,8,128]{4,3,2,1,0:T(8,128)S(1)}, f32[4,2,3,8,128]{4,3,2,1,0:T(8,128)S(1)}, u32[]{:S(2)}, u32[]{:S(2)}) collective-permute-start(f32[4,2,3,8,128]{4,3,2,1,0:T(8,128)S(1)} %get-tuple-element.32), channel_id=1, source_target_pairs={{0,0},{1,1},{2,2},{3,3},{4,4},{5,5},{6,6},{7,7},{8,16},{9,17},{10,... | collective-permute-start | bytes 294920 | tf_op jit(solution)/shard_map/ppermute | solution.py:264
  16.8 8.1 %collective-permute-start.6 = (f32[4,2,3,8,128]{4,3,2,1,0:T(8,128)S(1)}, f32[4,2,3,8,128]{4,3,2,1,0:T(8,128)S(1)}, u32[]{:S(2)}, u32[]{:S(2)}) collective-permute-start(f32[4,2,3,8,128]{4,3,2,1,0:T(8,128)S(1)} %get-tuple-element.33), channel_id=1, source_target_pairs={{0,8},{1,9},{2,10},{3,11},{4,12},{5,13},{6,14},{7,15},{8,0},{9,1},... | collective-permute-start | bytes 294920 | tf_op jit(solution)/shard_map/ppermute | solution.py:265
  16.9 8.3 %collective-permute-start.7 = (f32[4,2,3,8,128]{4,3,2,1,0:T(8,128)S(1)}, f32[4,2,3,8,128]{4,3,2,1,0:T(8,128)S(1)}, u32[]{:S(2)}, u32[]{:S(2)}) collective-permute-start(f32[4,2,3,8,128]{4,3,2,1,0:T(8,128)S(1)} %get-tuple-element.34), channel_id=1, source_target_pairs={{0,24},{1,25},{2,26},{3,27},{4,28},{5,29},{6,30},{7,31},{8,8},{9,9... | collective-permute-start | bytes 294920 | tf_op jit(solution)/shard_map/ppermute | solution.py:266
  20.6 4.3 %collective-permute-start.8 = (f32[1,2,3,8,128]{4,3,2,1,0:T(8,128)S(1)}, f32[1,2,3,8,128]{4,3,2,1,0:T(8,128)S(1)}, u32[]{:S(2)}, u32[]{:S(2)}) collective-permute-start(f32[1,2,3,8,128]{4,3,2,1,0:T(8,128)S(1)} %get-tuple-element.35), channel_id=1, source_target_pairs={{0,7},{1,2},{2,1},{3,4},{4,3},{5,6},{6,5},{7,0},{8,15},{9,10},{10,... | collective-permute-start | bytes 73736 | tf_op jit(solution)/shard_map/ppermute | solution.py:267
  21.7 3.2 %collective-permute-start.9 = (f32[1,2,3,8,128]{4,3,2,1,0:T(8,128)S(1)}, f32[1,2,3,8,128]{4,3,2,1,0:T(8,128)S(1)}, u32[]{:S(2)}, u32[]{:S(2)}) collective-permute-start(f32[1,2,3,8,128]{4,3,2,1,0:T(8,128)S(1)} %get-tuple-element.36), channel_id=1, source_target_pairs={{0,1},{1,0},{2,3},{3,2},{4,5},{5,4},{6,7},{7,6},{8,9},{9,8},{10,11... | collective-permute-start | bytes 73736 | tf_op jit(solution)/shard_map/ppermute | solution.py:268
  25.3 9.8 %collective-permute-start.10 = (f32[4,2,3,8,128]{4,3,2,1,0:T(8,128)S(1)}, f32[4,2,3,8,128]{4,3,2,1,0:T(8,128)S(1)}, u32[]{:S(2)}, u32[]{:S(2)}) collective-permute-start(f32[4,2,3,8,128]{4,3,2,1,0:T(8,128)S(1)} %get-tuple-element.39), channel_id=1, source_target_pairs={{0,0},{1,1},{2,2},{3,3},{4,4},{5,5},{6,6},{7,7},{8,16},{9,17},{10,... | collective-permute-start | bytes 294920 | tf_op jit(solution)/shard_map/ppermute | solution.py:264
  26.0 9.1 %collective-permute-start.11 = (f32[4,2,3,8,128]{4,3,2,1,0:T(8,128)S(1)}, f32[4,2,3,8,128]{4,3,2,1,0:T(8,128)S(1)}, u32[]{:S(2)}, u32[]{:S(2)}) collective-permute-start(f32[4,2,3,8,128]{4,3,2,1,0:T(8,128)S(1)} %get-tuple-element.40), channel_id=1, source_target_pairs={{0,8},{1,9},{2,10},{3,11},{4,12},{5,13},{6,14},{7,15},{8,0},{9,1},... | collective-permute-start | bytes 294920 | tf_op jit(solution)/shard_map/ppermute | solution.py:265
  27.0 8.3 %collective-permute-start.12 = (f32[4,2,3,8,128]{4,3,2,1,0:T(8,128)S(1)}, f32[4,2,3,8,128]{4,3,2,1,0:T(8,128)S(1)}, u32[]{:S(2)}, u32[]{:S(2)}) collective-permute-start(f32[4,2,3,8,128]{4,3,2,1,0:T(8,128)S(1)} %get-tuple-element.41), channel_id=1, source_target_pairs={{0,24},{1,25},{2,26},{3,27},{4,28},{5,29},{6,30},{7,31},{8,8},{9,9... | collective-permute-start | bytes 294920 | tf_op jit(solution)/shard_map/ppermute | solution.py:266
  30.9 4.2 %collective-permute-start.13 = (f32[1,2,3,8,128]{4,3,2,1,0:T(8,128)S(1)}, f32[1,2,3,8,128]{4,3,2,1,0:T(8,128)S(1)}, u32[]{:S(2)}, u32[]{:S(2)}) collective-permute-start(f32[1,2,3,8,128]{4,3,2,1,0:T(8,128)S(1)} %get-tuple-element.42), channel_id=1, source_target_pairs={{0,7},{1,2},{2,1},{3,4},{4,3},{5,6},{6,5},{7,0},{8,15},{9,10},{10,... | collective-permute-start | bytes 73736 | tf_op jit(solution)/shard_map/ppermute | solution.py:267
  31.0 4.1 %collective-permute-start.14 = (f32[1,2,3,8,128]{4,3,2,1,0:T(8,128)S(1)}, f32[1,2,3,8,128]{4,3,2,1,0:T(8,128)S(1)}, u32[]{:S(2)}, u32[]{:S(2)}) collective-permute-start(f32[1,2,3,8,128]{4,3,2,1,0:T(8,128)S(1)} %get-tuple-element.43), channel_id=1, source_target_pairs={{0,1},{1,0},{2,3},{3,2},{4,5},{5,4},{6,7},{7,6},{8,9},{9,8},{10,11... | collective-permute-start | bytes 73736 | tf_op jit(solution)/shard_map/ppermute | solution.py:268

commit v12 on v11

--- a/solution.py
+++ b/solution.py
@@ -68,6 +68,10 @@
     return plane, first_pos, lax.rem(plane, 2) == 1, lax.rem(first_pos // rows, 2) == 1
 
 
+def is_at_wrap(plane, rows):
+    return (plane == 0) | (plane == lax.axis_size("gz") * rows // BAND - 1)
+
+
 def taper_kernel(rows, source_ref, width_ref, steps_ref, coefs_ref):
     _, first_pos, _, _ = place(rows)
     ones = jnp.ones((8, 128), jnp.float32)
@@ -87,16 +91,20 @@
     store_field(near_ref, row, combine(lambda v, h: jnp.where(odd_plane, v, h), field, up))
 
 
-def store_t(rows, matrices, field_ref, outer_ref, inner_ref):
-    _, _, _, odd_block = place(rows)
+def store_t(rows, matrices, field_ref, outer_ref, middle_ref, wrap_ref):
+    plane, _, _, odd_block = place(rows)
     first = load_field(field_ref, 0)
     _, last = transport(matrices, None, load_field(field_ref, rows - 1))
     store_field(outer_ref, 0, combine(lambda p, q: jnp.where(odd_block, q, p), first, last))
-    store_field(inner_ref, 0, combine(lambda p, q: jnp.where(odd_block, p, q), first, last))
+    inner = combine(lambda p, q: jnp.where(odd_block, p, q), first, last)
+    at_wrap = is_at_wrap(plane, rows)
+    middle, wrap = load_field(middle_ref, 0), load_field(wrap_ref, 0)
+    store_field(middle_ref, 0, combine(lambda p, q: jnp.where(at_wrap, q, p), middle, inner))
+    store_field(wrap_ref, 0, combine(lambda p, q: jnp.where(at_wrap, p, q), wrap, inner))
 
 
 def begin_kernel(
-    rows, adjoint_hbm, links_hbm, middle_ref, near_ref, wrap_ref, outer_ref, inner_ref, adjoint_ref, links_ref, sems
+    rows, adjoint_hbm, links_hbm, middle_ref, near_ref, wrap_ref, outer_ref, adjoint_ref, links_ref, sems
 ):
     row_entries = SETS * MUS * ENTRIES
     z_first = (2 * MUS + 2) * ENTRIES
@@ -112,7 +120,7 @@
     for row in range(rows):
         matrices = links_ref.at[row], z_first - aligned
         store_z(rows, matrices, row, load_field(adjoint_ref, row), middle_ref, near_ref, wrap_ref)
-    store_t(rows, (links_ref.at[rows - 1], z_first + ENTRIES - aligned), adjoint_ref, outer_ref, inner_ref)
+    store_t(rows, (links_ref.at[rows - 1], z_first + ENTRIES - aligned), adjoint_ref, outer_ref, middle_ref, wrap_ref)
 
 
 def start_kernel(rows, link_set, coefs_ref, adjoint_ref, links_ref, sum_ref, start_ref):
@@ -155,9 +163,9 @@
 
 
 def arrived_sum(links_ref, link_set, row, rows, arrivals, coefs_ref=None):
-    sum_ref, middle_ref, near_ref, wrap_ref, outer_ref, inner_ref = arrivals
+    sum_ref, middle_ref, near_ref, wrap_ref, outer_ref = arrivals
     plane, first_pos, odd_plane, odd_block = place(rows)
-    at_wrap = (plane == 0) | (plane == lax.axis_size("gz") * rows // BAND - 1)
+    at_wrap = is_at_wrap(plane, rows)
     near = load_field(near_ref, row)
     far = combine(lambda p, q: jnp.where(at_wrap, q, p), load_field(middle_ref, row), load_field(wrap_ref, row))
     if coefs_ref is not None:
@@ -167,7 +175,8 @@
     total = combine(
         lambda s, f, p, q: s + f + jnp.where(odd_plane, q, p), load_field(sum_ref, row), ahead_z, far, near
     )
-    outer, inner = load_field(outer_ref, 0), load_field(inner_ref, 0)
+    outer = load_field(outer_ref, 0)
+    inner = combine(lambda p, q: jnp.where(at_wrap, p, q), load_field(middle_ref, 0), load_field(wrap_ref, 0))
     if row == 0:
         exists = jnp.where(first_pos != 0, 1.0, 0.0)
         if coefs_ref is not None:
@@ -184,19 +193,19 @@
 
 
 def third_kernel(rows, coefs_ref, links_ref, *refs):
-    arrivals, (third_ref, middle_ref, near_ref, wrap_ref, outer_ref, inner_ref) = refs[:6], refs[6:]
+    arrivals, (third_ref, middle_ref, near_ref, wrap_ref, outer_ref) = refs[:5], refs[5:]
     for row in range(rows):
         inside, eps = coefs_ref[row + 1], coefs_ref[rows + 2]
         total = arrived_sum(links_ref, 2, row, rows, arrivals, coefs_ref)
         third = combine(lambda s: 0.75 * (inside * (eps * s)), total)
         store_field(third_ref, row, third)
         store_z(rows, links_at(links_ref, row, 1, 2), row, third, middle_ref, near_ref, wrap_ref)
-    store_t(rows, links_at(links_ref, rows - 1, 1, 3), third_ref, outer_ref, inner_ref)
+    store_t(rows, links_at(links_ref, rows - 1, 1, 3), third_ref, outer_ref, middle_ref, wrap_ref)
 
 
 def second_kernel(rows, coefs_ref, links_ref, *refs):
-    arrivals, (start_ref, third_ref, mixed_ref, *sent, base_ref) = refs[:6], refs[6:]
-    middle_ref, near_ref, wrap_ref, outer_ref, inner_ref = sent
+    arrivals, (start_ref, third_ref, mixed_ref, *sent, base_ref) = refs[:5], refs[5:]
+    middle_ref, near_ref, wrap_ref, outer_ref = sent
     for row in range(rows):
         inside, eps = coefs_ref[row + 1], coefs_ref[rows + 2]
         total = arrived_sum(links_ref, 1, row, rows, arrivals)
@@ -206,11 +215,11 @@
         store_field(mixed_ref, row, mixed)
         store_field(base_ref, row, combine(lambda p, q: p + q, second, third))
         store_z(rows, links_at(links_ref, row, 0, 2), row, mixed, middle_ref, near_ref, wrap_ref)
-    store_t(rows, links_at(links_ref, rows - 1, 0, 3), mixed_ref, outer_ref, inner_ref)
+    store_t(rows, links_at(links_ref, rows - 1, 0, 3), mixed_ref, outer_ref, middle_ref, wrap_ref)
 
 
 def last_kernel(rows, coefs_ref, links_ref, *refs):
-    arrivals, (base_ref, out_ref) = refs[:6], refs[6:]
+    arrivals, (base_ref, out_ref) = refs[:5], refs[5:]
     for row in range(rows):
         inside, eps = coefs_ref[row + 1], coefs_ref[rows + 2]
         total = arrived_sum(links_ref, 0, row, rows, arrivals)
@@ -248,30 +257,28 @@
 
     planes = count // per_plane
 
-    def far_partner(i, over_wrap):
+    def far_or_inner(i, over_wrap):
         plane = i // per_plane
         if (plane in (0, planes - 1)) != over_wrap:
-            return i
+            return in_plane(i, -1 if i % 2 else 1)
         return in_line(i, 1 if plane % 2 else -1)
 
-    middle_pairs = [(i, far_partner(i, False)) for i in range(count)]
-    wrap_pairs = [(i, far_partner(i, True)) for i in range(count)]
+    middle_pairs = [(i, far_or_inner(i, False)) for i in range(count)]
+    wrap_pairs = [(i, far_or_inner(i, True)) for i in range(count)]
     near_pairs = [(i, in_line(i, -1 if i // per_plane % 2 else 1)) for i in range(count)]
     outer_pairs = [(i, in_plane(i, 1 if i % 2 else -1)) for i in range(count)]
-    inner_pairs = [(i, in_plane(i, -1 if i % 2 else 1)) for i in range(count)]
-
-    def sent_on(middle, near, wrap, outer, inner):
+
+    def sent_on(middle, near, wrap, outer):
         middle = lax.ppermute(middle, "gz", middle_pairs)
         near = lax.ppermute(near, "gz", near_pairs)
         wrap = lax.ppermute(wrap, "gz", wrap_pairs)
         outer = lax.ppermute(outer, "gz", outer_pairs)
-        inner = lax.ppermute(inner, "gz", inner_pairs)
-        return middle, near, wrap, outer, inner
+        return middle, near, wrap, outer
 
     def local(link_set, field):
         return call(functools.partial(local_kernel, rows, link_set), f"local_{link_set}", (field, links), whole, 22)
 
-    sent = (whole, whole, whole, one_row, one_row)
+    sent = (whole, whole, whole, one_row)
     copied = SETS * MUS * ENTRIES - (2 * MUS + 2) * ENTRIES // 8 * 8
     sending = call(
         functools.partial(begin_kernel, rows), "begin",

time: 36.3 us -> 28.5 us (0.79)
  starting transfers between devices: 23.7 us -> 15.9 us
    ppermute x3, starting transfers between devices: 11 us -> 5.05 us  [sent_on(): wrap = lax.ppermute(wrap, 'gz', wrap_pairs)]
    ppermute x3, starting transfers between devices: 2.28 us -> 5.64 us  [sent_on(): outer = lax.ppermute(outer, 'gz', outer_pairs)]
    ppermute x3, starting transfers between devices: 6.92 us -> 4.58 us  [sent_on(): near = lax.ppermute(near, 'gz', near_pairs)]
    ppermute x3, waiting for transfers between devices: 1 us -> 3.27 us  [sent_on(): wrap = lax.ppermute(wrap, 'gz', wrap_pairs)]
    ppermute x3, waiting for transfers between devices: 5.54 us -> 3.44 us  [sent_on(): outer = lax.ppermute(outer, 'gz', outer_pairs)]
    ppermute x3 -> x0, starting transfers between devices: 1.51 us -> none  [sent_on(): inner = lax.ppermute(inner, 'gz', inner_pairs)]
    ppermute x3, starting transfers between devices: 2 us -> 0.66 us  [sent_on(): middle = lax.ppermute(middle, 'gz', middle_pairs)]
  transfers between devices with their start and end apart: 15 -> 12, of which waited for: 6 -> 6; matrix products, arithmetic and copies ran while one was open for 0% -> 0% of each run, Pallas kernels for 4% -> 5%
where the time goes in v12:
time: 28.5 us; the launch traced here: 28.4 us
  starting transfers between devices  15.9 us (56%)
  waiting for transfers between devices  6.72 us (24%)
  Pallas kernels  3.67 us (13%)
  between operations  2.04 us (7%)
    ppermute x3, starting transfers between devices, sent_on(): outer = lax.ppermute(outer, 'gz', outer_pairs)  5.64 us
    ppermute x3, starting transfers between devices, sent_on(): wrap = lax.ppermute(wrap, 'gz', wrap_pairs)  5.05 us
    ppermute x3, starting transfers between devices, sent_on(): near = lax.ppermute(near, 'gz', near_pairs)  4.58 us
    pallas_call x8, Pallas kernels, call(): pl.pallas_call(kernel, name=name, out_shape=out_shapes, in_specs=[pl.Bloc...  3.67 us
    ppermute x3, waiting for transfers between devices, sent_on(): outer = lax.ppermute(outer, 'gz', outer_pairs)  3.44 us
    ppermute x3, waiting for transfers between devices, sent_on(): wrap = lax.ppermute(wrap, 'gz', wrap_pairs)  3.27 us
    ppermute x3, starting transfers between devices, sent_on(): middle = lax.ppermute(middle, 'gz', middle_pairs)  0.66 us
  transfers between devices with their start and end apart: 12, of which 6 were waited for; matrix products, arithmetic and copies ran while one was open for 0% of the time, Pallas kernels for 5%

profile of v12, /device:TPU:0, one launch (start us, length us, event | category | flops | bytes accessed | tf_op | source)
XLA Modules:
  0.0 28.4 jit_solution(15671140549147616051)
XLA Ops:
  0.0 1.1 %begin.1 = (f32[4,2,3,8,128]{4,3,2,1,0:T(8,128)S(1)}, f32[4,2,3,8,128]{4,3,2,1,0:T(8,128)S(1)}, f32[4,2,3,8,128]{4,3,2,1,0:T(8,128)S(1)}, f32[1,2,3,8,128]{4,3,2,1,0:T(8,128)S(1)}) custom-call(f32[4,2,3,8,128]{4,3,2,1,0:T(8,128)} %adjoint_hbm.1, f32[864,128]{1,0:T(8,128)} %bitcast.3), custom_call_target="tpu_custom_call" | custom-call | flops 368640 | bytes 368640 | tf_op jit(solution)/shard_map/begin/pallas_call | solution.py:231
  1.1 0.5 %collective-permute-start = (f32[4,2,3,8,128]{4,3,2,1,0:T(8,128)S(1)}, f32[4,2,3,8,128]{4,3,2,1,0:T(8,128)S(1)}, u32[]{:S(2)}, u32[]{:S(2)}) collective-permute-start(f32[4,2,3,8,128]{4,3,2,1,0:T(8,128)S(1)} %get-tuple-element.23), channel_id=1, source_target_pairs={{0,1},{1,0},{2,3},{3,2},{4,5},{5,4},{6,7},{7,6},{8,16},{9,17},{10,... | collective-permute-start | bytes 294920 | tf_op jit(solution)/shard_map/ppermute | solution.py:272
  1.6 4.1 %collective-permute-start.1 = (f32[4,2,3,8,128]{4,3,2,1,0:T(8,128)S(1)}, f32[4,2,3,8,128]{4,3,2,1,0:T(8,128)S(1)}, u32[]{:S(2)}, u32[]{:S(2)}) collective-permute-start(f32[4,2,3,8,128]{4,3,2,1,0:T(8,128)S(1)} %get-tuple-element.24), channel_id=1, source_target_pairs={{0,8},{1,9},{2,10},{3,11},{4,12},{5,13},{6,14},{7,15},{8,0},{9,1},... | collective-permute-start | bytes 294920 | tf_op jit(solution)/shard_map/ppermute | solution.py:273
  5.8 1.3 %collective-permute-start.2 = (f32[4,2,3,8,128]{4,3,2,1,0:T(8,128)S(1)}, f32[4,2,3,8,128]{4,3,2,1,0:T(8,128)S(1)}, u32[]{:S(2)}, u32[]{:S(2)}) collective-permute-start(f32[4,2,3,8,128]{4,3,2,1,0:T(8,128)S(1)} %get-tuple-element.25), channel_id=1, source_target_pairs={{0,24},{1,25},{2,26},{3,27},{4,28},{5,29},{6,30},{7,31},{8,9},{9,8... | collective-permute-start | bytes 294920 | tf_op jit(solution)/shard_map/ppermute | solution.py:274
  7.1 1.4 %collective-permute-start.3 = (f32[1,2,3,8,128]{4,3,2,1,0:T(8,128)S(1)}, f32[1,2,3,8,128]{4,3,2,1,0:T(8,128)S(1)}, u32[]{:S(2)}, u32[]{:S(2)}) collective-permute-start(f32[1,2,3,8,128]{4,3,2,1,0:T(8,128)S(1)} %get-tuple-element.26), channel_id=1, source_target_pairs={{0,7},{1,2},{2,1},{3,4},{4,3},{5,6},{6,5},{7,0},{8,15},{9,10},{10,... | collective-permute-start | bytes 73736 | tf_op jit(solution)/shard_map/ppermute | solution.py:275
  10.5 0.5 %start.1 = (f32[4,2,3,8,128]{4,3,2,1,0:T(8,128)S(1)}, f32[4,2,3,8,128]{4,3,2,1,0:T(8,128)S(1)}) custom-call(f32[7,8,128]{2,1,0:T(8,128)S(1)} %tapers.1.coefs_ref, f32[4,2,3,8,128]{4,3,2,1,0:T(8,128)S(1)} %copy-done.1, f32[864,128]{1,0:T(8,128)S(1)} %bitcast.4), custom_call_target="tpu_custom_call" | custom-call | flops 1622016 | bytes 1622016 | tf_op jit(solution)/shard_map/start/pallas_call | solution.py:231
  11.0 0.4 %collective-permute-done.3.refs_4_ = f32[1,2,3,8,128]{4,3,2,1,0:T(8,128)S(1)} collective-permute-done((f32[1,2,3,8,128]{4,3,2,1,0:T(8,128)S(1)}, f32[1,2,3,8,128]{4,3,2,1,0:T(8,128)S(1)}, u32[]{:S(2)}, u32[]{:S(2)}) %collective-permute-start.3) | collective-permute-done | bytes 24608 | tf_op jit(solution)/shard_map/ppermute | solution.py:275
  11.4 0.7 %collective-permute-done.2.refs_3_ = f32[4,2,3,8,128]{4,3,2,1,0:T(8,128)S(1)} collective-permute-done((f32[4,2,3,8,128]{4,3,2,1,0:T(8,128)S(1)}, f32[4,2,3,8,128]{4,3,2,1,0:T(8,128)S(1)}, u32[]{:S(2)}, u32[]{:S(2)}) %collective-permute-start.2) | collective-permute-done | bytes 98336 | tf_op jit(solution)/shard_map/ppermute | solution.py:274
  12.2 0.2 third.1
  12.3 0.1 collective-permute-start.4
  12.4 0.4 %collective-permute-start.5 = (f32[4,2,3,8,128]{4,3,2,1,0:T(8,128)S(1)}, f32[4,2,3,8,128]{4,3,2,1,0:T(8,128)S(1)}, u32[]{:S(2)}, u32[]{:S(2)}) collective-permute-start(f32[4,2,3,8,128]{4,3,2,1,0:T(8,128)S(1)} %get-tuple-element.29), channel_id=1, source_target_pairs={{0,8},{1,9},{2,10},{3,11},{4,12},{5,13},{6,14},{7,15},{8,0},{9,1},... | collective-permute-start | bytes 294920 | tf_op jit(solution)/shard_map/ppermute | solution.py:273
  12.8 1.9 %collective-permute-start.6 = (f32[4,2,3,8,128]{4,3,2,1,0:T(8,128)S(1)}, f32[4,2,3,8,128]{4,3,2,1,0:T(8,128)S(1)}, u32[]{:S(2)}, u32[]{:S(2)}) collective-permute-start(f32[4,2,3,8,128]{4,3,2,1,0:T(8,128)S(1)} %get-tuple-element.30), channel_id=1, source_target_pairs={{0,24},{1,25},{2,26},{3,27},{4,28},{5,29},{6,30},{7,31},{8,9},{9,8... | collective-permute-start | bytes 294920 | tf_op jit(solution)/shard_map/ppermute | solution.py:274
  14.7 2.1 %collective-permute-start.7 = (f32[1,2,3,8,128]{4,3,2,1,0:T(8,128)S(1)}, f32[1,2,3,8,128]{4,3,2,1,0:T(8,128)S(1)}, u32[]{:S(2)}, u32[]{:S(2)}) collective-permute-start(f32[1,2,3,8,128]{4,3,2,1,0:T(8,128)S(1)} %get-tuple-element.31), channel_id=1, source_target_pairs={{0,7},{1,2},{2,1},{3,4},{4,3},{5,6},{6,5},{7,0},{8,15},{9,10},{10,... | collective-permute-start | bytes 73736 | tf_op jit(solution)/shard_map/ppermute | solution.py:275
  16.8 0.5 %local_1.1.refs_0_ = f32[4,2,3,8,128]{4,3,2,1,0:T(8,128)S(1)} custom-call(f32[4,2,3,8,128]{4,3,2,1,0:T(8,128)S(1)} %get-tuple-element.27.field_ref.refs_6_, f32[864,128]{1,0:T(8,128)S(1)} %bitcast.6), custom_call_target="tpu_custom_call" | custom-call | flops 1622016 | bytes 1622016 | tf_op jit(solution)/shard_map/local_1/pallas_call | solution.py:231
  17.3 1.5 %collective-permute-done.7.refs_4_ = f32[1,2,3,8,128]{4,3,2,1,0:T(8,128)S(1)} collective-permute-done((f32[1,2,3,8,128]{4,3,2,1,0:T(8,128)S(1)}, f32[1,2,3,8,128]{4,3,2,1,0:T(8,128)S(1)}, u32[]{:S(2)}, u32[]{:S(2)}) %collective-permute-start.7) | collective-permute-done | bytes 24608 | tf_op jit(solution)/shard_map/ppermute | solution.py:275
  18.8 1.3 %collective-permute-done.6.refs_3_ = f32[4,2,3,8,128]{4,3,2,1,0:T(8,128)S(1)} collective-permute-done((f32[4,2,3,8,128]{4,3,2,1,0:T(8,128)S(1)}, f32[4,2,3,8,128]{4,3,2,1,0:T(8,128)S(1)}, u32[]{:S(2)}, u32[]{:S(2)}) %collective-permute-start.6) | collective-permute-done | bytes 98336 | tf_op jit(solution)/shard_map/ppermute | solution.py:274
  20.1 0.2 second.1
  20.2 0.1 collective-permute-start.8
  20.4 1.8 %collective-permute-start.10 = (f32[4,2,3,8,128]{4,3,2,1,0:T(8,128)S(1)}, f32[4,2,3,8,128]{4,3,2,1,0:T(8,128)S(1)}, u32[]{:S(2)}, u32[]{:S(2)}) collective-permute-start(f32[4,2,3,8,128]{4,3,2,1,0:T(8,128)S(1)} %get-tuple-element.36), channel_id=1, source_target_pairs={{0,24},{1,25},{2,26},{3,27},{4,28},{5,29},{6,30},{7,31},{8,9},{9,8... | collective-permute-start | bytes 294920 | tf_op jit(solution)/shard_map/ppermute | solution.py:274
  22.2 2.1 %collective-permute-start.11 = (f32[1,2,3,8,128]{4,3,2,1,0:T(8,128)S(1)}, f32[1,2,3,8,128]{4,3,2,1,0:T(8,128)S(1)}, u32[]{:S(2)}, u32[]{:S(2)}) collective-permute-start(f32[1,2,3,8,128]{4,3,2,1,0:T(8,128)S(1)} %get-tuple-element.37), channel_id=1, source_target_pairs={{0,7},{1,2},{2,1},{3,4},{4,3},{5,6},{6,5},{7,0},{8,15},{9,10},{10,... | collective-permute-start | bytes 73736 | tf_op jit(solution)/shard_map/ppermute | solution.py:275
  24.3 0.5 %local_0.1.refs_0_ = f32[4,2,3,8,128]{4,3,2,1,0:T(8,128)S(1)} custom-call(f32[4,2,3,8,128]{4,3,2,1,0:T(8,128)S(1)} %get-tuple-element.33.field_ref, f32[864,128]{1,0:T(8,128)S(1)} %bitcast.8), custom_call_target="tpu_custom_call" | custom-call | flops 1622016 | bytes 1622016 | tf_op jit(solution)/shard_map/local_0/pallas_call | solution.py:231
  24.9 1.5 %collective-permute-done.11.refs_4_ = f32[1,2,3,8,128]{4,3,2,1,0:T(8,128)S(1)} collective-permute-done((f32[1,2,3,8,128]{4,3,2,1,0:T(8,128)S(1)}, f32[1,2,3,8,128]{4,3,2,1,0:T(8,128)S(1)}, u32[]{:S(2)}, u32[]{:S(2)}) %collective-permute-start.11) | collective-permute-done | bytes 24608 | tf_op jit(solution)/shard_map/ppermute | solution.py:275
  26.4 1.3 %collective-permute-done.10.refs_3_ = f32[4,2,3,8,128]{4,3,2,1,0:T(8,128)S(1)} collective-permute-done((f32[4,2,3,8,128]{4,3,2,1,0:T(8,128)S(1)}, f32[4,2,3,8,128]{4,3,2,1,0:T(8,128)S(1)}, u32[]{:S(2)}, u32[]{:S(2)}) %collective-permute-start.10) | collective-permute-done | bytes 98336 | tf_op jit(solution)/shard_map/ppermute | solution.py:274
  27.6 0.7 %last.1 = f32[4,2,3,8,128]{4,3,2,1,0:T(8,128)} custom-call(f32[7,8,128]{2,1,0:T(8,128)S(1)} %tapers.1.coefs_ref, f32[864,128]{1,0:T(8,128)S(1)} %bitcast.9, f32[4,2,3,8,128]{4,3,2,1,0:T(8,128)S(1)} %local_0.1.refs_0_, f32[4,2,3,8,128]{4,3,2,1,0:T(8,128)S(1)} %collective-permute-done.8.refs_1_, f32[4,2,3,8,128]{4,3,2,1,0:T(8,128)S(1)} %collective-permute-done.9.refs_2_, ...), custom_call_target="tpu_custom_call" | custom-call | flops 368640 | bytes 368640 | tf_op jit(solution)/shard_map/last/pallas_call | solution.py:231
  (12 shorter events, 0.1 us)
Async XLA Ops:
  0.0 10.5 %copy-start = (f32[4,3,4,2,3,3,128]{6,3,5,4,2,1,0:T(2,128)S(1)}, f32[4,3,4,2,3,3,128]{6,3,5,4,2,1,0:T(2,128)}, u32[]{:S(2)}) copy-start(f32[4,3,4,2,3,3,128]{6,3,5,4,2,1,0:T(2,128)} %param.6) | copy-start | bytes 1327108
  0.0 10.5 %copy-start.1 = (f32[4,2,3,8,128]{4,3,2,1,0:T(8,128)S(1)}, f32[4,2,3,8,128]{4,3,2,1,0:T(8,128)}, u32[]{:S(2)}) copy-start(f32[4,2,3,8,128]{4,3,2,1,0:T(8,128)} %adjoint_hbm.1) | copy-start | bytes 294916
  1.1 10.3 %collective-permute-start = (f32[4,2,3,8,128]{4,3,2,1,0:T(8,128)S(1)}, f32[4,2,3,8,128]{4,3,2,1,0:T(8,128)S(1)}, u32[]{:S(2)}, u32[]{:S(2)}) collective-permute-start(f32[4,2,3,8,128]{4,3,2,1,0:T(8,128)S(1)} %get-tuple-element.23), channel_id=1, source_target_pairs={{0,1},{1,0},{2,3},{3,2},{4,5},{5,4},{6,7},{7,6},{8,16},{9,17},{10,... | collective-permute-start | bytes 294920 | tf_op jit(solution)/shard_map/ppermute | solution.py:272
  1.6 9.8 %collective-permute-start.1 = (f32[4,2,3,8,128]{4,3,2,1,0:T(8,128)S(1)}, f32[4,2,3,8,128]{4,3,2,1,0:T(8,128)S(1)}, u32[]{:S(2)}, u32[]{:S(2)}) collective-permute-start(f32[4,2,3,8,128]{4,3,2,1,0:T(8,128)S(1)} %get-tuple-element.24), channel_id=1, source_target_pairs={{0,8},{1,9},{2,10},{3,11},{4,12},{5,13},{6,14},{7,15},{8,0},{9,1},... | collective-permute-start | bytes 294920 | tf_op jit(solution)/shard_map/ppermute | solution.py:273
  5.8 6.4 %collective-permute-start.2 = (f32[4,2,3,8,128]{4,3,2,1,0:T(8,128)S(1)}, f32[4,2,3,8,128]{4,3,2,1,0:T(8,128)S(1)}, u32[]{:S(2)}, u32[]{:S(2)}) collective-permute-start(f32[4,2,3,8,128]{4,3,2,1,0:T(8,128)S(1)} %get-tuple-element.25), channel_id=1, source_target_pairs={{0,24},{1,25},{2,26},{3,27},{4,28},{5,29},{6,30},{7,31},{8,9},{9,8... | collective-permute-start | bytes 294920 | tf_op jit(solution)/shard_map/ppermute | solution.py:274
  7.1 4.3 %collective-permute-start.3 = (f32[1,2,3,8,128]{4,3,2,1,0:T(8,128)S(1)}, f32[1,2,3,8,128]{4,3,2,1,0:T(8,128)S(1)}, u32[]{:S(2)}, u32[]{:S(2)}) collective-permute-start(f32[1,2,3,8,128]{4,3,2,1,0:T(8,128)S(1)} %get-tuple-element.26), channel_id=1, source_target_pairs={{0,7},{1,2},{2,1},{3,4},{4,3},{5,6},{6,5},{7,0},{8,15},{9,10},{10,... | collective-permute-start | bytes 73736 | tf_op jit(solution)/shard_map/ppermute | solution.py:275
  12.3 6.5 %collective-permute-start.4 = (f32[4,2,3,8,128]{4,3,2,1,0:T(8,128)S(1)}, f32[4,2,3,8,128]{4,3,2,1,0:T(8,128)S(1)}, u32[]{:S(2)}, u32[]{:S(2)}) collective-permute-start(f32[4,2,3,8,128]{4,3,2,1,0:T(8,128)S(1)} %get-tuple-element.28), channel_id=1, source_target_pairs={{0,1},{1,0},{2,3},{3,2},{4,5},{5,4},{6,7},{7,6},{8,16},{9,17},{10,... | collective-permute-start | bytes 294920 | tf_op jit(solution)/shard_map/ppermute | solution.py:272
  12.4 6.4 %collective-permute-start.5 = (f32[4,2,3,8,128]{4,3,2,1,0:T(8,128)S(1)}, f32[4,2,3,8,128]{4,3,2,1,0:T(8,128)S(1)}, u32[]{:S(2)}, u32[]{:S(2)}) collective-permute-start(f32[4,2,3,8,128]{4,3,2,1,0:T(8,128)S(1)} %get-tuple-element.29), channel_id=1, source_target_pairs={{0,8},{1,9},{2,10},{3,11},{4,12},{5,13},{6,14},{7,15},{8,0},{9,1},... | collective-permute-start | bytes 294920 | tf_op jit(solution)/shard_map/ppermute | solution.py:273
  12.8 7.3 %collective-permute-start.6 = (f32[4,2,3,8,128]{4,3,2,1,0:T(8,128)S(1)}, f32[4,2,3,8,128]{4,3,2,1,0:T(8,128)S(1)}, u32[]{:S(2)}, u32[]{:S(2)}) collective-permute-start(f32[4,2,3,8,128]{4,3,2,1,0:T(8,128)S(1)} %get-tuple-element.30), channel_id=1, source_target_pairs={{0,24},{1,25},{2,26},{3,27},{4,28},{5,29},{6,30},{7,31},{8,9},{9,8... | collective-permute-start | bytes 294920 | tf_op jit(solution)/shard_map/ppermute | solution.py:274
  14.7 4.2 %collective-permute-start.7 = (f32[1,2,3,8,128]{4,3,2,1,0:T(8,128)S(1)}, f32[1,2,3,8,128]{4,3,2,1,0:T(8,128)S(1)}, u32[]{:S(2)}, u32[]{:S(2)}) collective-permute-start(f32[1,2,3,8,128]{4,3,2,1,0:T(8,128)S(1)} %get-tuple-element.31), channel_id=1, source_target_pairs={{0,7},{1,2},{2,1},{3,4},{4,3},{5,6},{6,5},{7,0},{8,15},{9,10},{10,... | collective-permute-start | bytes 73736 | tf_op jit(solution)/shard_map/ppermute | solution.py:275
  20.2 6.1 %collective-permute-start.8 = (f32[4,2,3,8,128]{4,3,2,1,0:T(8,128)S(1)}, f32[4,2,3,8,128]{4,3,2,1,0:T(8,128)S(1)}, u32[]{:S(2)}, u32[]{:S(2)}) collective-permute-start(f32[4,2,3,8,128]{4,3,2,1,0:T(8,128)S(1)} %get-tuple-element.34), channel_id=1, source_target_pairs={{0,1},{1,0},{2,3},{3,2},{4,5},{5,4},{6,7},{7,6},{8,16},{9,17},{10,... | collective-permute-start | bytes 294920 | tf_op jit(solution)/shard_map/ppermute | solution.py:272
  20.3 6.1 %collective-permute-start.9 = (f32[4,2,3,8,128]{4,3,2,1,0:T(8,128)S(1)}, f32[4,2,3,8,128]{4,3,2,1,0:T(8,128)S(1)}, u32[]{:S(2)}, u32[]{:S(2)}) collective-permute-start(f32[4,2,3,8,128]{4,3,2,1,0:T(8,128)S(1)} %get-tuple-element.35), channel_id=1, source_target_pairs={{0,8},{1,9},{2,10},{3,11},{4,12},{5,13},{6,14},{7,15},{8,0},{9,1},... | collective-permute-start | bytes 294920 | tf_op jit(solution)/shard_map/ppermute | solution.py:273
  20.4 7.2 %collective-permute-start.10 = (f32[4,2,3,8,128]{4,3,2,1,0:T(8,128)S(1)}, f32[4,2,3,8,128]{4,3,2,1,0:T(8,128)S(1)}, u32[]{:S(2)}, u32[]{:S(2)}) collective-permute-start(f32[4,2,3,8,128]{4,3,2,1,0:T(8,128)S(1)} %get-tuple-element.36), channel_id=1, source_target_pairs={{0,24},{1,25},{2,26},{3,27},{4,28},{5,29},{6,30},{7,31},{8,9},{9,8... | collective-permute-start | bytes 294920 | tf_op jit(solution)/shard_map/ppermute | solution.py:274
  22.2 4.2 %collective-permute-start.11 = (f32[1,2,3,8,128]{4,3,2,1,0:T(8,128)S(1)}, f32[1,2,3,8,128]{4,3,2,1,0:T(8,128)S(1)}, u32[]{:S(2)}, u32[]{:S(2)}) collective-permute-start(f32[1,2,3,8,128]{4,3,2,1,0:T(8,128)S(1)} %get-tuple-element.37), channel_id=1, source_target_pairs={{0,7},{1,2},{2,1},{3,4},{4,3},{5,6},{6,5},{7,0},{8,15},{9,10},{10,... | collective-permute-start | bytes 73736 | tf_op jit(solution)/shard_map/ppermute | solution.py:275

commit v13 on v8

--- a/solution.py
+++ b/solution.py
@@ -126,7 +126,7 @@
     at_last = x_pos == LX - 1
     at_first = x_pos == 0
 
-    def one(row, carry):
+    for row in range(rows):
         here = load_field(field_ref, row)
         ahead = combine(lambda v: jnp.where(at_last, roll(v, LX - 1), roll(v, -1)), here)
         ahead_x, hop = transport(links_at(links_ref, row, link_set, 0), ahead, here)
@@ -136,20 +136,12 @@
         ahead = combine(lambda v: roll(v, -LX), here)
         ahead_y, hop = transport(links_at(links_ref, row, link_set, 1), ahead, here)
         total = combine(lambda s, f, h: s + f + roll(h, LX), total, ahead_y, hop)
+        if row > 0:
+            total = combine(lambda s, h: s + h, total, earlier)
+        if row < rows - 1:
+            ahead_t, earlier = transport(links_at(links_ref, row, link_set, 3), load_field(field_ref, row + 1), here)
+            total = combine(lambda s, f: s + f, total, ahead_t)
         store_field(sum_ref, row, total)
-        return carry
-
-    lax.fori_loop(0, rows, one, 0)
-
-    def between(row, carry):
-        ahead_t, hop = transport(
-            links_at(links_ref, row, link_set, 3), load_field(field_ref, row + 1), load_field(field_ref, row)
-        )
-        store_field(sum_ref, row, combine(lambda s, f: s + f, load_field(sum_ref, row), ahead_t))
-        store_field(sum_ref, row + 1, combine(lambda s, h: s + h, load_field(sum_ref, row + 1), hop))
-        return carry
-
-    lax.fori_loop(0, rows - 1, between, 0)
 
 
 def arrived_sum(links_ref, link_set, row, rows, arrivals, coefs_ref=None):
@@ -205,21 +197,26 @@
 
 
 def last_kernel(rows, coefs_ref, links_ref, *refs):
-    arrivals, (base_ref, out_ref) = refs[:5], refs[5:]
+    arrivals, (base_ref, out_hbm, out_ref, sems) = refs[:5], refs[5:]
+    copies = []
     for row in range(rows):
         inside, eps = coefs_ref[row + 1], coefs_ref[rows + 2]
         total = arrived_sum(links_ref, 0, row, rows, arrivals)
         store_field(out_ref, row, combine(lambda p, s: p + inside * (eps * s), load_field(base_ref, row), total))
-
-
-def call(kernel, name, operands, out_shapes, matvecs, space=pltpu.VMEM, scratch=()):
-    vmem = pl.BlockSpec(memory_space=pltpu.VMEM)
+        copies.append(pltpu.make_async_copy(out_ref.at[row], out_hbm.at[row], sems.at[row]))
+        copies[-1].start()
+    for copy in copies:
+        copy.wait()
+
+
+def call(kernel, name, operands, out_shapes, matvecs, space=pltpu.VMEM, scratch=(), out_space=pltpu.VMEM):
+    out_spec = pl.BlockSpec(memory_space=out_space)
     return pl.pallas_call(
         kernel,
         name=name,
         out_shape=out_shapes,
         in_specs=[pl.BlockSpec(memory_space=space)] * len(operands),
-        out_specs=jax.tree.map(lambda _: vmem, out_shapes),
+        out_specs=jax.tree.map(lambda _: out_spec, out_shapes),
         scratch_shapes=scratch,
         cost_estimate=pl.CostEstimate(flops=matvecs * 72 * 1024, bytes_accessed=4096 * 18 * matvecs, transcendentals=0),
         compiler_params=pltpu.CompilerParams(vmem_limit_bytes=16 * 2**20),
@@ -285,7 +282,8 @@
     )
     arrived = sent_on(*sending)
     return call(
-        functools.partial(last_kernel, rows), "last", (coefs, links, local(0, mixed)) + arrived + (base,), whole, 5
+        functools.partial(last_kernel, rows), "last", (coefs, links, local(0, mixed)) + arrived + (base,), whole, 5,
+        scratch=[pltpu.VMEM(adjoint.shape, jnp.float32), pltpu.SemaphoreType.DMA((rows,))], out_space=pltpu.HBM,
     )
 
 

time: 27.5 us -> 27.3 us (level)
  Pallas kernels: 3.64 us -> 2.95 us
  waiting for transfers between devices: 5.92 us -> 6.24 us
    ppermute x3, waiting for transfers between devices: 4.58 us -> 5.31 us  [sent_on(): outer = lax.ppermute(outer, 'gz', outer_pairs)]
    pallas_call x8, Pallas kernels: 3.64 us -> 2.95 us  [call(): pl.pallas_call(kernel, name=name, out_shape=out_shapes, in_specs=[pl.Bloc...]
    ppermute x3, waiting for transfers between devices: 1.33 us -> 0.91 us  [sent_on(): far = lax.ppermute(far, 'gz', far_pairs)]
  transfers between devices with their start and end apart: 12 -> 12, of which waited for: 6 -> 5; matrix products, arithmetic and copies ran while one was open for 0% -> 0% of each run, Pallas kernels for 6% -> 3%
where the time goes in v13:
time: 27.3 us; the launch traced here: 27.1 us
  starting transfers between devices  15.9 us (58%)
  waiting for transfers between devices  6.24 us (23%)
  Pallas kernels  2.95 us (11%)
  between operations  2.01 us (7%)
    ppermute x3, starting transfers between devices, sent_on(): far = lax.ppermute(far, 'gz', far_pairs)  6.73 us
    ppermute x3, waiting for transfers between devices, sent_on(): outer = lax.ppermute(outer, 'gz', outer_pairs)  5.31 us
    ppermute x3, starting transfers between devices, sent_on(): near = lax.ppermute(near, 'gz', near_pairs)  4.37 us
    ppermute x3, starting transfers between devices, sent_on(): inner = lax.ppermute(inner, 'gz', inner_pairs)  3.49 us
    pallas_call x8, Pallas kernels, call(): pl.pallas_call(kernel, name=name, out_shape=out_shapes, in_specs=[pl.Bloc...  2.95 us
    ppermute x3, starting transfers between devices, sent_on(): outer = lax.ppermute(outer, 'gz', outer_pairs)  1.33 us
    ppermute x3, waiting for transfers between devices, sent_on(): far = lax.ppermute(far, 'gz', far_pairs)  0.91 us
  transfers between devices with their start and end apart: 12, of which 5 were waited for; matrix products, arithmetic and copies ran while one was open for 0% of the time, Pallas kernels for 3%

profile of v13, /device:TPU:0, one launch (start us, length us, event | category | flops | bytes accessed | tf_op | source)
XLA Modules:
  0.0 27.1 jit_solution(3556909007759700784)
XLA Ops:
  0.0 1.1 %begin.1 = (f32[4,2,3,8,128]{4,3,2,1,0:T(8,128)S(1)}, f32[4,2,3,8,128]{4,3,2,1,0:T(8,128)S(1)}, f32[1,2,3,8,128]{4,3,2,1,0:T(8,128)S(1)}, f32[1,2,3,8,128]{4,3,2,1,0:T(8,128)S(1)}) custom-call(f32[4,2,3,8,128]{4,3,2,1,0:T(8,128)} %adjoint_hbm.1, f32[864,128]{1,0:T(8,128)} %bitcast.3), custom_call_target="tpu_custom_call" | custom-call | flops 368640 | bytes 368640 | tf_op jit(solution)/shard_map/begin/pallas_call | solution.py:214
  1.1 3.1 %collective-permute-start = (f32[4,2,3,8,128]{4,3,2,1,0:T(8,128)S(1)}, f32[4,2,3,8,128]{4,3,2,1,0:T(8,128)S(1)}, u32[]{:S(2)}, u32[]{:S(2)}) collective-permute-start(f32[4,2,3,8,128]{4,3,2,1,0:T(8,128)S(1)} %get-tuple-element.23), channel_id=1, source_target_pairs={{0,8},{1,9},{2,10},{3,11},{4,12},{5,13},{6,14},{7,15},{8,0},{9,1},... | collective-permute-start | bytes 294920 | tf_op jit(solution)/shard_map/ppermute | solution.py:247
  4.2 2.5 %collective-permute-start.1 = (f32[4,2,3,8,128]{4,3,2,1,0:T(8,128)S(1)}, f32[4,2,3,8,128]{4,3,2,1,0:T(8,128)S(1)}, u32[]{:S(2)}, u32[]{:S(2)}) collective-permute-start(f32[4,2,3,8,128]{4,3,2,1,0:T(8,128)S(1)} %get-tuple-element.24), channel_id=1, source_target_pairs={{0,24},{1,25},{2,26},{3,27},{4,28},{5,29},{6,30},{7,31},{8,16},{9,... | collective-permute-start | bytes 294920 | tf_op jit(solution)/shard_map/ppermute | solution.py:248
  6.7 1.3 %collective-permute-start.2 = (f32[1,2,3,8,128]{4,3,2,1,0:T(8,128)S(1)}, f32[1,2,3,8,128]{4,3,2,1,0:T(8,128)S(1)}, u32[]{:S(2)}, u32[]{:S(2)}) collective-permute-start(f32[1,2,3,8,128]{4,3,2,1,0:T(8,128)S(1)} %get-tuple-element.25), channel_id=1, source_target_pairs={{0,7},{1,2},{2,1},{3,4},{4,3},{5,6},{6,5},{7,0},{8,15},{9,10},{10,... | collective-permute-start | bytes 73736 | tf_op jit(solution)/shard_map/ppermute | solution.py:249
  8.0 0.3 %collective-permute-start.3 = (f32[1,2,3,8,128]{4,3,2,1,0:T(8,128)S(1)}, f32[1,2,3,8,128]{4,3,2,1,0:T(8,128)S(1)}, u32[]{:S(2)}, u32[]{:S(2)}) collective-permute-start(f32[1,2,3,8,128]{4,3,2,1,0:T(8,128)S(1)} %get-tuple-element.26), channel_id=1, source_target_pairs={{0,1},{1,0},{2,3},{3,2},{4,5},{5,4},{6,7},{7,6},{8,9},{9,8},{10,11... | collective-permute-start | bytes 73736 | tf_op jit(solution)/shard_map/ppermute | solution.py:250
  10.3 0.3 start.1
  10.5 0.4 %collective-permute-done.2.refs_3_ = f32[1,2,3,8,128]{4,3,2,1,0:T(8,128)S(1)} collective-permute-done((f32[1,2,3,8,128]{4,3,2,1,0:T(8,128)S(1)}, f32[1,2,3,8,128]{4,3,2,1,0:T(8,128)S(1)}, u32[]{:S(2)}, u32[]{:S(2)}) %collective-permute-start.2) | collective-permute-done | bytes 24608 | tf_op jit(solution)/shard_map/ppermute | solution.py:249
  11.0 0.4 %collective-permute-done.1.refs_2_ = f32[4,2,3,8,128]{4,3,2,1,0:T(8,128)S(1)} collective-permute-done((f32[4,2,3,8,128]{4,3,2,1,0:T(8,128)S(1)}, f32[4,2,3,8,128]{4,3,2,1,0:T(8,128)S(1)}, u32[]{:S(2)}, u32[]{:S(2)}) %collective-permute-start.1) | collective-permute-done | bytes 98336 | tf_op jit(solution)/shard_map/ppermute | solution.py:248
  11.3 0.2 third.1
  11.5 0.7 %collective-permute-start.4 = (f32[4,2,3,8,128]{4,3,2,1,0:T(8,128)S(1)}, f32[4,2,3,8,128]{4,3,2,1,0:T(8,128)S(1)}, u32[]{:S(2)}, u32[]{:S(2)}) collective-permute-start(f32[4,2,3,8,128]{4,3,2,1,0:T(8,128)S(1)} %get-tuple-element.28), channel_id=1, source_target_pairs={{0,8},{1,9},{2,10},{3,11},{4,12},{5,13},{6,14},{7,15},{8,0},{9,1},... | collective-permute-start | bytes 294920 | tf_op jit(solution)/shard_map/ppermute | solution.py:247
  12.2 2.6 %collective-permute-start.5 = (f32[4,2,3,8,128]{4,3,2,1,0:T(8,128)S(1)}, f32[4,2,3,8,128]{4,3,2,1,0:T(8,128)S(1)}, u32[]{:S(2)}, u32[]{:S(2)}) collective-permute-start(f32[4,2,3,8,128]{4,3,2,1,0:T(8,128)S(1)} %get-tuple-element.29), channel_id=1, source_target_pairs={{0,24},{1,25},{2,26},{3,27},{4,28},{5,29},{6,30},{7,31},{8,16},{9,... | collective-permute-start | bytes 294920 | tf_op jit(solution)/shard_map/ppermute | solution.py:248
  14.8 1.6 %collective-permute-start.7 = (f32[1,2,3,8,128]{4,3,2,1,0:T(8,128)S(1)}, f32[1,2,3,8,128]{4,3,2,1,0:T(8,128)S(1)}, u32[]{:S(2)}, u32[]{:S(2)}) collective-permute-start(f32[1,2,3,8,128]{4,3,2,1,0:T(8,128)S(1)} %get-tuple-element.31), channel_id=1, source_target_pairs={{0,1},{1,0},{2,3},{3,2},{4,5},{5,4},{6,7},{7,6},{8,9},{9,8},{10,11... | collective-permute-start | bytes 73736 | tf_op jit(solution)/shard_map/ppermute | solution.py:250
  16.4 0.3 local_1.1.refs_0_
  16.7 2.4 %collective-permute-done.6.refs_3_ = f32[1,2,3,8,128]{4,3,2,1,0:T(8,128)S(1)} collective-permute-done((f32[1,2,3,8,128]{4,3,2,1,0:T(8,128)S(1)}, f32[1,2,3,8,128]{4,3,2,1,0:T(8,128)S(1)}, u32[]{:S(2)}, u32[]{:S(2)}) %collective-permute-start.6) | collective-permute-done | bytes 24608 | tf_op jit(solution)/shard_map/ppermute | solution.py:249
  19.1 0.0 collective-permute-done.7.refs_4_
  19.1 0.0 collective-permute-done.4.refs_1_
  19.1 0.2 second.1
  19.3 0.6 %collective-permute-start.8 = (f32[4,2,3,8,128]{4,3,2,1,0:T(8,128)S(1)}, f32[4,2,3,8,128]{4,3,2,1,0:T(8,128)S(1)}, u32[]{:S(2)}, u32[]{:S(2)}) collective-permute-start(f32[4,2,3,8,128]{4,3,2,1,0:T(8,128)S(1)} %get-tuple-element.34), channel_id=1, source_target_pairs={{0,8},{1,9},{2,10},{3,11},{4,12},{5,13},{6,14},{7,15},{8,0},{9,1},... | collective-permute-start | bytes 294920 | tf_op jit(solution)/shard_map/ppermute | solution.py:247
  19.9 1.6 %collective-permute-start.9 = (f32[4,2,3,8,128]{4,3,2,1,0:T(8,128)S(1)}, f32[4,2,3,8,128]{4,3,2,1,0:T(8,128)S(1)}, u32[]{:S(2)}, u32[]{:S(2)}) collective-permute-start(f32[4,2,3,8,128]{4,3,2,1,0:T(8,128)S(1)} %get-tuple-element.35), channel_id=1, source_target_pairs={{0,24},{1,25},{2,26},{3,27},{4,28},{5,29},{6,30},{7,31},{8,16},{9,... | collective-permute-start | bytes 294920 | tf_op jit(solution)/shard_map/ppermute | solution.py:248
  21.5 1.6 %collective-permute-start.11 = (f32[1,2,3,8,128]{4,3,2,1,0:T(8,128)S(1)}, f32[1,2,3,8,128]{4,3,2,1,0:T(8,128)S(1)}, u32[]{:S(2)}, u32[]{:S(2)}) collective-permute-start(f32[1,2,3,8,128]{4,3,2,1,0:T(8,128)S(1)} %get-tuple-element.37), channel_id=1, source_target_pairs={{0,1},{1,0},{2,3},{3,2},{4,5},{5,4},{6,7},{7,6},{8,9},{9,8},{10,11... | collective-permute-start | bytes 73736 | tf_op jit(solution)/shard_map/ppermute | solution.py:250
  23.1 0.3 local_0.1.refs_0_
  23.4 2.4 %collective-permute-done.10.refs_3_ = f32[1,2,3,8,128]{4,3,2,1,0:T(8,128)S(1)} collective-permute-done((f32[1,2,3,8,128]{4,3,2,1,0:T(8,128)S(1)}, f32[1,2,3,8,128]{4,3,2,1,0:T(8,128)S(1)}, u32[]{:S(2)}, u32[]{:S(2)}) %collective-permute-start.10) | collective-permute-done | bytes 24608 | tf_op jit(solution)/shard_map/ppermute | solution.py:249
  25.8 0.5 %collective-permute-done.9.refs_2_ = f32[4,2,3,8,128]{4,3,2,1,0:T(8,128)S(1)} collective-permute-done((f32[4,2,3,8,128]{4,3,2,1,0:T(8,128)S(1)}, f32[4,2,3,8,128]{4,3,2,1,0:T(8,128)S(1)}, u32[]{:S(2)}, u32[]{:S(2)}) %collective-permute-start.9) | collective-permute-done | bytes 98336 | tf_op jit(solution)/shard_map/ppermute | solution.py:248
  26.4 0.7 %last.1 = f32[4,2,3,8,128]{4,3,2,1,0:T(8,128)} custom-call(f32[7,8,128]{2,1,0:T(8,128)S(1)} %tapers.1.coefs_ref, f32[864,128]{1,0:T(8,128)S(1)} %bitcast.9, f32[4,2,3,8,128]{4,3,2,1,0:T(8,128)S(1)} %local_0.1.refs_0_, f32[4,2,3,8,128]{4,3,2,1,0:T(8,128)S(1)} %collective-permute-done.8.refs_1_, f32[4,2,3,8,128]{4,3,2,1,0:T(8,128)S(1)} %collective-permute-done.9.refs_2_, ...), custom_call_target="tpu_custom_call" | custom-call | flops 368640 | bytes 368640 | tf_op jit(solution)/shard_map/last/pallas_call | solution.py:214
  (12 shorter events, 0.1 us)
Async XLA Ops:
  0.0 10.2 %copy-start = (f32[4,3,4,2,3,3,128]{6,3,5,4,2,1,0:T(2,128)S(1)}, f32[4,3,4,2,3,3,128]{6,3,5,4,2,1,0:T(2,128)}, u32[]{:S(2)}) copy-start(f32[4,3,4,2,3,3,128]{6,3,5,4,2,1,0:T(2,128)} %param.6) | copy-start | bytes 1327108
  0.0 10.2 %copy-start.1 = (f32[4,2,3,8,128]{4,3,2,1,0:T(8,128)S(1)}, f32[4,2,3,8,128]{4,3,2,1,0:T(8,128)}, u32[]{:S(2)}) copy-start(f32[4,2,3,8,128]{4,3,2,1,0:T(8,128)} %adjoint_hbm.1) | copy-start | bytes 294916
  1.1 9.9 %collective-permute-start = (f32[4,2,3,8,128]{4,3,2,1,0:T(8,128)S(1)}, f32[4,2,3,8,128]{4,3,2,1,0:T(8,128)S(1)}, u32[]{:S(2)}, u32[]{:S(2)}) collective-permute-start(f32[4,2,3,8,128]{4,3,2,1,0:T(8,128)S(1)} %get-tuple-element.23), channel_id=1, source_target_pairs={{0,8},{1,9},{2,10},{3,11},{4,12},{5,13},{6,14},{7,15},{8,0},{9,1},... | collective-permute-start | bytes 294920 | tf_op jit(solution)/shard_map/ppermute | solution.py:247
  4.2 7.2 %collective-permute-start.1 = (f32[4,2,3,8,128]{4,3,2,1,0:T(8,128)S(1)}, f32[4,2,3,8,128]{4,3,2,1,0:T(8,128)S(1)}, u32[]{:S(2)}, u32[]{:S(2)}) collective-permute-start(f32[4,2,3,8,128]{4,3,2,1,0:T(8,128)S(1)} %get-tuple-element.24), channel_id=1, source_target_pairs={{0,24},{1,25},{2,26},{3,27},{4,28},{5,29},{6,30},{7,31},{8,16},{9,... | collective-permute-start | bytes 294920 | tf_op jit(solution)/shard_map/ppermute | solution.py:248
  6.7 4.3 %collective-permute-start.2 = (f32[1,2,3,8,128]{4,3,2,1,0:T(8,128)S(1)}, f32[1,2,3,8,128]{4,3,2,1,0:T(8,128)S(1)}, u32[]{:S(2)}, u32[]{:S(2)}) collective-permute-start(f32[1,2,3,8,128]{4,3,2,1,0:T(8,128)S(1)} %get-tuple-element.25), channel_id=1, source_target_pairs={{0,7},{1,2},{2,1},{3,4},{4,3},{5,6},{6,5},{7,0},{8,15},{9,10},{10,... | collective-permute-start | bytes 73736 | tf_op jit(solution)/shard_map/ppermute | solution.py:249
  8.0 3.0 %collective-permute-start.3 = (f32[1,2,3,8,128]{4,3,2,1,0:T(8,128)S(1)}, f32[1,2,3,8,128]{4,3,2,1,0:T(8,128)S(1)}, u32[]{:S(2)}, u32[]{:S(2)}) collective-permute-start(f32[1,2,3,8,128]{4,3,2,1,0:T(8,128)S(1)} %get-tuple-element.26), channel_id=1, source_target_pairs={{0,1},{1,0},{2,3},{3,2},{4,5},{5,4},{6,7},{7,6},{8,9},{9,8},{10,11... | collective-permute-start | bytes 73736 | tf_op jit(solution)/shard_map/ppermute | solution.py:250
  11.5 7.6 %collective-permute-start.4 = (f32[4,2,3,8,128]{4,3,2,1,0:T(8,128)S(1)}, f32[4,2,3,8,128]{4,3,2,1,0:T(8,128)S(1)}, u32[]{:S(2)}, u32[]{:S(2)}) collective-permute-start(f32[4,2,3,8,128]{4,3,2,1,0:T(8,128)S(1)} %get-tuple-element.28), channel_id=1, source_target_pairs={{0,8},{1,9},{2,10},{3,11},{4,12},{5,13},{6,14},{7,15},{8,0},{9,1},... | collective-permute-start | bytes 294920 | tf_op jit(solution)/shard_map/ppermute | solution.py:247
  12.2 7.0 %collective-permute-start.5 = (f32[4,2,3,8,128]{4,3,2,1,0:T(8,128)S(1)}, f32[4,2,3,8,128]{4,3,2,1,0:T(8,128)S(1)}, u32[]{:S(2)}, u32[]{:S(2)}) collective-permute-start(f32[4,2,3,8,128]{4,3,2,1,0:T(8,128)S(1)} %get-tuple-element.29), channel_id=1, source_target_pairs={{0,24},{1,25},{2,26},{3,27},{4,28},{5,29},{6,30},{7,31},{8,16},{9,... | collective-permute-start | bytes 294920 | tf_op jit(solution)/shard_map/ppermute | solution.py:248
  14.8 4.3 %collective-permute-start.6 = (f32[1,2,3,8,128]{4,3,2,1,0:T(8,128)S(1)}, f32[1,2,3,8,128]{4,3,2,1,0:T(8,128)S(1)}, u32[]{:S(2)}, u32[]{:S(2)}) collective-permute-start(f32[1,2,3,8,128]{4,3,2,1,0:T(8,128)S(1)} %get-tuple-element.30), channel_id=1, source_target_pairs={{0,7},{1,2},{2,1},{3,4},{4,3},{5,6},{6,5},{7,0},{8,15},{9,10},{10,... | collective-permute-start | bytes 73736 | tf_op jit(solution)/shard_map/ppermute | solution.py:249
  14.8 4.3 %collective-permute-start.7 = (f32[1,2,3,8,128]{4,3,2,1,0:T(8,128)S(1)}, f32[1,2,3,8,128]{4,3,2,1,0:T(8,128)S(1)}, u32[]{:S(2)}, u32[]{:S(2)}) collective-permute-start(f32[1,2,3,8,128]{4,3,2,1,0:T(8,128)S(1)} %get-tuple-element.31), channel_id=1, source_target_pairs={{0,1},{1,0},{2,3},{3,2},{4,5},{5,4},{6,7},{7,6},{8,9},{9,8},{10,11... | collective-permute-start | bytes 73736 | tf_op jit(solution)/shard_map/ppermute | solution.py:250
  19.3 6.5 %collective-permute-start.8 = (f32[4,2,3,8,128]{4,3,2,1,0:T(8,128)S(1)}, f32[4,2,3,8,128]{4,3,2,1,0:T(8,128)S(1)}, u32[]{:S(2)}, u32[]{:S(2)}) collective-permute-start(f32[4,2,3,8,128]{4,3,2,1,0:T(8,128)S(1)} %get-tuple-element.34), channel_id=1, source_target_pairs={{0,8},{1,9},{2,10},{3,11},{4,12},{5,13},{6,14},{7,15},{8,0},{9,1},... | collective-permute-start | bytes 294920 | tf_op jit(solution)/shard_map/ppermute | solution.py:247
  19.9 6.5 %collective-permute-start.9 = (f32[4,2,3,8,128]{4,3,2,1,0:T(8,128)S(1)}, f32[4,2,3,8,128]{4,3,2,1,0:T(8,128)S(1)}, u32[]{:S(2)}, u32[]{:S(2)}) collective-permute-start(f32[4,2,3,8,128]{4,3,2,1,0:T(8,128)S(1)} %get-tuple-element.35), channel_id=1, source_target_pairs={{0,24},{1,25},{2,26},{3,27},{4,28},{5,29},{6,30},{7,31},{8,16},{9,... | collective-permute-start | bytes 294920 | tf_op jit(solution)/shard_map/ppermute | solution.py:248
  21.5 4.3 %collective-permute-start.10 = (f32[1,2,3,8,128]{4,3,2,1,0:T(8,128)S(1)}, f32[1,2,3,8,128]{4,3,2,1,0:T(8,128)S(1)}, u32[]{:S(2)}, u32[]{:S(2)}) collective-permute-start(f32[1,2,3,8,128]{4,3,2,1,0:T(8,128)S(1)} %get-tuple-element.36), channel_id=1, source_target_pairs={{0,7},{1,2},{2,1},{3,4},{4,3},{5,6},{6,5},{7,0},{8,15},{9,10},{10,... | collective-permute-start | bytes 73736 | tf_op jit(solution)/shard_map/ppermute | solution.py:249
  21.5 4.3 %collective-permute-start.11 = (f32[1,2,3,8,128]{4,3,2,1,0:T(8,128)S(1)}, f32[1,2,3,8,128]{4,3,2,1,0:T(8,128)S(1)}, u32[]{:S(2)}, u32[]{:S(2)}) collective-permute-start(f32[1,2,3,8,128]{4,3,2,1,0:T(8,128)S(1)} %get-tuple-element.37), channel_id=1, source_target_pairs={{0,1},{1,0},{2,3},{3,2},{4,5},{5,4},{6,7},{7,6},{8,9},{9,8},{10,11... | collective-permute-start | bytes 73736 | tf_op jit(solution)/shard_map/ppermute | solution.py:250

commit v14 on v13

--- a/solution.py
+++ b/solution.py
@@ -68,14 +68,17 @@
     return plane, first_pos, lax.rem(plane, 2) == 1, lax.rem(first_pos // rows, 2) == 1
 
 
-def taper_kernel(rows, source_ref, width_ref, steps_ref, coefs_ref):
+def taper_kernel(rows, source_ref, width_ref, coefs_ref):
     _, first_pos, _, _ = place(rows)
     ones = jnp.ones((8, 128), jnp.float32)
     per_width = ones * width_ref[0].astype(jnp.float32)
     for i in range(rows + 2):
         distance = ones * (first_pos + i - 1 - source_ref[0]).astype(jnp.float32) / per_width
         coefs_ref[i] = 1.0 / (1.0 + distance * distance)
-    coefs_ref[rows + 2] = 0.25 / (ones * steps_ref[0].astype(jnp.float32))
+
+
+def eps_kernel(steps_ref, eps_ref):
+    eps_ref[...] = 0.25 / (jnp.ones((8, 128), jnp.float32) * steps_ref[0].astype(jnp.float32))
 
 
 def store_z(rows, matrices, row, field, far_ref, near_ref):
@@ -174,21 +177,24 @@
 def third_kernel(rows, coefs_ref, links_ref, *refs):
     arrivals, (third_ref, far_ref, near_ref, outer_ref, inner_ref) = refs[:5], refs[5:]
     for row in range(rows):
-        inside, eps = coefs_ref[row + 1], coefs_ref[rows + 2]
+        inside = coefs_ref[row + 1]
         total = arrived_sum(links_ref, 2, row, rows, arrivals, coefs_ref)
-        third = combine(lambda s: 0.75 * (inside * (eps * s)), total)
+        third = combine(lambda s: 0.75 * (inside * s), total)
         store_field(third_ref, row, third)
         store_z(rows, links_at(links_ref, row, 1, 2), row, third, far_ref, near_ref)
     store_t(rows, links_at(links_ref, rows - 1, 1, 3), third_ref, outer_ref, inner_ref)
 
 
-def second_kernel(rows, coefs_ref, links_ref, *refs):
+def second_kernel(rows, eps_ref, coefs_ref, links_ref, *refs):
     arrivals, (start_ref, third_ref, mixed_ref, far_ref, near_ref, outer_ref, inner_ref, base_ref) = refs[:5], refs[5:]
-    for row in range(rows):
-        inside, eps = coefs_ref[row + 1], coefs_ref[rows + 2]
+    eps = eps_ref[...]
+    for row in range(rows):
+        inside = coefs_ref[row + 1]
         total = arrived_sum(links_ref, 1, row, rows, arrivals)
-        third = load_field(third_ref, row)
-        second = combine(lambda v, s: v + (8.0 / 9.0) * (inside * (eps * s)), load_field(start_ref, row), total)
+        third = combine(lambda v: eps * v, load_field(third_ref, row))
+        second = combine(
+            lambda v, s: v + (8.0 / 9.0) * (inside * (eps * (eps * s))), load_field(start_ref, row), total
+        )
         mixed = combine(lambda p, q: 0.25 * p - (2.0 / 9.0) * q, second, third)
         store_field(mixed_ref, row, mixed)
         store_field(base_ref, row, combine(lambda p, q: p + q, second, third))
@@ -196,11 +202,11 @@
     store_t(rows, links_at(links_ref, rows - 1, 0, 3), mixed_ref, outer_ref, inner_ref)
 
 
-def last_kernel(rows, coefs_ref, links_ref, *refs):
+def last_kernel(rows, eps_ref, coefs_ref, links_ref, *refs):
     arrivals, (base_ref, out_hbm, out_ref, sems) = refs[:5], refs[5:]
     copies = []
     for row in range(rows):
-        inside, eps = coefs_ref[row + 1], coefs_ref[rows + 2]
+        inside, eps = coefs_ref[row + 1], eps_ref[...]
         total = arrived_sum(links_ref, 0, row, rows, arrivals)
         store_field(out_ref, row, combine(lambda p, s: p + inside * (eps * s), load_field(base_ref, row), total))
         copies.append(pltpu.make_async_copy(out_ref.at[row], out_hbm.at[row], sems.at[row]))
@@ -230,7 +236,7 @@
     links = jnp.transpose(flowed, (0, 1, 2, 4, 5, 3, 6)).reshape(-1, flowed.shape[-1])
     whole = jax.ShapeDtypeStruct(adjoint.shape, jnp.float32)
     one_row = jax.ShapeDtypeStruct((1,) + adjoint.shape[1:], jnp.float32)
-    coefs_shape = jax.ShapeDtypeStruct((rows + 3,) + adjoint.shape[3:], jnp.float32)
+    coefs_shape = jax.ShapeDtypeStruct((rows + 2,) + adjoint.shape[3:], jnp.float32)
 
     def in_plane(i, by):
         return i - i % per_plane + (i + by) % per_plane
@@ -266,9 +272,10 @@
     )
     arrived = sent_on(*sending)
     coefs = call(
-        functools.partial(taper_kernel, rows), "tapers", (source_slice, band_width, flow_steps), coefs_shape, 1,
-        pltpu.SMEM,
-    )
+        functools.partial(taper_kernel, rows), "tapers", (source_slice, band_width), coefs_shape, 1, pltpu.SMEM
+    )
+    eps_shape = jax.ShapeDtypeStruct(adjoint.shape[3:], jnp.float32)
+    eps = call(eps_kernel, "eps", (flow_steps,), eps_shape, 1, pltpu.SMEM)
     total, start = call(
         functools.partial(start_kernel, rows, 2), "start", (coefs, adjoint, links), (whole, whole), 22
     )
@@ -277,12 +284,12 @@
     )
     arrived = sent_on(*sending)
     mixed, *sending, base = call(
-        functools.partial(second_kernel, rows), "second", (coefs, links, local(1, third)) + arrived + (start, third),
+        functools.partial(second_kernel, rows), "second", (eps, coefs, links, local(1, third)) + arrived + (start, third),
         (whole,) + sent + (whole,), 10,
     )
     arrived = sent_on(*sending)
     return call(
-        functools.partial(last_kernel, rows), "last", (coefs, links, local(0, mixed)) + arrived + (base,), whole, 5,
+        functools.partial(last_kernel, rows), "last", (eps, coefs, links, local(0, mixed)) + arrived + (base,), whole, 5,
         scratch=[pltpu.VMEM(adjoint.shape, jnp.float32), pltpu.SemaphoreType.DMA((rows,))], out_space=pltpu.HBM,
     )
 

time: 27.3 us -> 27.1 us (level)
    ppermute x3, starting transfers between devices: 4.37 us -> 3.93 us  [sent_on(): near = lax.ppermute(near, 'gz', near_pairs)]
    ppermute x3, starting transfers between devices: 6.73 us -> 7.17 us  [sent_on(): far = lax.ppermute(far, 'gz', far_pairs)]
    pallas_call x8 -> x9, Pallas kernels: 2.95 us -> 2.96 us  [call(): pl.pallas_call(kernel, name=name, out_shape=out_shapes, in_specs=[pl.Bloc...]
where the time goes in v14:
time: 27.1 us; the launch traced here: 26.9 us
  starting transfers between devices  15.9 us (59%)
  waiting for transfers between devices  5.99 us (22%)
  Pallas kernels  2.96 us (11%)
  between operations  2.02 us (7%)
    ppermute x3, starting transfers between devices, sent_on(): far = lax.ppermute(far, 'gz', far_pairs)  7.17 us
    ppermute x3, waiting for transfers between devices, sent_on(): outer = lax.ppermute(outer, 'gz', outer_pairs)  5.29 us
    ppermute x3, starting transfers between devices, sent_on(): near = lax.ppermute(near, 'gz', near_pairs)  3.93 us
    ppermute x3, starting transfers between devices, sent_on(): inner = lax.ppermute(inner, 'gz', inner_pairs)  3.49 us
    pallas_call x9, Pallas kernels, call(): pl.pallas_call(kernel, name=name, out_shape=out_shapes, in_specs=[pl.Bloc...  2.96 us
    ppermute x3, starting transfers between devices, sent_on(): outer = lax.ppermute(outer, 'gz', outer_pairs)  1.33 us
    ppermute x3, waiting for transfers between devices, sent_on(): far = lax.ppermute(far, 'gz', far_pairs)  0.69 us
  transfers between devices with their start and end apart: 12, of which 5 were waited for; matrix products, arithmetic and copies ran while one was open for 0% of the time, Pallas kernels for 3%

profile of v14, /device:TPU:0, one launch (start us, length us, event | category | flops | bytes accessed | tf_op | source)
XLA Modules:
  0.0 26.9 jit_solution(4345043465708896051)
XLA Ops:
  0.0 1.1 %begin.1 = (f32[4,2,3,8,128]{4,3,2,1,0:T(8,128)S(1)}, f32[4,2,3,8,128]{4,3,2,1,0:T(8,128)S(1)}, f32[1,2,3,8,128]{4,3,2,1,0:T(8,128)S(1)}, f32[1,2,3,8,128]{4,3,2,1,0:T(8,128)S(1)}) custom-call(f32[4,2,3,8,128]{4,3,2,1,0:T(8,128)} %adjoint_hbm.1, f32[864,128]{1,0:T(8,128)} %bitcast.3), custom_call_target="tpu_custom_call" | custom-call | flops 368640 | bytes 368640 | tf_op jit(solution)/shard_map/begin/pallas_call | solution.py:220
  1.1 3.1 %collective-permute-start = (f32[4,2,3,8,128]{4,3,2,1,0:T(8,128)S(1)}, f32[4,2,3,8,128]{4,3,2,1,0:T(8,128)S(1)}, u32[]{:S(2)}, u32[]{:S(2)}) collective-permute-start(f32[4,2,3,8,128]{4,3,2,1,0:T(8,128)S(1)} %get-tuple-element.23), channel_id=1, source_target_pairs={{0,8},{1,9},{2,10},{3,11},{4,12},{5,13},{6,14},{7,15},{8,0},{9,1},... | collective-permute-start | bytes 294920 | tf_op jit(solution)/shard_map/ppermute | solution.py:253
  4.2 2.5 %collective-permute-start.1 = (f32[4,2,3,8,128]{4,3,2,1,0:T(8,128)S(1)}, f32[4,2,3,8,128]{4,3,2,1,0:T(8,128)S(1)}, u32[]{:S(2)}, u32[]{:S(2)}) collective-permute-start(f32[4,2,3,8,128]{4,3,2,1,0:T(8,128)S(1)} %get-tuple-element.24), channel_id=1, source_target_pairs={{0,24},{1,25},{2,26},{3,27},{4,28},{5,29},{6,30},{7,31},{8,16},{9,... | collective-permute-start | bytes 294920 | tf_op jit(solution)/shard_map/ppermute | solution.py:254
  6.7 1.3 %collective-permute-start.2 = (f32[1,2,3,8,128]{4,3,2,1,0:T(8,128)S(1)}, f32[1,2,3,8,128]{4,3,2,1,0:T(8,128)S(1)}, u32[]{:S(2)}, u32[]{:S(2)}) collective-permute-start(f32[1,2,3,8,128]{4,3,2,1,0:T(8,128)S(1)} %get-tuple-element.25), channel_id=1, source_target_pairs={{0,7},{1,2},{2,1},{3,4},{4,3},{5,6},{6,5},{7,0},{8,15},{9,10},{10,... | collective-permute-start | bytes 73736 | tf_op jit(solution)/shard_map/ppermute | solution.py:255
  8.0 0.3 %collective-permute-start.3 = (f32[1,2,3,8,128]{4,3,2,1,0:T(8,128)S(1)}, f32[1,2,3,8,128]{4,3,2,1,0:T(8,128)S(1)}, u32[]{:S(2)}, u32[]{:S(2)}) collective-permute-start(f32[1,2,3,8,128]{4,3,2,1,0:T(8,128)S(1)} %get-tuple-element.26), channel_id=1, source_target_pairs={{0,1},{1,0},{2,3},{3,2},{4,5},{5,4},{6,7},{7,6},{8,9},{9,8},{10,11... | collective-permute-start | bytes 73736 | tf_op jit(solution)/shard_map/ppermute | solution.py:256
  9.6 0.3 %start.1 = (f32[4,2,3,8,128]{4,3,2,1,0:T(8,128)S(1)}, f32[4,2,3,8,128]{4,3,2,1,0:T(8,128)S(1)}) custom-call(f32[6,8,128]{2,1,0:T(8,128)S(1)} %tapers.1.coefs_ref, f32[4,2,3,8,128]{4,3,2,1,0:T(8,128)S(1)} %copy-done.1, f32[864,128]{1,0:T(8,128)S(1)} %bitcast.4), custom_call_target="tpu_custom_call" | custom-call | flops 1622016 | bytes 1622016 | tf_op jit(solution)/shard_map/start/pallas_call | solution.py:220
  9.9 1.1 %collective-permute-done.2.refs_3_ = f32[1,2,3,8,128]{4,3,2,1,0:T(8,128)S(1)} collective-permute-done((f32[1,2,3,8,128]{4,3,2,1,0:T(8,128)S(1)}, f32[1,2,3,8,128]{4,3,2,1,0:T(8,128)S(1)}, u32[]{:S(2)}, u32[]{:S(2)}) %collective-permute-start.2) | collective-permute-done | bytes 24608 | tf_op jit(solution)/shard_map/ppermute | solution.py:255
  11.0 0.0 collective-permute-done.3.refs_4_
  11.0 0.4 %collective-permute-done.1.refs_2_ = f32[4,2,3,8,128]{4,3,2,1,0:T(8,128)S(1)} collective-permute-done((f32[4,2,3,8,128]{4,3,2,1,0:T(8,128)S(1)}, f32[4,2,3,8,128]{4,3,2,1,0:T(8,128)S(1)}, u32[]{:S(2)}, u32[]{:S(2)}) %collective-permute-start.1) | collective-permute-done | bytes 98336 | tf_op jit(solution)/shard_map/ppermute | solution.py:254
  11.3 0.1 third.1
  11.5 0.7 %collective-permute-start.4 = (f32[4,2,3,8,128]{4,3,2,1,0:T(8,128)S(1)}, f32[4,2,3,8,128]{4,3,2,1,0:T(8,128)S(1)}, u32[]{:S(2)}, u32[]{:S(2)}) collective-permute-start(f32[4,2,3,8,128]{4,3,2,1,0:T(8,128)S(1)} %get-tuple-element.28), channel_id=1, source_target_pairs={{0,8},{1,9},{2,10},{3,11},{4,12},{5,13},{6,14},{7,15},{8,0},{9,1},... | collective-permute-start | bytes 294920 | tf_op jit(solution)/shard_map/ppermute | solution.py:253
  12.2 2.6 %collective-permute-start.5 = (f32[4,2,3,8,128]{4,3,2,1,0:T(8,128)S(1)}, f32[4,2,3,8,128]{4,3,2,1,0:T(8,128)S(1)}, u32[]{:S(2)}, u32[]{:S(2)}) collective-permute-start(f32[4,2,3,8,128]{4,3,2,1,0:T(8,128)S(1)} %get-tuple-element.29), channel_id=1, source_target_pairs={{0,24},{1,25},{2,26},{3,27},{4,28},{5,29},{6,30},{7,31},{8,16},{9,... | collective-permute-start | bytes 294920 | tf_op jit(solution)/shard_map/ppermute | solution.py:254
  14.8 1.6 %collective-permute-start.7 = (f32[1,2,3,8,128]{4,3,2,1,0:T(8,128)S(1)}, f32[1,2,3,8,128]{4,3,2,1,0:T(8,128)S(1)}, u32[]{:S(2)}, u32[]{:S(2)}) collective-permute-start(f32[1,2,3,8,128]{4,3,2,1,0:T(8,128)S(1)} %get-tuple-element.31), channel_id=1, source_target_pairs={{0,1},{1,0},{2,3},{3,2},{4,5},{5,4},{6,7},{7,6},{8,9},{9,8},{10,11... | collective-permute-start | bytes 73736 | tf_op jit(solution)/shard_map/ppermute | solution.py:256
  17.1 0.3 %local_1.1.refs_0_ = f32[4,2,3,8,128]{4,3,2,1,0:T(8,128)S(1)} custom-call(f32[4,2,3,8,128]{4,3,2,1,0:T(8,128)S(1)} %get-tuple-element.27.field_ref.refs_6_, f32[864,128]{1,0:T(8,128)S(1)} %bitcast.6), custom_call_target="tpu_custom_call" | custom-call | flops 1622016 | bytes 1622016 | tf_op jit(solution)/shard_map/local_1/pallas_call | solution.py:220
  17.3 1.8 %collective-permute-done.6.refs_3_ = f32[1,2,3,8,128]{4,3,2,1,0:T(8,128)S(1)} collective-permute-done((f32[1,2,3,8,128]{4,3,2,1,0:T(8,128)S(1)}, f32[1,2,3,8,128]{4,3,2,1,0:T(8,128)S(1)}, u32[]{:S(2)}, u32[]{:S(2)}) %collective-permute-start.6) | collective-permute-done | bytes 24608 | tf_op jit(solution)/shard_map/ppermute | solution.py:255
  19.1 0.0 collective-permute-done.7.refs_4_
  19.1 0.2 second.1
  19.3 0.2 collective-permute-start.8
  19.5 2.1 %collective-permute-start.9 = (f32[4,2,3,8,128]{4,3,2,1,0:T(8,128)S(1)}, f32[4,2,3,8,128]{4,3,2,1,0:T(8,128)S(1)}, u32[]{:S(2)}, u32[]{:S(2)}) collective-permute-start(f32[4,2,3,8,128]{4,3,2,1,0:T(8,128)S(1)} %get-tuple-element.35), channel_id=1, source_target_pairs={{0,24},{1,25},{2,26},{3,27},{4,28},{5,29},{6,30},{7,31},{8,16},{9,... | collective-permute-start | bytes 294920 | tf_op jit(solution)/shard_map/ppermute | solution.py:254
  21.5 1.6 %collective-permute-start.11 = (f32[1,2,3,8,128]{4,3,2,1,0:T(8,128)S(1)}, f32[1,2,3,8,128]{4,3,2,1,0:T(8,128)S(1)}, u32[]{:S(2)}, u32[]{:S(2)}) collective-permute-start(f32[1,2,3,8,128]{4,3,2,1,0:T(8,128)S(1)} %get-tuple-element.37), channel_id=1, source_target_pairs={{0,1},{1,0},{2,3},{3,2},{4,5},{5,4},{6,7},{7,6},{8,9},{9,8},{10,11... | collective-permute-start | bytes 73736 | tf_op jit(solution)/shard_map/ppermute | solution.py:256
  23.1 0.3 local_0.1.refs_0_
  23.4 2.4 %collective-permute-done.10.refs_3_ = f32[1,2,3,8,128]{4,3,2,1,0:T(8,128)S(1)} collective-permute-done((f32[1,2,3,8,128]{4,3,2,1,0:T(8,128)S(1)}, f32[1,2,3,8,128]{4,3,2,1,0:T(8,128)S(1)}, u32[]{:S(2)}, u32[]{:S(2)}) %collective-permute-start.10) | collective-permute-done | bytes 24608 | tf_op jit(solution)/shard_map/ppermute | solution.py:255
  25.8 0.3 %collective-permute-done.9.refs_2_ = f32[4,2,3,8,128]{4,3,2,1,0:T(8,128)S(1)} collective-permute-done((f32[4,2,3,8,128]{4,3,2,1,0:T(8,128)S(1)}, f32[4,2,3,8,128]{4,3,2,1,0:T(8,128)S(1)}, u32[]{:S(2)}, u32[]{:S(2)}) %collective-permute-start.9) | collective-permute-done | bytes 98336 | tf_op jit(solution)/shard_map/ppermute | solution.py:254
  26.2 0.7 %last.1 = f32[4,2,3,8,128]{4,3,2,1,0:T(8,128)} custom-call(f32[8,128]{1,0:T(8,128)S(1)} %eps.1.eps_ref, f32[6,8,128]{2,1,0:T(8,128)S(1)} %tapers.1.coefs_ref, f32[864,128]{1,0:T(8,128)S(1)} %bitcast.9, f32[4,2,3,8,128]{4,3,2,1,0:T(8,128)S(1)} %local_0.1.refs_0_, f32[4,2,3,8,128]{4,3,2,1,0:T(8,128)S(1)} %collective-permute-done.8.refs_1_, ...), custom_call_target="tpu_custom_call" | custom-call | flops 368640 | bytes 368640 | tf_op jit(solution)/shard_map/last/pallas_call | solution.py:220
  (13 shorter events, 0.1 us)
Async XLA Ops:
  0.0 9.6 %copy-start = (f32[4,3,4,2,3,3,128]{6,3,5,4,2,1,0:T(2,128)S(1)}, f32[4,3,4,2,3,3,128]{6,3,5,4,2,1,0:T(2,128)}, u32[]{:S(2)}) copy-start(f32[4,3,4,2,3,3,128]{6,3,5,4,2,1,0:T(2,128)} %param.6) | copy-start | bytes 1327108
  0.0 9.6 %copy-start.1 = (f32[4,2,3,8,128]{4,3,2,1,0:T(8,128)S(1)}, f32[4,2,3,8,128]{4,3,2,1,0:T(8,128)}, u32[]{:S(2)}) copy-start(f32[4,2,3,8,128]{4,3,2,1,0:T(8,128)} %adjoint_hbm.1) | copy-start | bytes 294916
  1.1 9.9 %collective-permute-start = (f32[4,2,3,8,128]{4,3,2,1,0:T(8,128)S(1)}, f32[4,2,3,8,128]{4,3,2,1,0:T(8,128)S(1)}, u32[]{:S(2)}, u32[]{:S(2)}) collective-permute-start(f32[4,2,3,8,128]{4,3,2,1,0:T(8,128)S(1)} %get-tuple-element.23), channel_id=1, source_target_pairs={{0,8},{1,9},{2,10},{3,11},{4,12},{5,13},{6,14},{7,15},{8,0},{9,1},... | collective-permute-start | bytes 294920 | tf_op jit(solution)/shard_map/ppermute | solution.py:253
  4.2 7.2 %collective-permute-start.1 = (f32[4,2,3,8,128]{4,3,2,1,0:T(8,128)S(1)}, f32[4,2,3,8,128]{4,3,2,1,0:T(8,128)S(1)}, u32[]{:S(2)}, u32[]{:S(2)}) collective-permute-start(f32[4,2,3,8,128]{4,3,2,1,0:T(8,128)S(1)} %get-tuple-element.24), channel_id=1, source_target_pairs={{0,24},{1,25},{2,26},{3,27},{4,28},{5,29},{6,30},{7,31},{8,16},{9,... | collective-permute-start | bytes 294920 | tf_op jit(solution)/shard_map/ppermute | solution.py:254
  6.7 4.3 %collective-permute-start.2 = (f32[1,2,3,8,128]{4,3,2,1,0:T(8,128)S(1)}, f32[1,2,3,8,128]{4,3,2,1,0:T(8,128)S(1)}, u32[]{:S(2)}, u32[]{:S(2)}) collective-permute-start(f32[1,2,3,8,128]{4,3,2,1,0:T(8,128)S(1)} %get-tuple-element.25), channel_id=1, source_target_pairs={{0,7},{1,2},{2,1},{3,4},{4,3},{5,6},{6,5},{7,0},{8,15},{9,10},{10,... | collective-permute-start | bytes 73736 | tf_op jit(solution)/shard_map/ppermute | solution.py:255
  8.0 3.0 %collective-permute-start.3 = (f32[1,2,3,8,128]{4,3,2,1,0:T(8,128)S(1)}, f32[1,2,3,8,128]{4,3,2,1,0:T(8,128)S(1)}, u32[]{:S(2)}, u32[]{:S(2)}) collective-permute-start(f32[1,2,3,8,128]{4,3,2,1,0:T(8,128)S(1)} %get-tuple-element.26), channel_id=1, source_target_pairs={{0,1},{1,0},{2,3},{3,2},{4,5},{5,4},{6,7},{7,6},{8,9},{9,8},{10,11... | collective-permute-start | bytes 73736 | tf_op jit(solution)/shard_map/ppermute | solution.py:256
  11.5 7.6 %collective-permute-start.4 = (f32[4,2,3,8,128]{4,3,2,1,0:T(8,128)S(1)}, f32[4,2,3,8,128]{4,3,2,1,0:T(8,128)S(1)}, u32[]{:S(2)}, u32[]{:S(2)}) collective-permute-start(f32[4,2,3,8,128]{4,3,2,1,0:T(8,128)S(1)} %get-tuple-element.28), channel_id=1, source_target_pairs={{0,8},{1,9},{2,10},{3,11},{4,12},{5,13},{6,14},{7,15},{8,0},{9,1},... | collective-permute-start | bytes 294920 | tf_op jit(solution)/shard_map/ppermute | solution.py:253
  12.2 7.0 %collective-permute-start.5 = (f32[4,2,3,8,128]{4,3,2,1,0:T(8,128)S(1)}, f32[4,2,3,8,128]{4,3,2,1,0:T(8,128)S(1)}, u32[]{:S(2)}, u32[]{:S(2)}) collective-permute-start(f32[4,2,3,8,128]{4,3,2,1,0:T(8,128)S(1)} %get-tuple-element.29), channel_id=1, source_target_pairs={{0,24},{1,25},{2,26},{3,27},{4,28},{5,29},{6,30},{7,31},{8,16},{9,... | collective-permute-start | bytes 294920 | tf_op jit(solution)/shard_map/ppermute | solution.py:254
  14.8 4.3 %collective-permute-start.6 = (f32[1,2,3,8,128]{4,3,2,1,0:T(8,128)S(1)}, f32[1,2,3,8,128]{4,3,2,1,0:T(8,128)S(1)}, u32[]{:S(2)}, u32[]{:S(2)}) collective-permute-start(f32[1,2,3,8,128]{4,3,2,1,0:T(8,128)S(1)} %get-tuple-element.30), channel_id=1, source_target_pairs={{0,7},{1,2},{2,1},{3,4},{4,3},{5,6},{6,5},{7,0},{8,15},{9,10},{10,... | collective-permute-start | bytes 73736 | tf_op jit(solution)/shard_map/ppermute | solution.py:255
  14.8 4.3 %collective-permute-start.7 = (f32[1,2,3,8,128]{4,3,2,1,0:T(8,128)S(1)}, f32[1,2,3,8,128]{4,3,2,1,0:T(8,128)S(1)}, u32[]{:S(2)}, u32[]{:S(2)}) collective-permute-start(f32[1,2,3,8,128]{4,3,2,1,0:T(8,128)S(1)} %get-tuple-element.31), channel_id=1, source_target_pairs={{0,1},{1,0},{2,3},{3,2},{4,5},{5,4},{6,7},{7,6},{8,9},{9,8},{10,11... | collective-permute-start | bytes 73736 | tf_op jit(solution)/shard_map/ppermute | solution.py:256
  19.3 6.5 %collective-permute-start.8 = (f32[4,2,3,8,128]{4,3,2,1,0:T(8,128)S(1)}, f32[4,2,3,8,128]{4,3,2,1,0:T(8,128)S(1)}, u32[]{:S(2)}, u32[]{:S(2)}) collective-permute-start(f32[4,2,3,8,128]{4,3,2,1,0:T(8,128)S(1)} %get-tuple-element.34), channel_id=1, source_target_pairs={{0,8},{1,9},{2,10},{3,11},{4,12},{5,13},{6,14},{7,15},{8,0},{9,1},... | collective-permute-start | bytes 294920 | tf_op jit(solution)/shard_map/ppermute | solution.py:253
  19.5 6.7 %collective-permute-start.9 = (f32[4,2,3,8,128]{4,3,2,1,0:T(8,128)S(1)}, f32[4,2,3,8,128]{4,3,2,1,0:T(8,128)S(1)}, u32[]{:S(2)}, u32[]{:S(2)}) collective-permute-start(f32[4,2,3,8,128]{4,3,2,1,0:T(8,128)S(1)} %get-tuple-element.35), channel_id=1, source_target_pairs={{0,24},{1,25},{2,26},{3,27},{4,28},{5,29},{6,30},{7,31},{8,16},{9,... | collective-permute-start | bytes 294920 | tf_op jit(solution)/shard_map/ppermute | solution.py:254
  21.5 4.3 %collective-permute-start.10 = (f32[1,2,3,8,128]{4,3,2,1,0:T(8,128)S(1)}, f32[1,2,3,8,128]{4,3,2,1,0:T(8,128)S(1)}, u32[]{:S(2)}, u32[]{:S(2)}) collective-permute-start(f32[1,2,3,8,128]{4,3,2,1,0:T(8,128)S(1)} %get-tuple-element.36), channel_id=1, source_target_pairs={{0,7},{1,2},{2,1},{3,4},{4,3},{5,6},{6,5},{7,0},{8,15},{9,10},{10,... | collective-permute-start | bytes 73736 | tf_op jit(solution)/shard_map/ppermute | solution.py:255
  21.5 4.3 %collective-permute-start.11 = (f32[1,2,3,8,128]{4,3,2,1,0:T(8,128)S(1)}, f32[1,2,3,8,128]{4,3,2,1,0:T(8,128)S(1)}, u32[]{:S(2)}, u32[]{:S(2)}) collective-permute-start(f32[1,2,3,8,128]{4,3,2,1,0:T(8,128)S(1)} %get-tuple-element.37), channel_id=1, source_target_pairs={{0,1},{1,0},{2,3},{3,2},{4,5},{5,4},{6,7},{7,6},{8,9},{9,8},{10,11... | collective-permute-start | bytes 73736 | tf_op jit(solution)/shard_map/ppermute | solution.py:256

commit v15 on v14

--- a/solution.py
+++ b/solution.py
@@ -149,6 +149,8 @@
 
 def arrived_sum(links_ref, link_set, row, rows, arrivals, coefs_ref=None):
     sum_ref, near_ref, far_ref, outer_ref, inner_ref = arrivals
+    if coefs_ref is not None:
+        near_ref, far_ref = far_ref, near_ref
     _, first_pos, odd_plane, odd_block = place(rows)
     far, near = load_field(far_ref, row), load_field(near_ref, row)
     if coefs_ref is not None:
@@ -249,12 +251,12 @@
     outer_pairs = [(i, in_plane(i, 1 if i % 2 else -1)) for i in range(count)]
     inner_pairs = [(i, in_plane(i, -1 if i % 2 else 1)) for i in range(count)]
 
-    def sent_on(far, near, outer, inner):
+    def sent_on(far, near, outer, inner, far_first=False):
         near = lax.ppermute(near, "gz", near_pairs)
         far = lax.ppermute(far, "gz", far_pairs)
         outer = lax.ppermute(outer, "gz", outer_pairs)
         inner = lax.ppermute(inner, "gz", inner_pairs)
-        return near, far, outer, inner
+        return (far, near, outer, inner) if far_first else (near, far, outer, inner)
 
     def local(link_set, field):
         return call(functools.partial(local_kernel, rows, link_set), f"local_{link_set}", (field, links), whole, 22)
@@ -270,7 +272,7 @@
             pltpu.SemaphoreType.DMA((rows + 1,)),
         ],
     )
-    arrived = sent_on(*sending)
+    arrived = sent_on(*sending, far_first=True)
     coefs = call(
         functools.partial(taper_kernel, rows), "tapers", (source_slice, band_width), coefs_shape, 1, pltpu.SMEM
     )

time: 27.1 us -> 27.3 us (level)
  waiting for transfers between devices: 5.99 us -> 7.51 us
  starting transfers between devices: 15.9 us -> 14.6 us
    ppermute x3, starting transfers between devices: 3.93 us -> 1.81 us  [sent_on(): near = lax.ppermute(near, 'gz', near_pairs)]
    ppermute x3, waiting for transfers between devices: 0.69 us -> 1.51 us  [sent_on(): far = lax.ppermute(far, 'gz', far_pairs)]
    ppermute x3, starting transfers between devices: 7.17 us -> 7.97 us  [sent_on(): far = lax.ppermute(far, 'gz', far_pairs)]
    ppermute x3, waiting for transfers between devices: 0.01 us -> 0.7 us  [sent_on(): near = lax.ppermute(near, 'gz', near_pairs)]
    ppermute x3, starting transfers between devices: 1.33 us -> 1.63 us  [sent_on(): outer = lax.ppermute(outer, 'gz', outer_pairs)]
    ppermute x3, starting transfers between devices: 3.49 us -> 3.19 us  [sent_on(): inner = lax.ppermute(inner, 'gz', inner_pairs)]
  transfers between devices with their start and end apart: 12 -> 12, of which waited for: 5 -> 6; matrix products, arithmetic and copies ran while one was open for 0% -> 0% of each run, Pallas kernels for 3% -> 3%
where the time goes in v15:
time: 27.3 us; the launch traced here: 27.1 us
  starting transfers between devices  14.6 us (53%)
  waiting for transfers between devices  7.51 us (28%)
  Pallas kernels  2.94 us (11%)
  between operations  2.02 us (7%)
    ppermute x3, starting transfers between devices, sent_on(): far = lax.ppermute(far, 'gz', far_pairs)  7.97 us
    ppermute x3, waiting for transfers between devices, sent_on(): outer = lax.ppermute(outer, 'gz', outer_pairs)  5.28 us
    ppermute x3, starting transfers between devices, sent_on(): inner = lax.ppermute(inner, 'gz', inner_pairs)  3.19 us
    pallas_call x9, Pallas kernels, call(): pl.pallas_call(kernel, name=name, out_shape=out_shapes, in_specs=[pl.Bloc...  2.94 us
    ppermute x3, starting transfers between devices, sent_on(): near = lax.ppermute(near, 'gz', near_pairs)  1.81 us
    ppermute x3, starting transfers between devices, sent_on(): outer = lax.ppermute(outer, 'gz', outer_pairs)  1.63 us
    ppermute x3, waiting for transfers between devices, sent_on(): far = lax.ppermute(far, 'gz', far_pairs)  1.51 us
    ppermute x3, waiting for transfers between devices, sent_on(): near = lax.ppermute(near, 'gz', near_pairs)  0.7 us
  transfers between devices with their start and end apart: 12, of which 6 were waited for; matrix products, arithmetic and copies ran while one was open for 0% of the time, Pallas kernels for 3%

profile of v15, /device:TPU:0, one launch (start us, length us, event | category | flops | bytes accessed | tf_op | source)
XLA Modules:
  0.0 27.1 jit_solution(15298496783270346763)
XLA Ops:
  0.0 1.1 %begin.1 = (f32[4,2,3,8,128]{4,3,2,1,0:T(8,128)S(1)}, f32[4,2,3,8,128]{4,3,2,1,0:T(8,128)S(1)}, f32[1,2,3,8,128]{4,3,2,1,0:T(8,128)S(1)}, f32[1,2,3,8,128]{4,3,2,1,0:T(8,128)S(1)}) custom-call(f32[4,2,3,8,128]{4,3,2,1,0:T(8,128)} %adjoint_hbm.1, f32[864,128]{1,0:T(8,128)} %bitcast.3), custom_call_target="tpu_custom_call" | custom-call | flops 368640 | bytes 368640 | tf_op jit(solution)/shard_map/begin/pallas_call | solution.py:222
  1.1 5.1 %collective-permute-start = (f32[4,2,3,8,128]{4,3,2,1,0:T(8,128)S(1)}, f32[4,2,3,8,128]{4,3,2,1,0:T(8,128)S(1)}, u32[]{:S(2)}, u32[]{:S(2)}) collective-permute-start(f32[4,2,3,8,128]{4,3,2,1,0:T(8,128)S(1)} %get-tuple-element.23), channel_id=1, source_target_pairs={{0,24},{1,25},{2,26},{3,27},{4,28},{5,29},{6,30},{7,31},{8,16},{9,... | collective-permute-start | bytes 294920 | tf_op jit(solution)/shard_map/ppermute | solution.py:256
  6.2 0.0 collective-permute-start.1
  6.2 1.6 %collective-permute-start.2 = (f32[1,2,3,8,128]{4,3,2,1,0:T(8,128)S(1)}, f32[1,2,3,8,128]{4,3,2,1,0:T(8,128)S(1)}, u32[]{:S(2)}, u32[]{:S(2)}) collective-permute-start(f32[1,2,3,8,128]{4,3,2,1,0:T(8,128)S(1)} %get-tuple-element.25), channel_id=1, source_target_pairs={{0,7},{1,2},{2,1},{3,4},{4,3},{5,6},{6,5},{7,0},{8,15},{9,10},{10,... | collective-permute-start | bytes 73736 | tf_op jit(solution)/shard_map/ppermute | solution.py:257
  7.8 0.0 collective-permute-start.3
  9.2 0.3 start.1
  9.4 1.1 %collective-permute-done.2.refs_3_ = f32[1,2,3,8,128]{4,3,2,1,0:T(8,128)S(1)} collective-permute-done((f32[1,2,3,8,128]{4,3,2,1,0:T(8,128)S(1)}, f32[1,2,3,8,128]{4,3,2,1,0:T(8,128)S(1)}, u32[]{:S(2)}, u32[]{:S(2)}) %collective-permute-start.2) | collective-permute-done | bytes 24608 | tf_op jit(solution)/shard_map/ppermute | solution.py:257
  10.5 0.7 %collective-permute-done.1.refs_2_ = f32[4,2,3,8,128]{4,3,2,1,0:T(8,128)S(1)} collective-permute-done((f32[4,2,3,8,128]{4,3,2,1,0:T(8,128)S(1)}, f32[4,2,3,8,128]{4,3,2,1,0:T(8,128)S(1)}, u32[]{:S(2)}, u32[]{:S(2)}) %collective-permute-start.1) | collective-permute-done | bytes 98336 | tf_op jit(solution)/shard_map/ppermute | solution.py:255
  11.2 0.1 third.1
  11.4 1.7 %collective-permute-start.4 = (f32[4,2,3,8,128]{4,3,2,1,0:T(8,128)S(1)}, f32[4,2,3,8,128]{4,3,2,1,0:T(8,128)S(1)}, u32[]{:S(2)}, u32[]{:S(2)}) collective-permute-start(f32[4,2,3,8,128]{4,3,2,1,0:T(8,128)S(1)} %get-tuple-element.28), channel_id=1, source_target_pairs={{0,8},{1,9},{2,10},{3,11},{4,12},{5,13},{6,14},{7,15},{8,0},{9,1},... | collective-permute-start | bytes 294920 | tf_op jit(solution)/shard_map/ppermute | solution.py:255
  13.1 0.8 %collective-permute-start.5 = (f32[4,2,3,8,128]{4,3,2,1,0:T(8,128)S(1)}, f32[4,2,3,8,128]{4,3,2,1,0:T(8,128)S(1)}, u32[]{:S(2)}, u32[]{:S(2)}) collective-permute-start(f32[4,2,3,8,128]{4,3,2,1,0:T(8,128)S(1)} %get-tuple-element.29), channel_id=1, source_target_pairs={{0,24},{1,25},{2,26},{3,27},{4,28},{5,29},{6,30},{7,31},{8,16},{9,... | collective-permute-start | bytes 294920 | tf_op jit(solution)/shard_map/ppermute | solution.py:256
  13.9 0.0 collective-permute-start.6
  14.0 1.6 %collective-permute-start.7 = (f32[1,2,3,8,128]{4,3,2,1,0:T(8,128)S(1)}, f32[1,2,3,8,128]{4,3,2,1,0:T(8,128)S(1)}, u32[]{:S(2)}, u32[]{:S(2)}) collective-permute-start(f32[1,2,3,8,128]{4,3,2,1,0:T(8,128)S(1)} %get-tuple-element.31), channel_id=1, source_target_pairs={{0,1},{1,0},{2,3},{3,2},{4,5},{5,4},{6,7},{7,6},{8,9},{9,8},{10,11... | collective-permute-start | bytes 73736 | tf_op jit(solution)/shard_map/ppermute | solution.py:258
  16.2 0.3 %local_1.1.refs_0_ = f32[4,2,3,8,128]{4,3,2,1,0:T(8,128)S(1)} custom-call(f32[4,2,3,8,128]{4,3,2,1,0:T(8,128)S(1)} %get-tuple-element.27.field_ref.refs_6_, f32[864,128]{1,0:T(8,128)S(1)} %bitcast.6), custom_call_target="tpu_custom_call" | custom-call | flops 1622016 | bytes 1622016 | tf_op jit(solution)/shard_map/local_1/pallas_call | solution.py:222
  16.5 1.8 %collective-permute-done.6.refs_3_ = f32[1,2,3,8,128]{4,3,2,1,0:T(8,128)S(1)} collective-permute-done((f32[1,2,3,8,128]{4,3,2,1,0:T(8,128)S(1)}, f32[1,2,3,8,128]{4,3,2,1,0:T(8,128)S(1)}, u32[]{:S(2)}, u32[]{:S(2)}) %collective-permute-start.6) | collective-permute-done | bytes 24608 | tf_op jit(solution)/shard_map/ppermute | solution.py:257
  18.2 1.3 %collective-permute-done.5.refs_2_ = f32[4,2,3,8,128]{4,3,2,1,0:T(8,128)S(1)} collective-permute-done((f32[4,2,3,8,128]{4,3,2,1,0:T(8,128)S(1)}, f32[4,2,3,8,128]{4,3,2,1,0:T(8,128)S(1)}, u32[]{:S(2)}, u32[]{:S(2)}) %collective-permute-start.5) | collective-permute-done | bytes 98336 | tf_op jit(solution)/shard_map/ppermute | solution.py:256
  19.5 0.2 second.1
  19.7 0.1 collective-permute-start.8
  19.8 2.0 %collective-permute-start.9 = (f32[4,2,3,8,128]{4,3,2,1,0:T(8,128)S(1)}, f32[4,2,3,8,128]{4,3,2,1,0:T(8,128)S(1)}, u32[]{:S(2)}, u32[]{:S(2)}) collective-permute-start(f32[4,2,3,8,128]{4,3,2,1,0:T(8,128)S(1)} %get-tuple-element.35), channel_id=1, source_target_pairs={{0,24},{1,25},{2,26},{3,27},{4,28},{5,29},{6,30},{7,31},{8,16},{9,... | collective-permute-start | bytes 294920 | tf_op jit(solution)/shard_map/ppermute | solution.py:256
  21.8 1.6 %collective-permute-start.11 = (f32[1,2,3,8,128]{4,3,2,1,0:T(8,128)S(1)}, f32[1,2,3,8,128]{4,3,2,1,0:T(8,128)S(1)}, u32[]{:S(2)}, u32[]{:S(2)}) collective-permute-start(f32[1,2,3,8,128]{4,3,2,1,0:T(8,128)S(1)} %get-tuple-element.37), channel_id=1, source_target_pairs={{0,1},{1,0},{2,3},{3,2},{4,5},{5,4},{6,7},{7,6},{8,9},{9,8},{10,11... | collective-permute-start | bytes 73736 | tf_op jit(solution)/shard_map/ppermute | solution.py:258
  23.4 0.3 local_0.1.refs_0_
  23.7 2.4 %collective-permute-done.10.refs_3_ = f32[1,2,3,8,128]{4,3,2,1,0:T(8,128)S(1)} collective-permute-done((f32[1,2,3,8,128]{4,3,2,1,0:T(8,128)S(1)}, f32[1,2,3,8,128]{4,3,2,1,0:T(8,128)S(1)}, u32[]{:S(2)}, u32[]{:S(2)}) %collective-permute-start.10) | collective-permute-done | bytes 24608 | tf_op jit(solution)/shard_map/ppermute | solution.py:257
  26.1 0.2 collective-permute-done.9.refs_2_
  26.3 0.7 %last.1 = f32[4,2,3,8,128]{4,3,2,1,0:T(8,128)} custom-call(f32[8,128]{1,0:T(8,128)S(1)} %eps.1.eps_ref, f32[6,8,128]{2,1,0:T(8,128)S(1)} %tapers.1.coefs_ref, f32[864,128]{1,0:T(8,128)S(1)} %bitcast.9, f32[4,2,3,8,128]{4,3,2,1,0:T(8,128)S(1)} %local_0.1.refs_0_, f32[4,2,3,8,128]{4,3,2,1,0:T(8,128)S(1)} %collective-permute-done.8.refs_1_, ...), custom_call_target="tpu_custom_call" | custom-call | flops 368640 | bytes 368640 | tf_op jit(solution)/shard_map/last/pallas_call | solution.py:222
  (13 shorter events, 0.1 us)
Async XLA Ops:
  0.0 9.1 %copy-start = (f32[4,3,4,2,3,3,128]{6,3,5,4,2,1,0:T(2,128)S(1)}, f32[4,3,4,2,3,3,128]{6,3,5,4,2,1,0:T(2,128)}, u32[]{:S(2)}) copy-start(f32[4,3,4,2,3,3,128]{6,3,5,4,2,1,0:T(2,128)} %param.6) | copy-start | bytes 1327108
  0.0 9.2 %copy-start.1 = (f32[4,2,3,8,128]{4,3,2,1,0:T(8,128)S(1)}, f32[4,2,3,8,128]{4,3,2,1,0:T(8,128)}, u32[]{:S(2)}) copy-start(f32[4,2,3,8,128]{4,3,2,1,0:T(8,128)} %adjoint_hbm.1) | copy-start | bytes 294916
  1.1 9.4 %collective-permute-start = (f32[4,2,3,8,128]{4,3,2,1,0:T(8,128)S(1)}, f32[4,2,3,8,128]{4,3,2,1,0:T(8,128)S(1)}, u32[]{:S(2)}, u32[]{:S(2)}) collective-permute-start(f32[4,2,3,8,128]{4,3,2,1,0:T(8,128)S(1)} %get-tuple-element.23), channel_id=1, source_target_pairs={{0,24},{1,25},{2,26},{3,27},{4,28},{5,29},{6,30},{7,31},{8,16},{9,... | collective-permute-start | bytes 294920 | tf_op jit(solution)/shard_map/ppermute | solution.py:256
  6.2 5.0 %collective-permute-start.1 = (f32[4,2,3,8,128]{4,3,2,1,0:T(8,128)S(1)}, f32[4,2,3,8,128]{4,3,2,1,0:T(8,128)S(1)}, u32[]{:S(2)}, u32[]{:S(2)}) collective-permute-start(f32[4,2,3,8,128]{4,3,2,1,0:T(8,128)S(1)} %get-tuple-element.24), channel_id=1, source_target_pairs={{0,8},{1,9},{2,10},{3,11},{4,12},{5,13},{6,14},{7,15},{8,0},{9,1},... | collective-permute-start | bytes 294920 | tf_op jit(solution)/shard_map/ppermute | solution.py:255
  6.2 4.3 %collective-permute-start.2 = (f32[1,2,3,8,128]{4,3,2,1,0:T(8,128)S(1)}, f32[1,2,3,8,128]{4,3,2,1,0:T(8,128)S(1)}, u32[]{:S(2)}, u32[]{:S(2)}) collective-permute-start(f32[1,2,3,8,128]{4,3,2,1,0:T(8,128)S(1)} %get-tuple-element.25), channel_id=1, source_target_pairs={{0,7},{1,2},{2,1},{3,4},{4,3},{5,6},{6,5},{7,0},{8,15},{9,10},{10,... | collective-permute-start | bytes 73736 | tf_op jit(solution)/shard_map/ppermute | solution.py:257
  7.8 2.7 %collective-permute-start.3 = (f32[1,2,3,8,128]{4,3,2,1,0:T(8,128)S(1)}, f32[1,2,3,8,128]{4,3,2,1,0:T(8,128)S(1)}, u32[]{:S(2)}, u32[]{:S(2)}) collective-permute-start(f32[1,2,3,8,128]{4,3,2,1,0:T(8,128)S(1)} %get-tuple-element.26), channel_id=1, source_target_pairs={{0,1},{1,0},{2,3},{3,2},{4,5},{5,4},{6,7},{7,6},{8,9},{9,8},{10,11... | collective-permute-start | bytes 73736 | tf_op jit(solution)/shard_map/ppermute | solution.py:258
  11.4 6.9 %collective-permute-start.4 = (f32[4,2,3,8,128]{4,3,2,1,0:T(8,128)S(1)}, f32[4,2,3,8,128]{4,3,2,1,0:T(8,128)S(1)}, u32[]{:S(2)}, u32[]{:S(2)}) collective-permute-start(f32[4,2,3,8,128]{4,3,2,1,0:T(8,128)S(1)} %get-tuple-element.28), channel_id=1, source_target_pairs={{0,8},{1,9},{2,10},{3,11},{4,12},{5,13},{6,14},{7,15},{8,0},{9,1},... | collective-permute-start | bytes 294920 | tf_op jit(solution)/shard_map/ppermute | solution.py:255
  13.1 6.4 %collective-permute-start.5 = (f32[4,2,3,8,128]{4,3,2,1,0:T(8,128)S(1)}, f32[4,2,3,8,128]{4,3,2,1,0:T(8,128)S(1)}, u32[]{:S(2)}, u32[]{:S(2)}) collective-permute-start(f32[4,2,3,8,128]{4,3,2,1,0:T(8,128)S(1)} %get-tuple-element.29), channel_id=1, source_target_pairs={{0,24},{1,25},{2,26},{3,27},{4,28},{5,29},{6,30},{7,31},{8,16},{9,... | collective-permute-start | bytes 294920 | tf_op jit(solution)/shard_map/ppermute | solution.py:256
  13.9 4.3 %collective-permute-start.6 = (f32[1,2,3,8,128]{4,3,2,1,0:T(8,128)S(1)}, f32[1,2,3,8,128]{4,3,2,1,0:T(8,128)S(1)}, u32[]{:S(2)}, u32[]{:S(2)}) collective-permute-start(f32[1,2,3,8,128]{4,3,2,1,0:T(8,128)S(1)} %get-tuple-element.30), channel_id=1, source_target_pairs={{0,7},{1,2},{2,1},{3,4},{4,3},{5,6},{6,5},{7,0},{8,15},{9,10},{10,... | collective-permute-start | bytes 73736 | tf_op jit(solution)/shard_map/ppermute | solution.py:257
  14.0 4.3 %collective-permute-start.7 = (f32[1,2,3,8,128]{4,3,2,1,0:T(8,128)S(1)}, f32[1,2,3,8,128]{4,3,2,1,0:T(8,128)S(1)}, u32[]{:S(2)}, u32[]{:S(2)}) collective-permute-start(f32[1,2,3,8,128]{4,3,2,1,0:T(8,128)S(1)} %get-tuple-element.31), channel_id=1, source_target_pairs={{0,1},{1,0},{2,3},{3,2},{4,5},{5,4},{6,7},{7,6},{8,9},{9,8},{10,11... | collective-permute-start | bytes 73736 | tf_op jit(solution)/shard_map/ppermute | solution.py:258
  19.7 6.4 %collective-permute-start.8 = (f32[4,2,3,8,128]{4,3,2,1,0:T(8,128)S(1)}, f32[4,2,3,8,128]{4,3,2,1,0:T(8,128)S(1)}, u32[]{:S(2)}, u32[]{:S(2)}) collective-permute-start(f32[4,2,3,8,128]{4,3,2,1,0:T(8,128)S(1)} %get-tuple-element.34), channel_id=1, source_target_pairs={{0,8},{1,9},{2,10},{3,11},{4,12},{5,13},{6,14},{7,15},{8,0},{9,1},... | collective-permute-start | bytes 294920 | tf_op jit(solution)/shard_map/ppermute | solution.py:255
  19.8 6.6 %collective-permute-start.9 = (f32[4,2,3,8,128]{4,3,2,1,0:T(8,128)S(1)}, f32[4,2,3,8,128]{4,3,2,1,0:T(8,128)S(1)}, u32[]{:S(2)}, u32[]{:S(2)}) collective-permute-start(f32[4,2,3,8,128]{4,3,2,1,0:T(8,128)S(1)} %get-tuple-element.35), channel_id=1, source_target_pairs={{0,24},{1,25},{2,26},{3,27},{4,28},{5,29},{6,30},{7,31},{8,16},{9,... | collective-permute-start | bytes 294920 | tf_op jit(solution)/shard_map/ppermute | solution.py:256
  21.8 4.3 %collective-permute-start.10 = (f32[1,2,3,8,128]{4,3,2,1,0:T(8,128)S(1)}, f32[1,2,3,8,128]{4,3,2,1,0:T(8,128)S(1)}, u32[]{:S(2)}, u32[]{:S(2)}) collective-permute-start(f32[1,2,3,8,128]{4,3,2,1,0:T(8,128)S(1)} %get-tuple-element.36), channel_id=1, source_target_pairs={{0,7},{1,2},{2,1},{3,4},{4,3},{5,6},{6,5},{7,0},{8,15},{9,10},{10,... | collective-permute-start | bytes 73736 | tf_op jit(solution)/shard_map/ppermute | solution.py:257
  21.8 4.3 %collective-permute-start.11 = (f32[1,2,3,8,128]{4,3,2,1,0:T(8,128)S(1)}, f32[1,2,3,8,128]{4,3,2,1,0:T(8,128)S(1)}, u32[]{:S(2)}, u32[]{:S(2)}) collective-permute-start(f32[1,2,3,8,128]{4,3,2,1,0:T(8,128)S(1)} %get-tuple-element.37), channel_id=1, source_target_pairs={{0,1},{1,0},{2,3},{3,2},{4,5},{5,4},{6,7},{7,6},{8,9},{9,8},{10,11... | collective-permute-start | bytes 73736 | tf_op jit(solution)/shard_map/ppermute | solution.py:258

commit v16 on v14

--- a/solution.py
+++ b/solution.py
@@ -246,7 +246,14 @@
 
     far_pairs = [(i, in_line(i, 1 if i // per_plane % 2 else -1)) for i in range(count)]
     near_pairs = [(i, in_line(i, -1 if i // per_plane % 2 else 1)) for i in range(count)]
-    outer_pairs = [(i, in_plane(i, 1 if i % 2 else -1)) for i in range(count)]
+
+    def outer_partner(i):
+        block = i % per_plane
+        if block in (0, per_plane - 1):
+            return in_line(i, -1 if i // per_plane % 2 else 1)
+        return in_plane(i, 1 if block % 2 else -1)
+
+    outer_pairs = [(i, outer_partner(i)) for i in range(count)]
     inner_pairs = [(i, in_plane(i, -1 if i % 2 else 1)) for i in range(count)]
 
     def sent_on(far, near, outer, inner):

time: 27.1 us -> 27.3 us (level)
  waiting for transfers between devices: 5.99 us -> 6.28 us
    ppermute x3, starting transfers between devices: 7.17 us -> 6.7 us  [sent_on(): far = lax.ppermute(far, 'gz', far_pairs)]
    ppermute x3, starting transfers between devices: 3.93 us -> 4.35 us  [sent_on(): near = lax.ppermute(near, 'gz', near_pairs)]
    ppermute x3, starting transfers between devices: 1.33 us -> 1.73 us  [sent_on(): outer = lax.ppermute(outer, 'gz', outer_pairs)]
    ppermute x3, starting transfers between devices: 3.49 us -> 3.09 us  [sent_on(): inner = lax.ppermute(inner, 'gz', inner_pairs)]
    ppermute x3, waiting for transfers between devices: 5.29 us -> 5.6 us  [sent_on(): outer = lax.ppermute(outer, 'gz', outer_pairs)]
  transfers between devices with their start and end apart: 12 -> 12, of which waited for: 5 -> 4; matrix products, arithmetic and copies ran while one was open for 0% -> 0% of each run, Pallas kernels for 3% -> 3%
where the time goes in v16:
time: 27.3 us; the launch traced here: 27.1 us
  starting transfers between devices  15.9 us (58%)
  waiting for transfers between devices  6.28 us (23%)
  Pallas kernels  2.97 us (11%)
  between operations  2.02 us (7%)
    ppermute x3, starting transfers between devices, sent_on(): far = lax.ppermute(far, 'gz', far_pairs)  6.7 us
    ppermute x3, waiting for transfers between devices, sent_on(): outer = lax.ppermute(outer, 'gz', outer_pairs)  5.6 us
    ppermute x3, starting transfers between devices, sent_on(): near = lax.ppermute(near, 'gz', near_pairs)  4.35 us
    ppermute x3, starting transfers between devices, sent_on(): inner = lax.ppermute(inner, 'gz', inner_pairs)  3.09 us
    pallas_call x9, Pallas kernels, call(): pl.pallas_call(kernel, name=name, out_shape=out_shapes, in_specs=[pl.Bloc...  2.97 us
    ppermute x3, starting transfers between devices, sent_on(): outer = lax.ppermute(outer, 'gz', outer_pairs)  1.73 us
    ppermute x3, waiting for transfers between devices, sent_on(): far = lax.ppermute(far, 'gz', far_pairs)  0.66 us
  transfers between devices with their start and end apart: 12, of which 4 were waited for; matrix products, arithmetic and copies ran while one was open for 0% of the time, Pallas kernels for 3%

profile of v16, /device:TPU:0, one launch (start us, length us, event | category | flops | bytes accessed | tf_op | source)
XLA Modules:
  0.0 27.1 jit_solution(4850106356296827751)
XLA Ops:
  0.0 1.1 %begin.1 = (f32[4,2,3,8,128]{4,3,2,1,0:T(8,128)S(1)}, f32[4,2,3,8,128]{4,3,2,1,0:T(8,128)S(1)}, f32[1,2,3,8,128]{4,3,2,1,0:T(8,128)S(1)}, f32[1,2,3,8,128]{4,3,2,1,0:T(8,128)S(1)}) custom-call(f32[4,2,3,8,128]{4,3,2,1,0:T(8,128)} %adjoint_hbm.1, f32[864,128]{1,0:T(8,128)} %bitcast.3), custom_call_target="tpu_custom_call" | custom-call | flops 368640 | bytes 368640 | tf_op jit(solution)/shard_map/begin/pallas_call | solution.py:220
  1.1 3.1 %collective-permute-start = (f32[4,2,3,8,128]{4,3,2,1,0:T(8,128)S(1)}, f32[4,2,3,8,128]{4,3,2,1,0:T(8,128)S(1)}, u32[]{:S(2)}, u32[]{:S(2)}) collective-permute-start(f32[4,2,3,8,128]{4,3,2,1,0:T(8,128)S(1)} %get-tuple-element.23), channel_id=1, source_target_pairs={{0,8},{1,9},{2,10},{3,11},{4,12},{5,13},{6,14},{7,15},{8,0},{9,1},... | collective-permute-start | bytes 294920 | tf_op jit(solution)/shard_map/ppermute | solution.py:260
  4.2 2.5 %collective-permute-start.1 = (f32[4,2,3,8,128]{4,3,2,1,0:T(8,128)S(1)}, f32[4,2,3,8,128]{4,3,2,1,0:T(8,128)S(1)}, u32[]{:S(2)}, u32[]{:S(2)}) collective-permute-start(f32[4,2,3,8,128]{4,3,2,1,0:T(8,128)S(1)} %get-tuple-element.24), channel_id=1, source_target_pairs={{0,24},{1,25},{2,26},{3,27},{4,28},{5,29},{6,30},{7,31},{8,16},{9,... | collective-permute-start | bytes 294920 | tf_op jit(solution)/shard_map/ppermute | solution.py:261
  6.7 0.7 %collective-permute-start.2 = (f32[1,2,3,8,128]{4,3,2,1,0:T(8,128)S(1)}, f32[1,2,3,8,128]{4,3,2,1,0:T(8,128)S(1)}, u32[]{:S(2)}, u32[]{:S(2)}) collective-permute-start(f32[1,2,3,8,128]{4,3,2,1,0:T(8,128)S(1)} %get-tuple-element.25), channel_id=1, source_target_pairs={{0,8},{1,2},{2,1},{3,4},{4,3},{5,6},{6,5},{7,15},{8,0},{9,10},{10,... | collective-permute-start | bytes 73736 | tf_op jit(solution)/shard_map/ppermute | solution.py:262
  7.3 0.9 %collective-permute-start.3 = (f32[1,2,3,8,128]{4,3,2,1,0:T(8,128)S(1)}, f32[1,2,3,8,128]{4,3,2,1,0:T(8,128)S(1)}, u32[]{:S(2)}, u32[]{:S(2)}) collective-permute-start(f32[1,2,3,8,128]{4,3,2,1,0:T(8,128)S(1)} %get-tuple-element.26), channel_id=1, source_target_pairs={{0,1},{1,0},{2,3},{3,2},{4,5},{5,4},{6,7},{7,6},{8,9},{9,8},{10,11... | collective-permute-start | bytes 73736 | tf_op jit(solution)/shard_map/ppermute | solution.py:263
  9.6 0.3 start.1
  9.9 1.6 %collective-permute-done.2.refs_3_ = f32[1,2,3,8,128]{4,3,2,1,0:T(8,128)S(1)} collective-permute-done((f32[1,2,3,8,128]{4,3,2,1,0:T(8,128)S(1)}, f32[1,2,3,8,128]{4,3,2,1,0:T(8,128)S(1)}, u32[]{:S(2)}, u32[]{:S(2)}) %collective-permute-start.2) | collective-permute-done | bytes 24608 | tf_op jit(solution)/shard_map/ppermute | solution.py:262
  11.5 0.0 collective-permute-done.3.refs_4_
  11.5 0.0 collective-permute-done.refs_1_
  11.5 0.2 third.1
  11.7 0.5 %collective-permute-start.4 = (f32[4,2,3,8,128]{4,3,2,1,0:T(8,128)S(1)}, f32[4,2,3,8,128]{4,3,2,1,0:T(8,128)S(1)}, u32[]{:S(2)}, u32[]{:S(2)}) collective-permute-start(f32[4,2,3,8,128]{4,3,2,1,0:T(8,128)S(1)} %get-tuple-element.28), channel_id=1, source_target_pairs={{0,8},{1,9},{2,10},{3,11},{4,12},{5,13},{6,14},{7,15},{8,0},{9,1},... | collective-permute-start | bytes 294920 | tf_op jit(solution)/shard_map/ppermute | solution.py:260
  12.2 2.6 %collective-permute-start.5 = (f32[4,2,3,8,128]{4,3,2,1,0:T(8,128)S(1)}, f32[4,2,3,8,128]{4,3,2,1,0:T(8,128)S(1)}, u32[]{:S(2)}, u32[]{:S(2)}) collective-permute-start(f32[4,2,3,8,128]{4,3,2,1,0:T(8,128)S(1)} %get-tuple-element.29), channel_id=1, source_target_pairs={{0,24},{1,25},{2,26},{3,27},{4,28},{5,29},{6,30},{7,31},{8,16},{9,... | collective-permute-start | bytes 294920 | tf_op jit(solution)/shard_map/ppermute | solution.py:261
  14.8 1.6 %collective-permute-start.7 = (f32[1,2,3,8,128]{4,3,2,1,0:T(8,128)S(1)}, f32[1,2,3,8,128]{4,3,2,1,0:T(8,128)S(1)}, u32[]{:S(2)}, u32[]{:S(2)}) collective-permute-start(f32[1,2,3,8,128]{4,3,2,1,0:T(8,128)S(1)} %get-tuple-element.31), channel_id=1, source_target_pairs={{0,1},{1,0},{2,3},{3,2},{4,5},{5,4},{6,7},{7,6},{8,9},{9,8},{10,11... | collective-permute-start | bytes 73736 | tf_op jit(solution)/shard_map/ppermute | solution.py:263
  17.1 0.3 local_1.1.refs_0_
  17.3 1.6 %collective-permute-done.6.refs_3_ = f32[1,2,3,8,128]{4,3,2,1,0:T(8,128)S(1)} collective-permute-done((f32[1,2,3,8,128]{4,3,2,1,0:T(8,128)S(1)}, f32[1,2,3,8,128]{4,3,2,1,0:T(8,128)S(1)}, u32[]{:S(2)}, u32[]{:S(2)}) %collective-permute-start.6) | collective-permute-done | bytes 24608 | tf_op jit(solution)/shard_map/ppermute | solution.py:262
  19.0 0.2 second.1
  19.1 0.8 %collective-permute-start.8 = (f32[4,2,3,8,128]{4,3,2,1,0:T(8,128)S(1)}, f32[4,2,3,8,128]{4,3,2,1,0:T(8,128)S(1)}, u32[]{:S(2)}, u32[]{:S(2)}) collective-permute-start(f32[4,2,3,8,128]{4,3,2,1,0:T(8,128)S(1)} %get-tuple-element.34), channel_id=1, source_target_pairs={{0,8},{1,9},{2,10},{3,11},{4,12},{5,13},{6,14},{7,15},{8,0},{9,1},... | collective-permute-start | bytes 294920 | tf_op jit(solution)/shard_map/ppermute | solution.py:260
  19.9 1.6 %collective-permute-start.9 = (f32[4,2,3,8,128]{4,3,2,1,0:T(8,128)S(1)}, f32[4,2,3,8,128]{4,3,2,1,0:T(8,128)S(1)}, u32[]{:S(2)}, u32[]{:S(2)}) collective-permute-start(f32[4,2,3,8,128]{4,3,2,1,0:T(8,128)S(1)} %get-tuple-element.35), channel_id=1, source_target_pairs={{0,24},{1,25},{2,26},{3,27},{4,28},{5,29},{6,30},{7,31},{8,16},{9,... | collective-permute-start | bytes 294920 | tf_op jit(solution)/shard_map/ppermute | solution.py:261
  21.5 1.0 %collective-permute-start.10 = (f32[1,2,3,8,128]{4,3,2,1,0:T(8,128)S(1)}, f32[1,2,3,8,128]{4,3,2,1,0:T(8,128)S(1)}, u32[]{:S(2)}, u32[]{:S(2)}) collective-permute-start(f32[1,2,3,8,128]{4,3,2,1,0:T(8,128)S(1)} %get-tuple-element.36), channel_id=1, source_target_pairs={{0,8},{1,2},{2,1},{3,4},{4,3},{5,6},{6,5},{7,15},{8,0},{9,10},{10,... | collective-permute-start | bytes 73736 | tf_op jit(solution)/shard_map/ppermute | solution.py:262
  22.6 0.6 %collective-permute-start.11 = (f32[1,2,3,8,128]{4,3,2,1,0:T(8,128)S(1)}, f32[1,2,3,8,128]{4,3,2,1,0:T(8,128)S(1)}, u32[]{:S(2)}, u32[]{:S(2)}) collective-permute-start(f32[1,2,3,8,128]{4,3,2,1,0:T(8,128)S(1)} %get-tuple-element.37), channel_id=1, source_target_pairs={{0,1},{1,0},{2,3},{3,2},{4,5},{5,4},{6,7},{7,6},{8,9},{9,8},{10,11... | collective-permute-start | bytes 73736 | tf_op jit(solution)/shard_map/ppermute | solution.py:263
  23.1 0.3 local_0.1.refs_0_
  23.4 2.4 %collective-permute-done.10.refs_3_ = f32[1,2,3,8,128]{4,3,2,1,0:T(8,128)S(1)} collective-permute-done((f32[1,2,3,8,128]{4,3,2,1,0:T(8,128)S(1)}, f32[1,2,3,8,128]{4,3,2,1,0:T(8,128)S(1)}, u32[]{:S(2)}, u32[]{:S(2)}) %collective-permute-start.10) | collective-permute-done | bytes 24608 | tf_op jit(solution)/shard_map/ppermute | solution.py:262
  25.8 0.7 %collective-permute-done.9.refs_2_ = f32[4,2,3,8,128]{4,3,2,1,0:T(8,128)S(1)} collective-permute-done((f32[4,2,3,8,128]{4,3,2,1,0:T(8,128)S(1)}, f32[4,2,3,8,128]{4,3,2,1,0:T(8,128)S(1)}, u32[]{:S(2)}, u32[]{:S(2)}) %collective-permute-start.9) | collective-permute-done | bytes 98336 | tf_op jit(solution)/shard_map/ppermute | solution.py:261
  26.4 0.7 %last.1 = f32[4,2,3,8,128]{4,3,2,1,0:T(8,128)} custom-call(f32[8,128]{1,0:T(8,128)S(1)} %eps.1.eps_ref, f32[6,8,128]{2,1,0:T(8,128)S(1)} %tapers.1.coefs_ref, f32[864,128]{1,0:T(8,128)S(1)} %bitcast.9, f32[4,2,3,8,128]{4,3,2,1,0:T(8,128)S(1)} %local_0.1.refs_0_, f32[4,2,3,8,128]{4,3,2,1,0:T(8,128)S(1)} %collective-permute-done.8.refs_1_, ...), custom_call_target="tpu_custom_call" | custom-call | flops 368640 | bytes 368640 | tf_op jit(solution)/shard_map/last/pallas_call | solution.py:220
  (13 shorter events, 0.1 us)
Async XLA Ops:
  0.0 9.6 %copy-start = (f32[4,3,4,2,3,3,128]{6,3,5,4,2,1,0:T(2,128)S(1)}, f32[4,3,4,2,3,3,128]{6,3,5,4,2,1,0:T(2,128)}, u32[]{:S(2)}) copy-start(f32[4,3,4,2,3,3,128]{6,3,5,4,2,1,0:T(2,128)} %param.6) | copy-start | bytes 1327108
  0.0 9.6 %copy-start.1 = (f32[4,2,3,8,128]{4,3,2,1,0:T(8,128)S(1)}, f32[4,2,3,8,128]{4,3,2,1,0:T(8,128)}, u32[]{:S(2)}) copy-start(f32[4,2,3,8,128]{4,3,2,1,0:T(8,128)} %adjoint_hbm.1) | copy-start | bytes 294916
  1.1 10.5 %collective-permute-start = (f32[4,2,3,8,128]{4,3,2,1,0:T(8,128)S(1)}, f32[4,2,3,8,128]{4,3,2,1,0:T(8,128)S(1)}, u32[]{:S(2)}, u32[]{:S(2)}) collective-permute-start(f32[4,2,3,8,128]{4,3,2,1,0:T(8,128)S(1)} %get-tuple-element.23), channel_id=1, source_target_pairs={{0,8},{1,9},{2,10},{3,11},{4,12},{5,13},{6,14},{7,15},{8,0},{9,1},... | collective-permute-start | bytes 294920 | tf_op jit(solution)/shard_map/ppermute | solution.py:260
  4.2 7.4 %collective-permute-start.1 = (f32[4,2,3,8,128]{4,3,2,1,0:T(8,128)S(1)}, f32[4,2,3,8,128]{4,3,2,1,0:T(8,128)S(1)}, u32[]{:S(2)}, u32[]{:S(2)}) collective-permute-start(f32[4,2,3,8,128]{4,3,2,1,0:T(8,128)S(1)} %get-tuple-element.24), channel_id=1, source_target_pairs={{0,24},{1,25},{2,26},{3,27},{4,28},{5,29},{6,30},{7,31},{8,16},{9,... | collective-permute-start | bytes 294920 | tf_op jit(solution)/shard_map/ppermute | solution.py:261
  6.7 4.9 %collective-permute-start.2 = (f32[1,2,3,8,128]{4,3,2,1,0:T(8,128)S(1)}, f32[1,2,3,8,128]{4,3,2,1,0:T(8,128)S(1)}, u32[]{:S(2)}, u32[]{:S(2)}) collective-permute-start(f32[1,2,3,8,128]{4,3,2,1,0:T(8,128)S(1)} %get-tuple-element.25), channel_id=1, source_target_pairs={{0,8},{1,2},{2,1},{3,4},{4,3},{5,6},{6,5},{7,15},{8,0},{9,10},{10,... | collective-permute-start | bytes 73736 | tf_op jit(solution)/shard_map/ppermute | solution.py:262
  7.3 4.2 %collective-permute-start.3 = (f32[1,2,3,8,128]{4,3,2,1,0:T(8,128)S(1)}, f32[1,2,3,8,128]{4,3,2,1,0:T(8,128)S(1)}, u32[]{:S(2)}, u32[]{:S(2)}) collective-permute-start(f32[1,2,3,8,128]{4,3,2,1,0:T(8,128)S(1)} %get-tuple-element.26), channel_id=1, source_target_pairs={{0,1},{1,0},{2,3},{3,2},{4,5},{5,4},{6,7},{7,6},{8,9},{9,8},{10,11... | collective-permute-start | bytes 73736 | tf_op jit(solution)/shard_map/ppermute | solution.py:263
  11.7 7.2 %collective-permute-start.4 = (f32[4,2,3,8,128]{4,3,2,1,0:T(8,128)S(1)}, f32[4,2,3,8,128]{4,3,2,1,0:T(8,128)S(1)}, u32[]{:S(2)}, u32[]{:S(2)}) collective-permute-start(f32[4,2,3,8,128]{4,3,2,1,0:T(8,128)S(1)} %get-tuple-element.28), channel_id=1, source_target_pairs={{0,8},{1,9},{2,10},{3,11},{4,12},{5,13},{6,14},{7,15},{8,0},{9,1},... | collective-permute-start | bytes 294920 | tf_op jit(solution)/shard_map/ppermute | solution.py:260
  12.2 6.8 %collective-permute-start.5 = (f32[4,2,3,8,128]{4,3,2,1,0:T(8,128)S(1)}, f32[4,2,3,8,128]{4,3,2,1,0:T(8,128)S(1)}, u32[]{:S(2)}, u32[]{:S(2)}) collective-permute-start(f32[4,2,3,8,128]{4,3,2,1,0:T(8,128)S(1)} %get-tuple-element.29), channel_id=1, source_target_pairs={{0,24},{1,25},{2,26},{3,27},{4,28},{5,29},{6,30},{7,31},{8,16},{9,... | collective-permute-start | bytes 294920 | tf_op jit(solution)/shard_map/ppermute | solution.py:261
  14.8 4.1 %collective-permute-start.6 = (f32[1,2,3,8,128]{4,3,2,1,0:T(8,128)S(1)}, f32[1,2,3,8,128]{4,3,2,1,0:T(8,128)S(1)}, u32[]{:S(2)}, u32[]{:S(2)}) collective-permute-start(f32[1,2,3,8,128]{4,3,2,1,0:T(8,128)S(1)} %get-tuple-element.30), channel_id=1, source_target_pairs={{0,8},{1,2},{2,1},{3,4},{4,3},{5,6},{6,5},{7,15},{8,0},{9,10},{10,... | collective-permute-start | bytes 73736 | tf_op jit(solution)/shard_map/ppermute | solution.py:262
  14.8 4.1 %collective-permute-start.7 = (f32[1,2,3,8,128]{4,3,2,1,0:T(8,128)S(1)}, f32[1,2,3,8,128]{4,3,2,1,0:T(8,128)S(1)}, u32[]{:S(2)}, u32[]{:S(2)}) collective-permute-start(f32[1,2,3,8,128]{4,3,2,1,0:T(8,128)S(1)} %get-tuple-element.31), channel_id=1, source_target_pairs={{0,1},{1,0},{2,3},{3,2},{4,5},{5,4},{6,7},{7,6},{8,9},{9,8},{10,11... | collective-permute-start | bytes 73736 | tf_op jit(solution)/shard_map/ppermute | solution.py:263
  19.1 6.6 %collective-permute-start.8 = (f32[4,2,3,8,128]{4,3,2,1,0:T(8,128)S(1)}, f32[4,2,3,8,128]{4,3,2,1,0:T(8,128)S(1)}, u32[]{:S(2)}, u32[]{:S(2)}) collective-permute-start(f32[4,2,3,8,128]{4,3,2,1,0:T(8,128)S(1)} %get-tuple-element.34), channel_id=1, source_target_pairs={{0,8},{1,9},{2,10},{3,11},{4,12},{5,13},{6,14},{7,15},{8,0},{9,1},... | collective-permute-start | bytes 294920 | tf_op jit(solution)/shard_map/ppermute | solution.py:260
  19.9 6.5 %collective-permute-start.9 = (f32[4,2,3,8,128]{4,3,2,1,0:T(8,128)S(1)}, f32[4,2,3,8,128]{4,3,2,1,0:T(8,128)S(1)}, u32[]{:S(2)}, u32[]{:S(2)}) collective-permute-start(f32[4,2,3,8,128]{4,3,2,1,0:T(8,128)S(1)} %get-tuple-element.35), channel_id=1, source_target_pairs={{0,24},{1,25},{2,26},{3,27},{4,28},{5,29},{6,30},{7,31},{8,16},{9,... | collective-permute-start | bytes 294920 | tf_op jit(solution)/shard_map/ppermute | solution.py:261
  21.5 4.2 %collective-permute-start.10 = (f32[1,2,3,8,128]{4,3,2,1,0:T(8,128)S(1)}, f32[1,2,3,8,128]{4,3,2,1,0:T(8,128)S(1)}, u32[]{:S(2)}, u32[]{:S(2)}) collective-permute-start(f32[1,2,3,8,128]{4,3,2,1,0:T(8,128)S(1)} %get-tuple-element.36), channel_id=1, source_target_pairs={{0,8},{1,2},{2,1},{3,4},{4,3},{5,6},{6,5},{7,15},{8,0},{9,10},{10,... | collective-permute-start | bytes 73736 | tf_op jit(solution)/shard_map/ppermute | solution.py:262
  22.6 3.2 %collective-permute-start.11 = (f32[1,2,3,8,128]{4,3,2,1,0:T(8,128)S(1)}, f32[1,2,3,8,128]{4,3,2,1,0:T(8,128)S(1)}, u32[]{:S(2)}, u32[]{:S(2)}) collective-permute-start(f32[1,2,3,8,128]{4,3,2,1,0:T(8,128)S(1)} %get-tuple-element.37), channel_id=1, source_target_pairs={{0,1},{1,0},{2,3},{3,2},{4,5},{5,4},{6,7},{7,6},{8,9},{9,8},{10,11... | collective-permute-start | bytes 73736 | tf_op jit(solution)/shard_map/ppermute | solution.py:263

commit v17 on v15

--- a/solution.py
+++ b/solution.py
@@ -149,7 +149,7 @@
 
 def arrived_sum(links_ref, link_set, row, rows, arrivals, coefs_ref=None):
     sum_ref, near_ref, far_ref, outer_ref, inner_ref = arrivals
-    if coefs_ref is not None:
+    if coefs_ref is None:
         near_ref, far_ref = far_ref, near_ref
     _, first_pos, odd_plane, odd_block = place(rows)
     far, near = load_field(far_ref, row), load_field(near_ref, row)
@@ -251,7 +251,7 @@
     outer_pairs = [(i, in_plane(i, 1 if i % 2 else -1)) for i in range(count)]
     inner_pairs = [(i, in_plane(i, -1 if i % 2 else 1)) for i in range(count)]
 
-    def sent_on(far, near, outer, inner, far_first=False):
+    def sent_on(far, near, outer, inner, far_first=True):
         near = lax.ppermute(near, "gz", near_pairs)
         far = lax.ppermute(far, "gz", far_pairs)
         outer = lax.ppermute(outer, "gz", outer_pairs)
@@ -272,7 +272,7 @@
             pltpu.SemaphoreType.DMA((rows + 1,)),
         ],
     )
-    arrived = sent_on(*sending, far_first=True)
+    arrived = sent_on(*sending, far_first=False)
     coefs = call(
         functools.partial(taper_kernel, rows), "tapers", (source_slice, band_width), coefs_shape, 1, pltpu.SMEM
     )

time: 27.3 us -> 27.6 us (1.011)
    ppermute x3, starting transfers between devices: 1.81 us -> 3.66 us  [sent_on(): near = lax.ppermute(near, 'gz', near_pairs)]
    ppermute x3, starting transfers between devices: 7.97 us -> 6.29 us  [sent_on(): far = lax.ppermute(far, 'gz', far_pairs)]
    ppermute x3, waiting for transfers between devices: 0.7 us -> 1.74 us  [sent_on(): near = lax.ppermute(near, 'gz', near_pairs)]
    ppermute x3, waiting for transfers between devices: 1.51 us -> 0.68 us  [sent_on(): far = lax.ppermute(far, 'gz', far_pairs)]
    ppermute x3, starting transfers between devices: 1.63 us -> 1.33 us  [sent_on(): outer = lax.ppermute(outer, 'gz', outer_pairs)]
    ppermute x3, starting transfers between devices: 3.19 us -> 3.49 us  [sent_on(): inner = lax.ppermute(inner, 'gz', inner_pairs)]
  transfers between devices with their start and end apart: 12 -> 12, of which waited for: 6 -> 7; matrix products, arithmetic and copies ran while one was open for 0% -> 0% of each run, Pallas kernels for 3% -> 3%
where the time goes in v17:
time: 27.6 us; the launch traced here: 27.4 us
  starting transfers between devices  14.8 us (54%)
  waiting for transfers between devices  7.71 us (28%)
  Pallas kernels  2.95 us (11%)
  between operations  2.02 us (7%)
    ppermute x3, starting transfers between devices, sent_on(): far = lax.ppermute(far, 'gz', far_pairs)  6.29 us
    ppermute x3, waiting for transfers between devices, sent_on(): outer = lax.ppermute(outer, 'gz', outer_pairs)  5.29 us
    ppermute x3, starting transfers between devices, sent_on(): near = lax.ppermute(near, 'gz', near_pairs)  3.66 us
    ppermute x3, starting transfers between devices, sent_on(): inner = lax.ppermute(inner, 'gz', inner_pairs)  3.49 us
    pallas_call x9, Pallas kernels, call(): pl.pallas_call(kernel, name=name, out_shape=out_shapes, in_specs=[pl.Bloc...  2.95 us
    ppermute x3, waiting for transfers between devices, sent_on(): near = lax.ppermute(near, 'gz', near_pairs)  1.74 us
    ppermute x3, starting transfers between devices, sent_on(): outer = lax.ppermute(outer, 'gz', outer_pairs)  1.33 us
    ppermute x3, waiting for transfers between devices, sent_on(): far = lax.ppermute(far, 'gz', far_pairs)  0.68 us
  transfers between devices with their start and end apart: 12, of which 7 were waited for; matrix products, arithmetic and copies ran while one was open for 0% of the time, Pallas kernels for 3%

profile of v17, /device:TPU:0, one launch (start us, length us, event | category | flops | bytes accessed | tf_op | source)
XLA Modules:
  0.0 27.4 jit_solution(1069084115517596660)
XLA Ops:
  0.0 1.1 %begin.1 = (f32[4,2,3,8,128]{4,3,2,1,0:T(8,128)S(1)}, f32[4,2,3,8,128]{4,3,2,1,0:T(8,128)S(1)}, f32[1,2,3,8,128]{4,3,2,1,0:T(8,128)S(1)}, f32[1,2,3,8,128]{4,3,2,1,0:T(8,128)S(1)}) custom-call(f32[4,2,3,8,128]{4,3,2,1,0:T(8,128)} %adjoint_hbm.1, f32[864,128]{1,0:T(8,128)} %bitcast.3), custom_call_target="tpu_custom_call" | custom-call | flops 368640 | bytes 368640 | tf_op jit(solution)/shard_map/begin/pallas_call | solution.py:222
  1.1 3.1 %collective-permute-start = (f32[4,2,3,8,128]{4,3,2,1,0:T(8,128)S(1)}, f32[4,2,3,8,128]{4,3,2,1,0:T(8,128)S(1)}, u32[]{:S(2)}, u32[]{:S(2)}) collective-permute-start(f32[4,2,3,8,128]{4,3,2,1,0:T(8,128)S(1)} %get-tuple-element.23), channel_id=1, source_target_pairs={{0,8},{1,9},{2,10},{3,11},{4,12},{5,13},{6,14},{7,15},{8,0},{9,1},... | collective-permute-start | bytes 294920 | tf_op jit(solution)/shard_map/ppermute | solution.py:255
  4.2 2.5 %collective-permute-start.1 = (f32[4,2,3,8,128]{4,3,2,1,0:T(8,128)S(1)}, f32[4,2,3,8,128]{4,3,2,1,0:T(8,128)S(1)}, u32[]{:S(2)}, u32[]{:S(2)}) collective-permute-start(f32[4,2,3,8,128]{4,3,2,1,0:T(8,128)S(1)} %get-tuple-element.24), channel_id=1, source_target_pairs={{0,24},{1,25},{2,26},{3,27},{4,28},{5,29},{6,30},{7,31},{8,16},{9,... | collective-permute-start | bytes 294920 | tf_op jit(solution)/shard_map/ppermute | solution.py:256
  6.7 1.3 %collective-permute-start.2 = (f32[1,2,3,8,128]{4,3,2,1,0:T(8,128)S(1)}, f32[1,2,3,8,128]{4,3,2,1,0:T(8,128)S(1)}, u32[]{:S(2)}, u32[]{:S(2)}) collective-permute-start(f32[1,2,3,8,128]{4,3,2,1,0:T(8,128)S(1)} %get-tuple-element.25), channel_id=1, source_target_pairs={{0,7},{1,2},{2,1},{3,4},{4,3},{5,6},{6,5},{7,0},{8,15},{9,10},{10,... | collective-permute-start | bytes 73736 | tf_op jit(solution)/shard_map/ppermute | solution.py:257
  8.0 0.3 %collective-permute-start.3 = (f32[1,2,3,8,128]{4,3,2,1,0:T(8,128)S(1)}, f32[1,2,3,8,128]{4,3,2,1,0:T(8,128)S(1)}, u32[]{:S(2)}, u32[]{:S(2)}) collective-permute-start(f32[1,2,3,8,128]{4,3,2,1,0:T(8,128)S(1)} %get-tuple-element.26), channel_id=1, source_target_pairs={{0,1},{1,0},{2,3},{3,2},{4,5},{5,4},{6,7},{7,6},{8,9},{9,8},{10,11... | collective-permute-start | bytes 73736 | tf_op jit(solution)/shard_map/ppermute | solution.py:258
  9.6 0.3 start.1
  9.9 1.1 %collective-permute-done.2.refs_3_ = f32[1,2,3,8,128]{4,3,2,1,0:T(8,128)S(1)} collective-permute-done((f32[1,2,3,8,128]{4,3,2,1,0:T(8,128)S(1)}, f32[1,2,3,8,128]{4,3,2,1,0:T(8,128)S(1)}, u32[]{:S(2)}, u32[]{:S(2)}) %collective-permute-start.2) | collective-permute-done | bytes 24608 | tf_op jit(solution)/shard_map/ppermute | solution.py:257
  11.0 0.4 %collective-permute-done.1.refs_2_ = f32[4,2,3,8,128]{4,3,2,1,0:T(8,128)S(1)} collective-permute-done((f32[4,2,3,8,128]{4,3,2,1,0:T(8,128)S(1)}, f32[4,2,3,8,128]{4,3,2,1,0:T(8,128)S(1)}, u32[]{:S(2)}, u32[]{:S(2)}) %collective-permute-start.1) | collective-permute-done | bytes 98336 | tf_op jit(solution)/shard_map/ppermute | solution.py:256
  11.3 0.1 third.1
  11.5 1.9 %collective-permute-start.4 = (f32[4,2,3,8,128]{4,3,2,1,0:T(8,128)S(1)}, f32[4,2,3,8,128]{4,3,2,1,0:T(8,128)S(1)}, u32[]{:S(2)}, u32[]{:S(2)}) collective-permute-start(f32[4,2,3,8,128]{4,3,2,1,0:T(8,128)S(1)} %get-tuple-element.28), channel_id=1, source_target_pairs={{0,24},{1,25},{2,26},{3,27},{4,28},{5,29},{6,30},{7,31},{8,16},{9,... | collective-permute-start | bytes 294920 | tf_op jit(solution)/shard_map/ppermute | solution.py:256
  13.3 0.6 %collective-permute-start.5 = (f32[4,2,3,8,128]{4,3,2,1,0:T(8,128)S(1)}, f32[4,2,3,8,128]{4,3,2,1,0:T(8,128)S(1)}, u32[]{:S(2)}, u32[]{:S(2)}) collective-permute-start(f32[4,2,3,8,128]{4,3,2,1,0:T(8,128)S(1)} %get-tuple-element.29), channel_id=1, source_target_pairs={{0,8},{1,9},{2,10},{3,11},{4,12},{5,13},{6,14},{7,15},{8,0},{9,1},... | collective-permute-start | bytes 294920 | tf_op jit(solution)/shard_map/ppermute | solution.py:255
  13.9 0.0 collective-permute-start.6
  13.9 1.6 %collective-permute-start.7 = (f32[1,2,3,8,128]{4,3,2,1,0:T(8,128)S(1)}, f32[1,2,3,8,128]{4,3,2,1,0:T(8,128)S(1)}, u32[]{:S(2)}, u32[]{:S(2)}) collective-permute-start(f32[1,2,3,8,128]{4,3,2,1,0:T(8,128)S(1)} %get-tuple-element.31), channel_id=1, source_target_pairs={{0,1},{1,0},{2,3},{3,2},{4,5},{5,4},{6,7},{7,6},{8,9},{9,8},{10,11... | collective-permute-start | bytes 73736 | tf_op jit(solution)/shard_map/ppermute | solution.py:258
  16.2 0.3 local_1.1.refs_0_
  16.4 1.8 %collective-permute-done.6.refs_3_ = f32[1,2,3,8,128]{4,3,2,1,0:T(8,128)S(1)} collective-permute-done((f32[1,2,3,8,128]{4,3,2,1,0:T(8,128)S(1)}, f32[1,2,3,8,128]{4,3,2,1,0:T(8,128)S(1)}, u32[]{:S(2)}, u32[]{:S(2)}) %collective-permute-start.6) | collective-permute-done | bytes 24608 | tf_op jit(solution)/shard_map/ppermute | solution.py:257
  18.2 0.8 %collective-permute-done.5.refs_2_ = f32[4,2,3,8,128]{4,3,2,1,0:T(8,128)S(1)} collective-permute-done((f32[4,2,3,8,128]{4,3,2,1,0:T(8,128)S(1)}, f32[4,2,3,8,128]{4,3,2,1,0:T(8,128)S(1)}, u32[]{:S(2)}, u32[]{:S(2)}) %collective-permute-start.5) | collective-permute-done | bytes 98336 | tf_op jit(solution)/shard_map/ppermute | solution.py:255
  19.0 0.2 second.1
  19.2 2.0 %collective-permute-start.8 = (f32[4,2,3,8,128]{4,3,2,1,0:T(8,128)S(1)}, f32[4,2,3,8,128]{4,3,2,1,0:T(8,128)S(1)}, u32[]{:S(2)}, u32[]{:S(2)}) collective-permute-start(f32[4,2,3,8,128]{4,3,2,1,0:T(8,128)S(1)} %get-tuple-element.34), channel_id=1, source_target_pairs={{0,24},{1,25},{2,26},{3,27},{4,28},{5,29},{6,30},{7,31},{8,16},{9,... | collective-permute-start | bytes 294920 | tf_op jit(solution)/shard_map/ppermute | solution.py:256
  21.1 1.6 %collective-permute-start.11 = (f32[1,2,3,8,128]{4,3,2,1,0:T(8,128)S(1)}, f32[1,2,3,8,128]{4,3,2,1,0:T(8,128)S(1)}, u32[]{:S(2)}, u32[]{:S(2)}) collective-permute-start(f32[1,2,3,8,128]{4,3,2,1,0:T(8,128)S(1)} %get-tuple-element.37), channel_id=1, source_target_pairs={{0,1},{1,0},{2,3},{3,2},{4,5},{5,4},{6,7},{7,6},{8,9},{9,8},{10,11... | collective-permute-start | bytes 73736 | tf_op jit(solution)/shard_map/ppermute | solution.py:258
  22.7 0.3 local_0.1.refs_0_
  23.0 2.4 %collective-permute-done.10.refs_3_ = f32[1,2,3,8,128]{4,3,2,1,0:T(8,128)S(1)} collective-permute-done((f32[1,2,3,8,128]{4,3,2,1,0:T(8,128)S(1)}, f32[1,2,3,8,128]{4,3,2,1,0:T(8,128)S(1)}, u32[]{:S(2)}, u32[]{:S(2)}) %collective-permute-start.10) | collective-permute-done | bytes 24608 | tf_op jit(solution)/shard_map/ppermute | solution.py:257
  25.5 0.3 %collective-permute-done.8.refs_1_ = f32[4,2,3,8,128]{4,3,2,1,0:T(8,128)S(1)} collective-permute-done((f32[4,2,3,8,128]{4,3,2,1,0:T(8,128)S(1)}, f32[4,2,3,8,128]{4,3,2,1,0:T(8,128)S(1)}, u32[]{:S(2)}, u32[]{:S(2)}) %collective-permute-start.8) | collective-permute-done | bytes 98336 | tf_op jit(solution)/shard_map/ppermute | solution.py:256
  25.8 0.9 %collective-permute-done.9.refs_2_ = f32[4,2,3,8,128]{4,3,2,1,0:T(8,128)S(1)} collective-permute-done((f32[4,2,3,8,128]{4,3,2,1,0:T(8,128)S(1)}, f32[4,2,3,8,128]{4,3,2,1,0:T(8,128)S(1)}, u32[]{:S(2)}, u32[]{:S(2)}) %collective-permute-start.9) | collective-permute-done | bytes 98336 | tf_op jit(solution)/shard_map/ppermute | solution.py:255
  26.7 0.7 %last.1 = f32[4,2,3,8,128]{4,3,2,1,0:T(8,128)} custom-call(f32[8,128]{1,0:T(8,128)S(1)} %eps.1.eps_ref, f32[6,8,128]{2,1,0:T(8,128)S(1)} %tapers.1.coefs_ref, f32[864,128]{1,0:T(8,128)S(1)} %bitcast.9, f32[4,2,3,8,128]{4,3,2,1,0:T(8,128)S(1)} %local_0.1.refs_0_, f32[4,2,3,8,128]{4,3,2,1,0:T(8,128)S(1)} %collective-permute-done.8.refs_1_, ...), custom_call_target="tpu_custom_call" | custom-call | flops 368640 | bytes 368640 | tf_op jit(solution)/shard_map/last/pallas_call | solution.py:222
  (13 shorter events, 0.1 us)
Async XLA Ops:
  0.0 9.6 %copy-start = (f32[4,3,4,2,3,3,128]{6,3,5,4,2,1,0:T(2,128)S(1)}, f32[4,3,4,2,3,3,128]{6,3,5,4,2,1,0:T(2,128)}, u32[]{:S(2)}) copy-start(f32[4,3,4,2,3,3,128]{6,3,5,4,2,1,0:T(2,128)} %param.6) | copy-start | bytes 1327108
  0.0 9.6 %copy-start.1 = (f32[4,2,3,8,128]{4,3,2,1,0:T(8,128)S(1)}, f32[4,2,3,8,128]{4,3,2,1,0:T(8,128)}, u32[]{:S(2)}) copy-start(f32[4,2,3,8,128]{4,3,2,1,0:T(8,128)} %adjoint_hbm.1) | copy-start | bytes 294916
  1.1 9.9 %collective-permute-start = (f32[4,2,3,8,128]{4,3,2,1,0:T(8,128)S(1)}, f32[4,2,3,8,128]{4,3,2,1,0:T(8,128)S(1)}, u32[]{:S(2)}, u32[]{:S(2)}) collective-permute-start(f32[4,2,3,8,128]{4,3,2,1,0:T(8,128)S(1)} %get-tuple-element.23), channel_id=1, source_target_pairs={{0,8},{1,9},{2,10},{3,11},{4,12},{5,13},{6,14},{7,15},{8,0},{9,1},... | collective-permute-start | bytes 294920 | tf_op jit(solution)/shard_map/ppermute | solution.py:255
  4.2 7.2 %collective-permute-start.1 = (f32[4,2,3,8,128]{4,3,2,1,0:T(8,128)S(1)}, f32[4,2,3,8,128]{4,3,2,1,0:T(8,128)S(1)}, u32[]{:S(2)}, u32[]{:S(2)}) collective-permute-start(f32[4,2,3,8,128]{4,3,2,1,0:T(8,128)S(1)} %get-tuple-element.24), channel_id=1, source_target_pairs={{0,24},{1,25},{2,26},{3,27},{4,28},{5,29},{6,30},{7,31},{8,16},{9,... | collective-permute-start | bytes 294920 | tf_op jit(solution)/shard_map/ppermute | solution.py:256
  6.7 4.3 %collective-permute-start.2 = (f32[1,2,3,8,128]{4,3,2,1,0:T(8,128)S(1)}, f32[1,2,3,8,128]{4,3,2,1,0:T(8,128)S(1)}, u32[]{:S(2)}, u32[]{:S(2)}) collective-permute-start(f32[1,2,3,8,128]{4,3,2,1,0:T(8,128)S(1)} %get-tuple-element.25), channel_id=1, source_target_pairs={{0,7},{1,2},{2,1},{3,4},{4,3},{5,6},{6,5},{7,0},{8,15},{9,10},{10,... | collective-permute-start | bytes 73736 | tf_op jit(solution)/shard_map/ppermute | solution.py:257
  8.0 3.0 %collective-permute-start.3 = (f32[1,2,3,8,128]{4,3,2,1,0:T(8,128)S(1)}, f32[1,2,3,8,128]{4,3,2,1,0:T(8,128)S(1)}, u32[]{:S(2)}, u32[]{:S(2)}) collective-permute-start(f32[1,2,3,8,128]{4,3,2,1,0:T(8,128)S(1)} %get-tuple-element.26), channel_id=1, source_target_pairs={{0,1},{1,0},{2,3},{3,2},{4,5},{5,4},{6,7},{7,6},{8,9},{9,8},{10,11... | collective-permute-start | bytes 73736 | tf_op jit(solution)/shard_map/ppermute | solution.py:258
  11.5 6.7 %collective-permute-start.4 = (f32[4,2,3,8,128]{4,3,2,1,0:T(8,128)S(1)}, f32[4,2,3,8,128]{4,3,2,1,0:T(8,128)S(1)}, u32[]{:S(2)}, u32[]{:S(2)}) collective-permute-start(f32[4,2,3,8,128]{4,3,2,1,0:T(8,128)S(1)} %get-tuple-element.28), channel_id=1, source_target_pairs={{0,24},{1,25},{2,26},{3,27},{4,28},{5,29},{6,30},{7,31},{8,16},{9,... | collective-permute-start | bytes 294920 | tf_op jit(solution)/shard_map/ppermute | solution.py:256
  13.3 5.7 %collective-permute-start.5 = (f32[4,2,3,8,128]{4,3,2,1,0:T(8,128)S(1)}, f32[4,2,3,8,128]{4,3,2,1,0:T(8,128)S(1)}, u32[]{:S(2)}, u32[]{:S(2)}) collective-permute-start(f32[4,2,3,8,128]{4,3,2,1,0:T(8,128)S(1)} %get-tuple-element.29), channel_id=1, source_target_pairs={{0,8},{1,9},{2,10},{3,11},{4,12},{5,13},{6,14},{7,15},{8,0},{9,1},... | collective-permute-start | bytes 294920 | tf_op jit(solution)/shard_map/ppermute | solution.py:255
  13.9 4.3 %collective-permute-start.6 = (f32[1,2,3,8,128]{4,3,2,1,0:T(8,128)S(1)}, f32[1,2,3,8,128]{4,3,2,1,0:T(8,128)S(1)}, u32[]{:S(2)}, u32[]{:S(2)}) collective-permute-start(f32[1,2,3,8,128]{4,3,2,1,0:T(8,128)S(1)} %get-tuple-element.30), channel_id=1, source_target_pairs={{0,7},{1,2},{2,1},{3,4},{4,3},{5,6},{6,5},{7,0},{8,15},{9,10},{10,... | collective-permute-start | bytes 73736 | tf_op jit(solution)/shard_map/ppermute | solution.py:257
  13.9 4.3 %collective-permute-start.7 = (f32[1,2,3,8,128]{4,3,2,1,0:T(8,128)S(1)}, f32[1,2,3,8,128]{4,3,2,1,0:T(8,128)S(1)}, u32[]{:S(2)}, u32[]{:S(2)}) collective-permute-start(f32[1,2,3,8,128]{4,3,2,1,0:T(8,128)S(1)} %get-tuple-element.31), channel_id=1, source_target_pairs={{0,1},{1,0},{2,3},{3,2},{4,5},{5,4},{6,7},{7,6},{8,9},{9,8},{10,11... | collective-permute-start | bytes 73736 | tf_op jit(solution)/shard_map/ppermute | solution.py:258
  19.2 6.6 %collective-permute-start.8 = (f32[4,2,3,8,128]{4,3,2,1,0:T(8,128)S(1)}, f32[4,2,3,8,128]{4,3,2,1,0:T(8,128)S(1)}, u32[]{:S(2)}, u32[]{:S(2)}) collective-permute-start(f32[4,2,3,8,128]{4,3,2,1,0:T(8,128)S(1)} %get-tuple-element.34), channel_id=1, source_target_pairs={{0,24},{1,25},{2,26},{3,27},{4,28},{5,29},{6,30},{7,31},{8,16},{9,... | collective-permute-start | bytes 294920 | tf_op jit(solution)/shard_map/ppermute | solution.py:256
  21.1 5.6 %collective-permute-start.9 = (f32[4,2,3,8,128]{4,3,2,1,0:T(8,128)S(1)}, f32[4,2,3,8,128]{4,3,2,1,0:T(8,128)S(1)}, u32[]{:S(2)}, u32[]{:S(2)}) collective-permute-start(f32[4,2,3,8,128]{4,3,2,1,0:T(8,128)S(1)} %get-tuple-element.35), channel_id=1, source_target_pairs={{0,8},{1,9},{2,10},{3,11},{4,12},{5,13},{6,14},{7,15},{8,0},{9,1},... | collective-permute-start | bytes 294920 | tf_op jit(solution)/shard_map/ppermute | solution.py:255
  21.1 4.3 %collective-permute-start.10 = (f32[1,2,3,8,128]{4,3,2,1,0:T(8,128)S(1)}, f32[1,2,3,8,128]{4,3,2,1,0:T(8,128)S(1)}, u32[]{:S(2)}, u32[]{:S(2)}) collective-permute-start(f32[1,2,3,8,128]{4,3,2,1,0:T(8,128)S(1)} %get-tuple-element.36), channel_id=1, source_target_pairs={{0,7},{1,2},{2,1},{3,4},{4,3},{5,6},{6,5},{7,0},{8,15},{9,10},{10,... | collective-permute-start | bytes 73736 | tf_op jit(solution)/shard_map/ppermute | solution.py:257
  21.1 4.3 %collective-permute-start.11 = (f32[1,2,3,8,128]{4,3,2,1,0:T(8,128)S(1)}, f32[1,2,3,8,128]{4,3,2,1,0:T(8,128)S(1)}, u32[]{:S(2)}, u32[]{:S(2)}) collective-permute-start(f32[1,2,3,8,128]{4,3,2,1,0:T(8,128)S(1)} %get-tuple-element.37), channel_id=1, source_target_pairs={{0,1},{1,0},{2,3},{3,2},{4,5},{5,4},{6,7},{7,6},{8,9},{9,8},{10,11... | collective-permute-start | bytes 73736 | tf_op jit(solution)/shard_map/ppermute | solution.py:258

commit v18 on v15

--- a/solution.py
+++ b/solution.py
@@ -149,7 +149,7 @@
 
 def arrived_sum(links_ref, link_set, row, rows, arrivals, coefs_ref=None):
     sum_ref, near_ref, far_ref, outer_ref, inner_ref = arrivals
-    if coefs_ref is not None:
+    if link_set == 1:
         near_ref, far_ref = far_ref, near_ref
     _, first_pos, odd_plane, odd_block = place(rows)
     far, near = load_field(far_ref, row), load_field(near_ref, row)
@@ -272,7 +272,7 @@
             pltpu.SemaphoreType.DMA((rows + 1,)),
         ],
     )
-    arrived = sent_on(*sending, far_first=True)
+    arrived = sent_on(*sending)
     coefs = call(
         functools.partial(taper_kernel, rows), "tapers", (source_slice, band_width), coefs_shape, 1, pltpu.SMEM
     )
@@ -284,7 +284,7 @@
     third, *sending = call(
         functools.partial(third_kernel, rows), "third", (coefs, links, total) + arrived, (whole,) + sent, 10
     )
-    arrived = sent_on(*sending)
+    arrived = sent_on(*sending, far_first=True)
     mixed, *sending, base = call(
         functools.partial(second_kernel, rows), "second", (eps, coefs, links, local(1, third)) + arrived + (start, third),
         (whole,) + sent + (whole,), 10,

time: 27.3 us -> 27.4 us (level)
  starting transfers between devices: 14.6 us -> 15.1 us
  waiting for transfers between devices: 7.51 us -> 7.13 us
    ppermute x3, starting transfers between devices: 1.81 us -> 4.41 us  [sent_on(): near = lax.ppermute(near, 'gz', near_pairs)]
    ppermute x3, starting transfers between devices: 7.97 us -> 6.36 us  [sent_on(): far = lax.ppermute(far, 'gz', far_pairs)]
    ppermute x3, waiting for transfers between devices: 1.51 us -> 0.7 us  [sent_on(): far = lax.ppermute(far, 'gz', far_pairs)]
    ppermute x3, waiting for transfers between devices: 5.28 us -> 5.63 us  [sent_on(): outer = lax.ppermute(outer, 'gz', outer_pairs)]
    ppermute x3, starting transfers between devices: 1.63 us -> 1.33 us  [sent_on(): outer = lax.ppermute(outer, 'gz', outer_pairs)]
where the time goes in v18:
time: 27.4 us; the launch traced here: 27.2 us
  starting transfers between devices  15.1 us (55%)
  waiting for transfers between devices  7.13 us (26%)
  Pallas kernels  2.94 us (11%)
  between operations  2.02 us (7%)
    ppermute x3, starting transfers between devices, sent_on(): far = lax.ppermute(far, 'gz', far_pairs)  6.36 us
    ppermute x3, waiting for transfers between devices, sent_on(): outer = lax.ppermute(outer, 'gz', outer_pairs)  5.63 us
    ppermute x3, starting transfers between devices, sent_on(): near = lax.ppermute(near, 'gz', near_pairs)  4.41 us
    ppermute x3, starting transfers between devices, sent_on(): inner = lax.ppermute(inner, 'gz', inner_pairs)  2.99 us
    pallas_call x9, Pallas kernels, call(): pl.pallas_call(kernel, name=name, out_shape=out_shapes, in_specs=[pl.Bloc...  2.94 us
    ppermute x3, starting transfers between devices, sent_on(): outer = lax.ppermute(outer, 'gz', outer_pairs)  1.33 us
    ppermute x3, waiting for transfers between devices, sent_on(): near = lax.ppermute(near, 'gz', near_pairs)  0.79 us
    ppermute x3, waiting for transfers between devices, sent_on(): far = lax.ppermute(far, 'gz', far_pairs)  0.7 us
  transfers between devices with their start and end apart: 12, of which 6 were waited for; matrix products, arithmetic and copies ran while one was open for 0% of the time, Pallas kernels for 3%

profile of v18, /device:TPU:0, one launch (start us, length us, event | category | flops | bytes accessed | tf_op | source)
XLA Modules:
  0.0 27.2 jit_solution(17848110981469951069)
XLA Ops:
  0.0 1.1 %begin.1 = (f32[4,2,3,8,128]{4,3,2,1,0:T(8,128)S(1)}, f32[4,2,3,8,128]{4,3,2,1,0:T(8,128)S(1)}, f32[1,2,3,8,128]{4,3,2,1,0:T(8,128)S(1)}, f32[1,2,3,8,128]{4,3,2,1,0:T(8,128)S(1)}) custom-call(f32[4,2,3,8,128]{4,3,2,1,0:T(8,128)} %adjoint_hbm.1, f32[864,128]{1,0:T(8,128)} %bitcast.3), custom_call_target="tpu_custom_call" | custom-call | flops 368640 | bytes 368640 | tf_op jit(solution)/shard_map/begin/pallas_call | solution.py:222
  1.1 3.1 %collective-permute-start = (f32[4,2,3,8,128]{4,3,2,1,0:T(8,128)S(1)}, f32[4,2,3,8,128]{4,3,2,1,0:T(8,128)S(1)}, u32[]{:S(2)}, u32[]{:S(2)}) collective-permute-start(f32[4,2,3,8,128]{4,3,2,1,0:T(8,128)S(1)} %get-tuple-element.23), channel_id=1, source_target_pairs={{0,8},{1,9},{2,10},{3,11},{4,12},{5,13},{6,14},{7,15},{8,0},{9,1},... | collective-permute-start | bytes 294920 | tf_op jit(solution)/shard_map/ppermute | solution.py:255
  4.2 2.5 %collective-permute-start.1 = (f32[4,2,3,8,128]{4,3,2,1,0:T(8,128)S(1)}, f32[4,2,3,8,128]{4,3,2,1,0:T(8,128)S(1)}, u32[]{:S(2)}, u32[]{:S(2)}) collective-permute-start(f32[4,2,3,8,128]{4,3,2,1,0:T(8,128)S(1)} %get-tuple-element.24), channel_id=1, source_target_pairs={{0,24},{1,25},{2,26},{3,27},{4,28},{5,29},{6,30},{7,31},{8,16},{9,... | collective-permute-start | bytes 294920 | tf_op jit(solution)/shard_map/ppermute | solution.py:256
  6.7 1.3 %collective-permute-start.2 = (f32[1,2,3,8,128]{4,3,2,1,0:T(8,128)S(1)}, f32[1,2,3,8,128]{4,3,2,1,0:T(8,128)S(1)}, u32[]{:S(2)}, u32[]{:S(2)}) collective-permute-start(f32[1,2,3,8,128]{4,3,2,1,0:T(8,128)S(1)} %get-tuple-element.25), channel_id=1, source_target_pairs={{0,7},{1,2},{2,1},{3,4},{4,3},{5,6},{6,5},{7,0},{8,15},{9,10},{10,... | collective-permute-start | bytes 73736 | tf_op jit(solution)/shard_map/ppermute | solution.py:257
  8.0 0.3 %collective-permute-start.3 = (f32[1,2,3,8,128]{4,3,2,1,0:T(8,128)S(1)}, f32[1,2,3,8,128]{4,3,2,1,0:T(8,128)S(1)}, u32[]{:S(2)}, u32[]{:S(2)}) collective-permute-start(f32[1,2,3,8,128]{4,3,2,1,0:T(8,128)S(1)} %get-tuple-element.26), channel_id=1, source_target_pairs={{0,1},{1,0},{2,3},{3,2},{4,5},{5,4},{6,7},{7,6},{8,9},{9,8},{10,11... | collective-permute-start | bytes 73736 | tf_op jit(solution)/shard_map/ppermute | solution.py:258
  9.6 0.3 start.1
  9.9 1.1 %collective-permute-done.2.refs_3_ = f32[1,2,3,8,128]{4,3,2,1,0:T(8,128)S(1)} collective-permute-done((f32[1,2,3,8,128]{4,3,2,1,0:T(8,128)S(1)}, f32[1,2,3,8,128]{4,3,2,1,0:T(8,128)S(1)}, u32[]{:S(2)}, u32[]{:S(2)}) %collective-permute-start.2) | collective-permute-done | bytes 24608 | tf_op jit(solution)/shard_map/ppermute | solution.py:257
  11.0 0.0 collective-permute-done.refs_1_
  11.0 0.4 %collective-permute-done.1.refs_2_ = f32[4,2,3,8,128]{4,3,2,1,0:T(8,128)S(1)} collective-permute-done((f32[4,2,3,8,128]{4,3,2,1,0:T(8,128)S(1)}, f32[4,2,3,8,128]{4,3,2,1,0:T(8,128)S(1)}, u32[]{:S(2)}, u32[]{:S(2)}) %collective-permute-start.1) | collective-permute-done | bytes 98336 | tf_op jit(solution)/shard_map/ppermute | solution.py:256
  11.3 0.1 third.1
  11.5 1.9 %collective-permute-start.4 = (f32[4,2,3,8,128]{4,3,2,1,0:T(8,128)S(1)}, f32[4,2,3,8,128]{4,3,2,1,0:T(8,128)S(1)}, u32[]{:S(2)}, u32[]{:S(2)}) collective-permute-start(f32[4,2,3,8,128]{4,3,2,1,0:T(8,128)S(1)} %get-tuple-element.28), channel_id=1, source_target_pairs={{0,24},{1,25},{2,26},{3,27},{4,28},{5,29},{6,30},{7,31},{8,16},{9,... | collective-permute-start | bytes 294920 | tf_op jit(solution)/shard_map/ppermute | solution.py:256
  13.3 0.6 %collective-permute-start.5 = (f32[4,2,3,8,128]{4,3,2,1,0:T(8,128)S(1)}, f32[4,2,3,8,128]{4,3,2,1,0:T(8,128)S(1)}, u32[]{:S(2)}, u32[]{:S(2)}) collective-permute-start(f32[4,2,3,8,128]{4,3,2,1,0:T(8,128)S(1)} %get-tuple-element.29), channel_id=1, source_target_pairs={{0,8},{1,9},{2,10},{3,11},{4,12},{5,13},{6,14},{7,15},{8,0},{9,1},... | collective-permute-start | bytes 294920 | tf_op jit(solution)/shard_map/ppermute | solution.py:255
  13.9 1.6 %collective-permute-start.7 = (f32[1,2,3,8,128]{4,3,2,1,0:T(8,128)S(1)}, f32[1,2,3,8,128]{4,3,2,1,0:T(8,128)S(1)}, u32[]{:S(2)}, u32[]{:S(2)}) collective-permute-start(f32[1,2,3,8,128]{4,3,2,1,0:T(8,128)S(1)} %get-tuple-element.31), channel_id=1, source_target_pairs={{0,1},{1,0},{2,3},{3,2},{4,5},{5,4},{6,7},{7,6},{8,9},{9,8},{10,11... | collective-permute-start | bytes 73736 | tf_op jit(solution)/shard_map/ppermute | solution.py:258
  16.2 0.3 local_1.1.refs_0_
  16.4 1.8 %collective-permute-done.6.refs_3_ = f32[1,2,3,8,128]{4,3,2,1,0:T(8,128)S(1)} collective-permute-done((f32[1,2,3,8,128]{4,3,2,1,0:T(8,128)S(1)}, f32[1,2,3,8,128]{4,3,2,1,0:T(8,128)S(1)}, u32[]{:S(2)}, u32[]{:S(2)}) %collective-permute-start.6) | collective-permute-done | bytes 24608 | tf_op jit(solution)/shard_map/ppermute | solution.py:257
  18.2 0.8 %collective-permute-done.5.refs_2_ = f32[4,2,3,8,128]{4,3,2,1,0:T(8,128)S(1)} collective-permute-done((f32[4,2,3,8,128]{4,3,2,1,0:T(8,128)S(1)}, f32[4,2,3,8,128]{4,3,2,1,0:T(8,128)S(1)}, u32[]{:S(2)}, u32[]{:S(2)}) %collective-permute-start.5) | collective-permute-done | bytes 98336 | tf_op jit(solution)/shard_map/ppermute | solution.py:255
  19.0 0.2 second.1
  19.2 0.8 %collective-permute-start.8 = (f32[4,2,3,8,128]{4,3,2,1,0:T(8,128)S(1)}, f32[4,2,3,8,128]{4,3,2,1,0:T(8,128)S(1)}, u32[]{:S(2)}, u32[]{:S(2)}) collective-permute-start(f32[4,2,3,8,128]{4,3,2,1,0:T(8,128)S(1)} %get-tuple-element.34), channel_id=1, source_target_pairs={{0,8},{1,9},{2,10},{3,11},{4,12},{5,13},{6,14},{7,15},{8,0},{9,1},... | collective-permute-start | bytes 294920 | tf_op jit(solution)/shard_map/ppermute | solution.py:255
  19.9 2.0 %collective-permute-start.9 = (f32[4,2,3,8,128]{4,3,2,1,0:T(8,128)S(1)}, f32[4,2,3,8,128]{4,3,2,1,0:T(8,128)S(1)}, u32[]{:S(2)}, u32[]{:S(2)}) collective-permute-start(f32[4,2,3,8,128]{4,3,2,1,0:T(8,128)S(1)} %get-tuple-element.35), channel_id=1, source_target_pairs={{0,24},{1,25},{2,26},{3,27},{4,28},{5,29},{6,30},{7,31},{8,16},{9,... | collective-permute-start | bytes 294920 | tf_op jit(solution)/shard_map/ppermute | solution.py:256
  22.0 1.1 %collective-permute-start.11 = (f32[1,2,3,8,128]{4,3,2,1,0:T(8,128)S(1)}, f32[1,2,3,8,128]{4,3,2,1,0:T(8,128)S(1)}, u32[]{:S(2)}, u32[]{:S(2)}) collective-permute-start(f32[1,2,3,8,128]{4,3,2,1,0:T(8,128)S(1)} %get-tuple-element.37), channel_id=1, source_target_pairs={{0,1},{1,0},{2,3},{3,2},{4,5},{5,4},{6,7},{7,6},{8,9},{9,8},{10,11... | collective-permute-start | bytes 73736 | tf_op jit(solution)/shard_map/ppermute | solution.py:258
  23.1 0.3 local_0.1.refs_0_
  23.3 2.8 %collective-permute-done.10.refs_3_ = f32[1,2,3,8,128]{4,3,2,1,0:T(8,128)S(1)} collective-permute-done((f32[1,2,3,8,128]{4,3,2,1,0:T(8,128)S(1)}, f32[1,2,3,8,128]{4,3,2,1,0:T(8,128)S(1)}, u32[]{:S(2)}, u32[]{:S(2)}) %collective-permute-start.10) | collective-permute-done | bytes 24608 | tf_op jit(solution)/shard_map/ppermute | solution.py:257
  26.1 0.3 %collective-permute-done.9.refs_2_ = f32[4,2,3,8,128]{4,3,2,1,0:T(8,128)S(1)} collective-permute-done((f32[4,2,3,8,128]{4,3,2,1,0:T(8,128)S(1)}, f32[4,2,3,8,128]{4,3,2,1,0:T(8,128)S(1)}, u32[]{:S(2)}, u32[]{:S(2)}) %collective-permute-start.9) | collective-permute-done | bytes 98336 | tf_op jit(solution)/shard_map/ppermute | solution.py:256
  26.5 0.7 %last.1 = f32[4,2,3,8,128]{4,3,2,1,0:T(8,128)} custom-call(f32[8,128]{1,0:T(8,128)S(1)} %eps.1.eps_ref, f32[6,8,128]{2,1,0:T(8,128)S(1)} %tapers.1.coefs_ref, f32[864,128]{1,0:T(8,128)S(1)} %bitcast.9, f32[4,2,3,8,128]{4,3,2,1,0:T(8,128)S(1)} %local_0.1.refs_0_, f32[4,2,3,8,128]{4,3,2,1,0:T(8,128)S(1)} %collective-permute-done.8.refs_1_, ...), custom_call_target="tpu_custom_call" | custom-call | flops 368640 | bytes 368640 | tf_op jit(solution)/shard_map/last/pallas_call | solution.py:222
  (13 shorter events, 0.1 us)
Async XLA Ops:
  0.0 9.6 %copy-start = (f32[4,3,4,2,3,3,128]{6,3,5,4,2,1,0:T(2,128)S(1)}, f32[4,3,4,2,3,3,128]{6,3,5,4,2,1,0:T(2,128)}, u32[]{:S(2)}) copy-start(f32[4,3,4,2,3,3,128]{6,3,5,4,2,1,0:T(2,128)} %param.6) | copy-start | bytes 1327108
  0.0 9.6 %copy-start.1 = (f32[4,2,3,8,128]{4,3,2,1,0:T(8,128)S(1)}, f32[4,2,3,8,128]{4,3,2,1,0:T(8,128)}, u32[]{:S(2)}) copy-start(f32[4,2,3,8,128]{4,3,2,1,0:T(8,128)} %adjoint_hbm.1) | copy-start | bytes 294916
  1.1 9.9 %collective-permute-start = (f32[4,2,3,8,128]{4,3,2,1,0:T(8,128)S(1)}, f32[4,2,3,8,128]{4,3,2,1,0:T(8,128)S(1)}, u32[]{:S(2)}, u32[]{:S(2)}) collective-permute-start(f32[4,2,3,8,128]{4,3,2,1,0:T(8,128)S(1)} %get-tuple-element.23), channel_id=1, source_target_pairs={{0,8},{1,9},{2,10},{3,11},{4,12},{5,13},{6,14},{7,15},{8,0},{9,1},... | collective-permute-start | bytes 294920 | tf_op jit(solution)/shard_map/ppermute | solution.py:255
  4.2 7.2 %collective-permute-start.1 = (f32[4,2,3,8,128]{4,3,2,1,0:T(8,128)S(1)}, f32[4,2,3,8,128]{4,3,2,1,0:T(8,128)S(1)}, u32[]{:S(2)}, u32[]{:S(2)}) collective-permute-start(f32[4,2,3,8,128]{4,3,2,1,0:T(8,128)S(1)} %get-tuple-element.24), channel_id=1, source_target_pairs={{0,24},{1,25},{2,26},{3,27},{4,28},{5,29},{6,30},{7,31},{8,16},{9,... | collective-permute-start | bytes 294920 | tf_op jit(solution)/shard_map/ppermute | solution.py:256
  6.7 4.3 %collective-permute-start.2 = (f32[1,2,3,8,128]{4,3,2,1,0:T(8,128)S(1)}, f32[1,2,3,8,128]{4,3,2,1,0:T(8,128)S(1)}, u32[]{:S(2)}, u32[]{:S(2)}) collective-permute-start(f32[1,2,3,8,128]{4,3,2,1,0:T(8,128)S(1)} %get-tuple-element.25), channel_id=1, source_target_pairs={{0,7},{1,2},{2,1},{3,4},{4,3},{5,6},{6,5},{7,0},{8,15},{9,10},{10,... | collective-permute-start | bytes 73736 | tf_op jit(solution)/shard_map/ppermute | solution.py:257
  8.0 3.0 %collective-permute-start.3 = (f32[1,2,3,8,128]{4,3,2,1,0:T(8,128)S(1)}, f32[1,2,3,8,128]{4,3,2,1,0:T(8,128)S(1)}, u32[]{:S(2)}, u32[]{:S(2)}) collective-permute-start(f32[1,2,3,8,128]{4,3,2,1,0:T(8,128)S(1)} %get-tuple-element.26), channel_id=1, source_target_pairs={{0,1},{1,0},{2,3},{3,2},{4,5},{5,4},{6,7},{7,6},{8,9},{9,8},{10,11... | collective-permute-start | bytes 73736 | tf_op jit(solution)/shard_map/ppermute | solution.py:258
  11.5 6.7 %collective-permute-start.4 = (f32[4,2,3,8,128]{4,3,2,1,0:T(8,128)S(1)}, f32[4,2,3,8,128]{4,3,2,1,0:T(8,128)S(1)}, u32[]{:S(2)}, u32[]{:S(2)}) collective-permute-start(f32[4,2,3,8,128]{4,3,2,1,0:T(8,128)S(1)} %get-tuple-element.28), channel_id=1, source_target_pairs={{0,24},{1,25},{2,26},{3,27},{4,28},{5,29},{6,30},{7,31},{8,16},{9,... | collective-permute-start | bytes 294920 | tf_op jit(solution)/shard_map/ppermute | solution.py:256
  13.3 5.7 %collective-permute-start.5 = (f32[4,2,3,8,128]{4,3,2,1,0:T(8,128)S(1)}, f32[4,2,3,8,128]{4,3,2,1,0:T(8,128)S(1)}, u32[]{:S(2)}, u32[]{:S(2)}) collective-permute-start(f32[4,2,3,8,128]{4,3,2,1,0:T(8,128)S(1)} %get-tuple-element.29), channel_id=1, source_target_pairs={{0,8},{1,9},{2,10},{3,11},{4,12},{5,13},{6,14},{7,15},{8,0},{9,1},... | collective-permute-start | bytes 294920 | tf_op jit(solution)/shard_map/ppermute | solution.py:255
  13.9 4.3 %collective-permute-start.6 = (f32[1,2,3,8,128]{4,3,2,1,0:T(8,128)S(1)}, f32[1,2,3,8,128]{4,3,2,1,0:T(8,128)S(1)}, u32[]{:S(2)}, u32[]{:S(2)}) collective-permute-start(f32[1,2,3,8,128]{4,3,2,1,0:T(8,128)S(1)} %get-tuple-element.30), channel_id=1, source_target_pairs={{0,7},{1,2},{2,1},{3,4},{4,3},{5,6},{6,5},{7,0},{8,15},{9,10},{10,... | collective-permute-start | bytes 73736 | tf_op jit(solution)/shard_map/ppermute | solution.py:257
  13.9 4.3 %collective-permute-start.7 = (f32[1,2,3,8,128]{4,3,2,1,0:T(8,128)S(1)}, f32[1,2,3,8,128]{4,3,2,1,0:T(8,128)S(1)}, u32[]{:S(2)}, u32[]{:S(2)}) collective-permute-start(f32[1,2,3,8,128]{4,3,2,1,0:T(8,128)S(1)} %get-tuple-element.31), channel_id=1, source_target_pairs={{0,1},{1,0},{2,3},{3,2},{4,5},{5,4},{6,7},{7,6},{8,9},{9,8},{10,11... | collective-permute-start | bytes 73736 | tf_op jit(solution)/shard_map/ppermute | solution.py:258
  19.2 7.0 %collective-permute-start.8 = (f32[4,2,3,8,128]{4,3,2,1,0:T(8,128)S(1)}, f32[4,2,3,8,128]{4,3,2,1,0:T(8,128)S(1)}, u32[]{:S(2)}, u32[]{:S(2)}) collective-permute-start(f32[4,2,3,8,128]{4,3,2,1,0:T(8,128)S(1)} %get-tuple-element.34), channel_id=1, source_target_pairs={{0,8},{1,9},{2,10},{3,11},{4,12},{5,13},{6,14},{7,15},{8,0},{9,1},... | collective-permute-start | bytes 294920 | tf_op jit(solution)/shard_map/ppermute | solution.py:255
  19.9 6.5 %collective-permute-start.9 = (f32[4,2,3,8,128]{4,3,2,1,0:T(8,128)S(1)}, f32[4,2,3,8,128]{4,3,2,1,0:T(8,128)S(1)}, u32[]{:S(2)}, u32[]{:S(2)}) collective-permute-start(f32[4,2,3,8,128]{4,3,2,1,0:T(8,128)S(1)} %get-tuple-element.35), channel_id=1, source_target_pairs={{0,24},{1,25},{2,26},{3,27},{4,28},{5,29},{6,30},{7,31},{8,16},{9,... | collective-permute-start | bytes 294920 | tf_op jit(solution)/shard_map/ppermute | solution.py:256
  22.0 4.2 %collective-permute-start.10 = (f32[1,2,3,8,128]{4,3,2,1,0:T(8,128)S(1)}, f32[1,2,3,8,128]{4,3,2,1,0:T(8,128)S(1)}, u32[]{:S(2)}, u32[]{:S(2)}) collective-permute-start(f32[1,2,3,8,128]{4,3,2,1,0:T(8,128)S(1)} %get-tuple-element.36), channel_id=1, source_target_pairs={{0,7},{1,2},{2,1},{3,4},{4,3},{5,6},{6,5},{7,0},{8,15},{9,10},{10,... | collective-permute-start | bytes 73736 | tf_op jit(solution)/shard_map/ppermute | solution.py:257
  22.0 4.2 %collective-permute-start.11 = (f32[1,2,3,8,128]{4,3,2,1,0:T(8,128)S(1)}, f32[1,2,3,8,128]{4,3,2,1,0:T(8,128)S(1)}, u32[]{:S(2)}, u32[]{:S(2)}) collective-permute-start(f32[1,2,3,8,128]{4,3,2,1,0:T(8,128)S(1)} %get-tuple-element.37), channel_id=1, source_target_pairs={{0,1},{1,0},{2,3},{3,2},{4,5},{5,4},{6,7},{7,6},{8,9},{9,8},{10,11... | collective-permute-start | bytes 73736 | tf_op jit(solution)/shard_map/ppermute | solution.py:258

commit v19 on v14

--- a/solution.py
+++ b/solution.py
@@ -99,18 +99,17 @@
 def begin_kernel(
     rows, adjoint_hbm, links_hbm, far_ref, near_ref, outer_ref, inner_ref, adjoint_ref, links_ref, sems
 ):
-    row_entries = SETS * MUS * ENTRIES
     z_first = (2 * MUS + 2) * ENTRIES
     aligned = z_first // 8 * 8
-    copies = [pltpu.make_async_copy(adjoint_hbm, adjoint_ref, sems.at[rows])]
-    for row in range(rows):
-        part = links_hbm.at[pl.ds(row * row_entries + aligned, row_entries - aligned), :]
-        copies.append(pltpu.make_async_copy(part, links_ref.at[row], sems.at[row]))
+    part = links_hbm.at[:, pl.ds(aligned, SETS * MUS * ENTRIES - aligned), :]
+    copies = [pltpu.make_async_copy(part, links_ref, sems.at[rows])]
+    for row in range(rows):
+        copies.append(pltpu.make_async_copy(adjoint_hbm.at[row], adjoint_ref.at[row], sems.at[row]))
     for copy in copies:
         copy.start()
-    for copy in copies:
-        copy.wait()
-    for row in range(rows):
+    copies[0].wait()
+    for row in range(rows):
+        copies[row + 1].wait()
         matrices = links_ref.at[row], z_first - aligned
         store_z(rows, matrices, row, load_field(adjoint_ref, row), far_ref, near_ref)
     store_t(rows, (links_ref.at[rows - 1], z_first + ENTRIES - aligned), adjoint_ref, outer_ref, inner_ref)
@@ -263,7 +262,10 @@
     copied = SETS * MUS * ENTRIES - (2 * MUS + 2) * ENTRIES // 8 * 8
     sending = call(
         functools.partial(begin_kernel, rows), "begin",
-        tuple(pltpu.with_memory_space_constraint(a, pltpu.HBM) for a in (adjoint, links)), sent, 5, pltpu.HBM,
+        tuple(
+            pltpu.with_memory_space_constraint(a, pltpu.HBM)
+            for a in (adjoint, links.reshape(rows, -1, flowed.shape[-1]))
+        ), sent, 5, pltpu.HBM,
         [
             pltpu.VMEM(adjoint.shape, jnp.float32),
             pltpu.VMEM((rows, copied, flowed.shape[-1]), jnp.float32),

time: 27.1 us -> 27.1 us (level)
  no operation moved by 1% of the time
where the time goes in v19:
time: 27.1 us; the launch traced here: 26.9 us
  starting transfers between devices  15.9 us (59%)
  waiting for transfers between devices  5.99 us (22%)
  Pallas kernels  2.96 us (11%)
  between operations  2.02 us (7%)
    ppermute x3, starting transfers between devices, sent_on(): far = lax.ppermute(far, 'gz', far_pairs)  7.17 us
    ppermute x3, waiting for transfers between devices, sent_on(): outer = lax.ppermute(outer, 'gz', outer_pairs)  5.29 us
    ppermute x3, starting transfers between devices, sent_on(): near = lax.ppermute(near, 'gz', near_pairs)  3.93 us
    ppermute x3, starting transfers between devices, sent_on(): inner = lax.ppermute(inner, 'gz', inner_pairs)  3.49 us
    pallas_call x9, Pallas kernels, call(): pl.pallas_call(kernel, name=name, out_shape=out_shapes, in_specs=[pl.Bloc...  2.96 us
    ppermute x3, starting transfers between devices, sent_on(): outer = lax.ppermute(outer, 'gz', outer_pairs)  1.33 us
    ppermute x3, waiting for transfers between devices, sent_on(): far = lax.ppermute(far, 'gz', far_pairs)  0.69 us
  transfers between devices with their start and end apart: 12, of which 5 were waited for; matrix products, arithmetic and copies ran while one was open for 0% of the time, Pallas kernels for 3%

profile of v19, /device:TPU:0, one launch (start us, length us, event | category | flops | bytes accessed | tf_op | source)
XLA Modules:
  0.0 26.9 jit_solution(8079591926772491807)
XLA Ops:
  0.0 1.1 %begin.1 = (f32[4,2,3,8,128]{4,3,2,1,0:T(8,128)S(1)}, f32[4,2,3,8,128]{4,3,2,1,0:T(8,128)S(1)}, f32[1,2,3,8,128]{4,3,2,1,0:T(8,128)S(1)}, f32[1,2,3,8,128]{4,3,2,1,0:T(8,128)S(1)}) custom-call(f32[4,2,3,8,128]{4,3,2,1,0:T(8,128)} %adjoint_hbm.1, f32[4,216,128]{2,1,0:T(8,128)} %bitcast.5), custom_call_target="tpu_custom_call" | custom-call | flops 368640 | bytes 368640 | tf_op jit(solution)/shard_map/begin/pallas_call | solution.py:219
  1.1 3.1 %collective-permute-start = (f32[4,2,3,8,128]{4,3,2,1,0:T(8,128)S(1)}, f32[4,2,3,8,128]{4,3,2,1,0:T(8,128)S(1)}, u32[]{:S(2)}, u32[]{:S(2)}) collective-permute-start(f32[4,2,3,8,128]{4,3,2,1,0:T(8,128)S(1)} %get-tuple-element.23), channel_id=1, source_target_pairs={{0,8},{1,9},{2,10},{3,11},{4,12},{5,13},{6,14},{7,15},{8,0},{9,1},... | collective-permute-start | bytes 294920 | tf_op jit(solution)/shard_map/ppermute | solution.py:252
  4.2 2.5 %collective-permute-start.1 = (f32[4,2,3,8,128]{4,3,2,1,0:T(8,128)S(1)}, f32[4,2,3,8,128]{4,3,2,1,0:T(8,128)S(1)}, u32[]{:S(2)}, u32[]{:S(2)}) collective-permute-start(f32[4,2,3,8,128]{4,3,2,1,0:T(8,128)S(1)} %get-tuple-element.24), channel_id=1, source_target_pairs={{0,24},{1,25},{2,26},{3,27},{4,28},{5,29},{6,30},{7,31},{8,16},{9,... | collective-permute-start | bytes 294920 | tf_op jit(solution)/shard_map/ppermute | solution.py:253
  6.7 1.3 %collective-permute-start.2 = (f32[1,2,3,8,128]{4,3,2,1,0:T(8,128)S(1)}, f32[1,2,3,8,128]{4,3,2,1,0:T(8,128)S(1)}, u32[]{:S(2)}, u32[]{:S(2)}) collective-permute-start(f32[1,2,3,8,128]{4,3,2,1,0:T(8,128)S(1)} %get-tuple-element.25), channel_id=1, source_target_pairs={{0,7},{1,2},{2,1},{3,4},{4,3},{5,6},{6,5},{7,0},{8,15},{9,10},{10,... | collective-permute-start | bytes 73736 | tf_op jit(solution)/shard_map/ppermute | solution.py:254
  8.0 0.3 %collective-permute-start.3 = (f32[1,2,3,8,128]{4,3,2,1,0:T(8,128)S(1)}, f32[1,2,3,8,128]{4,3,2,1,0:T(8,128)S(1)}, u32[]{:S(2)}, u32[]{:S(2)}) collective-permute-start(f32[1,2,3,8,128]{4,3,2,1,0:T(8,128)S(1)} %get-tuple-element.26), channel_id=1, source_target_pairs={{0,1},{1,0},{2,3},{3,2},{4,5},{5,4},{6,7},{7,6},{8,9},{9,8},{10,11... | collective-permute-start | bytes 73736 | tf_op jit(solution)/shard_map/ppermute | solution.py:255
  9.6 0.3 %start.1 = (f32[4,2,3,8,128]{4,3,2,1,0:T(8,128)S(1)}, f32[4,2,3,8,128]{4,3,2,1,0:T(8,128)S(1)}) custom-call(f32[6,8,128]{2,1,0:T(8,128)S(1)} %tapers.1.coefs_ref, f32[4,2,3,8,128]{4,3,2,1,0:T(8,128)S(1)} %copy-done.1, f32[864,128]{1,0:T(8,128)S(1)} %bitcast.6), custom_call_target="tpu_custom_call" | custom-call | flops 1622016 | bytes 1622016 | tf_op jit(solution)/shard_map/start/pallas_call | solution.py:219
  9.9 1.1 %collective-permute-done.2.refs_3_ = f32[1,2,3,8,128]{4,3,2,1,0:T(8,128)S(1)} collective-permute-done((f32[1,2,3,8,128]{4,3,2,1,0:T(8,128)S(1)}, f32[1,2,3,8,128]{4,3,2,1,0:T(8,128)S(1)}, u32[]{:S(2)}, u32[]{:S(2)}) %collective-permute-start.2) | collective-permute-done | bytes 24608 | tf_op jit(solution)/shard_map/ppermute | solution.py:254
  11.0 0.0 collective-permute-done.3.refs_4_
  11.0 0.0 collective-permute-done.refs_1_
  11.0 0.4 %collective-permute-done.1.refs_2_ = f32[4,2,3,8,128]{4,3,2,1,0:T(8,128)S(1)} collective-permute-done((f32[4,2,3,8,128]{4,3,2,1,0:T(8,128)S(1)}, f32[4,2,3,8,128]{4,3,2,1,0:T(8,128)S(1)}, u32[]{:S(2)}, u32[]{:S(2)}) %collective-permute-start.1) | collective-permute-done | bytes 98336 | tf_op jit(solution)/shard_map/ppermute | solution.py:253
  11.3 0.1 third.1
  11.5 0.7 %collective-permute-start.4 = (f32[4,2,3,8,128]{4,3,2,1,0:T(8,128)S(1)}, f32[4,2,3,8,128]{4,3,2,1,0:T(8,128)S(1)}, u32[]{:S(2)}, u32[]{:S(2)}) collective-permute-start(f32[4,2,3,8,128]{4,3,2,1,0:T(8,128)S(1)} %get-tuple-element.28), channel_id=1, source_target_pairs={{0,8},{1,9},{2,10},{3,11},{4,12},{5,13},{6,14},{7,15},{8,0},{9,1},... | collective-permute-start | bytes 294920 | tf_op jit(solution)/shard_map/ppermute | solution.py:252
  12.2 2.6 %collective-permute-start.5 = (f32[4,2,3,8,128]{4,3,2,1,0:T(8,128)S(1)}, f32[4,2,3,8,128]{4,3,2,1,0:T(8,128)S(1)}, u32[]{:S(2)}, u32[]{:S(2)}) collective-permute-start(f32[4,2,3,8,128]{4,3,2,1,0:T(8,128)S(1)} %get-tuple-element.29), channel_id=1, source_target_pairs={{0,24},{1,25},{2,26},{3,27},{4,28},{5,29},{6,30},{7,31},{8,16},{9,... | collective-permute-start | bytes 294920 | tf_op jit(solution)/shard_map/ppermute | solution.py:253
  14.8 1.6 %collective-permute-start.7 = (f32[1,2,3,8,128]{4,3,2,1,0:T(8,128)S(1)}, f32[1,2,3,8,128]{4,3,2,1,0:T(8,128)S(1)}, u32[]{:S(2)}, u32[]{:S(2)}) collective-permute-start(f32[1,2,3,8,128]{4,3,2,1,0:T(8,128)S(1)} %get-tuple-element.31), channel_id=1, source_target_pairs={{0,1},{1,0},{2,3},{3,2},{4,5},{5,4},{6,7},{7,6},{8,9},{9,8},{10,11... | collective-permute-start | bytes 73736 | tf_op jit(solution)/shard_map/ppermute | solution.py:255
  17.1 0.3 %local_1.1.refs_0_ = f32[4,2,3,8,128]{4,3,2,1,0:T(8,128)S(1)} custom-call(f32[4,2,3,8,128]{4,3,2,1,0:T(8,128)S(1)} %get-tuple-element.27.field_ref.refs_6_, f32[864,128]{1,0:T(8,128)S(1)} %bitcast.8), custom_call_target="tpu_custom_call" | custom-call | flops 1622016 | bytes 1622016 | tf_op jit(solution)/shard_map/local_1/pallas_call | solution.py:219
  17.3 1.8 %collective-permute-done.6.refs_3_ = f32[1,2,3,8,128]{4,3,2,1,0:T(8,128)S(1)} collective-permute-done((f32[1,2,3,8,128]{4,3,2,1,0:T(8,128)S(1)}, f32[1,2,3,8,128]{4,3,2,1,0:T(8,128)S(1)}, u32[]{:S(2)}, u32[]{:S(2)}) %collective-permute-start.6) | collective-permute-done | bytes 24608 | tf_op jit(solution)/shard_map/ppermute | solution.py:254
  19.1 0.2 second.1
  19.3 0.2 collective-permute-start.8
  19.5 2.1 %collective-permute-start.9 = (f32[4,2,3,8,128]{4,3,2,1,0:T(8,128)S(1)}, f32[4,2,3,8,128]{4,3,2,1,0:T(8,128)S(1)}, u32[]{:S(2)}, u32[]{:S(2)}) collective-permute-start(f32[4,2,3,8,128]{4,3,2,1,0:T(8,128)S(1)} %get-tuple-element.35), channel_id=1, source_target_pairs={{0,24},{1,25},{2,26},{3,27},{4,28},{5,29},{6,30},{7,31},{8,16},{9,... | collective-permute-start | bytes 294920 | tf_op jit(solution)/shard_map/ppermute | solution.py:253
  21.5 1.6 %collective-permute-start.11 = (f32[1,2,3,8,128]{4,3,2,1,0:T(8,128)S(1)}, f32[1,2,3,8,128]{4,3,2,1,0:T(8,128)S(1)}, u32[]{:S(2)}, u32[]{:S(2)}) collective-permute-start(f32[1,2,3,8,128]{4,3,2,1,0:T(8,128)S(1)} %get-tuple-element.37), channel_id=1, source_target_pairs={{0,1},{1,0},{2,3},{3,2},{4,5},{5,4},{6,7},{7,6},{8,9},{9,8},{10,11... | collective-permute-start | bytes 73736 | tf_op jit(solution)/shard_map/ppermute | solution.py:255
  23.1 0.3 local_0.1.refs_0_
  23.4 2.4 %collective-permute-done.10.refs_3_ = f32[1,2,3,8,128]{4,3,2,1,0:T(8,128)S(1)} collective-permute-done((f32[1,2,3,8,128]{4,3,2,1,0:T(8,128)S(1)}, f32[1,2,3,8,128]{4,3,2,1,0:T(8,128)S(1)}, u32[]{:S(2)}, u32[]{:S(2)}) %collective-permute-start.10) | collective-permute-done | bytes 24608 | tf_op jit(solution)/shard_map/ppermute | solution.py:254
  25.8 0.3 %collective-permute-done.9.refs_2_ = f32[4,2,3,8,128]{4,3,2,1,0:T(8,128)S(1)} collective-permute-done((f32[4,2,3,8,128]{4,3,2,1,0:T(8,128)S(1)}, f32[4,2,3,8,128]{4,3,2,1,0:T(8,128)S(1)}, u32[]{:S(2)}, u32[]{:S(2)}) %collective-permute-start.9) | collective-permute-done | bytes 98336 | tf_op jit(solution)/shard_map/ppermute | solution.py:253
  26.2 0.7 %last.1 = f32[4,2,3,8,128]{4,3,2,1,0:T(8,128)} custom-call(f32[8,128]{1,0:T(8,128)S(1)} %eps.1.eps_ref, f32[6,8,128]{2,1,0:T(8,128)S(1)} %tapers.1.coefs_ref, f32[864,128]{1,0:T(8,128)S(1)} %bitcast.11, f32[4,2,3,8,128]{4,3,2,1,0:T(8,128)S(1)} %local_0.1.refs_0_, f32[4,2,3,8,128]{4,3,2,1,0:T(8,128)S(1)} %collective-permute-done.8.refs_1_, ...), custom_call_target="tpu_custom_call" | custom-call | flops 368640 | bytes 368640 | tf_op jit(solution)/shard_map/last/pallas_call | solution.py:219
  (13 shorter events, 0.1 us)
Async XLA Ops:
  0.0 9.6 %copy-start = (f32[4,3,4,2,3,3,128]{6,3,5,4,2,1,0:T(2,128)S(1)}, f32[4,3,4,2,3,3,128]{6,3,5,4,2,1,0:T(2,128)}, u32[]{:S(2)}) copy-start(f32[4,3,4,2,3,3,128]{6,3,5,4,2,1,0:T(2,128)} %param.6) | copy-start | bytes 1327108
  0.0 9.6 %copy-start.1 = (f32[4,2,3,8,128]{4,3,2,1,0:T(8,128)S(1)}, f32[4,2,3,8,128]{4,3,2,1,0:T(8,128)}, u32[]{:S(2)}) copy-start(f32[4,2,3,8,128]{4,3,2,1,0:T(8,128)} %adjoint_hbm.1) | copy-start | bytes 294916
  1.1 9.9 %collective-permute-start = (f32[4,2,3,8,128]{4,3,2,1,0:T(8,128)S(1)}, f32[4,2,3,8,128]{4,3,2,1,0:T(8,128)S(1)}, u32[]{:S(2)}, u32[]{:S(2)}) collective-permute-start(f32[4,2,3,8,128]{4,3,2,1,0:T(8,128)S(1)} %get-tuple-element.23), channel_id=1, source_target_pairs={{0,8},{1,9},{2,10},{3,11},{4,12},{5,13},{6,14},{7,15},{8,0},{9,1},... | collective-permute-start | bytes 294920 | tf_op jit(solution)/shard_map/ppermute | solution.py:252
  4.2 7.2 %collective-permute-start.1 = (f32[4,2,3,8,128]{4,3,2,1,0:T(8,128)S(1)}, f32[4,2,3,8,128]{4,3,2,1,0:T(8,128)S(1)}, u32[]{:S(2)}, u32[]{:S(2)}) collective-permute-start(f32[4,2,3,8,128]{4,3,2,1,0:T(8,128)S(1)} %get-tuple-element.24), channel_id=1, source_target_pairs={{0,24},{1,25},{2,26},{3,27},{4,28},{5,29},{6,30},{7,31},{8,16},{9,... | collective-permute-start | bytes 294920 | tf_op jit(solution)/shard_map/ppermute | solution.py:253
  6.7 4.3 %collective-permute-start.2 = (f32[1,2,3,8,128]{4,3,2,1,0:T(8,128)S(1)}, f32[1,2,3,8,128]{4,3,2,1,0:T(8,128)S(1)}, u32[]{:S(2)}, u32[]{:S(2)}) collective-permute-start(f32[1,2,3,8,128]{4,3,2,1,0:T(8,128)S(1)} %get-tuple-element.25), channel_id=1, source_target_pairs={{0,7},{1,2},{2,1},{3,4},{4,3},{5,6},{6,5},{7,0},{8,15},{9,10},{10,... | collective-permute-start | bytes 73736 | tf_op jit(solution)/shard_map/ppermute | solution.py:254
  8.0 3.0 %collective-permute-start.3 = (f32[1,2,3,8,128]{4,3,2,1,0:T(8,128)S(1)}, f32[1,2,3,8,128]{4,3,2,1,0:T(8,128)S(1)}, u32[]{:S(2)}, u32[]{:S(2)}) collective-permute-start(f32[1,2,3,8,128]{4,3,2,1,0:T(8,128)S(1)} %get-tuple-element.26), channel_id=1, source_target_pairs={{0,1},{1,0},{2,3},{3,2},{4,5},{5,4},{6,7},{7,6},{8,9},{9,8},{10,11... | collective-permute-start | bytes 73736 | tf_op jit(solution)/shard_map/ppermute | solution.py:255
  11.5 7.6 %collective-permute-start.4 = (f32[4,2,3,8,128]{4,3,2,1,0:T(8,128)S(1)}, f32[4,2,3,8,128]{4,3,2,1,0:T(8,128)S(1)}, u32[]{:S(2)}, u32[]{:S(2)}) collective-permute-start(f32[4,2,3,8,128]{4,3,2,1,0:T(8,128)S(1)} %get-tuple-element.28), channel_id=1, source_target_pairs={{0,8},{1,9},{2,10},{3,11},{4,12},{5,13},{6,14},{7,15},{8,0},{9,1},... | collective-permute-start | bytes 294920 | tf_op jit(solution)/shard_map/ppermute | solution.py:252
  12.2 7.0 %collective-permute-start.5 = (f32[4,2,3,8,128]{4,3,2,1,0:T(8,128)S(1)}, f32[4,2,3,8,128]{4,3,2,1,0:T(8,128)S(1)}, u32[]{:S(2)}, u32[]{:S(2)}) collective-permute-start(f32[4,2,3,8,128]{4,3,2,1,0:T(8,128)S(1)} %get-tuple-element.29), channel_id=1, source_target_pairs={{0,24},{1,25},{2,26},{3,27},{4,28},{5,29},{6,30},{7,31},{8,16},{9,... | collective-permute-start | bytes 294920 | tf_op jit(solution)/shard_map/ppermute | solution.py:253
  14.8 4.3 %collective-permute-start.6 = (f32[1,2,3,8,128]{4,3,2,1,0:T(8,128)S(1)}, f32[1,2,3,8,128]{4,3,2,1,0:T(8,128)S(1)}, u32[]{:S(2)}, u32[]{:S(2)}) collective-permute-start(f32[1,2,3,8,128]{4,3,2,1,0:T(8,128)S(1)} %get-tuple-element.30), channel_id=1, source_target_pairs={{0,7},{1,2},{2,1},{3,4},{4,3},{5,6},{6,5},{7,0},{8,15},{9,10},{10,... | collective-permute-start | bytes 73736 | tf_op jit(solution)/shard_map/ppermute | solution.py:254
  14.8 4.3 %collective-permute-start.7 = (f32[1,2,3,8,128]{4,3,2,1,0:T(8,128)S(1)}, f32[1,2,3,8,128]{4,3,2,1,0:T(8,128)S(1)}, u32[]{:S(2)}, u32[]{:S(2)}) collective-permute-start(f32[1,2,3,8,128]{4,3,2,1,0:T(8,128)S(1)} %get-tuple-element.31), channel_id=1, source_target_pairs={{0,1},{1,0},{2,3},{3,2},{4,5},{5,4},{6,7},{7,6},{8,9},{9,8},{10,11... | collective-permute-start | bytes 73736 | tf_op jit(solution)/shard_map/ppermute | solution.py:255
  19.3 6.5 %collective-permute-start.8 = (f32[4,2,3,8,128]{4,3,2,1,0:T(8,128)S(1)}, f32[4,2,3,8,128]{4,3,2,1,0:T(8,128)S(1)}, u32[]{:S(2)}, u32[]{:S(2)}) collective-permute-start(f32[4,2,3,8,128]{4,3,2,1,0:T(8,128)S(1)} %get-tuple-element.34), channel_id=1, source_target_pairs={{0,8},{1,9},{2,10},{3,11},{4,12},{5,13},{6,14},{7,15},{8,0},{9,1},... | collective-permute-start | bytes 294920 | tf_op jit(solution)/shard_map/ppermute | solution.py:252
  19.5 6.7 %collective-permute-start.9 = (f32[4,2,3,8,128]{4,3,2,1,0:T(8,128)S(1)}, f32[4,2,3,8,128]{4,3,2,1,0:T(8,128)S(1)}, u32[]{:S(2)}, u32[]{:S(2)}) collective-permute-start(f32[4,2,3,8,128]{4,3,2,1,0:T(8,128)S(1)} %get-tuple-element.35), channel_id=1, source_target_pairs={{0,24},{1,25},{2,26},{3,27},{4,28},{5,29},{6,30},{7,31},{8,16},{9,... | collective-permute-start | bytes 294920 | tf_op jit(solution)/shard_map/ppermute | solution.py:253
  21.5 4.3 %collective-permute-start.10 = (f32[1,2,3,8,128]{4,3,2,1,0:T(8,128)S(1)}, f32[1,2,3,8,128]{4,3,2,1,0:T(8,128)S(1)}, u32[]{:S(2)}, u32[]{:S(2)}) collective-permute-start(f32[1,2,3,8,128]{4,3,2,1,0:T(8,128)S(1)} %get-tuple-element.36), channel_id=1, source_target_pairs={{0,7},{1,2},{2,1},{3,4},{4,3},{5,6},{6,5},{7,0},{8,15},{9,10},{10,... | collective-permute-start | bytes 73736 | tf_op jit(solution)/shard_map/ppermute | solution.py:254
  21.5 4.3 %collective-permute-start.11 = (f32[1,2,3,8,128]{4,3,2,1,0:T(8,128)S(1)}, f32[1,2,3,8,128]{4,3,2,1,0:T(8,128)S(1)}, u32[]{:S(2)}, u32[]{:S(2)}) collective-permute-start(f32[1,2,3,8,128]{4,3,2,1,0:T(8,128)S(1)} %get-tuple-element.37), channel_id=1, source_target_pairs={{0,1},{1,0},{2,3},{3,2},{4,5},{5,4},{6,7},{7,6},{8,9},{9,8},{10,11... | collective-permute-start | bytes 73736 | tf_op jit(solution)/shard_map/ppermute | solution.py:255

commit v20 on v14

--- a/solution.py
+++ b/solution.py
@@ -88,6 +88,12 @@
     store_field(near_ref, row, combine(lambda v, h: jnp.where(odd_plane, v, h), field, up))
 
 
+def store_up_and_down(matrices, row, field, up_ref, down_ref):
+    _, up = transport(matrices, None, field)
+    store_field(up_ref, row, up)
+    store_field(down_ref, row, field)
+
+
 def store_t(rows, matrices, field_ref, outer_ref, inner_ref):
     _, _, _, odd_block = place(rows)
     first = load_field(field_ref, 0)
@@ -97,7 +103,7 @@
 
 
 def begin_kernel(
-    rows, adjoint_hbm, links_hbm, far_ref, near_ref, outer_ref, inner_ref, adjoint_ref, links_ref, sems
+    rows, adjoint_hbm, links_hbm, up_ref, down_ref, outer_ref, inner_ref, adjoint_ref, links_ref, sems
 ):
     row_entries = SETS * MUS * ENTRIES
     z_first = (2 * MUS + 2) * ENTRIES
@@ -112,7 +118,7 @@
         copy.wait()
     for row in range(rows):
         matrices = links_ref.at[row], z_first - aligned
-        store_z(rows, matrices, row, load_field(adjoint_ref, row), far_ref, near_ref)
+        store_up_and_down(matrices, row, load_field(adjoint_ref, row), up_ref, down_ref)
     store_t(rows, (links_ref.at[rows - 1], z_first + ENTRIES - aligned), adjoint_ref, outer_ref, inner_ref)
 
 
@@ -148,16 +154,16 @@
 
 
 def arrived_sum(links_ref, link_set, row, rows, arrivals, coefs_ref=None):
-    sum_ref, near_ref, far_ref, outer_ref, inner_ref = arrivals
+    sum_ref, one_ref, two_ref, outer_ref, inner_ref = arrivals
     _, first_pos, odd_plane, odd_block = place(rows)
-    far, near = load_field(far_ref, row), load_field(near_ref, row)
+    one, two = load_field(one_ref, row), load_field(two_ref, row)
     if coefs_ref is not None:
-        far, near = (combine(lambda v: coefs_ref[row + 1] * v, f) for f in (far, near))
-    above = combine(lambda p, q: jnp.where(odd_plane, p, q), far, near)
+        below, above = (combine(lambda v: coefs_ref[row + 1] * v, f) for f in (one, two))
+    else:
+        below = combine(lambda near, far: jnp.where(odd_plane, near, far), one, two)
+        above = combine(lambda near, far: jnp.where(odd_plane, far, near), one, two)
     ahead_z, _ = transport(links_at(links_ref, row, link_set, 2), above, None)
-    total = combine(
-        lambda s, f, p, q: s + f + jnp.where(odd_plane, q, p), load_field(sum_ref, row), ahead_z, far, near
-    )
+    total = combine(lambda s, f, h: s + f + h, load_field(sum_ref, row), ahead_z, below)
     outer, inner = load_field(outer_ref, 0), load_field(inner_ref, 0)
     if row == 0:
         exists = jnp.where(first_pos != 0, 1.0, 0.0)
@@ -249,12 +255,22 @@
     outer_pairs = [(i, in_plane(i, 1 if i % 2 else -1)) for i in range(count)]
     inner_pairs = [(i, in_plane(i, -1 if i % 2 else 1)) for i in range(count)]
 
+    up_pairs = [(i, in_line(i, 1)) for i in range(count)]
+    down_pairs = [(i, in_line(i, -1)) for i in range(count)]
+
     def sent_on(far, near, outer, inner):
         near = lax.ppermute(near, "gz", near_pairs)
         far = lax.ppermute(far, "gz", far_pairs)
         outer = lax.ppermute(outer, "gz", outer_pairs)
         inner = lax.ppermute(inner, "gz", inner_pairs)
         return near, far, outer, inner
+
+    def shifted_on(up, down, outer, inner):
+        below = lax.ppermute(up, "gz", up_pairs)
+        above = lax.ppermute(down, "gz", down_pairs)
+        outer = lax.ppermute(outer, "gz", outer_pairs)
+        inner = lax.ppermute(inner, "gz", inner_pairs)
+        return below, above, outer, inner
 
     def local(link_set, field):
         return call(functools.partial(local_kernel, rows, link_set), f"local_{link_set}", (field, links), whole, 22)
@@ -270,7 +286,7 @@
             pltpu.SemaphoreType.DMA((rows + 1,)),
         ],
     )
-    arrived = sent_on(*sending)
+    arrived = shifted_on(*sending)
     coefs = call(
         functools.partial(taper_kernel, rows), "tapers", (source_slice, band_width), coefs_shape, 1, pltpu.SMEM
     )

time: 27.1 us -> 27 us (level)
    ppermute x0 -> x4, starting transfers between devices: none -> 6.93 us  [the longest x1 3.08 us: shifted_on(): below = lax.ppermute(up, 'gz', up_pairs)]
    ppermute x3 -> x2, starting transfers between devices: 7.17 us -> 3.6 us  [sent_on(): far = lax.ppermute(far, 'gz', far_pairs)]
    ppermute x3 -> x2, starting transfers between devices: 3.93 us -> 2.41 us  [sent_on(): near = lax.ppermute(near, 'gz', near_pairs)]
    ppermute x3 -> x2, starting transfers between devices: 3.49 us -> 2.32 us  [sent_on(): inner = lax.ppermute(inner, 'gz', inner_pairs)]
    ppermute x0 -> x4, waiting for transfers between devices: none -> 0.88 us  [the longest x1 0.77 us: shifted_on(): outer = lax.ppermute(outer, 'gz', outer_pairs)]
    ppermute x3 -> x2, waiting for transfers between devices: 5.29 us -> 4.5 us  [sent_on(): outer = lax.ppermute(outer, 'gz', outer_pairs)]
    ppermute x3 -> x2, starting transfers between devices: 1.33 us -> 0.62 us  [sent_on(): outer = lax.ppermute(outer, 'gz', outer_pairs)]
    ppermute x3 -> x2, waiting for transfers between devices: 0.69 us -> 0.63 us  [sent_on(): far = lax.ppermute(far, 'gz', far_pairs)]
  transfers between devices with their start and end apart: 12 -> 12, of which waited for: 5 -> 6; matrix products, arithmetic and copies ran while one was open for 0% -> 0% of each run, Pallas kernels for 3% -> 3%
where the time goes in v20:
time: 27 us; the launch traced here: 26.8 us
  starting transfers between devices  15.9 us (59%)
  waiting for transfers between devices  6.02 us (22%)
  Pallas kernels  2.93 us (11%)
  between operations  2.02 us (7%)
    ppermute x2, waiting for transfers between devices, sent_on(): outer = lax.ppermute(outer, 'gz', outer_pairs)  4.5 us
    ppermute x2, starting transfers between devices, sent_on(): far = lax.ppermute(far, 'gz', far_pairs)  3.6 us
    ppermute x1, starting transfers between devices, shifted_on(): below = lax.ppermute(up, 'gz', up_pairs)  3.08 us
    pallas_call x9, Pallas kernels, call(): pl.pallas_call(kernel, name=name, out_shape=out_shapes, in_specs=[pl.Bloc...  2.93 us
    ppermute x2, starting transfers between devices, sent_on(): near = lax.ppermute(near, 'gz', near_pairs)  2.41 us
    ppermute x2, starting transfers between devices, sent_on(): inner = lax.ppermute(inner, 'gz', inner_pairs)  2.32 us
    ppermute x1, starting transfers between devices, shifted_on(): above = lax.ppermute(down, 'gz', down_pairs)  2.09 us
    ppermute x1, starting transfers between devices, shifted_on(): outer = lax.ppermute(outer, 'gz', outer_pairs)  1.61 us
  transfers between devices with their start and end apart: 12, of which 6 were waited for; matrix products, arithmetic and copies ran while one was open for 0% of the time, Pallas kernels for 3%

profile of v20, /device:TPU:0, one launch (start us, length us, event | category | flops | bytes accessed | tf_op | source)
XLA Modules:
  0.0 26.8 jit_solution(11984570275907375146)
XLA Ops:
  0.0 1.1 %begin.1 = (f32[4,2,3,8,128]{4,3,2,1,0:T(8,128)S(1)}, f32[4,2,3,8,128]{4,3,2,1,0:T(8,128)S(1)}, f32[1,2,3,8,128]{4,3,2,1,0:T(8,128)S(1)}, f32[1,2,3,8,128]{4,3,2,1,0:T(8,128)S(1)}) custom-call(f32[4,2,3,8,128]{4,3,2,1,0:T(8,128)} %adjoint_hbm.1, f32[864,128]{1,0:T(8,128)} %bitcast.3), custom_call_target="tpu_custom_call" | custom-call | flops 368640 | bytes 368640 | tf_op jit(solution)/shard_map/begin/pallas_call | solution.py:226
  1.1 3.1 %collective-permute-start = (f32[4,2,3,8,128]{4,3,2,1,0:T(8,128)S(1)}, f32[4,2,3,8,128]{4,3,2,1,0:T(8,128)S(1)}, u32[]{:S(2)}, u32[]{:S(2)}) collective-permute-start(f32[4,2,3,8,128]{4,3,2,1,0:T(8,128)S(1)} %get-tuple-element.23), channel_id=1, source_target_pairs={{0,8},{1,9},{2,10},{3,11},{4,12},{5,13},{6,14},{7,15},{8,16},{9,17... | collective-permute-start | bytes 294920 | tf_op jit(solution)/shard_map/ppermute | solution.py:269
  4.2 2.1 %collective-permute-start.1 = (f32[4,2,3,8,128]{4,3,2,1,0:T(8,128)S(1)}, f32[4,2,3,8,128]{4,3,2,1,0:T(8,128)S(1)}, u32[]{:S(2)}, u32[]{:S(2)}) collective-permute-start(f32[4,2,3,8,128]{4,3,2,1,0:T(8,128)S(1)} %get-tuple-element.24), channel_id=1, source_target_pairs={{0,24},{1,25},{2,26},{3,27},{4,28},{5,29},{6,30},{7,31},{8,0},{9,1... | collective-permute-start | bytes 294920 | tf_op jit(solution)/shard_map/ppermute | solution.py:270
  6.2 1.6 %collective-permute-start.2 = (f32[1,2,3,8,128]{4,3,2,1,0:T(8,128)S(1)}, f32[1,2,3,8,128]{4,3,2,1,0:T(8,128)S(1)}, u32[]{:S(2)}, u32[]{:S(2)}) collective-permute-start(f32[1,2,3,8,128]{4,3,2,1,0:T(8,128)S(1)} %get-tuple-element.25), channel_id=1, source_target_pairs={{0,7},{1,2},{2,1},{3,4},{4,3},{5,6},{6,5},{7,0},{8,15},{9,10},{10,... | collective-permute-start | bytes 73736 | tf_op jit(solution)/shard_map/ppermute | solution.py:271
  7.9 0.2 collective-permute-start.3
  9.4 0.3 %start.1 = (f32[4,2,3,8,128]{4,3,2,1,0:T(8,128)S(1)}, f32[4,2,3,8,128]{4,3,2,1,0:T(8,128)S(1)}) custom-call(f32[6,8,128]{2,1,0:T(8,128)S(1)} %tapers.1.coefs_ref, f32[4,2,3,8,128]{4,3,2,1,0:T(8,128)S(1)} %copy-done.1, f32[864,128]{1,0:T(8,128)S(1)} %bitcast.4), custom_call_target="tpu_custom_call" | custom-call | flops 1622016 | bytes 1622016 | tf_op jit(solution)/shard_map/start/pallas_call | solution.py:226
  9.6 0.8 %collective-permute-done.2.refs_3_ = f32[1,2,3,8,128]{4,3,2,1,0:T(8,128)S(1)} collective-permute-done((f32[1,2,3,8,128]{4,3,2,1,0:T(8,128)S(1)}, f32[1,2,3,8,128]{4,3,2,1,0:T(8,128)S(1)}, u32[]{:S(2)}, u32[]{:S(2)}) %collective-permute-start.2) | collective-permute-done | bytes 24608 | tf_op jit(solution)/shard_map/ppermute | solution.py:271
  10.4 0.1 collective-permute-done.1.refs_2_
  10.5 0.1 third.1
  10.7 1.2 %collective-permute-start.4 = (f32[4,2,3,8,128]{4,3,2,1,0:T(8,128)S(1)}, f32[4,2,3,8,128]{4,3,2,1,0:T(8,128)S(1)}, u32[]{:S(2)}, u32[]{:S(2)}) collective-permute-start(f32[4,2,3,8,128]{4,3,2,1,0:T(8,128)S(1)} %get-tuple-element.28), channel_id=1, source_target_pairs={{0,8},{1,9},{2,10},{3,11},{4,12},{5,13},{6,14},{7,15},{8,0},{9,1},... | collective-permute-start | bytes 294920 | tf_op jit(solution)/shard_map/ppermute | solution.py:262
  11.8 1.7 %collective-permute-start.5 = (f32[4,2,3,8,128]{4,3,2,1,0:T(8,128)S(1)}, f32[4,2,3,8,128]{4,3,2,1,0:T(8,128)S(1)}, u32[]{:S(2)}, u32[]{:S(2)}) collective-permute-start(f32[4,2,3,8,128]{4,3,2,1,0:T(8,128)S(1)} %get-tuple-element.29), channel_id=1, source_target_pairs={{0,24},{1,25},{2,26},{3,27},{4,28},{5,29},{6,30},{7,31},{8,16},{9,... | collective-permute-start | bytes 294920 | tf_op jit(solution)/shard_map/ppermute | solution.py:263
  13.6 0.6 %collective-permute-start.6 = (f32[1,2,3,8,128]{4,3,2,1,0:T(8,128)S(1)}, f32[1,2,3,8,128]{4,3,2,1,0:T(8,128)S(1)}, u32[]{:S(2)}, u32[]{:S(2)}) collective-permute-start(f32[1,2,3,8,128]{4,3,2,1,0:T(8,128)S(1)} %get-tuple-element.30), channel_id=1, source_target_pairs={{0,7},{1,2},{2,1},{3,4},{4,3},{5,6},{6,5},{7,0},{8,15},{9,10},{10,... | collective-permute-start | bytes 73736 | tf_op jit(solution)/shard_map/ppermute | solution.py:264
  14.2 0.8 %collective-permute-start.7 = (f32[1,2,3,8,128]{4,3,2,1,0:T(8,128)S(1)}, f32[1,2,3,8,128]{4,3,2,1,0:T(8,128)S(1)}, u32[]{:S(2)}, u32[]{:S(2)}) collective-permute-start(f32[1,2,3,8,128]{4,3,2,1,0:T(8,128)S(1)} %get-tuple-element.31), channel_id=1, source_target_pairs={{0,1},{1,0},{2,3},{3,2},{4,5},{5,4},{6,7},{7,6},{8,9},{9,8},{10,11... | collective-permute-start | bytes 73736 | tf_op jit(solution)/shard_map/ppermute | solution.py:265
  15.6 0.3 %local_1.1.refs_0_ = f32[4,2,3,8,128]{4,3,2,1,0:T(8,128)S(1)} custom-call(f32[4,2,3,8,128]{4,3,2,1,0:T(8,128)S(1)} %get-tuple-element.27.field_ref.refs_6_, f32[864,128]{1,0:T(8,128)S(1)} %bitcast.6), custom_call_target="tpu_custom_call" | custom-call | flops 1622016 | bytes 1622016 | tf_op jit(solution)/shard_map/local_1/pallas_call | solution.py:226
  15.9 2.0 %collective-permute-done.6.refs_3_ = f32[1,2,3,8,128]{4,3,2,1,0:T(8,128)S(1)} collective-permute-done((f32[1,2,3,8,128]{4,3,2,1,0:T(8,128)S(1)}, f32[1,2,3,8,128]{4,3,2,1,0:T(8,128)S(1)}, u32[]{:S(2)}, u32[]{:S(2)}) %collective-permute-start.6) | collective-permute-done | bytes 24608 | tf_op jit(solution)/shard_map/ppermute | solution.py:264
  17.8 0.5 %collective-permute-done.5.refs_2_ = f32[4,2,3,8,128]{4,3,2,1,0:T(8,128)S(1)} collective-permute-done((f32[4,2,3,8,128]{4,3,2,1,0:T(8,128)S(1)}, f32[4,2,3,8,128]{4,3,2,1,0:T(8,128)S(1)}, u32[]{:S(2)}, u32[]{:S(2)}) %collective-permute-start.5) | collective-permute-done | bytes 98336 | tf_op jit(solution)/shard_map/ppermute | solution.py:263
  18.3 0.2 second.1
  18.5 1.2 %collective-permute-start.8 = (f32[4,2,3,8,128]{4,3,2,1,0:T(8,128)S(1)}, f32[4,2,3,8,128]{4,3,2,1,0:T(8,128)S(1)}, u32[]{:S(2)}, u32[]{:S(2)}) collective-permute-start(f32[4,2,3,8,128]{4,3,2,1,0:T(8,128)S(1)} %get-tuple-element.34), channel_id=1, source_target_pairs={{0,8},{1,9},{2,10},{3,11},{4,12},{5,13},{6,14},{7,15},{8,0},{9,1},... | collective-permute-start | bytes 294920 | tf_op jit(solution)/shard_map/ppermute | solution.py:262
  19.7 1.9 %collective-permute-start.9 = (f32[4,2,3,8,128]{4,3,2,1,0:T(8,128)S(1)}, f32[4,2,3,8,128]{4,3,2,1,0:T(8,128)S(1)}, u32[]{:S(2)}, u32[]{:S(2)}) collective-permute-start(f32[4,2,3,8,128]{4,3,2,1,0:T(8,128)S(1)} %get-tuple-element.35), channel_id=1, source_target_pairs={{0,24},{1,25},{2,26},{3,27},{4,28},{5,29},{6,30},{7,31},{8,16},{9,... | collective-permute-start | bytes 294920 | tf_op jit(solution)/shard_map/ppermute | solution.py:263
  21.6 1.6 %collective-permute-start.11 = (f32[1,2,3,8,128]{4,3,2,1,0:T(8,128)S(1)}, f32[1,2,3,8,128]{4,3,2,1,0:T(8,128)S(1)}, u32[]{:S(2)}, u32[]{:S(2)}) collective-permute-start(f32[1,2,3,8,128]{4,3,2,1,0:T(8,128)S(1)} %get-tuple-element.37), channel_id=1, source_target_pairs={{0,1},{1,0},{2,3},{3,2},{4,5},{5,4},{6,7},{7,6},{8,9},{9,8},{10,11... | collective-permute-start | bytes 73736 | tf_op jit(solution)/shard_map/ppermute | solution.py:265
  23.2 0.3 local_0.1.refs_0_
  23.4 2.5 %collective-permute-done.10.refs_3_ = f32[1,2,3,8,128]{4,3,2,1,0:T(8,128)S(1)} collective-permute-done((f32[1,2,3,8,128]{4,3,2,1,0:T(8,128)S(1)}, f32[1,2,3,8,128]{4,3,2,1,0:T(8,128)S(1)}, u32[]{:S(2)}, u32[]{:S(2)}) %collective-permute-start.10) | collective-permute-done | bytes 24608 | tf_op jit(solution)/shard_map/ppermute | solution.py:264
  26.0 0.2 collective-permute-done.9.refs_2_
  26.1 0.7 %last.1 = f32[4,2,3,8,128]{4,3,2,1,0:T(8,128)} custom-call(f32[8,128]{1,0:T(8,128)S(1)} %eps.1.eps_ref, f32[6,8,128]{2,1,0:T(8,128)S(1)} %tapers.1.coefs_ref, f32[864,128]{1,0:T(8,128)S(1)} %bitcast.9, f32[4,2,3,8,128]{4,3,2,1,0:T(8,128)S(1)} %local_0.1.refs_0_, f32[4,2,3,8,128]{4,3,2,1,0:T(8,128)S(1)} %collective-permute-done.8.refs_1_, ...), custom_call_target="tpu_custom_call" | custom-call | flops 368640 | bytes 368640 | tf_op jit(solution)/shard_map/last/pallas_call | solution.py:226
  (13 shorter events, 0.1 us)
Async XLA Ops:
  0.0 9.3 %copy-start = (f32[4,3,4,2,3,3,128]{6,3,5,4,2,1,0:T(2,128)S(1)}, f32[4,3,4,2,3,3,128]{6,3,5,4,2,1,0:T(2,128)}, u32[]{:S(2)}) copy-start(f32[4,3,4,2,3,3,128]{6,3,5,4,2,1,0:T(2,128)} %param.6) | copy-start | bytes 1327108
  0.0 9.3 %copy-start.1 = (f32[4,2,3,8,128]{4,3,2,1,0:T(8,128)S(1)}, f32[4,2,3,8,128]{4,3,2,1,0:T(8,128)}, u32[]{:S(2)}) copy-start(f32[4,2,3,8,128]{4,3,2,1,0:T(8,128)} %adjoint_hbm.1) | copy-start | bytes 294916
  1.1 9.3 %collective-permute-start = (f32[4,2,3,8,128]{4,3,2,1,0:T(8,128)S(1)}, f32[4,2,3,8,128]{4,3,2,1,0:T(8,128)S(1)}, u32[]{:S(2)}, u32[]{:S(2)}) collective-permute-start(f32[4,2,3,8,128]{4,3,2,1,0:T(8,128)S(1)} %get-tuple-element.23), channel_id=1, source_target_pairs={{0,8},{1,9},{2,10},{3,11},{4,12},{5,13},{6,14},{7,15},{8,16},{9,17... | collective-permute-start | bytes 294920 | tf_op jit(solution)/shard_map/ppermute | solution.py:269
  4.2 6.4 %collective-permute-start.1 = (f32[4,2,3,8,128]{4,3,2,1,0:T(8,128)S(1)}, f32[4,2,3,8,128]{4,3,2,1,0:T(8,128)S(1)}, u32[]{:S(2)}, u32[]{:S(2)}) collective-permute-start(f32[4,2,3,8,128]{4,3,2,1,0:T(8,128)S(1)} %get-tuple-element.24), channel_id=1, source_target_pairs={{0,24},{1,25},{2,26},{3,27},{4,28},{5,29},{6,30},{7,31},{8,0},{9,1... | collective-permute-start | bytes 294920 | tf_op jit(solution)/shard_map/ppermute | solution.py:270
  6.2 4.2 %collective-permute-start.2 = (f32[1,2,3,8,128]{4,3,2,1,0:T(8,128)S(1)}, f32[1,2,3,8,128]{4,3,2,1,0:T(8,128)S(1)}, u32[]{:S(2)}, u32[]{:S(2)}) collective-permute-start(f32[1,2,3,8,128]{4,3,2,1,0:T(8,128)S(1)} %get-tuple-element.25), channel_id=1, source_target_pairs={{0,7},{1,2},{2,1},{3,4},{4,3},{5,6},{6,5},{7,0},{8,15},{9,10},{10,... | collective-permute-start | bytes 73736 | tf_op jit(solution)/shard_map/ppermute | solution.py:271
  7.9 2.6 %collective-permute-start.3 = (f32[1,2,3,8,128]{4,3,2,1,0:T(8,128)S(1)}, f32[1,2,3,8,128]{4,3,2,1,0:T(8,128)S(1)}, u32[]{:S(2)}, u32[]{:S(2)}) collective-permute-start(f32[1,2,3,8,128]{4,3,2,1,0:T(8,128)S(1)} %get-tuple-element.26), channel_id=1, source_target_pairs={{0,1},{1,0},{2,3},{3,2},{4,5},{5,4},{6,7},{7,6},{8,9},{9,8},{10,11... | collective-permute-start | bytes 73736 | tf_op jit(solution)/shard_map/ppermute | solution.py:272
  10.7 7.2 %collective-permute-start.4 = (f32[4,2,3,8,128]{4,3,2,1,0:T(8,128)S(1)}, f32[4,2,3,8,128]{4,3,2,1,0:T(8,128)S(1)}, u32[]{:S(2)}, u32[]{:S(2)}) collective-permute-start(f32[4,2,3,8,128]{4,3,2,1,0:T(8,128)S(1)} %get-tuple-element.28), channel_id=1, source_target_pairs={{0,8},{1,9},{2,10},{3,11},{4,12},{5,13},{6,14},{7,15},{8,0},{9,1},... | collective-permute-start | bytes 294920 | tf_op jit(solution)/shard_map/ppermute | solution.py:262
  11.8 6.5 %collective-permute-start.5 = (f32[4,2,3,8,128]{4,3,2,1,0:T(8,128)S(1)}, f32[4,2,3,8,128]{4,3,2,1,0:T(8,128)S(1)}, u32[]{:S(2)}, u32[]{:S(2)}) collective-permute-start(f32[4,2,3,8,128]{4,3,2,1,0:T(8,128)S(1)} %get-tuple-element.29), channel_id=1, source_target_pairs={{0,24},{1,25},{2,26},{3,27},{4,28},{5,29},{6,30},{7,31},{8,16},{9,... | collective-permute-start | bytes 294920 | tf_op jit(solution)/shard_map/ppermute | solution.py:263
  13.6 4.3 %collective-permute-start.6 = (f32[1,2,3,8,128]{4,3,2,1,0:T(8,128)S(1)}, f32[1,2,3,8,128]{4,3,2,1,0:T(8,128)S(1)}, u32[]{:S(2)}, u32[]{:S(2)}) collective-permute-start(f32[1,2,3,8,128]{4,3,2,1,0:T(8,128)S(1)} %get-tuple-element.30), channel_id=1, source_target_pairs={{0,7},{1,2},{2,1},{3,4},{4,3},{5,6},{6,5},{7,0},{8,15},{9,10},{10,... | collective-permute-start | bytes 73736 | tf_op jit(solution)/shard_map/ppermute | solution.py:264
  14.2 3.7 %collective-permute-start.7 = (f32[1,2,3,8,128]{4,3,2,1,0:T(8,128)S(1)}, f32[1,2,3,8,128]{4,3,2,1,0:T(8,128)S(1)}, u32[]{:S(2)}, u32[]{:S(2)}) collective-permute-start(f32[1,2,3,8,128]{4,3,2,1,0:T(8,128)S(1)} %get-tuple-element.31), channel_id=1, source_target_pairs={{0,1},{1,0},{2,3},{3,2},{4,5},{5,4},{6,7},{7,6},{8,9},{9,8},{10,11... | collective-permute-start | bytes 73736 | tf_op jit(solution)/shard_map/ppermute | solution.py:265
  18.5 7.5 %collective-permute-start.8 = (f32[4,2,3,8,128]{4,3,2,1,0:T(8,128)S(1)}, f32[4,2,3,8,128]{4,3,2,1,0:T(8,128)S(1)}, u32[]{:S(2)}, u32[]{:S(2)}) collective-permute-start(f32[4,2,3,8,128]{4,3,2,1,0:T(8,128)S(1)} %get-tuple-element.34), channel_id=1, source_target_pairs={{0,8},{1,9},{2,10},{3,11},{4,12},{5,13},{6,14},{7,15},{8,0},{9,1},... | collective-permute-start | bytes 294920 | tf_op jit(solution)/shard_map/ppermute | solution.py:262
  19.7 6.4 %collective-permute-start.9 = (f32[4,2,3,8,128]{4,3,2,1,0:T(8,128)S(1)}, f32[4,2,3,8,128]{4,3,2,1,0:T(8,128)S(1)}, u32[]{:S(2)}, u32[]{:S(2)}) collective-permute-start(f32[4,2,3,8,128]{4,3,2,1,0:T(8,128)S(1)} %get-tuple-element.35), channel_id=1, source_target_pairs={{0,24},{1,25},{2,26},{3,27},{4,28},{5,29},{6,30},{7,31},{8,16},{9,... | collective-permute-start | bytes 294920 | tf_op jit(solution)/shard_map/ppermute | solution.py:263
  21.6 4.4 %collective-permute-start.10 = (f32[1,2,3,8,128]{4,3,2,1,0:T(8,128)S(1)}, f32[1,2,3,8,128]{4,3,2,1,0:T(8,128)S(1)}, u32[]{:S(2)}, u32[]{:S(2)}) collective-permute-start(f32[1,2,3,8,128]{4,3,2,1,0:T(8,128)S(1)} %get-tuple-element.36), channel_id=1, source_target_pairs={{0,7},{1,2},{2,1},{3,4},{4,3},{5,6},{6,5},{7,0},{8,15},{9,10},{10,... | collective-permute-start | bytes 73736 | tf_op jit(solution)/shard_map/ppermute | solution.py:264
  21.6 4.4 %collective-permute-start.11 = (f32[1,2,3,8,128]{4,3,2,1,0:T(8,128)S(1)}, f32[1,2,3,8,128]{4,3,2,1,0:T(8,128)S(1)}, u32[]{:S(2)}, u32[]{:S(2)}) collective-permute-start(f32[1,2,3,8,128]{4,3,2,1,0:T(8,128)S(1)} %get-tuple-element.37), channel_id=1, source_target_pairs={{0,1},{1,0},{2,3},{3,2},{4,5},{5,4},{6,7},{7,6},{8,9},{9,8},{10,11... | collective-permute-start | bytes 73736 | tf_op jit(solution)/shard_map/ppermute | solution.py:265

commit v21 on v20

--- a/solution.py
+++ b/solution.py
@@ -155,6 +155,8 @@
 
 def arrived_sum(links_ref, link_set, row, rows, arrivals, coefs_ref=None):
     sum_ref, one_ref, two_ref, outer_ref, inner_ref = arrivals
+    if link_set == 1:
+        one_ref, two_ref = two_ref, one_ref
     _, first_pos, odd_plane, odd_block = place(rows)
     one, two = load_field(one_ref, row), load_field(two_ref, row)
     if coefs_ref is not None:
@@ -258,12 +260,12 @@
     up_pairs = [(i, in_line(i, 1)) for i in range(count)]
     down_pairs = [(i, in_line(i, -1)) for i in range(count)]
 
-    def sent_on(far, near, outer, inner):
+    def sent_on(far, near, outer, inner, far_first):
         near = lax.ppermute(near, "gz", near_pairs)
         far = lax.ppermute(far, "gz", far_pairs)
         outer = lax.ppermute(outer, "gz", outer_pairs)
         inner = lax.ppermute(inner, "gz", inner_pairs)
-        return near, far, outer, inner
+        return (far, near, outer, inner) if far_first else (near, far, outer, inner)
 
     def shifted_on(up, down, outer, inner):
         below = lax.ppermute(up, "gz", up_pairs)
@@ -298,12 +300,12 @@
     third, *sending = call(
         functools.partial(third_kernel, rows), "third", (coefs, links, total) + arrived, (whole,) + sent, 10
     )
-    arrived = sent_on(*sending)
+    arrived = sent_on(*sending, far_first=True)
     mixed, *sending, base = call(
         functools.partial(second_kernel, rows), "second", (eps, coefs, links, local(1, third)) + arrived + (start, third),
         (whole,) + sent + (whole,), 10,
     )
-    arrived = sent_on(*sending)
+    arrived = sent_on(*sending, far_first=False)
     return call(
         functools.partial(last_kernel, rows), "last", (eps, coefs, links, local(0, mixed)) + arrived + (base,), whole, 5,
         scratch=[pltpu.VMEM(adjoint.shape, jnp.float32), pltpu.SemaphoreType.DMA((rows,))], out_space=pltpu.HBM,

time: 27 us -> 27.1 us (level)
  waiting for transfers between devices: 6.02 us -> 6.96 us
  starting transfers between devices: 15.9 us -> 15 us
    ppermute x2, starting transfers between devices: 2.41 us -> 1.03 us  [sent_on(): near = lax.ppermute(near, 'gz', near_pairs)]
    ppermute x2, starting transfers between devices: 0.62 us -> 1.27 us  [sent_on(): outer = lax.ppermute(outer, 'gz', outer_pairs)]
    ppermute x2, waiting for transfers between devices: 0.01 us -> 0.64 us  [sent_on(): near = lax.ppermute(near, 'gz', near_pairs)]
    ppermute x2, waiting for transfers between devices: 0.63 us -> 1.1 us  [sent_on(): far = lax.ppermute(far, 'gz', far_pairs)]
    ppermute x2, starting transfers between devices: 2.32 us -> 1.88 us  [sent_on(): inner = lax.ppermute(inner, 'gz', inner_pairs)]
    ppermute x2, starting transfers between devices: 3.6 us -> 3.89 us  [sent_on(): far = lax.ppermute(far, 'gz', far_pairs)]
  transfers between devices with their start and end apart: 12 -> 12, of which waited for: 6 -> 7; matrix products, arithmetic and copies ran while one was open for 0% -> 0% of each run, Pallas kernels for 3% -> 3%
where the time goes in v21:
time: 27.1 us; the launch traced here: 26.9 us
  starting transfers between devices  15 us (55%)
  waiting for transfers between devices  6.96 us (26%)
  Pallas kernels  2.93 us (11%)
  between operations  2.02 us (7%)
    ppermute x2, waiting for transfers between devices, sent_on(): outer = lax.ppermute(outer, 'gz', outer_pairs)  4.33 us
    ppermute x2, starting transfers between devices, sent_on(): far = lax.ppermute(far, 'gz', far_pairs)  3.89 us
    ppermute x1, starting transfers between devices, shifted_on(): below = lax.ppermute(up, 'gz', up_pairs)  3.08 us
    pallas_call x9, Pallas kernels, call(): pl.pallas_call(kernel, name=name, out_shape=out_shapes, in_specs=[pl.Bloc...  2.93 us
    ppermute x1, starting transfers between devices, shifted_on(): above = lax.ppermute(down, 'gz', down_pairs)  2.09 us
    ppermute x2, starting transfers between devices, sent_on(): inner = lax.ppermute(inner, 'gz', inner_pairs)  1.88 us
    ppermute x1, starting transfers between devices, shifted_on(): outer = lax.ppermute(outer, 'gz', outer_pairs)  1.61 us
    ppermute x2, starting transfers between devices, sent_on(): outer = lax.ppermute(outer, 'gz', outer_pairs)  1.27 us
  transfers between devices with their start and end apart: 12, of which 7 were waited for; matrix products, arithmetic and copies ran while one was open for 0% of the time, Pallas kernels for 3%

profile of v21, /device:TPU:0, one launch (start us, length us, event | category | flops | bytes accessed | tf_op | source)
XLA Modules:
  0.0 26.9 jit_solution(14527684366537809561)
XLA Ops:
  0.0 1.1 %begin.1 = (f32[4,2,3,8,128]{4,3,2,1,0:T(8,128)S(1)}, f32[4,2,3,8,128]{4,3,2,1,0:T(8,128)S(1)}, f32[1,2,3,8,128]{4,3,2,1,0:T(8,128)S(1)}, f32[1,2,3,8,128]{4,3,2,1,0:T(8,128)S(1)}) custom-call(f32[4,2,3,8,128]{4,3,2,1,0:T(8,128)} %adjoint_hbm.1, f32[864,128]{1,0:T(8,128)} %bitcast.3), custom_call_target="tpu_custom_call" | custom-call | flops 368640 | bytes 368640 | tf_op jit(solution)/shard_map/begin/pallas_call | solution.py:228
  1.1 3.1 %collective-permute-start = (f32[4,2,3,8,128]{4,3,2,1,0:T(8,128)S(1)}, f32[4,2,3,8,128]{4,3,2,1,0:T(8,128)S(1)}, u32[]{:S(2)}, u32[]{:S(2)}) collective-permute-start(f32[4,2,3,8,128]{4,3,2,1,0:T(8,128)S(1)} %get-tuple-element.23), channel_id=1, source_target_pairs={{0,8},{1,9},{2,10},{3,11},{4,12},{5,13},{6,14},{7,15},{8,16},{9,17... | collective-permute-start | bytes 294920 | tf_op jit(solution)/shard_map/ppermute | solution.py:271
  4.2 2.1 %collective-permute-start.1 = (f32[4,2,3,8,128]{4,3,2,1,0:T(8,128)S(1)}, f32[4,2,3,8,128]{4,3,2,1,0:T(8,128)S(1)}, u32[]{:S(2)}, u32[]{:S(2)}) collective-permute-start(f32[4,2,3,8,128]{4,3,2,1,0:T(8,128)S(1)} %get-tuple-element.24), channel_id=1, source_target_pairs={{0,24},{1,25},{2,26},{3,27},{4,28},{5,29},{6,30},{7,31},{8,0},{9,1... | collective-permute-start | bytes 294920 | tf_op jit(solution)/shard_map/ppermute | solution.py:272
  6.2 1.6 %collective-permute-start.2 = (f32[1,2,3,8,128]{4,3,2,1,0:T(8,128)S(1)}, f32[1,2,3,8,128]{4,3,2,1,0:T(8,128)S(1)}, u32[]{:S(2)}, u32[]{:S(2)}) collective-permute-start(f32[1,2,3,8,128]{4,3,2,1,0:T(8,128)S(1)} %get-tuple-element.25), channel_id=1, source_target_pairs={{0,7},{1,2},{2,1},{3,4},{4,3},{5,6},{6,5},{7,0},{8,15},{9,10},{10,... | collective-permute-start | bytes 73736 | tf_op jit(solution)/shard_map/ppermute | solution.py:273
  7.9 0.2 collective-permute-start.3
  9.4 0.3 %start.1 = (f32[4,2,3,8,128]{4,3,2,1,0:T(8,128)S(1)}, f32[4,2,3,8,128]{4,3,2,1,0:T(8,128)S(1)}) custom-call(f32[6,8,128]{2,1,0:T(8,128)S(1)} %tapers.1.coefs_ref, f32[4,2,3,8,128]{4,3,2,1,0:T(8,128)S(1)} %copy-done.1, f32[864,128]{1,0:T(8,128)S(1)} %bitcast.4), custom_call_target="tpu_custom_call" | custom-call | flops 1622016 | bytes 1622016 | tf_op jit(solution)/shard_map/start/pallas_call | solution.py:228
  9.6 0.8 %collective-permute-done.2.refs_3_ = f32[1,2,3,8,128]{4,3,2,1,0:T(8,128)S(1)} collective-permute-done((f32[1,2,3,8,128]{4,3,2,1,0:T(8,128)S(1)}, f32[1,2,3,8,128]{4,3,2,1,0:T(8,128)S(1)}, u32[]{:S(2)}, u32[]{:S(2)}) %collective-permute-start.2) | collective-permute-done | bytes 24608 | tf_op jit(solution)/shard_map/ppermute | solution.py:273
  10.5 0.1 third.1
  10.7 2.5 %collective-permute-start.4 = (f32[4,2,3,8,128]{4,3,2,1,0:T(8,128)S(1)}, f32[4,2,3,8,128]{4,3,2,1,0:T(8,128)S(1)}, u32[]{:S(2)}, u32[]{:S(2)}) collective-permute-start(f32[4,2,3,8,128]{4,3,2,1,0:T(8,128)S(1)} %get-tuple-element.28), channel_id=1, source_target_pairs={{0,24},{1,25},{2,26},{3,27},{4,28},{5,29},{6,30},{7,31},{8,16},{9,... | collective-permute-start | bytes 294920 | tf_op jit(solution)/shard_map/ppermute | solution.py:265
  13.1 0.8 %collective-permute-start.6 = (f32[1,2,3,8,128]{4,3,2,1,0:T(8,128)S(1)}, f32[1,2,3,8,128]{4,3,2,1,0:T(8,128)S(1)}, u32[]{:S(2)}, u32[]{:S(2)}) collective-permute-start(f32[1,2,3,8,128]{4,3,2,1,0:T(8,128)S(1)} %get-tuple-element.30), channel_id=1, source_target_pairs={{0,7},{1,2},{2,1},{3,4},{4,3},{5,6},{6,5},{7,0},{8,15},{9,10},{10,... | collective-permute-start | bytes 73736 | tf_op jit(solution)/shard_map/ppermute | solution.py:266
  13.9 0.8 %collective-permute-start.7 = (f32[1,2,3,8,128]{4,3,2,1,0:T(8,128)S(1)}, f32[1,2,3,8,128]{4,3,2,1,0:T(8,128)S(1)}, u32[]{:S(2)}, u32[]{:S(2)}) collective-permute-start(f32[1,2,3,8,128]{4,3,2,1,0:T(8,128)S(1)} %get-tuple-element.31), channel_id=1, source_target_pairs={{0,1},{1,0},{2,3},{3,2},{4,5},{5,4},{6,7},{7,6},{8,9},{9,8},{10,11... | collective-permute-start | bytes 73736 | tf_op jit(solution)/shard_map/ppermute | solution.py:267
  15.4 0.3 %local_1.1.refs_0_ = f32[4,2,3,8,128]{4,3,2,1,0:T(8,128)S(1)} custom-call(f32[4,2,3,8,128]{4,3,2,1,0:T(8,128)S(1)} %get-tuple-element.27.field_ref.refs_6_, f32[864,128]{1,0:T(8,128)S(1)} %bitcast.6), custom_call_target="tpu_custom_call" | custom-call | flops 1622016 | bytes 1622016 | tf_op jit(solution)/shard_map/local_1/pallas_call | solution.py:228
  15.7 1.8 %collective-permute-done.6.refs_3_ = f32[1,2,3,8,128]{4,3,2,1,0:T(8,128)S(1)} collective-permute-done((f32[1,2,3,8,128]{4,3,2,1,0:T(8,128)S(1)}, f32[1,2,3,8,128]{4,3,2,1,0:T(8,128)S(1)}, u32[]{:S(2)}, u32[]{:S(2)}) %collective-permute-start.6) | collective-permute-done | bytes 24608 | tf_op jit(solution)/shard_map/ppermute | solution.py:266
  17.4 0.4 %collective-permute-done.4.refs_1_ = f32[4,2,3,8,128]{4,3,2,1,0:T(8,128)S(1)} collective-permute-done((f32[4,2,3,8,128]{4,3,2,1,0:T(8,128)S(1)}, f32[4,2,3,8,128]{4,3,2,1,0:T(8,128)S(1)}, u32[]{:S(2)}, u32[]{:S(2)}) %collective-permute-start.4) | collective-permute-done | bytes 98336 | tf_op jit(solution)/shard_map/ppermute | solution.py:265
  17.9 0.6 %collective-permute-done.5.refs_2_ = f32[4,2,3,8,128]{4,3,2,1,0:T(8,128)S(1)} collective-permute-done((f32[4,2,3,8,128]{4,3,2,1,0:T(8,128)S(1)}, f32[4,2,3,8,128]{4,3,2,1,0:T(8,128)S(1)}, u32[]{:S(2)}, u32[]{:S(2)}) %collective-permute-start.5) | collective-permute-done | bytes 98336 | tf_op jit(solution)/shard_map/ppermute | solution.py:264
  18.5 0.2 second.1
  18.7 1.0 %collective-permute-start.8 = (f32[4,2,3,8,128]{4,3,2,1,0:T(8,128)S(1)}, f32[4,2,3,8,128]{4,3,2,1,0:T(8,128)S(1)}, u32[]{:S(2)}, u32[]{:S(2)}) collective-permute-start(f32[4,2,3,8,128]{4,3,2,1,0:T(8,128)S(1)} %get-tuple-element.34), channel_id=1, source_target_pairs={{0,8},{1,9},{2,10},{3,11},{4,12},{5,13},{6,14},{7,15},{8,0},{9,1},... | collective-permute-start | bytes 294920 | tf_op jit(solution)/shard_map/ppermute | solution.py:264
  19.7 1.4 %collective-permute-start.9 = (f32[4,2,3,8,128]{4,3,2,1,0:T(8,128)S(1)}, f32[4,2,3,8,128]{4,3,2,1,0:T(8,128)S(1)}, u32[]{:S(2)}, u32[]{:S(2)}) collective-permute-start(f32[4,2,3,8,128]{4,3,2,1,0:T(8,128)S(1)} %get-tuple-element.35), channel_id=1, source_target_pairs={{0,24},{1,25},{2,26},{3,27},{4,28},{5,29},{6,30},{7,31},{8,16},{9,... | collective-permute-start | bytes 294920 | tf_op jit(solution)/shard_map/ppermute | solution.py:265
  21.1 0.5 %collective-permute-start.10 = (f32[1,2,3,8,128]{4,3,2,1,0:T(8,128)S(1)}, f32[1,2,3,8,128]{4,3,2,1,0:T(8,128)S(1)}, u32[]{:S(2)}, u32[]{:S(2)}) collective-permute-start(f32[1,2,3,8,128]{4,3,2,1,0:T(8,128)S(1)} %get-tuple-element.36), channel_id=1, source_target_pairs={{0,7},{1,2},{2,1},{3,4},{4,3},{5,6},{6,5},{7,0},{8,15},{9,10},{10,... | collective-permute-start | bytes 73736 | tf_op jit(solution)/shard_map/ppermute | solution.py:266
  21.6 1.1 %collective-permute-start.11 = (f32[1,2,3,8,128]{4,3,2,1,0:T(8,128)S(1)}, f32[1,2,3,8,128]{4,3,2,1,0:T(8,128)S(1)}, u32[]{:S(2)}, u32[]{:S(2)}) collective-permute-start(f32[1,2,3,8,128]{4,3,2,1,0:T(8,128)S(1)} %get-tuple-element.37), channel_id=1, source_target_pairs={{0,1},{1,0},{2,3},{3,2},{4,5},{5,4},{6,7},{7,6},{8,9},{9,8},{10,11... | collective-permute-start | bytes 73736 | tf_op jit(solution)/shard_map/ppermute | solution.py:267
  22.7 0.3 local_0.1.refs_0_
  23.0 2.6 %collective-permute-done.10.refs_3_ = f32[1,2,3,8,128]{4,3,2,1,0:T(8,128)S(1)} collective-permute-done((f32[1,2,3,8,128]{4,3,2,1,0:T(8,128)S(1)}, f32[1,2,3,8,128]{4,3,2,1,0:T(8,128)S(1)}, u32[]{:S(2)}, u32[]{:S(2)}) %collective-permute-start.10) | collective-permute-done | bytes 24608 | tf_op jit(solution)/shard_map/ppermute | solution.py:266
  25.5 0.7 %collective-permute-done.9.refs_2_ = f32[4,2,3,8,128]{4,3,2,1,0:T(8,128)S(1)} collective-permute-done((f32[4,2,3,8,128]{4,3,2,1,0:T(8,128)S(1)}, f32[4,2,3,8,128]{4,3,2,1,0:T(8,128)S(1)}, u32[]{:S(2)}, u32[]{:S(2)}) %collective-permute-start.9) | collective-permute-done | bytes 98336 | tf_op jit(solution)/shard_map/ppermute | solution.py:265
  26.2 0.7 %last.1 = f32[4,2,3,8,128]{4,3,2,1,0:T(8,128)} custom-call(f32[8,128]{1,0:T(8,128)S(1)} %eps.1.eps_ref, f32[6,8,128]{2,1,0:T(8,128)S(1)} %tapers.1.coefs_ref, f32[864,128]{1,0:T(8,128)S(1)} %bitcast.9, f32[4,2,3,8,128]{4,3,2,1,0:T(8,128)S(1)} %local_0.1.refs_0_, f32[4,2,3,8,128]{4,3,2,1,0:T(8,128)S(1)} %collective-permute-done.8.refs_1_, ...), custom_call_target="tpu_custom_call" | custom-call | flops 368640 | bytes 368640 | tf_op jit(solution)/shard_map/last/pallas_call | solution.py:228
  (13 shorter events, 0.2 us)
Async XLA Ops:
  0.0 9.3 %copy-start = (f32[4,3,4,2,3,3,128]{6,3,5,4,2,1,0:T(2,128)S(1)}, f32[4,3,4,2,3,3,128]{6,3,5,4,2,1,0:T(2,128)}, u32[]{:S(2)}) copy-start(f32[4,3,4,2,3,3,128]{6,3,5,4,2,1,0:T(2,128)} %param.6) | copy-start | bytes 1327108
  0.0 9.3 %copy-start.1 = (f32[4,2,3,8,128]{4,3,2,1,0:T(8,128)S(1)}, f32[4,2,3,8,128]{4,3,2,1,0:T(8,128)}, u32[]{:S(2)}) copy-start(f32[4,2,3,8,128]{4,3,2,1,0:T(8,128)} %adjoint_hbm.1) | copy-start | bytes 294916
  1.1 9.3 %collective-permute-start = (f32[4,2,3,8,128]{4,3,2,1,0:T(8,128)S(1)}, f32[4,2,3,8,128]{4,3,2,1,0:T(8,128)S(1)}, u32[]{:S(2)}, u32[]{:S(2)}) collective-permute-start(f32[4,2,3,8,128]{4,3,2,1,0:T(8,128)S(1)} %get-tuple-element.23), channel_id=1, source_target_pairs={{0,8},{1,9},{2,10},{3,11},{4,12},{5,13},{6,14},{7,15},{8,16},{9,17... | collective-permute-start | bytes 294920 | tf_op jit(solution)/shard_map/ppermute | solution.py:271
  4.2 6.4 %collective-permute-start.1 = (f32[4,2,3,8,128]{4,3,2,1,0:T(8,128)S(1)}, f32[4,2,3,8,128]{4,3,2,1,0:T(8,128)S(1)}, u32[]{:S(2)}, u32[]{:S(2)}) collective-permute-start(f32[4,2,3,8,128]{4,3,2,1,0:T(8,128)S(1)} %get-tuple-element.24), channel_id=1, source_target_pairs={{0,24},{1,25},{2,26},{3,27},{4,28},{5,29},{6,30},{7,31},{8,0},{9,1... | collective-permute-start | bytes 294920 | tf_op jit(solution)/shard_map/ppermute | solution.py:272
  6.2 4.2 %collective-permute-start.2 = (f32[1,2,3,8,128]{4,3,2,1,0:T(8,128)S(1)}, f32[1,2,3,8,128]{4,3,2,1,0:T(8,128)S(1)}, u32[]{:S(2)}, u32[]{:S(2)}) collective-permute-start(f32[1,2,3,8,128]{4,3,2,1,0:T(8,128)S(1)} %get-tuple-element.25), channel_id=1, source_target_pairs={{0,7},{1,2},{2,1},{3,4},{4,3},{5,6},{6,5},{7,0},{8,15},{9,10},{10,... | collective-permute-start | bytes 73736 | tf_op jit(solution)/shard_map/ppermute | solution.py:273
  7.9 2.6 %collective-permute-start.3 = (f32[1,2,3,8,128]{4,3,2,1,0:T(8,128)S(1)}, f32[1,2,3,8,128]{4,3,2,1,0:T(8,128)S(1)}, u32[]{:S(2)}, u32[]{:S(2)}) collective-permute-start(f32[1,2,3,8,128]{4,3,2,1,0:T(8,128)S(1)} %get-tuple-element.26), channel_id=1, source_target_pairs={{0,1},{1,0},{2,3},{3,2},{4,5},{5,4},{6,7},{7,6},{8,9},{9,8},{10,11... | collective-permute-start | bytes 73736 | tf_op jit(solution)/shard_map/ppermute | solution.py:274
  10.7 7.2 %collective-permute-start.4 = (f32[4,2,3,8,128]{4,3,2,1,0:T(8,128)S(1)}, f32[4,2,3,8,128]{4,3,2,1,0:T(8,128)S(1)}, u32[]{:S(2)}, u32[]{:S(2)}) collective-permute-start(f32[4,2,3,8,128]{4,3,2,1,0:T(8,128)S(1)} %get-tuple-element.28), channel_id=1, source_target_pairs={{0,24},{1,25},{2,26},{3,27},{4,28},{5,29},{6,30},{7,31},{8,16},{9,... | collective-permute-start | bytes 294920 | tf_op jit(solution)/shard_map/ppermute | solution.py:265
  13.1 5.4 %collective-permute-start.5 = (f32[4,2,3,8,128]{4,3,2,1,0:T(8,128)S(1)}, f32[4,2,3,8,128]{4,3,2,1,0:T(8,128)S(1)}, u32[]{:S(2)}, u32[]{:S(2)}) collective-permute-start(f32[4,2,3,8,128]{4,3,2,1,0:T(8,128)S(1)} %get-tuple-element.29), channel_id=1, source_target_pairs={{0,8},{1,9},{2,10},{3,11},{4,12},{5,13},{6,14},{7,15},{8,0},{9,1},... | collective-permute-start | bytes 294920 | tf_op jit(solution)/shard_map/ppermute | solution.py:264
  13.1 4.3 %collective-permute-start.6 = (f32[1,2,3,8,128]{4,3,2,1,0:T(8,128)S(1)}, f32[1,2,3,8,128]{4,3,2,1,0:T(8,128)S(1)}, u32[]{:S(2)}, u32[]{:S(2)}) collective-permute-start(f32[1,2,3,8,128]{4,3,2,1,0:T(8,128)S(1)} %get-tuple-element.30), channel_id=1, source_target_pairs={{0,7},{1,2},{2,1},{3,4},{4,3},{5,6},{6,5},{7,0},{8,15},{9,10},{10,... | collective-permute-start | bytes 73736 | tf_op jit(solution)/shard_map/ppermute | solution.py:266
  13.9 3.5 %collective-permute-start.7 = (f32[1,2,3,8,128]{4,3,2,1,0:T(8,128)S(1)}, f32[1,2,3,8,128]{4,3,2,1,0:T(8,128)S(1)}, u32[]{:S(2)}, u32[]{:S(2)}) collective-permute-start(f32[1,2,3,8,128]{4,3,2,1,0:T(8,128)S(1)} %get-tuple-element.31), channel_id=1, source_target_pairs={{0,1},{1,0},{2,3},{3,2},{4,5},{5,4},{6,7},{7,6},{8,9},{9,8},{10,11... | collective-permute-start | bytes 73736 | tf_op jit(solution)/shard_map/ppermute | solution.py:267
  18.7 6.8 %collective-permute-start.8 = (f32[4,2,3,8,128]{4,3,2,1,0:T(8,128)S(1)}, f32[4,2,3,8,128]{4,3,2,1,0:T(8,128)S(1)}, u32[]{:S(2)}, u32[]{:S(2)}) collective-permute-start(f32[4,2,3,8,128]{4,3,2,1,0:T(8,128)S(1)} %get-tuple-element.34), channel_id=1, source_target_pairs={{0,8},{1,9},{2,10},{3,11},{4,12},{5,13},{6,14},{7,15},{8,0},{9,1},... | collective-permute-start | bytes 294920 | tf_op jit(solution)/shard_map/ppermute | solution.py:264
  19.7 6.5 %collective-permute-start.9 = (f32[4,2,3,8,128]{4,3,2,1,0:T(8,128)S(1)}, f32[4,2,3,8,128]{4,3,2,1,0:T(8,128)S(1)}, u32[]{:S(2)}, u32[]{:S(2)}) collective-permute-start(f32[4,2,3,8,128]{4,3,2,1,0:T(8,128)S(1)} %get-tuple-element.35), channel_id=1, source_target_pairs={{0,24},{1,25},{2,26},{3,27},{4,28},{5,29},{6,30},{7,31},{8,16},{9,... | collective-permute-start | bytes 294920 | tf_op jit(solution)/shard_map/ppermute | solution.py:265
  21.1 4.4 %collective-permute-start.10 = (f32[1,2,3,8,128]{4,3,2,1,0:T(8,128)S(1)}, f32[1,2,3,8,128]{4,3,2,1,0:T(8,128)S(1)}, u32[]{:S(2)}, u32[]{:S(2)}) collective-permute-start(f32[1,2,3,8,128]{4,3,2,1,0:T(8,128)S(1)} %get-tuple-element.36), channel_id=1, source_target_pairs={{0,7},{1,2},{2,1},{3,4},{4,3},{5,6},{6,5},{7,0},{8,15},{9,10},{10,... | collective-permute-start | bytes 73736 | tf_op jit(solution)/shard_map/ppermute | solution.py:266
  21.6 3.9 %collective-permute-start.11 = (f32[1,2,3,8,128]{4,3,2,1,0:T(8,128)S(1)}, f32[1,2,3,8,128]{4,3,2,1,0:T(8,128)S(1)}, u32[]{:S(2)}, u32[]{:S(2)}) collective-permute-start(f32[1,2,3,8,128]{4,3,2,1,0:T(8,128)S(1)} %get-tuple-element.37), channel_id=1, source_target_pairs={{0,1},{1,0},{2,3},{3,2},{4,5},{5,4},{6,7},{7,6},{8,9},{9,8},{10,11... | collective-permute-start | bytes 73736 | tf_op jit(solution)/shard_map/ppermute | solution.py:267

commit v22 on v21

--- a/solution.py
+++ b/solution.py
@@ -155,7 +155,7 @@
 
 def arrived_sum(links_ref, link_set, row, rows, arrivals, coefs_ref=None):
     sum_ref, one_ref, two_ref, outer_ref, inner_ref = arrivals
-    if link_set == 1:
+    if link_set == 0:
         one_ref, two_ref = two_ref, one_ref
     _, first_pos, odd_plane, odd_block = place(rows)
     one, two = load_field(one_ref, row), load_field(two_ref, row)
@@ -300,12 +300,12 @@
     third, *sending = call(
         functools.partial(third_kernel, rows), "third", (coefs, links, total) + arrived, (whole,) + sent, 10
     )
-    arrived = sent_on(*sending, far_first=True)
+    arrived = sent_on(*sending, far_first=False)
     mixed, *sending, base = call(
         functools.partial(second_kernel, rows), "second", (eps, coefs, links, local(1, third)) + arrived + (start, third),
         (whole,) + sent + (whole,), 10,
     )
-    arrived = sent_on(*sending, far_first=False)
+    arrived = sent_on(*sending, far_first=True)
     return call(
         functools.partial(last_kernel, rows), "last", (eps, coefs, links, local(0, mixed)) + arrived + (base,), whole, 5,
         scratch=[pltpu.VMEM(adjoint.shape, jnp.float32), pltpu.SemaphoreType.DMA((rows,))], out_space=pltpu.HBM,

time: 27.1 us -> 26.9 us (level)
    ppermute x2, waiting for transfers between devices: 1.1 us -> 0.47 us  [sent_on(): far = lax.ppermute(far, 'gz', far_pairs)]
    ppermute x2, waiting for transfers between devices: 0.64 us -> 0.97 us  [sent_on(): near = lax.ppermute(near, 'gz', near_pairs)]
    ppermute x2, starting transfers between devices: 1.88 us -> 1.57 us  [sent_on(): inner = lax.ppermute(inner, 'gz', inner_pairs)]
  transfers between devices with their start and end apart: 12 -> 12, of which waited for: 7 -> 6; matrix products, arithmetic and copies ran while one was open for 0% -> 0% of each run, Pallas kernels for 3% -> 3%
where the time goes in v22:
time: 26.9 us; the launch traced here: 26.8 us
  starting transfers between devices  15 us (56%)
  waiting for transfers between devices  6.82 us (25%)
  Pallas kernels  2.92 us (11%)
  between operations  2.02 us (8%)
    ppermute x2, waiting for transfers between devices, sent_on(): outer = lax.ppermute(outer, 'gz', outer_pairs)  4.5 us
    ppermute x2, starting transfers between devices, sent_on(): far = lax.ppermute(far, 'gz', far_pairs)  3.9 us
    ppermute x1, starting transfers between devices, shifted_on(): below = lax.ppermute(up, 'gz', up_pairs)  3.08 us
    pallas_call x9, Pallas kernels, call(): pl.pallas_call(kernel, name=name, out_shape=out_shapes, in_specs=[pl.Bloc...  2.92 us
    ppermute x1, starting transfers between devices, shifted_on(): above = lax.ppermute(down, 'gz', down_pairs)  2.09 us
    ppermute x1, starting transfers between devices, shifted_on(): outer = lax.ppermute(outer, 'gz', outer_pairs)  1.61 us
    ppermute x2, starting transfers between devices, sent_on(): inner = lax.ppermute(inner, 'gz', inner_pairs)  1.57 us
    ppermute x2, starting transfers between devices, sent_on(): outer = lax.ppermute(outer, 'gz', outer_pairs)  1.36 us
  transfers between devices with their start and end apart: 12, of which 6 were waited for; matrix products, arithmetic and copies ran while one was open for 0% of the time, Pallas kernels for 3%

profile of v22, /device:TPU:0, one launch (start us, length us, event | category | flops | bytes accessed | tf_op | source)
XLA Modules:
  0.0 26.8 jit_solution(9717303089786432346)
XLA Ops:
  0.0 1.1 %begin.1 = (f32[4,2,3,8,128]{4,3,2,1,0:T(8,128)S(1)}, f32[4,2,3,8,128]{4,3,2,1,0:T(8,128)S(1)}, f32[1,2,3,8,128]{4,3,2,1,0:T(8,128)S(1)}, f32[1,2,3,8,128]{4,3,2,1,0:T(8,128)S(1)}) custom-call(f32[4,2,3,8,128]{4,3,2,1,0:T(8,128)} %adjoint_hbm.1, f32[864,128]{1,0:T(8,128)} %bitcast.3), custom_call_target="tpu_custom_call" | custom-call | flops 368640 | bytes 368640 | tf_op jit(solution)/shard_map/begin/pallas_call | solution.py:228
  1.1 3.1 %collective-permute-start = (f32[4,2,3,8,128]{4,3,2,1,0:T(8,128)S(1)}, f32[4,2,3,8,128]{4,3,2,1,0:T(8,128)S(1)}, u32[]{:S(2)}, u32[]{:S(2)}) collective-permute-start(f32[4,2,3,8,128]{4,3,2,1,0:T(8,128)S(1)} %get-tuple-element.23), channel_id=1, source_target_pairs={{0,8},{1,9},{2,10},{3,11},{4,12},{5,13},{6,14},{7,15},{8,16},{9,17... | collective-permute-start | bytes 294920 | tf_op jit(solution)/shard_map/ppermute | solution.py:271
  4.2 2.1 %collective-permute-start.1 = (f32[4,2,3,8,128]{4,3,2,1,0:T(8,128)S(1)}, f32[4,2,3,8,128]{4,3,2,1,0:T(8,128)S(1)}, u32[]{:S(2)}, u32[]{:S(2)}) collective-permute-start(f32[4,2,3,8,128]{4,3,2,1,0:T(8,128)S(1)} %get-tuple-element.24), channel_id=1, source_target_pairs={{0,24},{1,25},{2,26},{3,27},{4,28},{5,29},{6,30},{7,31},{8,0},{9,1... | collective-permute-start | bytes 294920 | tf_op jit(solution)/shard_map/ppermute | solution.py:272
  6.2 1.6 %collective-permute-start.2 = (f32[1,2,3,8,128]{4,3,2,1,0:T(8,128)S(1)}, f32[1,2,3,8,128]{4,3,2,1,0:T(8,128)S(1)}, u32[]{:S(2)}, u32[]{:S(2)}) collective-permute-start(f32[1,2,3,8,128]{4,3,2,1,0:T(8,128)S(1)} %get-tuple-element.25), channel_id=1, source_target_pairs={{0,7},{1,2},{2,1},{3,4},{4,3},{5,6},{6,5},{7,0},{8,15},{9,10},{10,... | collective-permute-start | bytes 73736 | tf_op jit(solution)/shard_map/ppermute | solution.py:273
  7.9 0.2 collective-permute-start.3
  9.4 0.3 %start.1 = (f32[4,2,3,8,128]{4,3,2,1,0:T(8,128)S(1)}, f32[4,2,3,8,128]{4,3,2,1,0:T(8,128)S(1)}) custom-call(f32[6,8,128]{2,1,0:T(8,128)S(1)} %tapers.1.coefs_ref, f32[4,2,3,8,128]{4,3,2,1,0:T(8,128)S(1)} %copy-done.1, f32[864,128]{1,0:T(8,128)S(1)} %bitcast.4), custom_call_target="tpu_custom_call" | custom-call | flops 1622016 | bytes 1622016 | tf_op jit(solution)/shard_map/start/pallas_call | solution.py:228
  9.6 0.8 %collective-permute-done.2.refs_3_ = f32[1,2,3,8,128]{4,3,2,1,0:T(8,128)S(1)} collective-permute-done((f32[1,2,3,8,128]{4,3,2,1,0:T(8,128)S(1)}, f32[1,2,3,8,128]{4,3,2,1,0:T(8,128)S(1)}, u32[]{:S(2)}, u32[]{:S(2)}) %collective-permute-start.2) | collective-permute-done | bytes 24608 | tf_op jit(solution)/shard_map/ppermute | solution.py:273
  10.4 0.1 collective-permute-done.1.refs_2_
  10.5 0.1 third.1
  10.7 1.2 %collective-permute-start.4 = (f32[4,2,3,8,128]{4,3,2,1,0:T(8,128)S(1)}, f32[4,2,3,8,128]{4,3,2,1,0:T(8,128)S(1)}, u32[]{:S(2)}, u32[]{:S(2)}) collective-permute-start(f32[4,2,3,8,128]{4,3,2,1,0:T(8,128)S(1)} %get-tuple-element.28), channel_id=1, source_target_pairs={{0,8},{1,9},{2,10},{3,11},{4,12},{5,13},{6,14},{7,15},{8,0},{9,1},... | collective-permute-start | bytes 294920 | tf_op jit(solution)/shard_map/ppermute | solution.py:264
  11.8 1.7 %collective-permute-start.5 = (f32[4,2,3,8,128]{4,3,2,1,0:T(8,128)S(1)}, f32[4,2,3,8,128]{4,3,2,1,0:T(8,128)S(1)}, u32[]{:S(2)}, u32[]{:S(2)}) collective-permute-start(f32[4,2,3,8,128]{4,3,2,1,0:T(8,128)S(1)} %get-tuple-element.29), channel_id=1, source_target_pairs={{0,24},{1,25},{2,26},{3,27},{4,28},{5,29},{6,30},{7,31},{8,16},{9,... | collective-permute-start | bytes 294920 | tf_op jit(solution)/shard_map/ppermute | solution.py:265
  13.6 0.6 %collective-permute-start.6 = (f32[1,2,3,8,128]{4,3,2,1,0:T(8,128)S(1)}, f32[1,2,3,8,128]{4,3,2,1,0:T(8,128)S(1)}, u32[]{:S(2)}, u32[]{:S(2)}) collective-permute-start(f32[1,2,3,8,128]{4,3,2,1,0:T(8,128)S(1)} %get-tuple-element.30), channel_id=1, source_target_pairs={{0,7},{1,2},{2,1},{3,4},{4,3},{5,6},{6,5},{7,0},{8,15},{9,10},{10,... | collective-permute-start | bytes 73736 | tf_op jit(solution)/shard_map/ppermute | solution.py:266
  14.2 0.8 %collective-permute-start.7 = (f32[1,2,3,8,128]{4,3,2,1,0:T(8,128)S(1)}, f32[1,2,3,8,128]{4,3,2,1,0:T(8,128)S(1)}, u32[]{:S(2)}, u32[]{:S(2)}) collective-permute-start(f32[1,2,3,8,128]{4,3,2,1,0:T(8,128)S(1)} %get-tuple-element.31), channel_id=1, source_target_pairs={{0,1},{1,0},{2,3},{3,2},{4,5},{5,4},{6,7},{7,6},{8,9},{9,8},{10,11... | collective-permute-start | bytes 73736 | tf_op jit(solution)/shard_map/ppermute | solution.py:267
  15.6 0.3 %local_1.1.refs_0_ = f32[4,2,3,8,128]{4,3,2,1,0:T(8,128)S(1)} custom-call(f32[4,2,3,8,128]{4,3,2,1,0:T(8,128)S(1)} %get-tuple-element.27.field_ref.refs_6_, f32[864,128]{1,0:T(8,128)S(1)} %bitcast.6), custom_call_target="tpu_custom_call" | custom-call | flops 1622016 | bytes 1622016 | tf_op jit(solution)/shard_map/local_1/pallas_call | solution.py:228
  15.9 2.0 %collective-permute-done.6.refs_3_ = f32[1,2,3,8,128]{4,3,2,1,0:T(8,128)S(1)} collective-permute-done((f32[1,2,3,8,128]{4,3,2,1,0:T(8,128)S(1)}, f32[1,2,3,8,128]{4,3,2,1,0:T(8,128)S(1)}, u32[]{:S(2)}, u32[]{:S(2)}) %collective-permute-start.6) | collective-permute-done | bytes 24608 | tf_op jit(solution)/shard_map/ppermute | solution.py:266
  17.8 0.5 %collective-permute-done.5.refs_2_ = f32[4,2,3,8,128]{4,3,2,1,0:T(8,128)S(1)} collective-permute-done((f32[4,2,3,8,128]{4,3,2,1,0:T(8,128)S(1)}, f32[4,2,3,8,128]{4,3,2,1,0:T(8,128)S(1)}, u32[]{:S(2)}, u32[]{:S(2)}) %collective-permute-start.5) | collective-permute-done | bytes 98336 | tf_op jit(solution)/shard_map/ppermute | solution.py:265
  18.3 0.2 second.1
  18.5 2.2 %collective-permute-start.8 = (f32[4,2,3,8,128]{4,3,2,1,0:T(8,128)S(1)}, f32[4,2,3,8,128]{4,3,2,1,0:T(8,128)S(1)}, u32[]{:S(2)}, u32[]{:S(2)}) collective-permute-start(f32[4,2,3,8,128]{4,3,2,1,0:T(8,128)S(1)} %get-tuple-element.34), channel_id=1, source_target_pairs={{0,24},{1,25},{2,26},{3,27},{4,28},{5,29},{6,30},{7,31},{8,16},{9,... | collective-permute-start | bytes 294920 | tf_op jit(solution)/shard_map/ppermute | solution.py:265
  20.7 0.7 %collective-permute-start.10 = (f32[1,2,3,8,128]{4,3,2,1,0:T(8,128)S(1)}, f32[1,2,3,8,128]{4,3,2,1,0:T(8,128)S(1)}, u32[]{:S(2)}, u32[]{:S(2)}) collective-permute-start(f32[1,2,3,8,128]{4,3,2,1,0:T(8,128)S(1)} %get-tuple-element.36), channel_id=1, source_target_pairs={{0,7},{1,2},{2,1},{3,4},{4,3},{5,6},{6,5},{7,0},{8,15},{9,10},{10,... | collective-permute-start | bytes 73736 | tf_op jit(solution)/shard_map/ppermute | solution.py:266
  21.4 0.8 %collective-permute-start.11 = (f32[1,2,3,8,128]{4,3,2,1,0:T(8,128)S(1)}, f32[1,2,3,8,128]{4,3,2,1,0:T(8,128)S(1)}, u32[]{:S(2)}, u32[]{:S(2)}) collective-permute-start(f32[1,2,3,8,128]{4,3,2,1,0:T(8,128)S(1)} %get-tuple-element.37), channel_id=1, source_target_pairs={{0,1},{1,0},{2,3},{3,2},{4,5},{5,4},{6,7},{7,6},{8,9},{9,8},{10,11... | collective-permute-start | bytes 73736 | tf_op jit(solution)/shard_map/ppermute | solution.py:267
  22.3 0.3 local_0.1.refs_0_
  22.5 2.5 %collective-permute-done.10.refs_3_ = f32[1,2,3,8,128]{4,3,2,1,0:T(8,128)S(1)} collective-permute-done((f32[1,2,3,8,128]{4,3,2,1,0:T(8,128)S(1)}, f32[1,2,3,8,128]{4,3,2,1,0:T(8,128)S(1)}, u32[]{:S(2)}, u32[]{:S(2)}) %collective-permute-start.10) | collective-permute-done | bytes 24608 | tf_op jit(solution)/shard_map/ppermute | solution.py:266
  25.1 1.0 %collective-permute-done.9.refs_2_ = f32[4,2,3,8,128]{4,3,2,1,0:T(8,128)S(1)} collective-permute-done((f32[4,2,3,8,128]{4,3,2,1,0:T(8,128)S(1)}, f32[4,2,3,8,128]{4,3,2,1,0:T(8,128)S(1)}, u32[]{:S(2)}, u32[]{:S(2)}) %collective-permute-start.9) | collective-permute-done | bytes 98336 | tf_op jit(solution)/shard_map/ppermute | solution.py:264
  26.0 0.7 %last.1 = f32[4,2,3,8,128]{4,3,2,1,0:T(8,128)} custom-call(f32[8,128]{1,0:T(8,128)S(1)} %eps.1.eps_ref, f32[6,8,128]{2,1,0:T(8,128)S(1)} %tapers.1.coefs_ref, f32[864,128]{1,0:T(8,128)S(1)} %bitcast.9, f32[4,2,3,8,128]{4,3,2,1,0:T(8,128)S(1)} %local_0.1.refs_0_, f32[4,2,3,8,128]{4,3,2,1,0:T(8,128)S(1)} %collective-permute-done.8.refs_1_, ...), custom_call_target="tpu_custom_call" | custom-call | flops 368640 | bytes 368640 | tf_op jit(solution)/shard_map/last/pallas_call | solution.py:228
  (13 shorter events, 0.1 us)
Async XLA Ops:
  0.0 9.3 %copy-start = (f32[4,3,4,2,3,3,128]{6,3,5,4,2,1,0:T(2,128)S(1)}, f32[4,3,4,2,3,3,128]{6,3,5,4,2,1,0:T(2,128)}, u32[]{:S(2)}) copy-start(f32[4,3,4,2,3,3,128]{6,3,5,4,2,1,0:T(2,128)} %param.6) | copy-start | bytes 1327108
  0.0 9.3 %copy-start.1 = (f32[4,2,3,8,128]{4,3,2,1,0:T(8,128)S(1)}, f32[4,2,3,8,128]{4,3,2,1,0:T(8,128)}, u32[]{:S(2)}) copy-start(f32[4,2,3,8,128]{4,3,2,1,0:T(8,128)} %adjoint_hbm.1) | copy-start | bytes 294916
  1.1 9.3 %collective-permute-start = (f32[4,2,3,8,128]{4,3,2,1,0:T(8,128)S(1)}, f32[4,2,3,8,128]{4,3,2,1,0:T(8,128)S(1)}, u32[]{:S(2)}, u32[]{:S(2)}) collective-permute-start(f32[4,2,3,8,128]{4,3,2,1,0:T(8,128)S(1)} %get-tuple-element.23), channel_id=1, source_target_pairs={{0,8},{1,9},{2,10},{3,11},{4,12},{5,13},{6,14},{7,15},{8,16},{9,17... | collective-permute-start | bytes 294920 | tf_op jit(solution)/shard_map/ppermute | solution.py:271
  4.2 6.4 %collective-permute-start.1 = (f32[4,2,3,8,128]{4,3,2,1,0:T(8,128)S(1)}, f32[4,2,3,8,128]{4,3,2,1,0:T(8,128)S(1)}, u32[]{:S(2)}, u32[]{:S(2)}) collective-permute-start(f32[4,2,3,8,128]{4,3,2,1,0:T(8,128)S(1)} %get-tuple-element.24), channel_id=1, source_target_pairs={{0,24},{1,25},{2,26},{3,27},{4,28},{5,29},{6,30},{7,31},{8,0},{9,1... | collective-permute-start | bytes 294920 | tf_op jit(solution)/shard_map/ppermute | solution.py:272
  6.2 4.2 %collective-permute-start.2 = (f32[1,2,3,8,128]{4,3,2,1,0:T(8,128)S(1)}, f32[1,2,3,8,128]{4,3,2,1,0:T(8,128)S(1)}, u32[]{:S(2)}, u32[]{:S(2)}) collective-permute-start(f32[1,2,3,8,128]{4,3,2,1,0:T(8,128)S(1)} %get-tuple-element.25), channel_id=1, source_target_pairs={{0,7},{1,2},{2,1},{3,4},{4,3},{5,6},{6,5},{7,0},{8,15},{9,10},{10,... | collective-permute-start | bytes 73736 | tf_op jit(solution)/shard_map/ppermute | solution.py:273
  7.9 2.6 %collective-permute-start.3 = (f32[1,2,3,8,128]{4,3,2,1,0:T(8,128)S(1)}, f32[1,2,3,8,128]{4,3,2,1,0:T(8,128)S(1)}, u32[]{:S(2)}, u32[]{:S(2)}) collective-permute-start(f32[1,2,3,8,128]{4,3,2,1,0:T(8,128)S(1)} %get-tuple-element.26), channel_id=1, source_target_pairs={{0,1},{1,0},{2,3},{3,2},{4,5},{5,4},{6,7},{7,6},{8,9},{9,8},{10,11... | collective-permute-start | bytes 73736 | tf_op jit(solution)/shard_map/ppermute | solution.py:274
  10.7 7.2 %collective-permute-start.4 = (f32[4,2,3,8,128]{4,3,2,1,0:T(8,128)S(1)}, f32[4,2,3,8,128]{4,3,2,1,0:T(8,128)S(1)}, u32[]{:S(2)}, u32[]{:S(2)}) collective-permute-start(f32[4,2,3,8,128]{4,3,2,1,0:T(8,128)S(1)} %get-tuple-element.28), channel_id=1, source_target_pairs={{0,8},{1,9},{2,10},{3,11},{4,12},{5,13},{6,14},{7,15},{8,0},{9,1},... | collective-permute-start | bytes 294920 | tf_op jit(solution)/shard_map/ppermute | solution.py:264
  11.8 6.5 %collective-permute-start.5 = (f32[4,2,3,8,128]{4,3,2,1,0:T(8,128)S(1)}, f32[4,2,3,8,128]{4,3,2,1,0:T(8,128)S(1)}, u32[]{:S(2)}, u32[]{:S(2)}) collective-permute-start(f32[4,2,3,8,128]{4,3,2,1,0:T(8,128)S(1)} %get-tuple-element.29), channel_id=1, source_target_pairs={{0,24},{1,25},{2,26},{3,27},{4,28},{5,29},{6,30},{7,31},{8,16},{9,... | collective-permute-start | bytes 294920 | tf_op jit(solution)/shard_map/ppermute | solution.py:265
  13.6 4.3 %collective-permute-start.6 = (f32[1,2,3,8,128]{4,3,2,1,0:T(8,128)S(1)}, f32[1,2,3,8,128]{4,3,2,1,0:T(8,128)S(1)}, u32[]{:S(2)}, u32[]{:S(2)}) collective-permute-start(f32[1,2,3,8,128]{4,3,2,1,0:T(8,128)S(1)} %get-tuple-element.30), channel_id=1, source_target_pairs={{0,7},{1,2},{2,1},{3,4},{4,3},{5,6},{6,5},{7,0},{8,15},{9,10},{10,... | collective-permute-start | bytes 73736 | tf_op jit(solution)/shard_map/ppermute | solution.py:266
  14.2 3.7 %collective-permute-start.7 = (f32[1,2,3,8,128]{4,3,2,1,0:T(8,128)S(1)}, f32[1,2,3,8,128]{4,3,2,1,0:T(8,128)S(1)}, u32[]{:S(2)}, u32[]{:S(2)}) collective-permute-start(f32[1,2,3,8,128]{4,3,2,1,0:T(8,128)S(1)} %get-tuple-element.31), channel_id=1, source_target_pairs={{0,1},{1,0},{2,3},{3,2},{4,5},{5,4},{6,7},{7,6},{8,9},{9,8},{10,11... | collective-permute-start | bytes 73736 | tf_op jit(solution)/shard_map/ppermute | solution.py:267
  18.5 6.6 %collective-permute-start.8 = (f32[4,2,3,8,128]{4,3,2,1,0:T(8,128)S(1)}, f32[4,2,3,8,128]{4,3,2,1,0:T(8,128)S(1)}, u32[]{:S(2)}, u32[]{:S(2)}) collective-permute-start(f32[4,2,3,8,128]{4,3,2,1,0:T(8,128)S(1)} %get-tuple-element.34), channel_id=1, source_target_pairs={{0,24},{1,25},{2,26},{3,27},{4,28},{5,29},{6,30},{7,31},{8,16},{9,... | collective-permute-start | bytes 294920 | tf_op jit(solution)/shard_map/ppermute | solution.py:265
  20.7 5.3 %collective-permute-start.9 = (f32[4,2,3,8,128]{4,3,2,1,0:T(8,128)S(1)}, f32[4,2,3,8,128]{4,3,2,1,0:T(8,128)S(1)}, u32[]{:S(2)}, u32[]{:S(2)}) collective-permute-start(f32[4,2,3,8,128]{4,3,2,1,0:T(8,128)S(1)} %get-tuple-element.35), channel_id=1, source_target_pairs={{0,8},{1,9},{2,10},{3,11},{4,12},{5,13},{6,14},{7,15},{8,0},{9,1},... | collective-permute-start | bytes 294920 | tf_op jit(solution)/shard_map/ppermute | solution.py:264
  20.7 4.4 %collective-permute-start.10 = (f32[1,2,3,8,128]{4,3,2,1,0:T(8,128)S(1)}, f32[1,2,3,8,128]{4,3,2,1,0:T(8,128)S(1)}, u32[]{:S(2)}, u32[]{:S(2)}) collective-permute-start(f32[1,2,3,8,128]{4,3,2,1,0:T(8,128)S(1)} %get-tuple-element.36), channel_id=1, source_target_pairs={{0,7},{1,2},{2,1},{3,4},{4,3},{5,6},{6,5},{7,0},{8,15},{9,10},{10,... | collective-permute-start | bytes 73736 | tf_op jit(solution)/shard_map/ppermute | solution.py:266
  21.4 3.6 %collective-permute-start.11 = (f32[1,2,3,8,128]{4,3,2,1,0:T(8,128)S(1)}, f32[1,2,3,8,128]{4,3,2,1,0:T(8,128)S(1)}, u32[]{:S(2)}, u32[]{:S(2)}) collective-permute-start(f32[1,2,3,8,128]{4,3,2,1,0:T(8,128)S(1)} %get-tuple-element.37), channel_id=1, source_target_pairs={{0,1},{1,0},{2,3},{3,2},{4,5},{5,4},{6,7},{7,6},{8,9},{9,8},{10,11... | collective-permute-start | bytes 73736 | tf_op jit(solution)/shard_map/ppermute | solution.py:267

commit v23 on v22

--- a/solution.py
+++ b/solution.py
@@ -160,6 +160,7 @@
     _, first_pos, odd_plane, odd_block = place(rows)
     one, two = load_field(one_ref, row), load_field(two_ref, row)
     if coefs_ref is not None:
+        outer_ref, inner_ref = inner_ref, outer_ref
         below, above = (combine(lambda v: coefs_ref[row + 1] * v, f) for f in (one, two))
     else:
         below = combine(lambda near, far: jnp.where(odd_plane, near, far), one, two)
@@ -272,7 +273,7 @@
         above = lax.ppermute(down, "gz", down_pairs)
         outer = lax.ppermute(outer, "gz", outer_pairs)
         inner = lax.ppermute(inner, "gz", inner_pairs)
-        return below, above, outer, inner
+        return below, above, inner, outer
 
     def local(link_set, field):
         return call(functools.partial(local_kernel, rows, link_set), f"local_{link_set}", (field, links), whole, 22)

time: 26.9 us -> 26.9 us (level)
  waiting for transfers between devices: 6.82 us -> 5.49 us
  starting transfers between devices: 15 us -> 16.3 us
    ppermute x2, starting transfers between devices: 1.36 us -> 2.55 us  [sent_on(): outer = lax.ppermute(outer, 'gz', outer_pairs)]
    ppermute x1, starting transfers between devices: 1.61 us -> 2.72 us  [shifted_on(): outer = lax.ppermute(outer, 'gz', outer_pairs)]
    ppermute x1, waiting for transfers between devices: 0.77 us -> 0.01 us  [shifted_on(): outer = lax.ppermute(outer, 'gz', outer_pairs)]
    ppermute x2, starting transfers between devices: 1.57 us -> 0.86 us  [sent_on(): inner = lax.ppermute(inner, 'gz', inner_pairs)]
    ppermute x2, waiting for transfers between devices: 4.5 us -> 3.82 us  [sent_on(): outer = lax.ppermute(outer, 'gz', outer_pairs)]
  transfers between devices with their start and end apart: 12 -> 12, of which waited for: 6 -> 5; matrix products, arithmetic and copies ran while one was open for 0% -> 0% of each run, Pallas kernels for 3% -> 3%
where the time goes in v23:
time: 26.9 us; the launch traced here: 26.8 us
  starting transfers between devices  16.3 us (61%)
  waiting for transfers between devices  5.49 us (20%)
  Pallas kernels  2.93 us (11%)
  between operations  2.05 us (8%)
    ppermute x2, starting transfers between devices, sent_on(): far = lax.ppermute(far, 'gz', far_pairs)  3.85 us
    ppermute x2, waiting for transfers between devices, sent_on(): outer = lax.ppermute(outer, 'gz', outer_pairs)  3.82 us
    ppermute x1, starting transfers between devices, shifted_on(): below = lax.ppermute(up, 'gz', up_pairs)  3.08 us
    pallas_call x9, Pallas kernels, call(): pl.pallas_call(kernel, name=name, out_shape=out_shapes, in_specs=[pl.Bloc...  2.93 us
    ppermute x1, starting transfers between devices, shifted_on(): outer = lax.ppermute(outer, 'gz', outer_pairs)  2.72 us
    ppermute x2, starting transfers between devices, sent_on(): outer = lax.ppermute(outer, 'gz', outer_pairs)  2.55 us
    ppermute x1, starting transfers between devices, shifted_on(): above = lax.ppermute(down, 'gz', down_pairs)  2.09 us
    ppermute x2, starting transfers between devices, sent_on(): near = lax.ppermute(near, 'gz', near_pairs)  1.14 us
  transfers between devices with their start and end apart: 12, of which 5 were waited for; matrix products, arithmetic and copies ran while one was open for 0% of the time, Pallas kernels for 3%

profile of v23, /device:TPU:0, one launch (start us, length us, event | category | flops | bytes accessed | tf_op | source)
XLA Modules:
  0.0 26.8 jit_solution(12689579256163852126)
XLA Ops:
  0.0 1.1 %begin.1 = (f32[4,2,3,8,128]{4,3,2,1,0:T(8,128)S(1)}, f32[4,2,3,8,128]{4,3,2,1,0:T(8,128)S(1)}, f32[1,2,3,8,128]{4,3,2,1,0:T(8,128)S(1)}, f32[1,2,3,8,128]{4,3,2,1,0:T(8,128)S(1)}) custom-call(f32[4,2,3,8,128]{4,3,2,1,0:T(8,128)} %adjoint_hbm.1, f32[864,128]{1,0:T(8,128)} %bitcast.3), custom_call_target="tpu_custom_call" | custom-call | flops 368640 | bytes 368640 | tf_op jit(solution)/shard_map/begin/pallas_call | solution.py:229
  1.1 3.1 %collective-permute-start = (f32[4,2,3,8,128]{4,3,2,1,0:T(8,128)S(1)}, f32[4,2,3,8,128]{4,3,2,1,0:T(8,128)S(1)}, u32[]{:S(2)}, u32[]{:S(2)}) collective-permute-start(f32[4,2,3,8,128]{4,3,2,1,0:T(8,128)S(1)} %get-tuple-element.23), channel_id=1, source_target_pairs={{0,8},{1,9},{2,10},{3,11},{4,12},{5,13},{6,14},{7,15},{8,16},{9,17... | collective-permute-start | bytes 294920 | tf_op jit(solution)/shard_map/ppermute | solution.py:272
  4.2 2.1 %collective-permute-start.1 = (f32[4,2,3,8,128]{4,3,2,1,0:T(8,128)S(1)}, f32[4,2,3,8,128]{4,3,2,1,0:T(8,128)S(1)}, u32[]{:S(2)}, u32[]{:S(2)}) collective-permute-start(f32[4,2,3,8,128]{4,3,2,1,0:T(8,128)S(1)} %get-tuple-element.24), channel_id=1, source_target_pairs={{0,24},{1,25},{2,26},{3,27},{4,28},{5,29},{6,30},{7,31},{8,0},{9,1... | collective-permute-start | bytes 294920 | tf_op jit(solution)/shard_map/ppermute | solution.py:273
  6.2 2.7 %collective-permute-start.3 = (f32[1,2,3,8,128]{4,3,2,1,0:T(8,128)S(1)}, f32[1,2,3,8,128]{4,3,2,1,0:T(8,128)S(1)}, u32[]{:S(2)}, u32[]{:S(2)}) collective-permute-start(f32[1,2,3,8,128]{4,3,2,1,0:T(8,128)S(1)} %get-tuple-element.26), channel_id=1, source_target_pairs={{0,7},{1,2},{2,1},{3,4},{4,3},{5,6},{6,5},{7,0},{8,15},{9,10},{10,... | collective-permute-start | bytes 73736 | tf_op jit(solution)/shard_map/ppermute | solution.py:274
  10.3 0.3 %start.1 = (f32[4,2,3,8,128]{4,3,2,1,0:T(8,128)S(1)}, f32[4,2,3,8,128]{4,3,2,1,0:T(8,128)S(1)}) custom-call(f32[6,8,128]{2,1,0:T(8,128)S(1)} %tapers.1.coefs_ref, f32[4,2,3,8,128]{4,3,2,1,0:T(8,128)S(1)} %copy-done.1, f32[864,128]{1,0:T(8,128)S(1)} %bitcast.4), custom_call_target="tpu_custom_call" | custom-call | flops 1622016 | bytes 1622016 | tf_op jit(solution)/shard_map/start/pallas_call | solution.py:229
  10.6 0.0 collective-permute-done.refs_1_
  10.6 0.1 third.1
  10.8 1.1 %collective-permute-start.4 = (f32[4,2,3,8,128]{4,3,2,1,0:T(8,128)S(1)}, f32[4,2,3,8,128]{4,3,2,1,0:T(8,128)S(1)}, u32[]{:S(2)}, u32[]{:S(2)}) collective-permute-start(f32[4,2,3,8,128]{4,3,2,1,0:T(8,128)S(1)} %get-tuple-element.28), channel_id=1, source_target_pairs={{0,8},{1,9},{2,10},{3,11},{4,12},{5,13},{6,14},{7,15},{8,0},{9,1},... | collective-permute-start | bytes 294920 | tf_op jit(solution)/shard_map/ppermute | solution.py:265
  11.8 1.7 %collective-permute-start.5 = (f32[4,2,3,8,128]{4,3,2,1,0:T(8,128)S(1)}, f32[4,2,3,8,128]{4,3,2,1,0:T(8,128)S(1)}, u32[]{:S(2)}, u32[]{:S(2)}) collective-permute-start(f32[4,2,3,8,128]{4,3,2,1,0:T(8,128)S(1)} %get-tuple-element.29), channel_id=1, source_target_pairs={{0,24},{1,25},{2,26},{3,27},{4,28},{5,29},{6,30},{7,31},{8,16},{9,... | collective-permute-start | bytes 294920 | tf_op jit(solution)/shard_map/ppermute | solution.py:266
  13.6 1.5 %collective-permute-start.6 = (f32[1,2,3,8,128]{4,3,2,1,0:T(8,128)S(1)}, f32[1,2,3,8,128]{4,3,2,1,0:T(8,128)S(1)}, u32[]{:S(2)}, u32[]{:S(2)}) collective-permute-start(f32[1,2,3,8,128]{4,3,2,1,0:T(8,128)S(1)} %get-tuple-element.30), channel_id=1, source_target_pairs={{0,7},{1,2},{2,1},{3,4},{4,3},{5,6},{6,5},{7,0},{8,15},{9,10},{10,... | collective-permute-start | bytes 73736 | tf_op jit(solution)/shard_map/ppermute | solution.py:267
  15.0 0.0 collective-permute-start.7
  15.7 0.3 %local_1.1.refs_0_ = f32[4,2,3,8,128]{4,3,2,1,0:T(8,128)S(1)} custom-call(f32[4,2,3,8,128]{4,3,2,1,0:T(8,128)S(1)} %get-tuple-element.27.field_ref.refs_6_, f32[864,128]{1,0:T(8,128)S(1)} %bitcast.6), custom_call_target="tpu_custom_call" | custom-call | flops 1622016 | bytes 1622016 | tf_op jit(solution)/shard_map/local_1/pallas_call | solution.py:229
  16.0 1.9 %collective-permute-done.6.refs_3_ = f32[1,2,3,8,128]{4,3,2,1,0:T(8,128)S(1)} collective-permute-done((f32[1,2,3,8,128]{4,3,2,1,0:T(8,128)S(1)}, f32[1,2,3,8,128]{4,3,2,1,0:T(8,128)S(1)}, u32[]{:S(2)}, u32[]{:S(2)}) %collective-permute-start.6) | collective-permute-done | bytes 24608 | tf_op jit(solution)/shard_map/ppermute | solution.py:267
  17.8 0.5 %collective-permute-done.5.refs_2_ = f32[4,2,3,8,128]{4,3,2,1,0:T(8,128)S(1)} collective-permute-done((f32[4,2,3,8,128]{4,3,2,1,0:T(8,128)S(1)}, f32[4,2,3,8,128]{4,3,2,1,0:T(8,128)S(1)}, u32[]{:S(2)}, u32[]{:S(2)}) %collective-permute-start.5) | collective-permute-done | bytes 98336 | tf_op jit(solution)/shard_map/ppermute | solution.py:266
  18.3 0.2 second.1
  18.5 2.1 %collective-permute-start.8 = (f32[4,2,3,8,128]{4,3,2,1,0:T(8,128)S(1)}, f32[4,2,3,8,128]{4,3,2,1,0:T(8,128)S(1)}, u32[]{:S(2)}, u32[]{:S(2)}) collective-permute-start(f32[4,2,3,8,128]{4,3,2,1,0:T(8,128)S(1)} %get-tuple-element.34), channel_id=1, source_target_pairs={{0,24},{1,25},{2,26},{3,27},{4,28},{5,29},{6,30},{7,31},{8,16},{9,... | collective-permute-start | bytes 294920 | tf_op jit(solution)/shard_map/ppermute | solution.py:266
  20.6 0.1 collective-permute-start.9
  20.7 1.1 %collective-permute-start.10 = (f32[1,2,3,8,128]{4,3,2,1,0:T(8,128)S(1)}, f32[1,2,3,8,128]{4,3,2,1,0:T(8,128)S(1)}, u32[]{:S(2)}, u32[]{:S(2)}) collective-permute-start(f32[1,2,3,8,128]{4,3,2,1,0:T(8,128)S(1)} %get-tuple-element.36), channel_id=1, source_target_pairs={{0,7},{1,2},{2,1},{3,4},{4,3},{5,6},{6,5},{7,0},{8,15},{9,10},{10,... | collective-permute-start | bytes 73736 | tf_op jit(solution)/shard_map/ppermute | solution.py:267
  21.8 0.9 %collective-permute-start.11 = (f32[1,2,3,8,128]{4,3,2,1,0:T(8,128)S(1)}, f32[1,2,3,8,128]{4,3,2,1,0:T(8,128)S(1)}, u32[]{:S(2)}, u32[]{:S(2)}) collective-permute-start(f32[1,2,3,8,128]{4,3,2,1,0:T(8,128)S(1)} %get-tuple-element.37), channel_id=1, source_target_pairs={{0,1},{1,0},{2,3},{3,2},{4,5},{5,4},{6,7},{7,6},{8,9},{9,8},{10,11... | collective-permute-start | bytes 73736 | tf_op jit(solution)/shard_map/ppermute | solution.py:268
  22.6 0.3 local_0.1.refs_0_
  22.9 1.9 %collective-permute-done.10.refs_3_ = f32[1,2,3,8,128]{4,3,2,1,0:T(8,128)S(1)} collective-permute-done((f32[1,2,3,8,128]{4,3,2,1,0:T(8,128)S(1)}, f32[1,2,3,8,128]{4,3,2,1,0:T(8,128)S(1)}, u32[]{:S(2)}, u32[]{:S(2)}) %collective-permute-start.10) | collective-permute-done | bytes 24608 | tf_op jit(solution)/shard_map/ppermute | solution.py:267
  24.8 0.2 collective-permute-done.8.refs_1_
  25.1 1.0 %collective-permute-done.9.refs_2_ = f32[4,2,3,8,128]{4,3,2,1,0:T(8,128)S(1)} collective-permute-done((f32[4,2,3,8,128]{4,3,2,1,0:T(8,128)S(1)}, f32[4,2,3,8,128]{4,3,2,1,0:T(8,128)S(1)}, u32[]{:S(2)}, u32[]{:S(2)}) %collective-permute-start.9) | collective-permute-done | bytes 98336 | tf_op jit(solution)/shard_map/ppermute | solution.py:265
  26.0 0.7 %last.1 = f32[4,2,3,8,128]{4,3,2,1,0:T(8,128)} custom-call(f32[8,128]{1,0:T(8,128)S(1)} %eps.1.eps_ref, f32[6,8,128]{2,1,0:T(8,128)S(1)} %tapers.1.coefs_ref, f32[864,128]{1,0:T(8,128)S(1)} %bitcast.9, f32[4,2,3,8,128]{4,3,2,1,0:T(8,128)S(1)} %local_0.1.refs_0_, f32[4,2,3,8,128]{4,3,2,1,0:T(8,128)S(1)} %collective-permute-done.8.refs_1_, ...), custom_call_target="tpu_custom_call" | custom-call | flops 368640 | bytes 368640 | tf_op jit(solution)/shard_map/last/pallas_call | solution.py:229
  (13 shorter events, 0.1 us)
Async XLA Ops:
  0.0 10.3 %copy-start = (f32[4,3,4,2,3,3,128]{6,3,5,4,2,1,0:T(2,128)S(1)}, f32[4,3,4,2,3,3,128]{6,3,5,4,2,1,0:T(2,128)}, u32[]{:S(2)}) copy-start(f32[4,3,4,2,3,3,128]{6,3,5,4,2,1,0:T(2,128)} %param.6) | copy-start | bytes 1327108
  0.0 10.3 %copy-start.1 = (f32[4,2,3,8,128]{4,3,2,1,0:T(8,128)S(1)}, f32[4,2,3,8,128]{4,3,2,1,0:T(8,128)}, u32[]{:S(2)}) copy-start(f32[4,2,3,8,128]{4,3,2,1,0:T(8,128)} %adjoint_hbm.1) | copy-start | bytes 294916
  1.1 9.5 %collective-permute-start = (f32[4,2,3,8,128]{4,3,2,1,0:T(8,128)S(1)}, f32[4,2,3,8,128]{4,3,2,1,0:T(8,128)S(1)}, u32[]{:S(2)}, u32[]{:S(2)}) collective-permute-start(f32[4,2,3,8,128]{4,3,2,1,0:T(8,128)S(1)} %get-tuple-element.23), channel_id=1, source_target_pairs={{0,8},{1,9},{2,10},{3,11},{4,12},{5,13},{6,14},{7,15},{8,16},{9,17... | collective-permute-start | bytes 294920 | tf_op jit(solution)/shard_map/ppermute | solution.py:272
  4.2 6.5 %collective-permute-start.1 = (f32[4,2,3,8,128]{4,3,2,1,0:T(8,128)S(1)}, f32[4,2,3,8,128]{4,3,2,1,0:T(8,128)S(1)}, u32[]{:S(2)}, u32[]{:S(2)}) collective-permute-start(f32[4,2,3,8,128]{4,3,2,1,0:T(8,128)S(1)} %get-tuple-element.24), channel_id=1, source_target_pairs={{0,24},{1,25},{2,26},{3,27},{4,28},{5,29},{6,30},{7,31},{8,0},{9,1... | collective-permute-start | bytes 294920 | tf_op jit(solution)/shard_map/ppermute | solution.py:273
  6.2 4.3 %collective-permute-start.2 = (f32[1,2,3,8,128]{4,3,2,1,0:T(8,128)S(1)}, f32[1,2,3,8,128]{4,3,2,1,0:T(8,128)S(1)}, u32[]{:S(2)}, u32[]{:S(2)}) collective-permute-start(f32[1,2,3,8,128]{4,3,2,1,0:T(8,128)S(1)} %get-tuple-element.25), channel_id=1, source_target_pairs={{0,1},{1,0},{2,3},{3,2},{4,5},{5,4},{6,7},{7,6},{8,9},{9,8},{10,11... | collective-permute-start | bytes 73736 | tf_op jit(solution)/shard_map/ppermute | solution.py:275
  6.2 4.4 %collective-permute-start.3 = (f32[1,2,3,8,128]{4,3,2,1,0:T(8,128)S(1)}, f32[1,2,3,8,128]{4,3,2,1,0:T(8,128)S(1)}, u32[]{:S(2)}, u32[]{:S(2)}) collective-permute-start(f32[1,2,3,8,128]{4,3,2,1,0:T(8,128)S(1)} %get-tuple-element.26), channel_id=1, source_target_pairs={{0,7},{1,2},{2,1},{3,4},{4,3},{5,6},{6,5},{7,0},{8,15},{9,10},{10,... | collective-permute-start | bytes 73736 | tf_op jit(solution)/shard_map/ppermute | solution.py:274
  10.8 7.1 %collective-permute-start.4 = (f32[4,2,3,8,128]{4,3,2,1,0:T(8,128)S(1)}, f32[4,2,3,8,128]{4,3,2,1,0:T(8,128)S(1)}, u32[]{:S(2)}, u32[]{:S(2)}) collective-permute-start(f32[4,2,3,8,128]{4,3,2,1,0:T(8,128)S(1)} %get-tuple-element.28), channel_id=1, source_target_pairs={{0,8},{1,9},{2,10},{3,11},{4,12},{5,13},{6,14},{7,15},{8,0},{9,1},... | collective-permute-start | bytes 294920 | tf_op jit(solution)/shard_map/ppermute | solution.py:265
  11.8 6.5 %collective-permute-start.5 = (f32[4,2,3,8,128]{4,3,2,1,0:T(8,128)S(1)}, f32[4,2,3,8,128]{4,3,2,1,0:T(8,128)S(1)}, u32[]{:S(2)}, u32[]{:S(2)}) collective-permute-start(f32[4,2,3,8,128]{4,3,2,1,0:T(8,128)S(1)} %get-tuple-element.29), channel_id=1, source_target_pairs={{0,24},{1,25},{2,26},{3,27},{4,28},{5,29},{6,30},{7,31},{8,16},{9,... | collective-permute-start | bytes 294920 | tf_op jit(solution)/shard_map/ppermute | solution.py:266
  13.6 4.3 %collective-permute-start.6 = (f32[1,2,3,8,128]{4,3,2,1,0:T(8,128)S(1)}, f32[1,2,3,8,128]{4,3,2,1,0:T(8,128)S(1)}, u32[]{:S(2)}, u32[]{:S(2)}) collective-permute-start(f32[1,2,3,8,128]{4,3,2,1,0:T(8,128)S(1)} %get-tuple-element.30), channel_id=1, source_target_pairs={{0,7},{1,2},{2,1},{3,4},{4,3},{5,6},{6,5},{7,0},{8,15},{9,10},{10,... | collective-permute-start | bytes 73736 | tf_op jit(solution)/shard_map/ppermute | solution.py:267
  15.0 2.8 %collective-permute-start.7 = (f32[1,2,3,8,128]{4,3,2,1,0:T(8,128)S(1)}, f32[1,2,3,8,128]{4,3,2,1,0:T(8,128)S(1)}, u32[]{:S(2)}, u32[]{:S(2)}) collective-permute-start(f32[1,2,3,8,128]{4,3,2,1,0:T(8,128)S(1)} %get-tuple-element.31), channel_id=1, source_target_pairs={{0,1},{1,0},{2,3},{3,2},{4,5},{5,4},{6,7},{7,6},{8,9},{9,8},{10,11... | collective-permute-start | bytes 73736 | tf_op jit(solution)/shard_map/ppermute | solution.py:268
  18.5 6.6 %collective-permute-start.8 = (f32[4,2,3,8,128]{4,3,2,1,0:T(8,128)S(1)}, f32[4,2,3,8,128]{4,3,2,1,0:T(8,128)S(1)}, u32[]{:S(2)}, u32[]{:S(2)}) collective-permute-start(f32[4,2,3,8,128]{4,3,2,1,0:T(8,128)S(1)} %get-tuple-element.34), channel_id=1, source_target_pairs={{0,24},{1,25},{2,26},{3,27},{4,28},{5,29},{6,30},{7,31},{8,16},{9,... | collective-permute-start | bytes 294920 | tf_op jit(solution)/shard_map/ppermute | solution.py:266
  20.6 5.4 %collective-permute-start.9 = (f32[4,2,3,8,128]{4,3,2,1,0:T(8,128)S(1)}, f32[4,2,3,8,128]{4,3,2,1,0:T(8,128)S(1)}, u32[]{:S(2)}, u32[]{:S(2)}) collective-permute-start(f32[4,2,3,8,128]{4,3,2,1,0:T(8,128)S(1)} %get-tuple-element.35), channel_id=1, source_target_pairs={{0,8},{1,9},{2,10},{3,11},{4,12},{5,13},{6,14},{7,15},{8,0},{9,1},... | collective-permute-start | bytes 294920 | tf_op jit(solution)/shard_map/ppermute | solution.py:265
  20.7 4.2 %collective-permute-start.10 = (f32[1,2,3,8,128]{4,3,2,1,0:T(8,128)S(1)}, f32[1,2,3,8,128]{4,3,2,1,0:T(8,128)S(1)}, u32[]{:S(2)}, u32[]{:S(2)}) collective-permute-start(f32[1,2,3,8,128]{4,3,2,1,0:T(8,128)S(1)} %get-tuple-element.36), channel_id=1, source_target_pairs={{0,7},{1,2},{2,1},{3,4},{4,3},{5,6},{6,5},{7,0},{8,15},{9,10},{10,... | collective-permute-start | bytes 73736 | tf_op jit(solution)/shard_map/ppermute | solution.py:267
  21.8 3.1 %collective-permute-start.11 = (f32[1,2,3,8,128]{4,3,2,1,0:T(8,128)S(1)}, f32[1,2,3,8,128]{4,3,2,1,0:T(8,128)S(1)}, u32[]{:S(2)}, u32[]{:S(2)}) collective-permute-start(f32[1,2,3,8,128]{4,3,2,1,0:T(8,128)S(1)} %get-tuple-element.37), channel_id=1, source_target_pairs={{0,1},{1,0},{2,3},{3,2},{4,5},{5,4},{6,7},{7,6},{8,9},{9,8},{10,11... | collective-permute-start | bytes 73736 | tf_op jit(solution)/shard_map/ppermute | solution.py:268

commit v24 on v20

--- a/solution.py
+++ b/solution.py
@@ -155,6 +155,8 @@
 
 def arrived_sum(links_ref, link_set, row, rows, arrivals, coefs_ref=None):
     sum_ref, one_ref, two_ref, outer_ref, inner_ref = arrivals
+    if coefs_ref is None:
+        one_ref, two_ref = two_ref, one_ref
     _, first_pos, odd_plane, odd_block = place(rows)
     one, two = load_field(one_ref, row), load_field(two_ref, row)
     if coefs_ref is not None:
@@ -263,7 +265,7 @@
         far = lax.ppermute(far, "gz", far_pairs)
         outer = lax.ppermute(outer, "gz", outer_pairs)
         inner = lax.ppermute(inner, "gz", inner_pairs)
-        return near, far, outer, inner
+        return far, near, outer, inner
 
     def shifted_on(up, down, outer, inner):
         below = lax.ppermute(up, "gz", up_pairs)

time: 27 us -> 27.1 us (level)
  waiting for transfers between devices: 6.02 us -> 7.32 us
  starting transfers between devices: 15.9 us -> 14.7 us
    ppermute x2, starting transfers between devices: 2.41 us -> 0.01 us  [sent_on(): near = lax.ppermute(near, 'gz', near_pairs)]
    ppermute x2, waiting for transfers between devices: 0.01 us -> 1.6 us  [sent_on(): near = lax.ppermute(near, 'gz', near_pairs)]
    ppermute x2, starting transfers between devices: 3.6 us -> 4.53 us  [sent_on(): far = lax.ppermute(far, 'gz', far_pairs)]
    ppermute x2, starting transfers between devices: 0.62 us -> 0.96 us  [sent_on(): outer = lax.ppermute(outer, 'gz', outer_pairs)]
    ppermute x2, waiting for transfers between devices: 4.5 us -> 4.2 us  [sent_on(): outer = lax.ppermute(outer, 'gz', outer_pairs)]
  transfers between devices with their start and end apart: 12 -> 12, of which waited for: 6 -> 8; matrix products, arithmetic and copies ran while one was open for 0% -> 0% of each run, Pallas kernels for 3% -> 3%
where the time goes in v24:
time: 27.1 us; the launch traced here: 26.9 us
  starting transfers between devices  14.7 us (54%)
  waiting for transfers between devices  7.32 us (27%)
  Pallas kernels  2.92 us (11%)
  between operations  2.02 us (7%)
    ppermute x2, starting transfers between devices, sent_on(): far = lax.ppermute(far, 'gz', far_pairs)  4.53 us
    ppermute x2, waiting for transfers between devices, sent_on(): outer = lax.ppermute(outer, 'gz', outer_pairs)  4.2 us
    ppermute x1, starting transfers between devices, shifted_on(): below = lax.ppermute(up, 'gz', up_pairs)  3.08 us
    pallas_call x9, Pallas kernels, call(): pl.pallas_call(kernel, name=name, out_shape=out_shapes, in_specs=[pl.Bloc...  2.92 us
    ppermute x2, starting transfers between devices, sent_on(): inner = lax.ppermute(inner, 'gz', inner_pairs)  2.26 us
    ppermute x1, starting transfers between devices, shifted_on(): above = lax.ppermute(down, 'gz', down_pairs)  2.09 us
    ppermute x1, starting transfers between devices, shifted_on(): outer = lax.ppermute(outer, 'gz', outer_pairs)  1.61 us
    ppermute x2, waiting for transfers between devices, sent_on(): near = lax.ppermute(near, 'gz', near_pairs)  1.6 us
  transfers between devices with their start and end apart: 12, of which 8 were waited for; matrix products, arithmetic and copies ran while one was open for 0% of the time, Pallas kernels for 3%

profile of v24, /device:TPU:0, one launch (start us, length us, event | category | flops | bytes accessed | tf_op | source)
XLA Modules:
  0.0 26.9 jit_solution(16453018157742089824)
XLA Ops:
  0.0 1.1 %begin.1 = (f32[4,2,3,8,128]{4,3,2,1,0:T(8,128)S(1)}, f32[4,2,3,8,128]{4,3,2,1,0:T(8,128)S(1)}, f32[1,2,3,8,128]{4,3,2,1,0:T(8,128)S(1)}, f32[1,2,3,8,128]{4,3,2,1,0:T(8,128)S(1)}) custom-call(f32[4,2,3,8,128]{4,3,2,1,0:T(8,128)} %adjoint_hbm.1, f32[864,128]{1,0:T(8,128)} %bitcast.3), custom_call_target="tpu_custom_call" | custom-call | flops 368640 | bytes 368640 | tf_op jit(solution)/shard_map/begin/pallas_call | solution.py:228
  1.1 3.1 %collective-permute-start = (f32[4,2,3,8,128]{4,3,2,1,0:T(8,128)S(1)}, f32[4,2,3,8,128]{4,3,2,1,0:T(8,128)S(1)}, u32[]{:S(2)}, u32[]{:S(2)}) collective-permute-start(f32[4,2,3,8,128]{4,3,2,1,0:T(8,128)S(1)} %get-tuple-element.23), channel_id=1, source_target_pairs={{0,8},{1,9},{2,10},{3,11},{4,12},{5,13},{6,14},{7,15},{8,16},{9,17... | collective-permute-start | bytes 294920 | tf_op jit(solution)/shard_map/ppermute | solution.py:271
  4.2 2.1 %collective-permute-start.1 = (f32[4,2,3,8,128]{4,3,2,1,0:T(8,128)S(1)}, f32[4,2,3,8,128]{4,3,2,1,0:T(8,128)S(1)}, u32[]{:S(2)}, u32[]{:S(2)}) collective-permute-start(f32[4,2,3,8,128]{4,3,2,1,0:T(8,128)S(1)} %get-tuple-element.24), channel_id=1, source_target_pairs={{0,24},{1,25},{2,26},{3,27},{4,28},{5,29},{6,30},{7,31},{8,0},{9,1... | collective-permute-start | bytes 294920 | tf_op jit(solution)/shard_map/ppermute | solution.py:272
  6.2 1.6 %collective-permute-start.2 = (f32[1,2,3,8,128]{4,3,2,1,0:T(8,128)S(1)}, f32[1,2,3,8,128]{4,3,2,1,0:T(8,128)S(1)}, u32[]{:S(2)}, u32[]{:S(2)}) collective-permute-start(f32[1,2,3,8,128]{4,3,2,1,0:T(8,128)S(1)} %get-tuple-element.25), channel_id=1, source_target_pairs={{0,7},{1,2},{2,1},{3,4},{4,3},{5,6},{6,5},{7,0},{8,15},{9,10},{10,... | collective-permute-start | bytes 73736 | tf_op jit(solution)/shard_map/ppermute | solution.py:273
  7.9 0.2 collective-permute-start.3
  9.4 0.3 %start.1 = (f32[4,2,3,8,128]{4,3,2,1,0:T(8,128)S(1)}, f32[4,2,3,8,128]{4,3,2,1,0:T(8,128)S(1)}) custom-call(f32[6,8,128]{2,1,0:T(8,128)S(1)} %tapers.1.coefs_ref, f32[4,2,3,8,128]{4,3,2,1,0:T(8,128)S(1)} %copy-done.1, f32[864,128]{1,0:T(8,128)S(1)} %bitcast.4), custom_call_target="tpu_custom_call" | custom-call | flops 1622016 | bytes 1622016 | tf_op jit(solution)/shard_map/start/pallas_call | solution.py:228
  9.6 0.8 %collective-permute-done.2.refs_3_ = f32[1,2,3,8,128]{4,3,2,1,0:T(8,128)S(1)} collective-permute-done((f32[1,2,3,8,128]{4,3,2,1,0:T(8,128)S(1)}, f32[1,2,3,8,128]{4,3,2,1,0:T(8,128)S(1)}, u32[]{:S(2)}, u32[]{:S(2)}) %collective-permute-start.2) | collective-permute-done | bytes 24608 | tf_op jit(solution)/shard_map/ppermute | solution.py:273
  10.5 0.1 third.1
  10.7 2.5 %collective-permute-start.4 = (f32[4,2,3,8,128]{4,3,2,1,0:T(8,128)S(1)}, f32[4,2,3,8,128]{4,3,2,1,0:T(8,128)S(1)}, u32[]{:S(2)}, u32[]{:S(2)}) collective-permute-start(f32[4,2,3,8,128]{4,3,2,1,0:T(8,128)S(1)} %get-tuple-element.28), channel_id=1, source_target_pairs={{0,24},{1,25},{2,26},{3,27},{4,28},{5,29},{6,30},{7,31},{8,16},{9,... | collective-permute-start | bytes 294920 | tf_op jit(solution)/shard_map/ppermute | solution.py:265
  13.1 0.8 %collective-permute-start.6 = (f32[1,2,3,8,128]{4,3,2,1,0:T(8,128)S(1)}, f32[1,2,3,8,128]{4,3,2,1,0:T(8,128)S(1)}, u32[]{:S(2)}, u32[]{:S(2)}) collective-permute-start(f32[1,2,3,8,128]{4,3,2,1,0:T(8,128)S(1)} %get-tuple-element.30), channel_id=1, source_target_pairs={{0,7},{1,2},{2,1},{3,4},{4,3},{5,6},{6,5},{7,0},{8,15},{9,10},{10,... | collective-permute-start | bytes 73736 | tf_op jit(solution)/shard_map/ppermute | solution.py:266
  13.9 0.8 %collective-permute-start.7 = (f32[1,2,3,8,128]{4,3,2,1,0:T(8,128)S(1)}, f32[1,2,3,8,128]{4,3,2,1,0:T(8,128)S(1)}, u32[]{:S(2)}, u32[]{:S(2)}) collective-permute-start(f32[1,2,3,8,128]{4,3,2,1,0:T(8,128)S(1)} %get-tuple-element.31), channel_id=1, source_target_pairs={{0,1},{1,0},{2,3},{3,2},{4,5},{5,4},{6,7},{7,6},{8,9},{9,8},{10,11... | collective-permute-start | bytes 73736 | tf_op jit(solution)/shard_map/ppermute | solution.py:267
  15.4 0.3 %local_1.1.refs_0_ = f32[4,2,3,8,128]{4,3,2,1,0:T(8,128)S(1)} custom-call(f32[4,2,3,8,128]{4,3,2,1,0:T(8,128)S(1)} %get-tuple-element.27.field_ref.refs_6_, f32[864,128]{1,0:T(8,128)S(1)} %bitcast.6), custom_call_target="tpu_custom_call" | custom-call | flops 1622016 | bytes 1622016 | tf_op jit(solution)/shard_map/local_1/pallas_call | solution.py:228
  15.7 1.8 %collective-permute-done.6.refs_3_ = f32[1,2,3,8,128]{4,3,2,1,0:T(8,128)S(1)} collective-permute-done((f32[1,2,3,8,128]{4,3,2,1,0:T(8,128)S(1)}, f32[1,2,3,8,128]{4,3,2,1,0:T(8,128)S(1)}, u32[]{:S(2)}, u32[]{:S(2)}) %collective-permute-start.6) | collective-permute-done | bytes 24608 | tf_op jit(solution)/shard_map/ppermute | solution.py:266
  17.4 0.4 %collective-permute-done.4.refs_1_ = f32[4,2,3,8,128]{4,3,2,1,0:T(8,128)S(1)} collective-permute-done((f32[4,2,3,8,128]{4,3,2,1,0:T(8,128)S(1)}, f32[4,2,3,8,128]{4,3,2,1,0:T(8,128)S(1)}, u32[]{:S(2)}, u32[]{:S(2)}) %collective-permute-start.4) | collective-permute-done | bytes 98336 | tf_op jit(solution)/shard_map/ppermute | solution.py:265
  17.9 0.6 %collective-permute-done.5.refs_2_ = f32[4,2,3,8,128]{4,3,2,1,0:T(8,128)S(1)} collective-permute-done((f32[4,2,3,8,128]{4,3,2,1,0:T(8,128)S(1)}, f32[4,2,3,8,128]{4,3,2,1,0:T(8,128)S(1)}, u32[]{:S(2)}, u32[]{:S(2)}) %collective-permute-start.5) | collective-permute-done | bytes 98336 | tf_op jit(solution)/shard_map/ppermute | solution.py:264
  18.5 0.2 second.1
  18.7 2.1 %collective-permute-start.8 = (f32[4,2,3,8,128]{4,3,2,1,0:T(8,128)S(1)}, f32[4,2,3,8,128]{4,3,2,1,0:T(8,128)S(1)}, u32[]{:S(2)}, u32[]{:S(2)}) collective-permute-start(f32[4,2,3,8,128]{4,3,2,1,0:T(8,128)S(1)} %get-tuple-element.34), channel_id=1, source_target_pairs={{0,24},{1,25},{2,26},{3,27},{4,28},{5,29},{6,30},{7,31},{8,16},{9,... | collective-permute-start | bytes 294920 | tf_op jit(solution)/shard_map/ppermute | solution.py:265
  20.8 0.1 collective-permute-start.10
  20.9 1.5 %collective-permute-start.11 = (f32[1,2,3,8,128]{4,3,2,1,0:T(8,128)S(1)}, f32[1,2,3,8,128]{4,3,2,1,0:T(8,128)S(1)}, u32[]{:S(2)}, u32[]{:S(2)}) collective-permute-start(f32[1,2,3,8,128]{4,3,2,1,0:T(8,128)S(1)} %get-tuple-element.37), channel_id=1, source_target_pairs={{0,1},{1,0},{2,3},{3,2},{4,5},{5,4},{6,7},{7,6},{8,9},{9,8},{10,11... | collective-permute-start | bytes 73736 | tf_op jit(solution)/shard_map/ppermute | solution.py:267
  22.4 0.3 local_0.1.refs_0_
  22.6 2.4 %collective-permute-done.10.refs_3_ = f32[1,2,3,8,128]{4,3,2,1,0:T(8,128)S(1)} collective-permute-done((f32[1,2,3,8,128]{4,3,2,1,0:T(8,128)S(1)}, f32[1,2,3,8,128]{4,3,2,1,0:T(8,128)S(1)}, u32[]{:S(2)}, u32[]{:S(2)}) %collective-permute-start.10) | collective-permute-done | bytes 24608 | tf_op jit(solution)/shard_map/ppermute | solution.py:266
  25.1 0.2 collective-permute-done.8.refs_1_
  25.2 1.0 %collective-permute-done.9.refs_2_ = f32[4,2,3,8,128]{4,3,2,1,0:T(8,128)S(1)} collective-permute-done((f32[4,2,3,8,128]{4,3,2,1,0:T(8,128)S(1)}, f32[4,2,3,8,128]{4,3,2,1,0:T(8,128)S(1)}, u32[]{:S(2)}, u32[]{:S(2)}) %collective-permute-start.9) | collective-permute-done | bytes 98336 | tf_op jit(solution)/shard_map/ppermute | solution.py:264
  26.2 0.7 %last.1 = f32[4,2,3,8,128]{4,3,2,1,0:T(8,128)} custom-call(f32[8,128]{1,0:T(8,128)S(1)} %eps.1.eps_ref, f32[6,8,128]{2,1,0:T(8,128)S(1)} %tapers.1.coefs_ref, f32[864,128]{1,0:T(8,128)S(1)} %bitcast.9, f32[4,2,3,8,128]{4,3,2,1,0:T(8,128)S(1)} %local_0.1.refs_0_, f32[4,2,3,8,128]{4,3,2,1,0:T(8,128)S(1)} %collective-permute-done.8.refs_1_, ...), custom_call_target="tpu_custom_call" | custom-call | flops 368640 | bytes 368640 | tf_op jit(solution)/shard_map/last/pallas_call | solution.py:228
  (13 shorter events, 0.2 us)
Async XLA Ops:
  0.0 9.3 %copy-start = (f32[4,3,4,2,3,3,128]{6,3,5,4,2,1,0:T(2,128)S(1)}, f32[4,3,4,2,3,3,128]{6,3,5,4,2,1,0:T(2,128)}, u32[]{:S(2)}) copy-start(f32[4,3,4,2,3,3,128]{6,3,5,4,2,1,0:T(2,128)} %param.6) | copy-start | bytes 1327108
  0.0 9.3 %copy-start.1 = (f32[4,2,3,8,128]{4,3,2,1,0:T(8,128)S(1)}, f32[4,2,3,8,128]{4,3,2,1,0:T(8,128)}, u32[]{:S(2)}) copy-start(f32[4,2,3,8,128]{4,3,2,1,0:T(8,128)} %adjoint_hbm.1) | copy-start | bytes 294916
  1.1 9.3 %collective-permute-start = (f32[4,2,3,8,128]{4,3,2,1,0:T(8,128)S(1)}, f32[4,2,3,8,128]{4,3,2,1,0:T(8,128)S(1)}, u32[]{:S(2)}, u32[]{:S(2)}) collective-permute-start(f32[4,2,3,8,128]{4,3,2,1,0:T(8,128)S(1)} %get-tuple-element.23), channel_id=1, source_target_pairs={{0,8},{1,9},{2,10},{3,11},{4,12},{5,13},{6,14},{7,15},{8,16},{9,17... | collective-permute-start | bytes 294920 | tf_op jit(solution)/shard_map/ppermute | solution.py:271
  4.2 6.4 %collective-permute-start.1 = (f32[4,2,3,8,128]{4,3,2,1,0:T(8,128)S(1)}, f32[4,2,3,8,128]{4,3,2,1,0:T(8,128)S(1)}, u32[]{:S(2)}, u32[]{:S(2)}) collective-permute-start(f32[4,2,3,8,128]{4,3,2,1,0:T(8,128)S(1)} %get-tuple-element.24), channel_id=1, source_target_pairs={{0,24},{1,25},{2,26},{3,27},{4,28},{5,29},{6,30},{7,31},{8,0},{9,1... | collective-permute-start | bytes 294920 | tf_op jit(solution)/shard_map/ppermute | solution.py:272
  6.2 4.2 %collective-permute-start.2 = (f32[1,2,3,8,128]{4,3,2,1,0:T(8,128)S(1)}, f32[1,2,3,8,128]{4,3,2,1,0:T(8,128)S(1)}, u32[]{:S(2)}, u32[]{:S(2)}) collective-permute-start(f32[1,2,3,8,128]{4,3,2,1,0:T(8,128)S(1)} %get-tuple-element.25), channel_id=1, source_target_pairs={{0,7},{1,2},{2,1},{3,4},{4,3},{5,6},{6,5},{7,0},{8,15},{9,10},{10,... | collective-permute-start | bytes 73736 | tf_op jit(solution)/shard_map/ppermute | solution.py:273
  7.9 2.6 %collective-permute-start.3 = (f32[1,2,3,8,128]{4,3,2,1,0:T(8,128)S(1)}, f32[1,2,3,8,128]{4,3,2,1,0:T(8,128)S(1)}, u32[]{:S(2)}, u32[]{:S(2)}) collective-permute-start(f32[1,2,3,8,128]{4,3,2,1,0:T(8,128)S(1)} %get-tuple-element.26), channel_id=1, source_target_pairs={{0,1},{1,0},{2,3},{3,2},{4,5},{5,4},{6,7},{7,6},{8,9},{9,8},{10,11... | collective-permute-start | bytes 73736 | tf_op jit(solution)/shard_map/ppermute | solution.py:274
  10.7 7.2 %collective-permute-start.4 = (f32[4,2,3,8,128]{4,3,2,1,0:T(8,128)S(1)}, f32[4,2,3,8,128]{4,3,2,1,0:T(8,128)S(1)}, u32[]{:S(2)}, u32[]{:S(2)}) collective-permute-start(f32[4,2,3,8,128]{4,3,2,1,0:T(8,128)S(1)} %get-tuple-element.28), channel_id=1, source_target_pairs={{0,24},{1,25},{2,26},{3,27},{4,28},{5,29},{6,30},{7,31},{8,16},{9,... | collective-permute-start | bytes 294920 | tf_op jit(solution)/shard_map/ppermute | solution.py:265
  13.1 5.4 %collective-permute-start.5 = (f32[4,2,3,8,128]{4,3,2,1,0:T(8,128)S(1)}, f32[4,2,3,8,128]{4,3,2,1,0:T(8,128)S(1)}, u32[]{:S(2)}, u32[]{:S(2)}) collective-permute-start(f32[4,2,3,8,128]{4,3,2,1,0:T(8,128)S(1)} %get-tuple-element.29), channel_id=1, source_target_pairs={{0,8},{1,9},{2,10},{3,11},{4,12},{5,13},{6,14},{7,15},{8,0},{9,1},... | collective-permute-start | bytes 294920 | tf_op jit(solution)/shard_map/ppermute | solution.py:264
  13.1 4.3 %collective-permute-start.6 = (f32[1,2,3,8,128]{4,3,2,1,0:T(8,128)S(1)}, f32[1,2,3,8,128]{4,3,2,1,0:T(8,128)S(1)}, u32[]{:S(2)}, u32[]{:S(2)}) collective-permute-start(f32[1,2,3,8,128]{4,3,2,1,0:T(8,128)S(1)} %get-tuple-element.30), channel_id=1, source_target_pairs={{0,7},{1,2},{2,1},{3,4},{4,3},{5,6},{6,5},{7,0},{8,15},{9,10},{10,... | collective-permute-start | bytes 73736 | tf_op jit(solution)/shard_map/ppermute | solution.py:266
  13.9 3.5 %collective-permute-start.7 = (f32[1,2,3,8,128]{4,3,2,1,0:T(8,128)S(1)}, f32[1,2,3,8,128]{4,3,2,1,0:T(8,128)S(1)}, u32[]{:S(2)}, u32[]{:S(2)}) collective-permute-start(f32[1,2,3,8,128]{4,3,2,1,0:T(8,128)S(1)} %get-tuple-element.31), channel_id=1, source_target_pairs={{0,1},{1,0},{2,3},{3,2},{4,5},{5,4},{6,7},{7,6},{8,9},{9,8},{10,11... | collective-permute-start | bytes 73736 | tf_op jit(solution)/shard_map/ppermute | solution.py:267
  18.7 6.6 %collective-permute-start.8 = (f32[4,2,3,8,128]{4,3,2,1,0:T(8,128)S(1)}, f32[4,2,3,8,128]{4,3,2,1,0:T(8,128)S(1)}, u32[]{:S(2)}, u32[]{:S(2)}) collective-permute-start(f32[4,2,3,8,128]{4,3,2,1,0:T(8,128)S(1)} %get-tuple-element.34), channel_id=1, source_target_pairs={{0,24},{1,25},{2,26},{3,27},{4,28},{5,29},{6,30},{7,31},{8,16},{9,... | collective-permute-start | bytes 294920 | tf_op jit(solution)/shard_map/ppermute | solution.py:265
  20.8 5.5 %collective-permute-start.9 = (f32[4,2,3,8,128]{4,3,2,1,0:T(8,128)S(1)}, f32[4,2,3,8,128]{4,3,2,1,0:T(8,128)S(1)}, u32[]{:S(2)}, u32[]{:S(2)}) collective-permute-start(f32[4,2,3,8,128]{4,3,2,1,0:T(8,128)S(1)} %get-tuple-element.35), channel_id=1, source_target_pairs={{0,8},{1,9},{2,10},{3,11},{4,12},{5,13},{6,14},{7,15},{8,0},{9,1},... | collective-permute-start | bytes 294920 | tf_op jit(solution)/shard_map/ppermute | solution.py:264
  20.8 4.3 %collective-permute-start.10 = (f32[1,2,3,8,128]{4,3,2,1,0:T(8,128)S(1)}, f32[1,2,3,8,128]{4,3,2,1,0:T(8,128)S(1)}, u32[]{:S(2)}, u32[]{:S(2)}) collective-permute-start(f32[1,2,3,8,128]{4,3,2,1,0:T(8,128)S(1)} %get-tuple-element.36), channel_id=1, source_target_pairs={{0,7},{1,2},{2,1},{3,4},{4,3},{5,6},{6,5},{7,0},{8,15},{9,10},{10,... | collective-permute-start | bytes 73736 | tf_op jit(solution)/shard_map/ppermute | solution.py:266
  20.9 4.2 %collective-permute-start.11 = (f32[1,2,3,8,128]{4,3,2,1,0:T(8,128)S(1)}, f32[1,2,3,8,128]{4,3,2,1,0:T(8,128)S(1)}, u32[]{:S(2)}, u32[]{:S(2)}) collective-permute-start(f32[1,2,3,8,128]{4,3,2,1,0:T(8,128)S(1)} %get-tuple-element.37), channel_id=1, source_target_pairs={{0,1},{1,0},{2,3},{3,2},{4,5},{5,4},{6,7},{7,6},{8,9},{9,8},{10,11... | collective-permute-start | bytes 73736 | tf_op jit(solution)/shard_map/ppermute | solution.py:267

commit v25 on v22

--- a/solution.py
+++ b/solution.py
@@ -155,9 +155,7 @@
 
 def arrived_sum(links_ref, link_set, row, rows, arrivals, coefs_ref=None):
     sum_ref, one_ref, two_ref, outer_ref, inner_ref = arrivals
-    if link_set == 0:
-        one_ref, two_ref = two_ref, one_ref
-    _, first_pos, odd_plane, odd_block = place(rows)
+    _, _, odd_plane, _ = place(rows)
     one, two = load_field(one_ref, row), load_field(two_ref, row)
     if coefs_ref is not None:
         below, above = (combine(lambda v: coefs_ref[row + 1] * v, f) for f in (one, two))
@@ -166,6 +164,11 @@
         above = combine(lambda near, far: jnp.where(odd_plane, far, near), one, two)
     ahead_z, _ = transport(links_at(links_ref, row, link_set, 2), above, None)
     total = combine(lambda s, f, h: s + f + h, load_field(sum_ref, row), ahead_z, below)
+    return with_edges(links_ref, link_set, row, rows, total, outer_ref, inner_ref, coefs_ref)
+
+
+def with_edges(links_ref, link_set, row, rows, total, outer_ref, inner_ref, coefs_ref=None):
+    _, first_pos, _, odd_block = place(rows)
     outer, inner = load_field(outer_ref, 0), load_field(inner_ref, 0)
     if row == 0:
         exists = jnp.where(first_pos != 0, 1.0, 0.0)
@@ -210,13 +213,32 @@
     store_t(rows, links_at(links_ref, rows - 1, 0, 3), mixed_ref, outer_ref, inner_ref)
 
 
-def last_kernel(rows, eps_ref, coefs_ref, links_ref, *refs):
-    arrivals, (base_ref, out_hbm, out_ref, sems) = refs[:5], refs[5:]
+def z_term(links_ref, row, field, from_above):
+    ahead, _ = transport(links_at(links_ref, row, 0, 2), field, None)
+    return combine(lambda f, h: jnp.where(from_above, f, h), ahead, field)
+
+
+def partial_kernel(
+    rows, eps_ref, coefs_ref, links_ref, sum_ref, far_ref, outer_ref, inner_ref, base_ref, partial_ref
+):
+    _, _, odd_plane, _ = place(rows)
+    for row in range(rows):
+        inside, eps = coefs_ref[row + 1], eps_ref[...]
+        far = z_term(links_ref, row, load_field(far_ref, row), odd_plane)
+        total = combine(lambda s, f: s + f, load_field(sum_ref, row), far)
+        total = with_edges(links_ref, 0, row, rows, total, outer_ref, inner_ref)
+        store_field(
+            partial_ref, row, combine(lambda p, s: p + inside * (eps * s), load_field(base_ref, row), total)
+        )
+
+
+def last_kernel(rows, eps_ref, coefs_ref, links_ref, near_ref, partial_ref, out_hbm, out_ref, sems):
+    _, _, odd_plane, _ = place(rows)
     copies = []
     for row in range(rows):
         inside, eps = coefs_ref[row + 1], eps_ref[...]
-        total = arrived_sum(links_ref, 0, row, rows, arrivals)
-        store_field(out_ref, row, combine(lambda p, s: p + inside * (eps * s), load_field(base_ref, row), total))
+        near = z_term(links_ref, row, load_field(near_ref, row), ~odd_plane)
+        store_field(out_ref, row, combine(lambda p, s: p + inside * (eps * s), load_field(partial_ref, row), near))
         copies.append(pltpu.make_async_copy(out_ref.at[row], out_hbm.at[row], sems.at[row]))
         copies[-1].start()
     for copy in copies:
@@ -305,9 +327,13 @@
         functools.partial(second_kernel, rows), "second", (eps, coefs, links, local(1, third)) + arrived + (start, third),
         (whole,) + sent + (whole,), 10,
     )
-    arrived = sent_on(*sending, far_first=True)
+    far, near, outer, inner = sent_on(*sending, far_first=True)
+    partial = call(
+        functools.partial(partial_kernel, rows), "partial",
+        (eps, coefs, links, local(0, mixed), far, outer, inner, base), whole, 5,
+    )
     return call(
-        functools.partial(last_kernel, rows), "last", (eps, coefs, links, local(0, mixed)) + arrived + (base,), whole, 5,
+        functools.partial(last_kernel, rows), "last", (eps, coefs, links, near, partial), whole, 4,
         scratch=[pltpu.VMEM(adjoint.shape, jnp.float32), pltpu.SemaphoreType.DMA((rows,))], out_space=pltpu.HBM,
     )
 

time: 26.9 us -> 26.9 us (level)
    pallas_call x9 -> x10, Pallas kernels: 2.92 us -> 2.97 us  [call(): pl.pallas_call(kernel, name=name, out_shape=out_shapes, in_specs=[pl.Bloc...]
where the time goes in v25:
time: 26.9 us; the launch traced here: 26.7 us
  starting transfers between devices  15 us (56%)
  waiting for transfers between devices  6.74 us (25%)
  Pallas kernels  2.97 us (11%)
  between operations  2.02 us (8%)
    ppermute x2, waiting for transfers between devices, sent_on(): outer = lax.ppermute(outer, 'gz', outer_pairs)  4.5 us
    ppermute x2, starting transfers between devices, sent_on(): far = lax.ppermute(far, 'gz', far_pairs)  3.9 us
    ppermute x1, starting transfers between devices, shifted_on(): below = lax.ppermute(up, 'gz', up_pairs)  3.08 us
    pallas_call x10, Pallas kernels, call(): pl.pallas_call(kernel, name=name, out_shape=out_shapes, in_specs=[pl.Bloc...  2.97 us
    ppermute x1, starting transfers between devices, shifted_on(): above = lax.ppermute(down, 'gz', down_pairs)  2.09 us
    ppermute x1, starting transfers between devices, shifted_on(): outer = lax.ppermute(outer, 'gz', outer_pairs)  1.61 us
    ppermute x2, starting transfers between devices, sent_on(): inner = lax.ppermute(inner, 'gz', inner_pairs)  1.57 us
    ppermute x2, starting transfers between devices, sent_on(): outer = lax.ppermute(outer, 'gz', outer_pairs)  1.36 us
  transfers between devices with their start and end apart: 12, of which 6 were waited for; matrix products, arithmetic and copies ran while one was open for 0% of the time, Pallas kernels for 3%

profile of v25, /device:TPU:0, one launch (start us, length us, event | category | flops | bytes accessed | tf_op | source)
XLA Modules:
  0.0 26.7 jit_solution(6606040365893572944)
XLA Ops:
  0.0 1.1 %begin.1 = (f32[4,2,3,8,128]{4,3,2,1,0:T(8,128)S(1)}, f32[4,2,3,8,128]{4,3,2,1,0:T(8,128)S(1)}, f32[1,2,3,8,128]{4,3,2,1,0:T(8,128)S(1)}, f32[1,2,3,8,128]{4,3,2,1,0:T(8,128)S(1)}) custom-call(f32[4,2,3,8,128]{4,3,2,1,0:T(8,128)} %adjoint_hbm.1, f32[864,128]{1,0:T(8,128)} %bitcast.3), custom_call_target="tpu_custom_call" | custom-call | flops 368640 | bytes 368640 | tf_op jit(solution)/shard_map/begin/pallas_call | solution.py:250
  1.1 3.1 %collective-permute-start = (f32[4,2,3,8,128]{4,3,2,1,0:T(8,128)S(1)}, f32[4,2,3,8,128]{4,3,2,1,0:T(8,128)S(1)}, u32[]{:S(2)}, u32[]{:S(2)}) collective-permute-start(f32[4,2,3,8,128]{4,3,2,1,0:T(8,128)S(1)} %get-tuple-element.23), channel_id=1, source_target_pairs={{0,8},{1,9},{2,10},{3,11},{4,12},{5,13},{6,14},{7,15},{8,16},{9,17... | collective-permute-start | bytes 294920 | tf_op jit(solution)/shard_map/ppermute | solution.py:293
  4.2 2.1 %collective-permute-start.1 = (f32[4,2,3,8,128]{4,3,2,1,0:T(8,128)S(1)}, f32[4,2,3,8,128]{4,3,2,1,0:T(8,128)S(1)}, u32[]{:S(2)}, u32[]{:S(2)}) collective-permute-start(f32[4,2,3,8,128]{4,3,2,1,0:T(8,128)S(1)} %get-tuple-element.24), channel_id=1, source_target_pairs={{0,24},{1,25},{2,26},{3,27},{4,28},{5,29},{6,30},{7,31},{8,0},{9,1... | collective-permute-start | bytes 294920 | tf_op jit(solution)/shard_map/ppermute | solution.py:294
  6.2 1.6 %collective-permute-start.2 = (f32[1,2,3,8,128]{4,3,2,1,0:T(8,128)S(1)}, f32[1,2,3,8,128]{4,3,2,1,0:T(8,128)S(1)}, u32[]{:S(2)}, u32[]{:S(2)}) collective-permute-start(f32[1,2,3,8,128]{4,3,2,1,0:T(8,128)S(1)} %get-tuple-element.25), channel_id=1, source_target_pairs={{0,7},{1,2},{2,1},{3,4},{4,3},{5,6},{6,5},{7,0},{8,15},{9,10},{10,... | collective-permute-start | bytes 73736 | tf_op jit(solution)/shard_map/ppermute | solution.py:295
  7.9 0.2 collective-permute-start.3
  9.4 0.3 %start.1 = (f32[4,2,3,8,128]{4,3,2,1,0:T(8,128)S(1)}, f32[4,2,3,8,128]{4,3,2,1,0:T(8,128)S(1)}) custom-call(f32[6,8,128]{2,1,0:T(8,128)S(1)} %tapers.1.coefs_ref, f32[4,2,3,8,128]{4,3,2,1,0:T(8,128)S(1)} %copy-done.1, f32[864,128]{1,0:T(8,128)S(1)} %bitcast.4), custom_call_target="tpu_custom_call" | custom-call | flops 1622016 | bytes 1622016 | tf_op jit(solution)/shard_map/start/pallas_call | solution.py:250
  9.6 0.8 %collective-permute-done.2.refs_3_ = f32[1,2,3,8,128]{4,3,2,1,0:T(8,128)S(1)} collective-permute-done((f32[1,2,3,8,128]{4,3,2,1,0:T(8,128)S(1)}, f32[1,2,3,8,128]{4,3,2,1,0:T(8,128)S(1)}, u32[]{:S(2)}, u32[]{:S(2)}) %collective-permute-start.2) | collective-permute-done | bytes 24608 | tf_op jit(solution)/shard_map/ppermute | solution.py:295
  10.4 0.1 collective-permute-done.1.refs_2_
  10.5 0.1 third.1
  10.7 1.2 %collective-permute-start.4 = (f32[4,2,3,8,128]{4,3,2,1,0:T(8,128)S(1)}, f32[4,2,3,8,128]{4,3,2,1,0:T(8,128)S(1)}, u32[]{:S(2)}, u32[]{:S(2)}) collective-permute-start(f32[4,2,3,8,128]{4,3,2,1,0:T(8,128)S(1)} %get-tuple-element.28), channel_id=1, source_target_pairs={{0,8},{1,9},{2,10},{3,11},{4,12},{5,13},{6,14},{7,15},{8,0},{9,1},... | collective-permute-start | bytes 294920 | tf_op jit(solution)/shard_map/ppermute | solution.py:286
  11.8 1.7 %collective-permute-start.5 = (f32[4,2,3,8,128]{4,3,2,1,0:T(8,128)S(1)}, f32[4,2,3,8,128]{4,3,2,1,0:T(8,128)S(1)}, u32[]{:S(2)}, u32[]{:S(2)}) collective-permute-start(f32[4,2,3,8,128]{4,3,2,1,0:T(8,128)S(1)} %get-tuple-element.29), channel_id=1, source_target_pairs={{0,24},{1,25},{2,26},{3,27},{4,28},{5,29},{6,30},{7,31},{8,16},{9,... | collective-permute-start | bytes 294920 | tf_op jit(solution)/shard_map/ppermute | solution.py:287
  13.6 0.6 %collective-permute-start.6 = (f32[1,2,3,8,128]{4,3,2,1,0:T(8,128)S(1)}, f32[1,2,3,8,128]{4,3,2,1,0:T(8,128)S(1)}, u32[]{:S(2)}, u32[]{:S(2)}) collective-permute-start(f32[1,2,3,8,128]{4,3,2,1,0:T(8,128)S(1)} %get-tuple-element.30), channel_id=1, source_target_pairs={{0,7},{1,2},{2,1},{3,4},{4,3},{5,6},{6,5},{7,0},{8,15},{9,10},{10,... | collective-permute-start | bytes 73736 | tf_op jit(solution)/shard_map/ppermute | solution.py:288
  14.2 0.8 %collective-permute-start.7 = (f32[1,2,3,8,128]{4,3,2,1,0:T(8,128)S(1)}, f32[1,2,3,8,128]{4,3,2,1,0:T(8,128)S(1)}, u32[]{:S(2)}, u32[]{:S(2)}) collective-permute-start(f32[1,2,3,8,128]{4,3,2,1,0:T(8,128)S(1)} %get-tuple-element.31), channel_id=1, source_target_pairs={{0,1},{1,0},{2,3},{3,2},{4,5},{5,4},{6,7},{7,6},{8,9},{9,8},{10,11... | collective-permute-start | bytes 73736 | tf_op jit(solution)/shard_map/ppermute | solution.py:289
  15.6 0.3 %local_1.1.refs_0_ = f32[4,2,3,8,128]{4,3,2,1,0:T(8,128)S(1)} custom-call(f32[4,2,3,8,128]{4,3,2,1,0:T(8,128)S(1)} %get-tuple-element.27.field_ref.refs_6_, f32[864,128]{1,0:T(8,128)S(1)} %bitcast.6), custom_call_target="tpu_custom_call" | custom-call | flops 1622016 | bytes 1622016 | tf_op jit(solution)/shard_map/local_1/pallas_call | solution.py:250
  15.9 2.0 %collective-permute-done.6.refs_3_ = f32[1,2,3,8,128]{4,3,2,1,0:T(8,128)S(1)} collective-permute-done((f32[1,2,3,8,128]{4,3,2,1,0:T(8,128)S(1)}, f32[1,2,3,8,128]{4,3,2,1,0:T(8,128)S(1)}, u32[]{:S(2)}, u32[]{:S(2)}) %collective-permute-start.6) | collective-permute-done | bytes 24608 | tf_op jit(solution)/shard_map/ppermute | solution.py:288
  17.8 0.5 %collective-permute-done.5.refs_2_ = f32[4,2,3,8,128]{4,3,2,1,0:T(8,128)S(1)} collective-permute-done((f32[4,2,3,8,128]{4,3,2,1,0:T(8,128)S(1)}, f32[4,2,3,8,128]{4,3,2,1,0:T(8,128)S(1)}, u32[]{:S(2)}, u32[]{:S(2)}) %collective-permute-start.5) | collective-permute-done | bytes 98336 | tf_op jit(solution)/shard_map/ppermute | solution.py:287
  18.3 0.2 second.1
  18.5 2.2 %collective-permute-start.9 = (f32[4,2,3,8,128]{4,3,2,1,0:T(8,128)S(1)}, f32[4,2,3,8,128]{4,3,2,1,0:T(8,128)S(1)}, u32[]{:S(2)}, u32[]{:S(2)}) collective-permute-start(f32[4,2,3,8,128]{4,3,2,1,0:T(8,128)S(1)} %get-tuple-element.35), channel_id=1, source_target_pairs={{0,24},{1,25},{2,26},{3,27},{4,28},{5,29},{6,30},{7,31},{8,16},{9,... | collective-permute-start | bytes 294920 | tf_op jit(solution)/shard_map/ppermute | solution.py:287
  20.7 0.7 %collective-permute-start.10 = (f32[1,2,3,8,128]{4,3,2,1,0:T(8,128)S(1)}, f32[1,2,3,8,128]{4,3,2,1,0:T(8,128)S(1)}, u32[]{:S(2)}, u32[]{:S(2)}) collective-permute-start(f32[1,2,3,8,128]{4,3,2,1,0:T(8,128)S(1)} %get-tuple-element.36), channel_id=1, source_target_pairs={{0,7},{1,2},{2,1},{3,4},{4,3},{5,6},{6,5},{7,0},{8,15},{9,10},{10,... | collective-permute-start | bytes 73736 | tf_op jit(solution)/shard_map/ppermute | solution.py:288
  21.4 0.8 %collective-permute-start.11 = (f32[1,2,3,8,128]{4,3,2,1,0:T(8,128)S(1)}, f32[1,2,3,8,128]{4,3,2,1,0:T(8,128)S(1)}, u32[]{:S(2)}, u32[]{:S(2)}) collective-permute-start(f32[1,2,3,8,128]{4,3,2,1,0:T(8,128)S(1)} %get-tuple-element.37), channel_id=1, source_target_pairs={{0,1},{1,0},{2,3},{3,2},{4,5},{5,4},{6,7},{7,6},{8,9},{9,8},{10,11... | collective-permute-start | bytes 73736 | tf_op jit(solution)/shard_map/ppermute | solution.py:289
  22.3 0.3 local_0.1.sum_ref
  22.5 2.5 %collective-permute-done.10.outer_ref = f32[1,2,3,8,128]{4,3,2,1,0:T(8,128)S(1)} collective-permute-done((f32[1,2,3,8,128]{4,3,2,1,0:T(8,128)S(1)}, f32[1,2,3,8,128]{4,3,2,1,0:T(8,128)S(1)}, u32[]{:S(2)}, u32[]{:S(2)}) %collective-permute-start.10) | collective-permute-done | bytes 24608 | tf_op jit(solution)/shard_map/ppermute | solution.py:288
  25.1 0.9 %collective-permute-done.8.near_ref = f32[4,2,3,8,128]{4,3,2,1,0:T(8,128)S(1)} collective-permute-done((f32[4,2,3,8,128]{4,3,2,1,0:T(8,128)S(1)}, f32[4,2,3,8,128]{4,3,2,1,0:T(8,128)S(1)}, u32[]{:S(2)}, u32[]{:S(2)}) %collective-permute-start.8) | collective-permute-done | bytes 98336 | tf_op jit(solution)/shard_map/ppermute | solution.py:286
  26.0 0.7 %last.1 = f32[4,2,3,8,128]{4,3,2,1,0:T(8,128)} custom-call(f32[8,128]{1,0:T(8,128)S(1)} %eps.1.eps_ref, f32[6,8,128]{2,1,0:T(8,128)S(1)} %tapers.1.coefs_ref, f32[864,128]{1,0:T(8,128)S(1)} %bitcast.10, f32[4,2,3,8,128]{4,3,2,1,0:T(8,128)S(1)} %collective-permute-done.8.near_ref, f32[4,2,3,8,128]{4,3,2,1,0:T(8,128)S(1)} %partial.1.partial_ref), custom_call_target="tpu_custom_call" | custom-call | flops 294912 | bytes 294912 | tf_op jit(solution)/shard_map/last/pallas_call | solution.py:250
  (14 shorter events, 0.2 us)
Async XLA Ops:
  0.0 9.3 %copy-start = (f32[4,3,4,2,3,3,128]{6,3,5,4,2,1,0:T(2,128)S(1)}, f32[4,3,4,2,3,3,128]{6,3,5,4,2,1,0:T(2,128)}, u32[]{:S(2)}) copy-start(f32[4,3,4,2,3,3,128]{6,3,5,4,2,1,0:T(2,128)} %param.6) | copy-start | bytes 1327108
  0.0 9.3 %copy-start.1 = (f32[4,2,3,8,128]{4,3,2,1,0:T(8,128)S(1)}, f32[4,2,3,8,128]{4,3,2,1,0:T(8,128)}, u32[]{:S(2)}) copy-start(f32[4,2,3,8,128]{4,3,2,1,0:T(8,128)} %adjoint_hbm.1) | copy-start | bytes 294916
  1.1 9.3 %collective-permute-start = (f32[4,2,3,8,128]{4,3,2,1,0:T(8,128)S(1)}, f32[4,2,3,8,128]{4,3,2,1,0:T(8,128)S(1)}, u32[]{:S(2)}, u32[]{:S(2)}) collective-permute-start(f32[4,2,3,8,128]{4,3,2,1,0:T(8,128)S(1)} %get-tuple-element.23), channel_id=1, source_target_pairs={{0,8},{1,9},{2,10},{3,11},{4,12},{5,13},{6,14},{7,15},{8,16},{9,17... | collective-permute-start | bytes 294920 | tf_op jit(solution)/shard_map/ppermute | solution.py:293
  4.2 6.4 %collective-permute-start.1 = (f32[4,2,3,8,128]{4,3,2,1,0:T(8,128)S(1)}, f32[4,2,3,8,128]{4,3,2,1,0:T(8,128)S(1)}, u32[]{:S(2)}, u32[]{:S(2)}) collective-permute-start(f32[4,2,3,8,128]{4,3,2,1,0:T(8,128)S(1)} %get-tuple-element.24), channel_id=1, source_target_pairs={{0,24},{1,25},{2,26},{3,27},{4,28},{5,29},{6,30},{7,31},{8,0},{9,1... | collective-permute-start | bytes 294920 | tf_op jit(solution)/shard_map/ppermute | solution.py:294
  6.2 4.2 %collective-permute-start.2 = (f32[1,2,3,8,128]{4,3,2,1,0:T(8,128)S(1)}, f32[1,2,3,8,128]{4,3,2,1,0:T(8,128)S(1)}, u32[]{:S(2)}, u32[]{:S(2)}) collective-permute-start(f32[1,2,3,8,128]{4,3,2,1,0:T(8,128)S(1)} %get-tuple-element.25), channel_id=1, source_target_pairs={{0,7},{1,2},{2,1},{3,4},{4,3},{5,6},{6,5},{7,0},{8,15},{9,10},{10,... | collective-permute-start | bytes 73736 | tf_op jit(solution)/shard_map/ppermute | solution.py:295
  7.9 2.6 %collective-permute-start.3 = (f32[1,2,3,8,128]{4,3,2,1,0:T(8,128)S(1)}, f32[1,2,3,8,128]{4,3,2,1,0:T(8,128)S(1)}, u32[]{:S(2)}, u32[]{:S(2)}) collective-permute-start(f32[1,2,3,8,128]{4,3,2,1,0:T(8,128)S(1)} %get-tuple-element.26), channel_id=1, source_target_pairs={{0,1},{1,0},{2,3},{3,2},{4,5},{5,4},{6,7},{7,6},{8,9},{9,8},{10,11... | collective-permute-start | bytes 73736 | tf_op jit(solution)/shard_map/ppermute | solution.py:296
  10.7 7.2 %collective-permute-start.4 = (f32[4,2,3,8,128]{4,3,2,1,0:T(8,128)S(1)}, f32[4,2,3,8,128]{4,3,2,1,0:T(8,128)S(1)}, u32[]{:S(2)}, u32[]{:S(2)}) collective-permute-start(f32[4,2,3,8,128]{4,3,2,1,0:T(8,128)S(1)} %get-tuple-element.28), channel_id=1, source_target_pairs={{0,8},{1,9},{2,10},{3,11},{4,12},{5,13},{6,14},{7,15},{8,0},{9,1},... | collective-permute-start | bytes 294920 | tf_op jit(solution)/shard_map/ppermute | solution.py:286
  11.8 6.5 %collective-permute-start.5 = (f32[4,2,3,8,128]{4,3,2,1,0:T(8,128)S(1)}, f32[4,2,3,8,128]{4,3,2,1,0:T(8,128)S(1)}, u32[]{:S(2)}, u32[]{:S(2)}) collective-permute-start(f32[4,2,3,8,128]{4,3,2,1,0:T(8,128)S(1)} %get-tuple-element.29), channel_id=1, source_target_pairs={{0,24},{1,25},{2,26},{3,27},{4,28},{5,29},{6,30},{7,31},{8,16},{9,... | collective-permute-start | bytes 294920 | tf_op jit(solution)/shard_map/ppermute | solution.py:287
  13.6 4.3 %collective-permute-start.6 = (f32[1,2,3,8,128]{4,3,2,1,0:T(8,128)S(1)}, f32[1,2,3,8,128]{4,3,2,1,0:T(8,128)S(1)}, u32[]{:S(2)}, u32[]{:S(2)}) collective-permute-start(f32[1,2,3,8,128]{4,3,2,1,0:T(8,128)S(1)} %get-tuple-element.30), channel_id=1, source_target_pairs={{0,7},{1,2},{2,1},{3,4},{4,3},{5,6},{6,5},{7,0},{8,15},{9,10},{10,... | collective-permute-start | bytes 73736 | tf_op jit(solution)/shard_map/ppermute | solution.py:288
  14.2 3.7 %collective-permute-start.7 = (f32[1,2,3,8,128]{4,3,2,1,0:T(8,128)S(1)}, f32[1,2,3,8,128]{4,3,2,1,0:T(8,128)S(1)}, u32[]{:S(2)}, u32[]{:S(2)}) collective-permute-start(f32[1,2,3,8,128]{4,3,2,1,0:T(8,128)S(1)} %get-tuple-element.31), channel_id=1, source_target_pairs={{0,1},{1,0},{2,3},{3,2},{4,5},{5,4},{6,7},{7,6},{8,9},{9,8},{10,11... | collective-permute-start | bytes 73736 | tf_op jit(solution)/shard_map/ppermute | solution.py:289
  18.5 6.6 %collective-permute-start.9 = (f32[4,2,3,8,128]{4,3,2,1,0:T(8,128)S(1)}, f32[4,2,3,8,128]{4,3,2,1,0:T(8,128)S(1)}, u32[]{:S(2)}, u32[]{:S(2)}) collective-permute-start(f32[4,2,3,8,128]{4,3,2,1,0:T(8,128)S(1)} %get-tuple-element.35), channel_id=1, source_target_pairs={{0,24},{1,25},{2,26},{3,27},{4,28},{5,29},{6,30},{7,31},{8,16},{9,... | collective-permute-start | bytes 294920 | tf_op jit(solution)/shard_map/ppermute | solution.py:287
  20.7 5.3 %collective-permute-start.8 = (f32[4,2,3,8,128]{4,3,2,1,0:T(8,128)S(1)}, f32[4,2,3,8,128]{4,3,2,1,0:T(8,128)S(1)}, u32[]{:S(2)}, u32[]{:S(2)}) collective-permute-start(f32[4,2,3,8,128]{4,3,2,1,0:T(8,128)S(1)} %get-tuple-element.33), channel_id=1, source_target_pairs={{0,8},{1,9},{2,10},{3,11},{4,12},{5,13},{6,14},{7,15},{8,0},{9,1},... | collective-permute-start | bytes 294920 | tf_op jit(solution)/shard_map/ppermute | solution.py:286
  20.7 4.4 %collective-permute-start.10 = (f32[1,2,3,8,128]{4,3,2,1,0:T(8,128)S(1)}, f32[1,2,3,8,128]{4,3,2,1,0:T(8,128)S(1)}, u32[]{:S(2)}, u32[]{:S(2)}) collective-permute-start(f32[1,2,3,8,128]{4,3,2,1,0:T(8,128)S(1)} %get-tuple-element.36), channel_id=1, source_target_pairs={{0,7},{1,2},{2,1},{3,4},{4,3},{5,6},{6,5},{7,0},{8,15},{9,10},{10,... | collective-permute-start | bytes 73736 | tf_op jit(solution)/shard_map/ppermute | solution.py:288
  21.4 3.6 %collective-permute-start.11 = (f32[1,2,3,8,128]{4,3,2,1,0:T(8,128)S(1)}, f32[1,2,3,8,128]{4,3,2,1,0:T(8,128)S(1)}, u32[]{:S(2)}, u32[]{:S(2)}) collective-permute-start(f32[1,2,3,8,128]{4,3,2,1,0:T(8,128)S(1)} %get-tuple-element.37), channel_id=1, source_target_pairs={{0,1},{1,0},{2,3},{3,2},{4,5},{5,4},{6,7},{7,6},{8,9},{9,8},{10,11... | collective-permute-start | bytes 73736 | tf_op jit(solution)/shard_map/ppermute | solution.py:289

commit v26 on v25

--- a/solution.py
+++ b/solution.py
@@ -196,12 +196,27 @@
     store_t(rows, links_at(links_ref, rows - 1, 1, 3), third_ref, outer_ref, inner_ref)
 
 
+def z_term(links_ref, link_set, row, field, from_above):
+    ahead, _ = transport(links_at(links_ref, row, link_set, 2), field, None)
+    return combine(lambda f, h: jnp.where(from_above, f, h), ahead, field)
+
+
+def waiting_kernel(rows, links_ref, sum_ref, near_ref, outer_ref, inner_ref, total_ref):
+    _, _, odd_plane, _ = place(rows)
+    for row in range(rows):
+        near = z_term(links_ref, 1, row, load_field(near_ref, row), ~odd_plane)
+        total = combine(lambda s, f: s + f, load_field(sum_ref, row), near)
+        store_field(total_ref, row, with_edges(links_ref, 1, row, rows, total, outer_ref, inner_ref))
+
+
 def second_kernel(rows, eps_ref, coefs_ref, links_ref, *refs):
-    arrivals, (start_ref, third_ref, mixed_ref, far_ref, near_ref, outer_ref, inner_ref, base_ref) = refs[:5], refs[5:]
+    total_ref, came_ref, start_ref, third_ref, mixed_ref, far_ref, near_ref, outer_ref, inner_ref, base_ref = refs
+    _, _, odd_plane, _ = place(rows)
     eps = eps_ref[...]
     for row in range(rows):
         inside = coefs_ref[row + 1]
-        total = arrived_sum(links_ref, 1, row, rows, arrivals)
+        far = z_term(links_ref, 1, row, load_field(came_ref, row), odd_plane)
+        total = combine(lambda s, f: s + f, load_field(total_ref, row), far)
         third = combine(lambda v: eps * v, load_field(third_ref, row))
         second = combine(
             lambda v, s: v + (8.0 / 9.0) * (inside * (eps * (eps * s))), load_field(start_ref, row), total
@@ -213,18 +228,13 @@
     store_t(rows, links_at(links_ref, rows - 1, 0, 3), mixed_ref, outer_ref, inner_ref)
 
 
-def z_term(links_ref, row, field, from_above):
-    ahead, _ = transport(links_at(links_ref, row, 0, 2), field, None)
-    return combine(lambda f, h: jnp.where(from_above, f, h), ahead, field)
-
-
 def partial_kernel(
     rows, eps_ref, coefs_ref, links_ref, sum_ref, far_ref, outer_ref, inner_ref, base_ref, partial_ref
 ):
     _, _, odd_plane, _ = place(rows)
     for row in range(rows):
         inside, eps = coefs_ref[row + 1], eps_ref[...]
-        far = z_term(links_ref, row, load_field(far_ref, row), odd_plane)
+        far = z_term(links_ref, 0, row, load_field(far_ref, row), odd_plane)
         total = combine(lambda s, f: s + f, load_field(sum_ref, row), far)
         total = with_edges(links_ref, 0, row, rows, total, outer_ref, inner_ref)
         store_field(
@@ -237,7 +247,7 @@
     copies = []
     for row in range(rows):
         inside, eps = coefs_ref[row + 1], eps_ref[...]
-        near = z_term(links_ref, row, load_field(near_ref, row), ~odd_plane)
+        near = z_term(links_ref, 0, row, load_field(near_ref, row), ~odd_plane)
         store_field(out_ref, row, combine(lambda p, s: p + inside * (eps * s), load_field(partial_ref, row), near))
         copies.append(pltpu.make_async_copy(out_ref.at[row], out_hbm.at[row], sems.at[row]))
         copies[-1].start()
@@ -322,9 +332,12 @@
     third, *sending = call(
         functools.partial(third_kernel, rows), "third", (coefs, links, total) + arrived, (whole,) + sent, 10
     )
-    arrived = sent_on(*sending, far_first=False)
+    near, far, outer, inner = sent_on(*sending, far_first=False)
+    total = call(
+        functools.partial(waiting_kernel, rows), "waiting", (links, local(1, third), near, outer, inner), whole, 5
+    )
     mixed, *sending, base = call(
-        functools.partial(second_kernel, rows), "second", (eps, coefs, links, local(1, third)) + arrived + (start, third),
+        functools.partial(second_kernel, rows), "second", (eps, coefs, links, total, far, start, third),
         (whole,) + sent + (whole,), 10,
     )
     far, near, outer, inner = sent_on(*sending, far_first=True)

time: 26.9 us -> 26.9 us (level)
    pallas_call x10 -> x11, Pallas kernels: 2.97 us -> 3.02 us  [call(): pl.pallas_call(kernel, name=name, out_shape=out_shapes, in_specs=[pl.Bloc...]
  transfers between devices with their start and end apart: 12 -> 12, of which waited for: 6 -> 6; matrix products, arithmetic and copies ran while one was open for 0% -> 0% of each run, Pallas kernels for 3% -> 4%
where the time goes in v26:
time: 26.9 us; the launch traced here: 26.7 us
  starting transfers between devices  15 us (56%)
  waiting for transfers between devices  6.67 us (25%)
  Pallas kernels  3.02 us (11%)
  between operations  2.03 us (8%)
    ppermute x2, waiting for transfers between devices, sent_on(): outer = lax.ppermute(outer, 'gz', outer_pairs)  4.5 us
    ppermute x2, starting transfers between devices, sent_on(): far = lax.ppermute(far, 'gz', far_pairs)  3.9 us
    ppermute x1, starting transfers between devices, shifted_on(): below = lax.ppermute(up, 'gz', up_pairs)  3.08 us
    pallas_call x11, Pallas kernels, call(): pl.pallas_call(kernel, name=name, out_shape=out_shapes, in_specs=[pl.Bloc...  3.02 us
    ppermute x1, starting transfers between devices, shifted_on(): above = lax.ppermute(down, 'gz', down_pairs)  2.09 us
    ppermute x1, starting transfers between devices, shifted_on(): outer = lax.ppermute(outer, 'gz', outer_pairs)  1.61 us
    ppermute x2, starting transfers between devices, sent_on(): inner = lax.ppermute(inner, 'gz', inner_pairs)  1.51 us
    ppermute x2, starting transfers between devices, sent_on(): outer = lax.ppermute(outer, 'gz', outer_pairs)  1.43 us
  transfers between devices with their start and end apart: 12, of which 6 were waited for; matrix products, arithmetic and copies ran while one was open for 0% of the time, Pallas kernels for 4%

profile of v26, /device:TPU:0, one launch (start us, length us, event | category | flops | bytes accessed | tf_op | source)
XLA Modules:
  0.0 26.7 jit_solution(9397268506300244396)
XLA Ops:
  0.0 1.1 %begin.1 = (f32[4,2,3,8,128]{4,3,2,1,0:T(8,128)S(1)}, f32[4,2,3,8,128]{4,3,2,1,0:T(8,128)S(1)}, f32[1,2,3,8,128]{4,3,2,1,0:T(8,128)S(1)}, f32[1,2,3,8,128]{4,3,2,1,0:T(8,128)S(1)}) custom-call(f32[4,2,3,8,128]{4,3,2,1,0:T(8,128)} %adjoint_hbm.1, f32[864,128]{1,0:T(8,128)} %bitcast.3), custom_call_target="tpu_custom_call" | custom-call | flops 368640 | bytes 368640 | tf_op jit(solution)/shard_map/begin/pallas_call | solution.py:260
  1.1 3.1 %collective-permute-start = (f32[4,2,3,8,128]{4,3,2,1,0:T(8,128)S(1)}, f32[4,2,3,8,128]{4,3,2,1,0:T(8,128)S(1)}, u32[]{:S(2)}, u32[]{:S(2)}) collective-permute-start(f32[4,2,3,8,128]{4,3,2,1,0:T(8,128)S(1)} %get-tuple-element.23), channel_id=1, source_target_pairs={{0,8},{1,9},{2,10},{3,11},{4,12},{5,13},{6,14},{7,15},{8,16},{9,17... | collective-permute-start | bytes 294920 | tf_op jit(solution)/shard_map/ppermute | solution.py:303
  4.2 2.1 %collective-permute-start.1 = (f32[4,2,3,8,128]{4,3,2,1,0:T(8,128)S(1)}, f32[4,2,3,8,128]{4,3,2,1,0:T(8,128)S(1)}, u32[]{:S(2)}, u32[]{:S(2)}) collective-permute-start(f32[4,2,3,8,128]{4,3,2,1,0:T(8,128)S(1)} %get-tuple-element.24), channel_id=1, source_target_pairs={{0,24},{1,25},{2,26},{3,27},{4,28},{5,29},{6,30},{7,31},{8,0},{9,1... | collective-permute-start | bytes 294920 | tf_op jit(solution)/shard_map/ppermute | solution.py:304
  6.2 1.6 %collective-permute-start.2 = (f32[1,2,3,8,128]{4,3,2,1,0:T(8,128)S(1)}, f32[1,2,3,8,128]{4,3,2,1,0:T(8,128)S(1)}, u32[]{:S(2)}, u32[]{:S(2)}) collective-permute-start(f32[1,2,3,8,128]{4,3,2,1,0:T(8,128)S(1)} %get-tuple-element.25), channel_id=1, source_target_pairs={{0,7},{1,2},{2,1},{3,4},{4,3},{5,6},{6,5},{7,0},{8,15},{9,10},{10,... | collective-permute-start | bytes 73736 | tf_op jit(solution)/shard_map/ppermute | solution.py:305
  7.9 0.2 collective-permute-start.3
  9.4 0.3 %start.1 = (f32[4,2,3,8,128]{4,3,2,1,0:T(8,128)S(1)}, f32[4,2,3,8,128]{4,3,2,1,0:T(8,128)S(1)}) custom-call(f32[6,8,128]{2,1,0:T(8,128)S(1)} %tapers.1.coefs_ref, f32[4,2,3,8,128]{4,3,2,1,0:T(8,128)S(1)} %copy-done.1, f32[864,128]{1,0:T(8,128)S(1)} %bitcast.4), custom_call_target="tpu_custom_call" | custom-call | flops 1622016 | bytes 1622016 | tf_op jit(solution)/shard_map/start/pallas_call | solution.py:260
  9.6 0.8 %collective-permute-done.2.refs_3_ = f32[1,2,3,8,128]{4,3,2,1,0:T(8,128)S(1)} collective-permute-done((f32[1,2,3,8,128]{4,3,2,1,0:T(8,128)S(1)}, f32[1,2,3,8,128]{4,3,2,1,0:T(8,128)S(1)}, u32[]{:S(2)}, u32[]{:S(2)}) %collective-permute-start.2) | collective-permute-done | bytes 24608 | tf_op jit(solution)/shard_map/ppermute | solution.py:305
  10.4 0.1 collective-permute-done.1.refs_2_
  10.5 0.1 third.1
  10.7 1.2 %collective-permute-start.4 = (f32[4,2,3,8,128]{4,3,2,1,0:T(8,128)S(1)}, f32[4,2,3,8,128]{4,3,2,1,0:T(8,128)S(1)}, u32[]{:S(2)}, u32[]{:S(2)}) collective-permute-start(f32[4,2,3,8,128]{4,3,2,1,0:T(8,128)S(1)} %get-tuple-element.28), channel_id=1, source_target_pairs={{0,8},{1,9},{2,10},{3,11},{4,12},{5,13},{6,14},{7,15},{8,0},{9,1},... | collective-permute-start | bytes 294920 | tf_op jit(solution)/shard_map/ppermute | solution.py:296
  11.8 1.7 %collective-permute-start.7 = (f32[4,2,3,8,128]{4,3,2,1,0:T(8,128)S(1)}, f32[4,2,3,8,128]{4,3,2,1,0:T(8,128)S(1)}, u32[]{:S(2)}, u32[]{:S(2)}) collective-permute-start(f32[4,2,3,8,128]{4,3,2,1,0:T(8,128)S(1)} %get-tuple-element.31), channel_id=1, source_target_pairs={{0,24},{1,25},{2,26},{3,27},{4,28},{5,29},{6,30},{7,31},{8,16},{9,... | collective-permute-start | bytes 294920 | tf_op jit(solution)/shard_map/ppermute | solution.py:297
  13.6 0.6 %collective-permute-start.5 = (f32[1,2,3,8,128]{4,3,2,1,0:T(8,128)S(1)}, f32[1,2,3,8,128]{4,3,2,1,0:T(8,128)S(1)}, u32[]{:S(2)}, u32[]{:S(2)}) collective-permute-start(f32[1,2,3,8,128]{4,3,2,1,0:T(8,128)S(1)} %get-tuple-element.29), channel_id=1, source_target_pairs={{0,7},{1,2},{2,1},{3,4},{4,3},{5,6},{6,5},{7,0},{8,15},{9,10},{10,... | collective-permute-start | bytes 73736 | tf_op jit(solution)/shard_map/ppermute | solution.py:298
  14.2 0.8 %collective-permute-start.6 = (f32[1,2,3,8,128]{4,3,2,1,0:T(8,128)S(1)}, f32[1,2,3,8,128]{4,3,2,1,0:T(8,128)S(1)}, u32[]{:S(2)}, u32[]{:S(2)}) collective-permute-start(f32[1,2,3,8,128]{4,3,2,1,0:T(8,128)S(1)} %get-tuple-element.30), channel_id=1, source_target_pairs={{0,1},{1,0},{2,3},{3,2},{4,5},{5,4},{6,7},{7,6},{8,9},{9,8},{10,11... | collective-permute-start | bytes 73736 | tf_op jit(solution)/shard_map/ppermute | solution.py:299
  15.6 0.3 local_1.1.sum_ref
  15.9 2.0 %collective-permute-done.5.outer_ref = f32[1,2,3,8,128]{4,3,2,1,0:T(8,128)S(1)} collective-permute-done((f32[1,2,3,8,128]{4,3,2,1,0:T(8,128)S(1)}, f32[1,2,3,8,128]{4,3,2,1,0:T(8,128)S(1)}, u32[]{:S(2)}, u32[]{:S(2)}) %collective-permute-start.5) | collective-permute-done | bytes 24608 | tf_op jit(solution)/shard_map/ppermute | solution.py:298
  17.9 0.4 %collective-permute-done.7.refs_1_ = f32[4,2,3,8,128]{4,3,2,1,0:T(8,128)S(1)} collective-permute-done((f32[4,2,3,8,128]{4,3,2,1,0:T(8,128)S(1)}, f32[4,2,3,8,128]{4,3,2,1,0:T(8,128)S(1)}, u32[]{:S(2)}, u32[]{:S(2)}) %collective-permute-start.7) | collective-permute-done | bytes 98336 | tf_op jit(solution)/shard_map/ppermute | solution.py:297
  18.3 0.1 second.1
  18.5 2.2 %collective-permute-start.9 = (f32[4,2,3,8,128]{4,3,2,1,0:T(8,128)S(1)}, f32[4,2,3,8,128]{4,3,2,1,0:T(8,128)S(1)}, u32[]{:S(2)}, u32[]{:S(2)}) collective-permute-start(f32[4,2,3,8,128]{4,3,2,1,0:T(8,128)S(1)} %get-tuple-element.35), channel_id=1, source_target_pairs={{0,24},{1,25},{2,26},{3,27},{4,28},{5,29},{6,30},{7,31},{8,16},{9,... | collective-permute-start | bytes 294920 | tf_op jit(solution)/shard_map/ppermute | solution.py:297
  20.7 0.8 %collective-permute-start.10 = (f32[1,2,3,8,128]{4,3,2,1,0:T(8,128)S(1)}, f32[1,2,3,8,128]{4,3,2,1,0:T(8,128)S(1)}, u32[]{:S(2)}, u32[]{:S(2)}) collective-permute-start(f32[1,2,3,8,128]{4,3,2,1,0:T(8,128)S(1)} %get-tuple-element.36), channel_id=1, source_target_pairs={{0,7},{1,2},{2,1},{3,4},{4,3},{5,6},{6,5},{7,0},{8,15},{9,10},{10,... | collective-permute-start | bytes 73736 | tf_op jit(solution)/shard_map/ppermute | solution.py:298
  21.5 0.8 %collective-permute-start.11 = (f32[1,2,3,8,128]{4,3,2,1,0:T(8,128)S(1)}, f32[1,2,3,8,128]{4,3,2,1,0:T(8,128)S(1)}, u32[]{:S(2)}, u32[]{:S(2)}) collective-permute-start(f32[1,2,3,8,128]{4,3,2,1,0:T(8,128)S(1)} %get-tuple-element.37), channel_id=1, source_target_pairs={{0,1},{1,0},{2,3},{3,2},{4,5},{5,4},{6,7},{7,6},{8,9},{9,8},{10,11... | collective-permute-start | bytes 73736 | tf_op jit(solution)/shard_map/ppermute | solution.py:299
  22.2 0.3 local_0.1.sum_ref
  22.5 2.5 %collective-permute-done.10.outer_ref = f32[1,2,3,8,128]{4,3,2,1,0:T(8,128)S(1)} collective-permute-done((f32[1,2,3,8,128]{4,3,2,1,0:T(8,128)S(1)}, f32[1,2,3,8,128]{4,3,2,1,0:T(8,128)S(1)}, u32[]{:S(2)}, u32[]{:S(2)}) %collective-permute-start.10) | collective-permute-done | bytes 24608 | tf_op jit(solution)/shard_map/ppermute | solution.py:298
  25.1 0.9 %collective-permute-done.8.near_ref = f32[4,2,3,8,128]{4,3,2,1,0:T(8,128)S(1)} collective-permute-done((f32[4,2,3,8,128]{4,3,2,1,0:T(8,128)S(1)}, f32[4,2,3,8,128]{4,3,2,1,0:T(8,128)S(1)}, u32[]{:S(2)}, u32[]{:S(2)}) %collective-permute-start.8) | collective-permute-done | bytes 98336 | tf_op jit(solution)/shard_map/ppermute | solution.py:296
  26.0 0.7 %last.1 = f32[4,2,3,8,128]{4,3,2,1,0:T(8,128)} custom-call(f32[8,128]{1,0:T(8,128)S(1)} %eps.1.eps_ref, f32[6,8,128]{2,1,0:T(8,128)S(1)} %tapers.1.coefs_ref, f32[864,128]{1,0:T(8,128)S(1)} %bitcast.11, f32[4,2,3,8,128]{4,3,2,1,0:T(8,128)S(1)} %collective-permute-done.8.near_ref, f32[4,2,3,8,128]{4,3,2,1,0:T(8,128)S(1)} %partial.1.partial_ref), custom_call_target="tpu_custom_call" | custom-call | flops 294912 | bytes 294912 | tf_op jit(solution)/shard_map/last/pallas_call | solution.py:260
  (15 shorter events, 0.2 us)
Async XLA Ops:
  0.0 9.3 %copy-start = (f32[4,3,4,2,3,3,128]{6,3,5,4,2,1,0:T(2,128)S(1)}, f32[4,3,4,2,3,3,128]{6,3,5,4,2,1,0:T(2,128)}, u32[]{:S(2)}) copy-start(f32[4,3,4,2,3,3,128]{6,3,5,4,2,1,0:T(2,128)} %param.6) | copy-start | bytes 1327108
  0.0 9.3 %copy-start.1 = (f32[4,2,3,8,128]{4,3,2,1,0:T(8,128)S(1)}, f32[4,2,3,8,128]{4,3,2,1,0:T(8,128)}, u32[]{:S(2)}) copy-start(f32[4,2,3,8,128]{4,3,2,1,0:T(8,128)} %adjoint_hbm.1) | copy-start | bytes 294916
  1.1 9.3 %collective-permute-start = (f32[4,2,3,8,128]{4,3,2,1,0:T(8,128)S(1)}, f32[4,2,3,8,128]{4,3,2,1,0:T(8,128)S(1)}, u32[]{:S(2)}, u32[]{:S(2)}) collective-permute-start(f32[4,2,3,8,128]{4,3,2,1,0:T(8,128)S(1)} %get-tuple-element.23), channel_id=1, source_target_pairs={{0,8},{1,9},{2,10},{3,11},{4,12},{5,13},{6,14},{7,15},{8,16},{9,17... | collective-permute-start | bytes 294920 | tf_op jit(solution)/shard_map/ppermute | solution.py:303
  4.2 6.4 %collective-permute-start.1 = (f32[4,2,3,8,128]{4,3,2,1,0:T(8,128)S(1)}, f32[4,2,3,8,128]{4,3,2,1,0:T(8,128)S(1)}, u32[]{:S(2)}, u32[]{:S(2)}) collective-permute-start(f32[4,2,3,8,128]{4,3,2,1,0:T(8,128)S(1)} %get-tuple-element.24), channel_id=1, source_target_pairs={{0,24},{1,25},{2,26},{3,27},{4,28},{5,29},{6,30},{7,31},{8,0},{9,1... | collective-permute-start | bytes 294920 | tf_op jit(solution)/shard_map/ppermute | solution.py:304
  6.2 4.2 %collective-permute-start.2 = (f32[1,2,3,8,128]{4,3,2,1,0:T(8,128)S(1)}, f32[1,2,3,8,128]{4,3,2,1,0:T(8,128)S(1)}, u32[]{:S(2)}, u32[]{:S(2)}) collective-permute-start(f32[1,2,3,8,128]{4,3,2,1,0:T(8,128)S(1)} %get-tuple-element.25), channel_id=1, source_target_pairs={{0,7},{1,2},{2,1},{3,4},{4,3},{5,6},{6,5},{7,0},{8,15},{9,10},{10,... | collective-permute-start | bytes 73736 | tf_op jit(solution)/shard_map/ppermute | solution.py:305
  7.9 2.6 %collective-permute-start.3 = (f32[1,2,3,8,128]{4,3,2,1,0:T(8,128)S(1)}, f32[1,2,3,8,128]{4,3,2,1,0:T(8,128)S(1)}, u32[]{:S(2)}, u32[]{:S(2)}) collective-permute-start(f32[1,2,3,8,128]{4,3,2,1,0:T(8,128)S(1)} %get-tuple-element.26), channel_id=1, source_target_pairs={{0,1},{1,0},{2,3},{3,2},{4,5},{5,4},{6,7},{7,6},{8,9},{9,8},{10,11... | collective-permute-start | bytes 73736 | tf_op jit(solution)/shard_map/ppermute | solution.py:306
  10.7 7.2 %collective-permute-start.4 = (f32[4,2,3,8,128]{4,3,2,1,0:T(8,128)S(1)}, f32[4,2,3,8,128]{4,3,2,1,0:T(8,128)S(1)}, u32[]{:S(2)}, u32[]{:S(2)}) collective-permute-start(f32[4,2,3,8,128]{4,3,2,1,0:T(8,128)S(1)} %get-tuple-element.28), channel_id=1, source_target_pairs={{0,8},{1,9},{2,10},{3,11},{4,12},{5,13},{6,14},{7,15},{8,0},{9,1},... | collective-permute-start | bytes 294920 | tf_op jit(solution)/shard_map/ppermute | solution.py:296
  11.8 6.5 %collective-permute-start.7 = (f32[4,2,3,8,128]{4,3,2,1,0:T(8,128)S(1)}, f32[4,2,3,8,128]{4,3,2,1,0:T(8,128)S(1)}, u32[]{:S(2)}, u32[]{:S(2)}) collective-permute-start(f32[4,2,3,8,128]{4,3,2,1,0:T(8,128)S(1)} %get-tuple-element.31), channel_id=1, source_target_pairs={{0,24},{1,25},{2,26},{3,27},{4,28},{5,29},{6,30},{7,31},{8,16},{9,... | collective-permute-start | bytes 294920 | tf_op jit(solution)/shard_map/ppermute | solution.py:297
  13.6 4.3 %collective-permute-start.5 = (f32[1,2,3,8,128]{4,3,2,1,0:T(8,128)S(1)}, f32[1,2,3,8,128]{4,3,2,1,0:T(8,128)S(1)}, u32[]{:S(2)}, u32[]{:S(2)}) collective-permute-start(f32[1,2,3,8,128]{4,3,2,1,0:T(8,128)S(1)} %get-tuple-element.29), channel_id=1, source_target_pairs={{0,7},{1,2},{2,1},{3,4},{4,3},{5,6},{6,5},{7,0},{8,15},{9,10},{10,... | collective-permute-start | bytes 73736 | tf_op jit(solution)/shard_map/ppermute | solution.py:298
  14.2 3.7 %collective-permute-start.6 = (f32[1,2,3,8,128]{4,3,2,1,0:T(8,128)S(1)}, f32[1,2,3,8,128]{4,3,2,1,0:T(8,128)S(1)}, u32[]{:S(2)}, u32[]{:S(2)}) collective-permute-start(f32[1,2,3,8,128]{4,3,2,1,0:T(8,128)S(1)} %get-tuple-element.30), channel_id=1, source_target_pairs={{0,1},{1,0},{2,3},{3,2},{4,5},{5,4},{6,7},{7,6},{8,9},{9,8},{10,11... | collective-permute-start | bytes 73736 | tf_op jit(solution)/shard_map/ppermute | solution.py:299
  18.5 6.6 %collective-permute-start.9 = (f32[4,2,3,8,128]{4,3,2,1,0:T(8,128)S(1)}, f32[4,2,3,8,128]{4,3,2,1,0:T(8,128)S(1)}, u32[]{:S(2)}, u32[]{:S(2)}) collective-permute-start(f32[4,2,3,8,128]{4,3,2,1,0:T(8,128)S(1)} %get-tuple-element.35), channel_id=1, source_target_pairs={{0,24},{1,25},{2,26},{3,27},{4,28},{5,29},{6,30},{7,31},{8,16},{9,... | collective-permute-start | bytes 294920 | tf_op jit(solution)/shard_map/ppermute | solution.py:297
  20.7 5.3 %collective-permute-start.8 = (f32[4,2,3,8,128]{4,3,2,1,0:T(8,128)S(1)}, f32[4,2,3,8,128]{4,3,2,1,0:T(8,128)S(1)}, u32[]{:S(2)}, u32[]{:S(2)}) collective-permute-start(f32[4,2,3,8,128]{4,3,2,1,0:T(8,128)S(1)} %get-tuple-element.33), channel_id=1, source_target_pairs={{0,8},{1,9},{2,10},{3,11},{4,12},{5,13},{6,14},{7,15},{8,0},{9,1},... | collective-permute-start | bytes 294920 | tf_op jit(solution)/shard_map/ppermute | solution.py:296
  20.7 4.4 %collective-permute-start.10 = (f32[1,2,3,8,128]{4,3,2,1,0:T(8,128)S(1)}, f32[1,2,3,8,128]{4,3,2,1,0:T(8,128)S(1)}, u32[]{:S(2)}, u32[]{:S(2)}) collective-permute-start(f32[1,2,3,8,128]{4,3,2,1,0:T(8,128)S(1)} %get-tuple-element.36), channel_id=1, source_target_pairs={{0,7},{1,2},{2,1},{3,4},{4,3},{5,6},{6,5},{7,0},{8,15},{9,10},{10,... | collective-permute-start | bytes 73736 | tf_op jit(solution)/shard_map/ppermute | solution.py:298
  21.5 3.5 %collective-permute-start.11 = (f32[1,2,3,8,128]{4,3,2,1,0:T(8,128)S(1)}, f32[1,2,3,8,128]{4,3,2,1,0:T(8,128)S(1)}, u32[]{:S(2)}, u32[]{:S(2)}) collective-permute-start(f32[1,2,3,8,128]{4,3,2,1,0:T(8,128)S(1)} %get-tuple-element.37), channel_id=1, source_target_pairs={{0,1},{1,0},{2,3},{3,2},{4,5},{5,4},{6,7},{7,6},{8,9},{9,8},{10,11... | collective-permute-start | bytes 73736 | tf_op jit(solution)/shard_map/ppermute | solution.py:299
